TPU v7x, 32 devices: a whole 2x2x4 slice. The times are simulated.
32 devices in a mesh: rep: 8 (over y, x, core), exp: 4 (over z).
Axes of the slice: x: 2, y: 2, z: 4, core: 2. Of those that a mesh axis runs over, the one named last changes fastest.
Arguments:
- tubelets: bfloat16 [4096, 1536], P(('rep', 'exp')), may hold values from -6 to 6
- embed_weight: bfloat16 [1536, 1024], replicated, may hold values from -0.15625 to 0.15625
- norm_gain: float32 [1024], replicated, may hold values from 0.1 to 1.9
- routes: int32 [4096, 2], P(('rep', 'exp')), may hold values from 0 to 31, all different within a row; in each aligned block of 128 rows (0 to 127, 128 to 255, ...) at most 12 rows name the same one
- gate_codes: int32 [4096, 2], P(('rep', 'exp')), may hold values from 0 to 8
- w_in: bfloat16 [32, 1024, 4096], P('exp', None, 'rep'), may hold values from -0.1875 to 0.1875
- w_down: bfloat16 [32, 1024, 4096], P('exp', None, 'rep'), may hold values from -0.09375 to 0.09375
Outputs:
- layer_out: bfloat16 [4096, 1024], P(('rep', 'exp'))
Inputs may be any that keep to these rules, and one draw needn't show every extreme that they name: Within each device's aligned block of 128 tokens no expert is named by more than 12 routes, a bound that some block reaches; a token's two experts differ.
All inputs are finite; a program needn't handle non-finite values.
Results may differ from a plain program's by a relative error of at most 0.012.
Values may be sent and summed in bfloat16 or wider, within the bound.
No kernel may reach another device: no remote copies, remote signals or barrier semaphores. Data moves between devices by JAX's collectives and lax.ppermute only.
A program may use at most 128 MiB of HBM per device.

v0:
```python
import jax
import jax.numpy as jnp
from jax import lax
from jax.sharding import PartitionSpec as P


def swapped(array, axis, distance):
    return lax.ppermute(array, axis, [(i, i ^ 1 << distance) for i in range(lax.axis_size(axis))])


def layer_norm(values, norm_gain):
    floats = values.astype(jnp.float32)
    average = jnp.mean(floats, axis=-1, keepdims=True)
    centred = floats - average
    variance = jnp.mean(centred * centred, axis=-1, keepdims=True)
    return (centred * lax.rsqrt(variance + 1e-06) * norm_gain).astype(jnp.bfloat16)


def on_device(tubelets, embed_weight, norm_gain, routes, gate_codes, w_in, w_down):
    embedded = jnp.dot(tubelets, embed_weight, preferred_element_type=jnp.float32).astype(
        jnp.bfloat16
    )
    normed = layer_norm(embedded, norm_gain)
    tok_count = tubelets.shape[0]
    model_width = embedded.shape[1]
    local_experts = w_in.shape[0]
    experts_all = local_experts * lax.axis_size("exp")
    capacity = 3 * tok_count // experts_all
    flat_routes = routes.reshape(-1)
    onehot = (flat_routes[:, None] == jnp.arange(experts_all, dtype=jnp.int32)[None, :]).astype(
        jnp.int32
    )
    slot_rank = jnp.sum((jnp.cumsum(onehot, axis=0) - 1) * onehot, axis=1)
    target = flat_routes * capacity + slot_rank
    rows_rep = jnp.repeat(normed, 2, axis=0)
    buffer = jnp.zeros((experts_all * capacity, model_width), jnp.bfloat16).at[target].set(rows_rep)
    buffer = buffer.reshape(experts_all, capacity, model_width)
    arrived = lax.all_to_all(buffer, "exp", split_axis=0, concat_axis=1, tiled=True)
    group_bits = 3
    position = lax.axis_index("rep")
    rep_bits = lax.axis_size("rep").bit_length() - 1
    collected = arrived
    for bit in range(group_bits):
        partner = swapped(collected, "rep", bit)
        upper = position // (1 << bit) % 2 == 1
        collected = jnp.where(
            upper,
            jnp.concatenate([partner, collected], axis=1),
            jnp.concatenate([collected, partner], axis=1),
        )
    panels = jnp.stack([w_in, w_down], axis=0)
    for bit in range(group_bits, rep_bits):
        partner = swapped(panels, "rep", bit)
        upper = position // (1 << bit) % 2 == 1
        panels = jnp.where(
            upper,
            jnp.concatenate([partner, panels], axis=3),
            jnp.concatenate([panels, partner], axis=3),
        )
    hidden = jax.nn.gelu(
        jnp.einsum("erd,edf->erf", collected, panels[0], preferred_element_type=jnp.float32)
    ).astype(jnp.bfloat16)
    partial_out = jnp.einsum("erf,edf->erd", hidden, panels[1], preferred_element_type=jnp.float32)
    for bit in range(group_bits - 1, -1, -1):
        half_rows = partial_out.shape[1] // 2
        lower_half = partial_out[:, :half_rows]
        upper_half = partial_out[:, half_rows:]
        upper = position // (1 << bit) % 2 == 1
        keeping = jnp.where(upper, upper_half, lower_half)
        sending = jnp.where(upper, lower_half, upper_half)
        partial_out = keeping + swapped(sending, "rep", bit)
    expert_out = partial_out.astype(jnp.bfloat16)
    returned = lax.all_to_all(expert_out, "exp", split_axis=1, concat_axis=0, tiled=True)
    picked = returned.reshape(-1, model_width)[target].astype(jnp.float32)
    gate_vals = 0.25 + 0.125 * gate_codes.reshape(-1).astype(jnp.float32)
    combined = jnp.sum((picked * gate_vals[:, None]).reshape(tok_count, 2, model_width), axis=1)
    return (embedded.astype(jnp.float32) + combined).astype(jnp.bfloat16)


def solution(mesh):
    return jax.shard_map(
        on_device,
        mesh=mesh,
        in_specs=(
            P(("rep", "exp"), None),
            P(),
            P(),
            P(("rep", "exp"), None),
            P(("rep", "exp"), None),
            P("exp", None, "rep"),
            P("exp", None, "rep"),
        ),
        out_specs=P(("rep", "exp"), None),
        check_vma=False,
    )
```

profile of v0, /device:TPU:0, one launch (start us, length us, event | category | flops | bytes accessed | tf_op | source)
XLA Modules:
  0.0 442.9 jit_solution(4227271564317946433)
XLA Ops:
  0.0 0.9 copy.21
  1.2 0.7 broadcast_multiply_fusion
  1.9 1.7 fusion.30
  3.8 0.6 copy-done.2
  5.0 0.6 reduce-window.6
  6.2 1.9 scatter_custom_fusion
  8.3 31.8 %all_to_all.33 = bf16[32,12,1024]{2,1,0:T(8,128)(2,1)S(1)} all-to-all(bf16[32,12,1024]{2,1,0:T(8,128)(2,1)S(1)} %reshape.89), channel_id=1, replica_groups=mesh['rep'=8,'exp'=4] {'exp'}, dimensions={0} | all-to-all | bytes 1572864 | tf_op jit(solution)/shard_map/all_to_all | solution.py:38
  40.7 2.3 collective-permute-done
  43.2 1.6 collective-permute-start.1
  44.8 35.0 %collective-permute-done.1 = bf16[8,96,1024]{2,0,1:T(8,128)(2,1)} collective-permute-done((bf16[8,96,1024]{2,0,1:T(8,128)(2,1)S(1)}, bf16[8,96,1024]{2,0,1:T(8,128)(2,1)}, u32[]{:S(2)}, u32[]{:S(2)}) %collective-permute-start.1) | collective-permute-done | bytes 1572896 | tf_op jit(solution)/shard_map/ppermute | solution.py:8
  79.8 3.1 maximum_select_fusion.1
  82.9 1.6 collective-permute-start.2
  84.5 67.9 %collective-permute-done.2 = bf16[8,192,1024]{2,0,1:T(8,128)(2,1)} collective-permute-done((bf16[8,192,1024]{2,0,1:T(8,128)(2,1)S(1)}, bf16[8,192,1024]{2,0,1:T(8,128)(2,1)}, u32[]{:S(2)}, u32[]{:S(2)}) %collective-permute-start.2) | collective-permute-done | bytes 3145760 | tf_op jit(solution)/shard_map/ppermute | solution.py:8
  152.4 6.5 %maximum_select_fusion = bf16[8,384,1024]{2,0,1:T(8,128)(2,1)} fusion(bf16[8,192,1024]{2,0,1:T(8,128)(2,1)S(1)} %maximum_select_fusion.1, bf16[8,192,1024]{2,0,1:T(8,128)(2,1)} %collective-permute-done.2, pred[]{:T(512)S(6)} %eq.46), kind=kLoop, calls=%fused_computation.11 | loop fusion | flops 9437184 | bytes 12582913 | tf_op jit(solution)/shard_map/jit(_where)/select_n | solution.py:46
  158.9 21.5 %fusion.10 = f32[8,384,1024]{2,1,0:T(8,128)} fusion(bf16[8,1024,512]{2,1,0:T(8,128)(2,1)} %param.13, bf16[8,1024,512]{2,1,0:T(8,128)(2,1)} %param.12, bf16[8,384,1024]{2,0,1:T(8,128)(2,1)} %maximum_select_fusion), kind=kOutput, calls=%fused_computation.16 | convolution fusion | flops 6456606720 | bytes 35651584 | tf_op jit(solution)/shard_map/erf,edf->erd/dot_general | solution.py:63
  180.4 6.1 %slice_select_fusion = f32[8,192,1024]{2,1,0:T(8,128)S(1)} fusion(f32[8,384,1024]{2,1,0:T(8,128)} %fusion.10, pred[]{:T(512)S(6)} %eq.46), kind=kLoop, calls=%fused_computation.15 | loop fusion | flops 1572864 | bytes 18874368 | tf_op jit(solution)/shard_map/jit(_where)/select_n | solution.py:70
  186.5 1.6 collective-permute-start.3
  188.0 134.4 %collective-permute-done.3 = f32[8,192,1024]{2,1,0:T(8,128)} collective-permute-done((f32[8,192,1024]{2,1,0:T(8,128)S(1)}, f32[8,192,1024]{2,1,0:T(8,128)}, u32[]{:S(2)}, u32[]{:S(2)}) %collective-permute-start.3) | collective-permute-done | bytes 6291488 | tf_op jit(solution)/shard_map/ppermute | solution.py:8
  322.4 8.7 %select_add_fusion = f32[8,192,1024]{2,1,0:T(8,128)S(1)} fusion(f32[8,192,1024]{2,1,0:T(8,128)} %collective-permute-done.3, f32[8,384,1024]{2,1,0:T(8,128)} %fusion.10, pred[]{:T(512)S(6)} %eq.46), kind=kLoop, calls=%fused_computation.14 | loop fusion | flops 3145728 | bytes 25165824 | tf_op jit(solution)/shard_map/add | solution.py:71
  331.1 0.7 slice_select_fusion.1
  331.8 1.6 collective-permute-start.4
  333.3 66.0 %collective-permute-done.4 = f32[8,96,1024]{2,1,0:T(8,128)S(1)} collective-permute-done((f32[8,96,1024]{2,1,0:T(8,128)S(1)}, f32[8,96,1024]{2,1,0:T(8,128)S(1)}, u32[]{:S(2)}, u32[]{:S(2)}) %collective-permute-start.4) | collective-permute-done | bytes 3145760 | tf_op jit(solution)/shard_map/ppermute | solution.py:8
  399.3 1.4 select_add_fusion.1
  401.1 3.4 collective-permute-done.5
  405.0 1.3 copy.27
  406.3 3.5 all-to-all-start.1
  410.0 20.5 %all-to-all-done.1 = bf16[8,48,1024]{2,0,1:T(8,128)(2,1)S(1)} async-done(((bf16[8,48,1024]{2,0,1:T(8,128)(2,1)}), bf16[8,48,1024]{2,0,1:T(8,128)(2,1)S(1)}, u32[]{:S(2)}, u32[]{:S(2)}) %all-to-all-start.1) | async-done | bytes 786464 | tf_op jit(solution)/shard_map/all_to_all | solution.py:73
  431.0 1.1 reshape.90
  432.0 3.8 gather_fusion
  435.8 2.7 reshape.91
  438.4 2.6 multiply_reduce_fusion
  441.1 1.8 add_convert_fusion.1
  (38 shorter events, 4.1 us)
Async XLA Ops:
  0.0 1.9 copy-start
  0.0 4.4 copy-start.4
  3.6 0.8 copy-start.2
  40.6 2.4 collective-permute-start
  43.2 1.6 copy-start.3
  43.2 36.6 %collective-permute-start.1 = (bf16[8,96,1024]{2,0,1:T(8,128)(2,1)S(1)}, bf16[8,96,1024]{2,0,1:T(8,128)(2,1)}, u32[]{:S(2)}, u32[]{:S(2)}) collective-permute-start(bf16[8,96,1024]{2,0,1:T(8,128)(2,1)S(1)} %maximum_select_fusion.2), channel_id=1, source_target_pairs={{0,8},{4,12},{8,0},{12,4},{16,24},{20,28},{24,16},{28,20},{1,9},{5... | collective-permute-start | bytes 4718600 | tf_op jit(solution)/shard_map/ppermute | solution.py:8
  82.9 69.5 %collective-permute-start.2 = (bf16[8,192,1024]{2,0,1:T(8,128)(2,1)S(1)}, bf16[8,192,1024]{2,0,1:T(8,128)(2,1)}, u32[]{:S(2)}, u32[]{:S(2)}) collective-permute-start(bf16[8,192,1024]{2,0,1:T(8,128)(2,1)S(1)} %maximum_select_fusion.1), channel_id=1, source_target_pairs={{0,16},{4,20},{8,24},{12,28},{16,0},{20,4},{24,8},{28,12},{1,17},{... | collective-permute-start | bytes 9437192 | tf_op jit(solution)/shard_map/ppermute | solution.py:8
  186.5 136.0 %collective-permute-start.3 = (f32[8,192,1024]{2,1,0:T(8,128)S(1)}, f32[8,192,1024]{2,1,0:T(8,128)}, u32[]{:S(2)}, u32[]{:S(2)}) collective-permute-start(f32[8,192,1024]{2,1,0:T(8,128)S(1)} %slice_select_fusion), channel_id=1, source_target_pairs={{0,16},{4,20},{8,24},{12,28},{16,0},{20,4},{24,8},{28,12},{1,17},{... | collective-permute-start | bytes 18874376 | tf_op jit(solution)/shard_map/ppermute | solution.py:8
  331.8 67.5 %collective-permute-start.4 = (f32[8,96,1024]{2,1,0:T(8,128)S(1)}, f32[8,96,1024]{2,1,0:T(8,128)S(1)}, u32[]{:S(2)}, u32[]{:S(2)}) collective-permute-start(f32[8,96,1024]{2,1,0:T(8,128)S(1)} %slice_select_fusion.1), channel_id=1, source_target_pairs={{0,8},{4,12},{8,0},{12,4},{16,24},{20,28},{24,16},{28,20},{1,9},{5... | collective-permute-start | bytes 9437192 | tf_op jit(solution)/shard_map/ppermute | solution.py:8
  401.0 8.9 %copy-start.5 = (s32[128,2]{0,1:T(2,128)S(1)}, s32[128,2]{0,1:T(2,128)}, u32[]{:S(2)}) copy-start(s32[128,2]{0,1:T(2,128)} %param.11) | copy-start | bytes 3076
  401.0 3.5 collective-permute-start.5
  406.3 24.2 %all-to-all-start.1 = ((bf16[8,48,1024]{2,0,1:T(8,128)(2,1)}), bf16[8,48,1024]{2,0,1:T(8,128)(2,1)S(1)}, u32[]{:S(2)}, u32[]{:S(2)}) async-start(bf16[8,48,1024]{2,0,1:T(8,128)(2,1)} %copy.27), calls=%async_computation.1 | async-start | bytes 1572864 | tf_op jit(solution)/shard_map/all_to_all | solution.py:73
  432.0 10.9 %copy-start.1 = (bf16[1536,1024]{1,0:T(8,128)(2,1)S(1)}, bf16[1536,1024]{1,0:T(8,128)(2,1)}, u32[]{:S(2)}) copy-start(bf16[1536,1024]{1,0:T(8,128)(2,1)} %param.8) | copy-start | bytes 9437188
where the time goes:
time: 443 us
  waiting for transfers between devices  329 us (74%)
  other arithmetic  33.7 us (8%)
  blocking collectives  31.8 us (7%)
  matrix products  23.1 us (5%)
  local copies, waits for them, and re-layouts  14.6 us (3%)
  starting transfers between devices  9.91 us (2%)
    ppermute x6, waiting for transfers between devices, swapped(): lax.ppermute(array, axis, [(i, i ^ 1 << distance) for i in range(lax.axis...  309 us
    all_to_all x1, blocking collectives, on_device(): lax.all_to_all(buffer, 'exp', split_axis=0, concat_axis=1, tiled=True)  31.8 us
    dot_general x1, matrix products, on_device(): jnp.einsum('erf,edf->erd', hidden, panels[1], preferred_element_type=jnp....  21.5 us
    all_to_all x1, waiting for transfers between devices, on_device(): lax.all_to_all(expert_out, 'exp', split_axis=1, concat_axis=0, tiled=True)  20.5 us
    add x2, other arithmetic, on_device(): partial_out = keeping + swapped(sending, 'rep', bit)  10.1 us
    select_n x3, other arithmetic, on_device(): jnp.where(upper, jnp.concatenate([partner, collected], axis=1), jnp.conca...  9.84 us
  transfers between devices with their start and end apart: 7, of which 7 were waited for; matrix products, arithmetic and copies ran while one was open for 0% of the time, Pallas kernels for 0%

commit v1 on v0

v1 whole, which is shorter than its diff:
```python
import functools

import jax
import jax.numpy as jnp
from jax import lax
from jax.experimental import pallas as pl
from jax.experimental.pallas import tpu as pltpu
from jax.sharding import PartitionSpec as P

F32 = jnp.float32
BF16 = jnp.bfloat16
CHUNKS = 2
CORE, NEAR_A, NEAR_B = 0, 1, 2
GROUP_BITS = 3
VMEM_LIMIT = 50 * 1024 * 1024


def swapped(array, axis, distance):
    return lax.ppermute(array, axis, [(i, i ^ distance) for i in range(lax.axis_size(axis))])


def mm(a, b, dims=((1,), (0,))):
    return lax.dot_general(a, b, (dims, ((), ())), preferred_element_type=F32)


def vmem():
    return pl.BlockSpec(memory_space=pltpu.VMEM)


def smem():
    return pl.BlockSpec(memory_space=pltpu.SMEM)


def dispatch_kernel(n_exp, half, cap, place_ref, own_ref, sib_ref, weight_ref, gain_ref, code_ref, sib_code_ref,
                    emb_ref, gate_ref, *piece_refs):
    tok = own_ref.shape[0]
    both = 2 * tok
    count = n_exp * half
    slots = 2 * cap
    rows = count * slots
    gain = gain_ref[...]

    def normed_of(ref, keep):
        embedded = mm(ref[...], weight_ref[...]).astype(BF16)
        if keep:
            emb_ref[...] = embedded
        floats = embedded.astype(F32)
        centred = floats - jnp.mean(floats, axis=-1, keepdims=True)
        variance = jnp.mean(centred * centred, axis=-1, keepdims=True)
        return (centred * lax.rsqrt(variance + 1e-06) * gain).astype(BF16)

    normed = jnp.concatenate([normed_of(own_ref, True), normed_of(sib_ref, False)], axis=0)
    codes = jnp.concatenate([code_ref[...], sib_code_ref[...]], axis=0)
    plane, core = place_ref[0], place_ref[1]

    column = lax.broadcasted_iota(jnp.int32, (both, count), 1)
    expert = (plane ^ (column // half)) * (2 * half) + core * half + column % half
    first = codes[:, 0:1] == expert
    second = codes[:, 1:2] == expert
    member = jnp.where(first | second, 1.0, 0.0)
    gates = 0.25 + 0.125 * codes[:, 2:4].astype(F32)
    gated = jnp.where(first, gates[:, 0:1], 0.0) + jnp.where(second, gates[:, 1:2], 0.0)
    earlier_t = lax.broadcasted_iota(jnp.int32, (both, both), 0)
    later_t = lax.broadcasted_iota(jnp.int32, (both, both), 1)
    same = (earlier_t // tok) == (later_t // tok)
    before = jnp.where(same & (earlier_t < later_t), 1.0, 0.0).astype(BF16)
    after = jnp.where(same & (later_t < earlier_t), 1.0, 0.0).astype(BF16)
    equal = jnp.where(earlier_t == later_t, 1.0, 0.0).astype(BF16)
    member16 = member.astype(BF16)
    rank_t = mm(member16, before, ((0,), (0,)))
    member_t = mm(member16, equal, ((0,), (0,)))
    block_t = jnp.where(lax.broadcasted_iota(jnp.int32, (count, both), 1) >= tok, float(cap), 0.0)
    pos_t = jnp.where(member_t > 0.5, rank_t + block_t, -1.0).astype(BF16)
    spread = jnp.where(
        lax.broadcasted_iota(jnp.int32, (rows, count), 0) // slots
        == lax.broadcasted_iota(jnp.int32, (rows, count), 1), 1.0, 0.0).astype(BF16)
    slot_t = (lax.broadcasted_iota(jnp.int32, (rows, both), 0) % slots).astype(F32)
    select = jnp.where(mm(spread, pos_t) == slot_t, 1.0, 0.0).astype(BF16)
    buffer = mm(select, normed)
    for index, ref in enumerate(piece_refs):
        per = ref.shape[0]
        for e in range(per):
            start = (index * per + e) * slots
            ref[e] = buffer[start:start + slots].astype(BF16)

    rank = mm(after, member16)
    block = jnp.where(lax.broadcasted_iota(jnp.int32, (both, count), 0) >= tok, float(cap), 0.0)
    pos = jnp.where(member > 0.5, rank + block, -1.0).astype(BF16)
    slot = (lax.broadcasted_iota(jnp.int32, (both, rows), 1) % slots).astype(F32)
    spread_gate = mm(gated.astype(BF16), spread, ((1,), (1,)))
    gate_ref[...] = jnp.where(mm(pos, spread, ((1,), (1,))) == slot, spread_gate, 0.0).astype(BF16)


def dispatch(place, own, sib, weight, gain, codes, sib_codes, n_exp, half, cap):
    tok, width = own.shape[0], weight.shape[1]
    rows = n_exp * half * 2 * cap
    per = half // CHUNKS
    outs = [jax.ShapeDtypeStruct((tok, width), BF16), jax.ShapeDtypeStruct((2 * tok, rows), BF16)]
    outs += [jax.ShapeDtypeStruct((per, 2 * cap, width), BF16)] * (n_exp * CHUNKS)
    result = pl.pallas_call(
        functools.partial(dispatch_kernel, n_exp, half, cap),
        out_shape=outs,
        in_specs=[smem()] + [vmem()] * 6,
        out_specs=[vmem()] * len(outs),
        compiler_params=pltpu.CompilerParams(vmem_limit_bytes=VMEM_LIMIT),
        cost_estimate=pl.CostEstimate(
            flops=4 * tok * own.shape[1] * width, bytes_accessed=weight.size * 2 + rows * width * 2, transcendentals=0),
        name="dispatch",
    )(place, own, sib, weight, gain.reshape(1, width), codes, sib_codes)
    pieces = result[2:]
    return result[0], result[1], [[pieces[s * CHUNKS + c] for s in range(n_exp)] for c in range(CHUNKS)]


def experts_kernel(place_ref, own_ref, a_ref, b_ref, d1_ref, d2_ref, in_own_ref, in_sib_ref, down_own_ref, down_sib_ref,
                   p_own_ref, p_a_ref, p_b_ref, p_d1_ref, p_d2_ref, x_ref, acc_ref):
    e, f = pl.program_id(0), pl.program_id(1)
    split = pl.num_programs(0) // 2
    m = own_ref.shape[1]

    @pl.when(f == 0)
    def _():
        x_ref[0:m] = own_ref[0]
        x_ref[m:2 * m] = a_ref[0]
        x_ref[2 * m:3 * m] = b_ref[0]

        @pl.when(e < split)
        def _():
            x_ref[3 * m:4 * m] = d1_ref[0]

        @pl.when(e >= split)
        def _():
            x_ref[3 * m:4 * m] = d2_ref[0]

    x = x_ref[...]
    h_own = jax.nn.gelu(mm(x, in_own_ref[0])).astype(BF16)
    h_sib = jax.nn.gelu(mm(x, in_sib_ref[0])).astype(BF16)
    total = mm(h_own, down_own_ref[0], ((1,), (1,))) + mm(h_sib, down_sib_ref[0], ((1,), (1,)))

    @pl.when(f == 0)
    def _():
        acc_ref[...] = total

    @pl.when(f > 0)
    def _():
        acc_ref[...] += total

    @pl.when(f == pl.num_programs(1) - 1)
    def _():
        p_own_ref[0] = acc_ref[0:m].astype(BF16)
        p_a_ref[0] = acc_ref[m:2 * m].astype(BF16)
        p_b_ref[0] = acc_ref[2 * m:3 * m].astype(BF16)

        @pl.when(e < split)
        def _():
            p_d1_ref[0] = acc_ref[3 * m:4 * m].astype(BF16)

        @pl.when(e >= split)
        def _():
            p_d2_ref[0] = acc_ref[3 * m:4 * m].astype(BF16)


def experts(place, chunk, own, near_a, near_b, d1, d2, in_own, in_sib, down_own, down_sib):
    per, m, width = own.shape
    half = in_sib.shape[0]
    ff = in_sib.shape[2]
    steps = 2 if ff % 512 == 0 else 1
    fb = ff // steps
    split = per // 2
    rows = pl.BlockSpec((1, m, width), lambda e, f, p: (e, 0, 0))
    rows1 = pl.BlockSpec((1, m, width), lambda e, f, p: (jnp.minimum(e, split - 1), 0, 0))
    rows2 = pl.BlockSpec((1, m, width), lambda e, f, p: (jnp.maximum(e - split, 0), 0, 0))
    w_own = pl.BlockSpec((1, width, fb), lambda e, f, p: (p[1] * half + chunk * per + e, 0, f))
    w_sib = pl.BlockSpec((1, width, fb), lambda e, f, p: (chunk * per + e, 0, f))
    shape = jax.ShapeDtypeStruct(own.shape, BF16)
    part = jax.ShapeDtypeStruct(d1.shape, BF16)
    return pl.pallas_call(
        experts_kernel,
        out_shape=[shape, shape, shape, part, part],
        grid_spec=pltpu.PrefetchScalarGridSpec(
            num_scalar_prefetch=1,
            grid=(per, steps),
            in_specs=[rows, rows, rows, rows1, rows2, w_own, w_sib, w_own, w_sib],
            out_specs=[rows, rows, rows, rows1, rows2],
            scratch_shapes=[pltpu.VMEM((4 * m, width), BF16), pltpu.VMEM((4 * m, width), F32)],
        ),
        compiler_params=pltpu.CompilerParams(
            vmem_limit_bytes=VMEM_LIMIT, dimension_semantics=("arbitrary", "arbitrary")),
        cost_estimate=pl.CostEstimate(
            flops=2 * per * 4 * m * width * 2 * ff * 2, bytes_accessed=per * width * ff * 8 + per * m * width * 16,
            transcendentals=per * 4 * m * 2 * ff),
        name="experts",
    )(place, own, near_a, near_b, d1, d2, in_own, in_sib, down_own, down_sib)


def combine_kernel(tok, gate_ref, emb_ref, *refs):
    piece_refs, (mine_ref, send_ref, rows_ref) = refs[:-3], refs[-3:]
    per, slots, _ = piece_refs[0].shape
    for index, ref in enumerate(piece_refs):
        for e in range(per):
            start = (index * per + e) * slots
            rows_ref[start:start + slots] = ref[e].astype(F32)
    total = mm(gate_ref[...], rows_ref[...].astype(BF16))
    mine_ref[...] = total[0:tok] + emb_ref[...].astype(F32)
    send_ref[...] = total[tok:2 * tok].astype(BF16)


def combine(gate, embedded, pieces):
    tok, width = embedded.shape
    rows = gate.shape[1]
    return pl.pallas_call(
        functools.partial(combine_kernel, tok),
        out_shape=[jax.ShapeDtypeStruct((tok, width), F32), jax.ShapeDtypeStruct((tok, width), BF16)],
        in_specs=[vmem()] * (2 + len(pieces)),
        out_specs=[vmem()] * 2,
        scratch_shapes=[pltpu.VMEM((rows, width), F32)],
        compiler_params=pltpu.CompilerParams(vmem_limit_bytes=VMEM_LIMIT),
        cost_estimate=pl.CostEstimate(flops=4 * tok * rows * width, bytes_accessed=rows * width * 2, transcendentals=0),
        name="combine",
    )(gate, embedded, *pieces)


def on_device(tubelets, embed_weight, norm_gain, routes, gate_codes, w_in, w_down):
    tok = tubelets.shape[0]
    n_exp = lax.axis_size("exp")
    half = w_in.shape[0] // 2
    cap = 3 * tok // (w_in.shape[0] * n_exp)
    position = lax.axis_index("rep")
    core = position % 2
    place = jnp.stack([lax.axis_index("exp"), core]).astype(jnp.int32)

    codes = jnp.concatenate([routes, gate_codes], axis=1)
    sib_codes = swapped(codes, "rep", 1 << CORE)
    sib_tubelets = swapped(tubelets, "rep", 1 << CORE)

    for bit in range(GROUP_BITS, lax.axis_size("rep").bit_length() - 1):
        upper = position // (1 << bit) % 2 == 1

        def gathered(panel):
            partner = swapped(panel, "rep", 1 << bit)
            return jnp.where(upper, jnp.concatenate([partner, panel], axis=2), jnp.concatenate([panel, partner], axis=2))

        w_in, w_down = gathered(w_in), gathered(w_down)

    embedded, gate, pieces = dispatch(
        place, tubelets, sib_tubelets, embed_weight, norm_gain, codes, sib_codes, n_exp, half, cap)

    in_sib = swapped(lax.dynamic_slice_in_dim(w_in, (1 - core) * half, half, 0), "rep", 1 << CORE)
    down_sib = swapped(lax.dynamic_slice_in_dim(w_down, (1 - core) * half, half, 0), "rep", 1 << CORE)

    returned = []
    for chunk in range(CHUNKS):
        arrived = [pieces[chunk][0]] + [swapped(pieces[chunk][s], "exp", s) for s in range(1, n_exp)]
        own = jnp.concatenate(arrived, axis=1)
        split = own.shape[0] // 2
        near_a = swapped(own, "rep", 1 << NEAR_A)
        near_b = swapped(own, "rep", 1 << NEAR_B)
        d1 = swapped(near_a[:split], "rep", 1 << NEAR_B)
        d2 = swapped(near_b[split:], "rep", 1 << NEAR_A)
        p_own, p_a, p_b, p_d1, p_d2 = experts(
            place, chunk, own, near_a, near_b, d1, d2, w_in, in_sib, w_down, down_sib)
        r1 = swapped(p_d1, "rep", 1 << NEAR_A)
        r2 = swapped(p_d2, "rep", 1 << NEAR_B)
        to_b = jnp.concatenate([p_b[:split] + r1, p_b[split:]], axis=0)
        to_a = jnp.concatenate([p_a[:split], p_a[split:] + r2], axis=0)
        from_a = swapped(to_a, "rep", 1 << NEAR_A)
        from_b = swapped(to_b, "rep", 1 << NEAR_B)
        done = (p_own.astype(F32) + from_a.astype(F32) + from_b.astype(F32)).astype(BF16)
        done = done.reshape(done.shape[0], n_exp, 2 * cap, done.shape[2])
        returned.append([done[:, 0]] + [swapped(done[:, s], "exp", s) for s in range(1, n_exp)])

    pieces_back = [returned[c][s] for s in range(n_exp) for c in range(CHUNKS)]
    mine, send = combine(gate, embedded, pieces_back)
    other = swapped(send, "rep", 1 << CORE)
    return (mine + other.astype(F32)).astype(BF16)


def solution(mesh):
    return jax.shard_map(
        on_device,
        mesh=mesh,
        in_specs=(
            P(("rep", "exp"), None),
            P(),
            P(),
            P(("rep", "exp"), None),
            P(("rep", "exp"), None),
            P("exp", None, "rep"),
            P("exp", None, "rep"),
        ),
        out_specs=P(("rep", "exp"), None),
        check_vma=False,
    )
```

time: 443 us -> 113 us (0.26)
  waiting for transfers between devices: 329 us -> 40.4 us
  starting transfers between devices: 9.91 us -> 42.5 us
  other arithmetic: 33.7 us -> 1.54 us
  blocking collectives: 31.8 us -> 0 us
  matrix products: 23.1 us -> 0 us
  Pallas kernels: 0 us -> 19.7 us
  local copies, waits for them, and re-layouts: 14.6 us -> 8.14 us
    ppermute x6 -> x33, waiting for transfers between devices: 309 us -> 40.4 us  [swapped(): lax.ppermute(array, axis, [(i, i ^ distance) for i in range(lax.axis_size...]
    ppermute x6 -> x33, starting transfers between devices: 6.41 us -> 42.5 us  [swapped(): lax.ppermute(array, axis, [(i, i ^ distance) for i in range(lax.axis_size...]
    all_to_all x1 -> x0, blocking collectives: 31.8 us -> none  [on_device(): lax.all_to_all(buffer, 'exp', split_axis=0, concat_axis=1, tiled=True)]
    dot_general x2 -> x0, matrix products: 23.1 us -> none  [the longest x1 21.5 us: on_device(): jnp.einsum('erf,edf->erd', hidden, panels[1], preferred_element_type=jnp....]
    all_to_all x1 -> x0, waiting for transfers between devices: 20.5 us -> none  [on_device(): lax.all_to_all(expert_out, 'exp', split_axis=1, concat_axis=0, tiled=True)]
    pallas_call x0 -> x4, Pallas kernels: none -> 19.7 us  [the longest x2 15.5 us: experts(): pl.pallas_call(experts_kernel, out_shape=[shape, shape, shape, part, part...]
    select_n x7 -> x0, other arithmetic: 16.8 us -> none  [the longest x3 9.84 us: on_device(): jnp.where(upper, jnp.concatenate([partner, collected], axis=1), jnp.conca...]
    add x3 -> x2, other arithmetic: 10.1 us -> 0.07 us  [on_device(): to_b = jnp.concatenate([p_b[:split] + r1, p_b[split:]], axis=0)]
  transfers between devices with their start and end apart: 7 -> 33, of which waited for: 7 -> 15; matrix products, arithmetic and copies ran while one was open for 0% -> 3% of each run, Pallas kernels for 0% -> 17%
where the time goes in v1:
time: 113 us; the launch traced here: 112 us
  starting transfers between devices  42.5 us (38%)
  waiting for transfers between devices  40.4 us (36%)
  Pallas kernels  19.7 us (17%)
  local copies, waits for them, and re-layouts  8.14 us (7%)
  other arithmetic  1.54 us (1%)
    ppermute x33, starting transfers between devices, swapped(): lax.ppermute(array, axis, [(i, i ^ distance) for i in range(lax.axis_size...  42.5 us
    ppermute x33, waiting for transfers between devices, swapped(): lax.ppermute(array, axis, [(i, i ^ distance) for i in range(lax.axis_size...  40.4 us
    pallas_call x2, Pallas kernels, experts(): pl.pallas_call(experts_kernel, out_shape=[shape, shape, shape, part, part...  15.5 us
    dynamic_slice x1, local copies, waits for them, and re-layouts, on_device(): lax.dynamic_slice_in_dim(w_down, (1 - core) * half, half, 0)  4.76 us
    pallas_call x1, Pallas kernels, dispatch(): pl.pallas_call(functools.partial(dispatch_kernel, n_exp, half, cap), out_...  3.77 us
  transfers between devices with their start and end apart: 33, of which 15 were waited for; matrix products, arithmetic and copies ran while one was open for 3% of the time, Pallas kernels for 17%

profile of v1, /device:TPU:0, one launch (start us, length us, event | category | flops | bytes accessed | tf_op | source)
XLA Modules:
  0.0 112.4 jit_solution(1441546825357338634)
XLA Ops:
  0.0 4.8 %constant_dynamic-slice_fusion = bf16[4,1024,512]{2,1,0:T(8,128)(2,1)} fusion(bf16[8,1024,512]{2,1,0:T(8,128)(2,1)} %down_own_ref.3, s32[]{:T(128)S(6)} %select_n.12), kind=kLoop, calls=%fused_computation.29 | loop fusion | bytes 8388612 | tf_op jit(solution)/shard_map/dynamic_slice | solution.py:248
  6.2 2.2 %constant_dynamic-slice_fusion.1 = bf16[4,1024,512]{2,1,0:T(8,128)(2,1)} fusion(bf16[8,1024,512]{2,1,0:T(8,128)(2,1)S(1)} %copy-done.2, s32[]{:T(128)S(6)} %select_n.12), kind=kLoop, calls=%fused_computation.30 | loop fusion | bytes 8388612 | tf_op jit(solution)/shard_map/dynamic_slice | solution.py:247
  9.6 3.8 %collective-permute-done.1.sib_code_ref = s32[128,4]{1,0:T(8,128)S(1)} collective-permute-done((s32[128,4]{1,0:T(8,128)S(1)}, s32[128,4]{1,0:T(8,128)S(1)}, u32[]{:S(2)}, u32[]{:S(2)}) %collective-permute-start.1) | collective-permute-done | bytes 2080 | tf_op jit(solution)/shard_map/ppermute | solution.py:19
  13.4 3.8 %dispatch.1 = (bf16[128,1024]{1,0:T(8,128)(2,1)S(1)}, bf16[256,384]{1,0:T(8,128)(2,1)S(1)}, bf16[2,24,1024]{2,1,0:T(8,128)(2,1)S(1)}, bf16[2,24,1024]{2,1,0:T(8,...) custom-call(s32[2]{0:T(128)S(1)} %pad_add_fusion.1.place_ref, ...), custom_call_target="tpu_custom_call" | custom-call | flops 805306368 | bytes 3932160 | tf_op jit(solution)/shard_map/dispatch/pallas_call | solution.py:100
  17.2 3.0 %collective-permute-start.15 = (bf16[2,24,1024]{2,1,0:T(8,128)(2,1)S(1)}, bf16[2,24,1024]{2,1,0:T(8,128)(2,1)S(1)}, u32[]{:S(2)}, u32[]{:S(2)}) collective-permute-start(bf16[2,24,1024]{2,1,0:T(8,128)(2,1)S(1)} %get-tuple-element.39), channel_id=1, source_target_pairs={{0,1},{1,0},{2,3},{3,2},{4,5},{5,4},{6,7},{7,6},{8,9},{9,8},{10,11... | collective-permute-start | bytes 294920 | tf_op jit(solution)/shard_map/ppermute | solution.py:19
  20.2 2.6 %collective-permute-start.16 = (bf16[2,24,1024]{2,1,0:T(8,128)(2,1)S(1)}, bf16[2,24,1024]{2,1,0:T(8,128)(2,1)S(1)}, u32[]{:S(2)}, u32[]{:S(2)}) collective-permute-start(bf16[2,24,1024]{2,1,0:T(8,128)(2,1)S(1)} %get-tuple-element.40), channel_id=1, source_target_pairs={{0,2},{1,3},{2,0},{3,1},{4,6},{5,7},{6,4},{7,5},{8,10},{9,11},{10,... | collective-permute-start | bytes 294920 | tf_op jit(solution)/shard_map/ppermute | solution.py:19
  23.3 1.7 %collective-permute-start.2 = (bf16[2,24,1024]{2,1,0:T(8,128)(2,1)S(1)}, bf16[2,24,1024]{2,1,0:T(8,128)(2,1)S(1)}, u32[]{:S(2)}, u32[]{:S(2)}) collective-permute-start(bf16[2,24,1024]{2,1,0:T(8,128)(2,1)S(1)} %get-tuple-element.30), channel_id=1, source_target_pairs={{0,1},{1,0},{2,3},{3,2},{4,5},{5,4},{6,7},{7,6},{8,9},{9,8},{10,11... | collective-permute-start | bytes 294920 | tf_op jit(solution)/shard_map/ppermute | solution.py:19
  25.0 5.8 %collective-permute-done.16 = bf16[2,24,1024]{2,1,0:T(8,128)(2,1)S(1)} collective-permute-done((bf16[2,24,1024]{2,1,0:T(8,128)(2,1)S(1)}, bf16[2,24,1024]{2,1,0:T(8,128)(2,1)S(1)}, u32[]{:S(2)}, u32[]{:S(2)}) %collective-permute-start.16) | collective-permute-done | bytes 98336 | tf_op jit(solution)/shard_map/ppermute | solution.py:19
  30.9 4.8 %collective-permute-start.4 = (bf16[2,24,1024]{2,1,0:T(8,128)(2,1)S(1)}, bf16[2,24,1024]{2,1,0:T(8,128)(2,1)S(1)}, u32[]{:S(2)}, u32[]{:S(2)}) collective-permute-start(bf16[2,24,1024]{2,1,0:T(8,128)(2,1)S(1)} %get-tuple-element.32), channel_id=1, source_target_pairs={{0,3},{1,2},{2,1},{3,0},{4,7},{5,6},{6,5},{7,4},{8,11},{9,10},{10,... | collective-permute-start | bytes 294920 | tf_op jit(solution)/shard_map/ppermute | solution.py:19
  36.1 3.2 %collective-permute-done.3 = bf16[2,24,1024]{2,1,0:T(8,128)(2,1)S(1)} collective-permute-done((bf16[2,24,1024]{2,1,0:T(8,128)(2,1)S(1)}, bf16[2,24,1024]{2,1,0:T(8,128)(2,1)S(1)}, u32[]{:S(2)}, u32[]{:S(2)}) %collective-permute-start.3) | collective-permute-done | bytes 98336 | tf_op jit(solution)/shard_map/ppermute | solution.py:19
  39.4 1.5 %collective-permute-start.19 = (bf16[2,96,1024]{2,1,0:T(8,128)(2,1)S(1)}, bf16[2,96,1024]{2,1,0:T(8,128)(2,1)S(1)}, u32[]{:S(2)}, u32[]{:S(2)}) collective-permute-start(bf16[2,96,1024]{2,1,0:T(8,128)(2,1)S(1)} %constant_dynamic-update-slice_fusion.4.own_ref), channel_id=1, source_target_pairs={{0,16},{4,20},{8,24},{12,28},{16,0},{20,4},{24,8},{28,12},{1,17},{... | collective-permute-start | bytes 1179656 | tf_op jit(solution)/shard_map/ppermute | solution.py:19
  40.9 1.6 %collective-permute-start.5 = (bf16[2,96,1024]{2,1,0:T(8,128)(2,1)S(1)}, bf16[2,96,1024]{2,1,0:T(8,128)(2,1)S(1)}, u32[]{:S(2)}, u32[]{:S(2)}) collective-permute-start(bf16[2,96,1024]{2,1,0:T(8,128)(2,1)S(1)} %constant_dynamic-update-slice_fusion.own_ref), channel_id=1, source_target_pairs={{0,8},{4,12},{8,0},{12,4},{16,24},{20,28},{24,16},{28,20},{1,9},{5... | collective-permute-start | bytes 1179656 | tf_op jit(solution)/shard_map/ppermute | solution.py:19
  42.5 4.8 %collective-permute-done.18.a_ref = bf16[2,96,1024]{2,1,0:T(8,128)(2,1)S(1)} collective-permute-done((bf16[2,96,1024]{2,1,0:T(8,128)(2,1)S(1)}, bf16[2,96,1024]{2,1,0:T(8,128)(2,1)S(1)}, u32[]{:S(2)}, u32[]{:S(2)}) %collective-permute-start.18) | collective-permute-done | bytes 393248 | tf_op jit(solution)/shard_map/ppermute | solution.py:19
  47.9 3.6 %collective-permute-done.19.b_ref = bf16[2,96,1024]{2,1,0:T(8,128)(2,1)S(1)} collective-permute-done((bf16[2,96,1024]{2,1,0:T(8,128)(2,1)S(1)}, bf16[2,96,1024]{2,1,0:T(8,128)(2,1)S(1)}, u32[]{:S(2)}, u32[]{:S(2)}) %collective-permute-start.19) | collective-permute-done | bytes 393248 | tf_op jit(solution)/shard_map/ppermute | solution.py:19
  51.4 1.5 %collective-permute-start.20 = (bf16[1,96,1024]{2,1,0:T(8,128)(2,1)S(1)}, bf16[1,96,1024]{2,1,0:T(8,128)(2,1)S(1)}, u32[]{:S(2)}, u32[]{:S(2)}) collective-permute-start(bf16[1,96,1024]{2,1,0:T(8,128)(2,1)S(1)} %slice.83), channel_id=1, source_target_pairs={{0,16},{4,20},{8,24},{12,28},{16,0},{20,4},{24,8},{28,12},{1,17},{... | collective-permute-start | bytes 589832 | tf_op jit(solution)/shard_map/ppermute | solution.py:19
  53.3 1.3 %collective-permute-start.21 = (bf16[1,96,1024]{2,1,0:T(8,128)(2,1)S(1)}, bf16[1,96,1024]{2,1,0:T(8,128)(2,1)S(1)}, u32[]{:S(2)}, u32[]{:S(2)}) collective-permute-start(bf16[1,96,1024]{2,1,0:T(8,128)(2,1)S(1)} %slice.84), channel_id=1, source_target_pairs={{0,8},{4,12},{8,0},{12,4},{16,24},{20,28},{24,16},{28,20},{1,9},{5... | collective-permute-start | bytes 589832 | tf_op jit(solution)/shard_map/ppermute | solution.py:19
  54.6 4.1 %collective-permute-done.6.b_ref = bf16[2,96,1024]{2,1,0:T(8,128)(2,1)S(1)} collective-permute-done((bf16[2,96,1024]{2,1,0:T(8,128)(2,1)S(1)}, bf16[2,96,1024]{2,1,0:T(8,128)(2,1)S(1)}, u32[]{:S(2)}, u32[]{:S(2)}) %collective-permute-start.6) | collective-permute-done | bytes 393248 | tf_op jit(solution)/shard_map/ppermute | solution.py:19
  58.6 1.5 %collective-permute-start.7 = (bf16[1,96,1024]{2,1,0:T(8,128)(2,1)S(1)}, bf16[1,96,1024]{2,1,0:T(8,128)(2,1)S(1)}, u32[]{:S(2)}, u32[]{:S(2)}) collective-permute-start(bf16[1,96,1024]{2,1,0:T(8,128)(2,1)S(1)} %slice.80), channel_id=1, source_target_pairs={{0,16},{4,20},{8,24},{12,28},{16,0},{20,4},{24,8},{28,12},{1,17},{... | collective-permute-start | bytes 589832 | tf_op jit(solution)/shard_map/ppermute | solution.py:19
  60.7 1.5 %collective-permute-start.8 = (bf16[1,96,1024]{2,1,0:T(8,128)(2,1)S(1)}, bf16[1,96,1024]{2,1,0:T(8,128)(2,1)S(1)}, u32[]{:S(2)}, u32[]{:S(2)}) collective-permute-start(bf16[1,96,1024]{2,1,0:T(8,128)(2,1)S(1)} %slice.81), channel_id=1, source_target_pairs={{0,8},{4,12},{8,0},{12,4},{16,24},{20,28},{24,16},{28,20},{1,9},{5... | collective-permute-start | bytes 589832 | tf_op jit(solution)/shard_map/ppermute | solution.py:19
  62.3 7.8 %experts.3 = (bf16[2,96,1024]{2,1,0:T(8,128)(2,1)S(1)}, bf16[2,96,1024]{2,1,0:T(8,128)(2,1)S(1)}, bf16[2,96,1024]{2,1,0:T(8,128)(2,1)S(1)}, bf16[1,96,1024]{2,1,0:T(8,128)(2,1)S(1)}, bf16[1,96,1024]{2,1,0:T(8,128)(2,1)S(1)}) custom-call(s32[2]{0:T(128)S(1)} %pad_add_fusion.1.place_ref, bf16[2,96,1024]{2,1,0:T(8,128)(2,1)S(1)} %constant_dynamic-update-slice_fusion.4.own_ref, ...), custom_call_target="tpu_custom_call" | custom-call | flops 3221225472 | bytes 11534336 | tf_op jit(solution)/shard_map/experts/pallas_call | solution.py:176
  70.0 1.6 %collective-permute-start.22 = (bf16[1,96,1024]{2,1,0:T(8,128)(2,1)S(1)}, bf16[1,96,1024]{2,1,0:T(8,128)(2,1)S(1)}, u32[]{:S(2)}, u32[]{:S(2)}) collective-permute-start(bf16[1,96,1024]{2,1,0:T(8,128)(2,1)S(1)} %get-tuple-element.44), channel_id=1, source_target_pairs={{0,16},{4,20},{8,24},{12,28},{16,0},{20,4},{24,8},{28,12},{1,17},{... | collective-permute-start | bytes 589832 | tf_op jit(solution)/shard_map/ppermute | solution.py:19
  72.2 7.7 %experts.2 = (bf16[2,96,1024]{2,1,0:T(8,128)(2,1)S(1)}, bf16[2,96,1024]{2,1,0:T(8,128)(2,1)S(1)}, bf16[2,96,1024]{2,1,0:T(8,128)(2,1)S(1)}, bf16[1,96,1024]{2,1,0:T(8,128)(2,1)S(1)}, bf16[1,96,1024]{2,1,0:T(8,128)(2,1)S(1)}) custom-call(s32[2]{0:T(128)S(1)} %pad_add_fusion.1.place_ref, bf16[2,96,1024]{2,1,0:T(8,128)(2,1)S(1)} %constant_dynamic-update-slice_fusion.own_ref, ...), custom_call_target="tpu_custom_call" | custom-call | flops 3221225472 | bytes 11534336 | tf_op jit(solution)/shard_map/experts/pallas_call | solution.py:176
  80.5 1.5 %collective-permute-start.13 = (bf16[1,96,1024]{2,1,0:T(8,128)(2,1)S(1)}, bf16[1,96,1024]{2,1,0:T(8,128)(2,1)S(1)}, u32[]{:S(2)}, u32[]{:S(2)}) collective-permute-start(bf16[1,96,1024]{2,1,0:T(8,128)(2,1)S(1)} %get-tuple-element.37), channel_id=1, source_target_pairs={{0,8},{4,12},{8,0},{12,4},{16,24},{20,28},{24,16},{28,20},{1,9},{5... | collective-permute-start | bytes 589832 | tf_op jit(solution)/shard_map/ppermute | solution.py:19
  82.8 1.6 %collective-permute-start.25 = (bf16[2,96,1024]{2,1,0:T(8,128)(2,1)S(1)}, bf16[2,96,1024]{2,1,0:T(8,128)(2,1)S(1)}, u32[]{:S(2)}, u32[]{:S(2)}) collective-permute-start(bf16[2,96,1024]{2,1,0:T(8,128)(2,1)S(1)} %pad_maximum_fusion.3), channel_id=1, source_target_pairs={{0,16},{4,20},{8,24},{12,28},{16,0},{20,4},{24,8},{28,12},{1,17},{... | collective-permute-start | bytes 1179656 | tf_op jit(solution)/shard_map/ppermute | solution.py:19
  84.3 3.5 %collective-permute-done.11 = bf16[1,96,1024]{2,1,0:T(8,128)(2,1)S(1)} collective-permute-done((bf16[1,96,1024]{2,1,0:T(8,128)(2,1)S(1)}, bf16[1,96,1024]{2,1,0:T(8,128)(2,1)S(1)}, u32[]{:S(2)}, u32[]{:S(2)}) %collective-permute-start.11) | collective-permute-done | bytes 196640 | tf_op jit(solution)/shard_map/ppermute | solution.py:19
  90.1 3.4 %collective-permute-done.23 = bf16[2,96,1024]{2,1,0:T(8,128)(2,1)S(1)} collective-permute-done((bf16[2,96,1024]{2,1,0:T(8,128)(2,1)S(1)}, bf16[2,96,1024]{2,1,0:T(8,128)(2,1)S(1)}, u32[]{:S(2)}, u32[]{:S(2)}) %collective-permute-start.23) | collective-permute-done | bytes 393248 | tf_op jit(solution)/shard_map/ppermute | solution.py:19
  93.7 1.7 %collective-permute-start.27 = (bf16[2,24,1024]{2,1,0:T(8,128)(2,1)S(1)}, bf16[2,24,1024]{2,1,0:T(8,128)(2,1)S(1)}, u32[]{:S(2)}, u32[]{:S(2)}) collective-permute-start(bf16[2,24,1024]{2,1,0:T(8,128)(2,1)S(1)} %get-tuple-element.51), channel_id=1, source_target_pairs={{0,1},{1,0},{2,3},{3,2},{4,5},{5,4},{6,7},{7,6},{8,9},{9,8},{10,11... | collective-permute-start | bytes 294920 | tf_op jit(solution)/shard_map/ppermute | solution.py:19
  95.4 3.1 %collective-permute-start.29 = (bf16[2,24,1024]{2,1,0:T(8,128)(2,1)S(1)}, bf16[2,24,1024]{2,1,0:T(8,128)(2,1)S(1)}, u32[]{:S(2)}, u32[]{:S(2)}) collective-permute-start(bf16[2,24,1024]{2,1,0:T(8,128)(2,1)S(1)} %get-tuple-element.50), channel_id=1, source_target_pairs={{0,2},{1,3},{2,0},{3,1},{4,6},{5,7},{6,4},{7,5},{8,10},{9,11},{10,... | collective-permute-start | bytes 294920 | tf_op jit(solution)/shard_map/ppermute | solution.py:19
  99.6 3.6 %collective-permute-start.28 = (bf16[2,24,1024]{2,1,0:T(8,128)(2,1)S(1)}, bf16[2,24,1024]{2,1,0:T(8,128)(2,1)S(1)}, u32[]{:S(2)}, u32[]{:S(2)}) collective-permute-start(bf16[2,24,1024]{2,1,0:T(8,128)(2,1)S(1)} %get-tuple-element.54), channel_id=1, source_target_pairs={{0,2},{1,3},{2,0},{3,1},{4,6},{5,7},{6,4},{7,5},{8,10},{9,11},{10,... | collective-permute-start | bytes 294920 | tf_op jit(solution)/shard_map/ppermute | solution.py:19
  105.0 2.3 %collective-permute-done.28.refs_4_ = bf16[2,24,1024]{2,1,0:T(8,128)(2,1)S(1)} collective-permute-done((bf16[2,24,1024]{2,1,0:T(8,128)(2,1)S(1)}, bf16[2,24,1024]{2,1,0:T(8,128)(2,1)S(1)}, u32[]{:S(2)}, u32[]{:S(2)}) %collective-permute-start.28) | collective-permute-done | bytes 98336 | tf_op jit(solution)/shard_map/ppermute | solution.py:19
  107.3 2.3 %collective-permute-done.30.refs_6_ = bf16[2,24,1024]{2,1,0:T(8,128)(2,1)S(1)} collective-permute-done((bf16[2,24,1024]{2,1,0:T(8,128)(2,1)S(1)}, bf16[2,24,1024]{2,1,0:T(8,128)(2,1)S(1)}, u32[]{:S(2)}, u32[]{:S(2)}) %collective-permute-start.30) | collective-permute-done | bytes 98336 | tf_op jit(solution)/shard_map/ppermute | solution.py:19
  110.1 1.5 %collective-permute-done.32 = bf16[128,1024]{1,0:T(8,128)(2,1)S(1)} collective-permute-done((bf16[128,1024]{1,0:T(8,128)(2,1)S(1)}, bf16[128,1024]{1,0:T(8,128)(2,1)S(1)}, u32[]{:S(2)}, u32[]{:S(2)}) %collective-permute-start.32) | collective-permute-done | bytes 262176 | tf_op jit(solution)/shard_map/ppermute | solution.py:19
  (78 shorter events, 13.7 us)
Async XLA Ops:
  4.8 57.5 %collective-permute-start.10 = (bf16[4,1024,512]{2,1,0:T(8,128)(2,1)}, bf16[4,1024,512]{2,1,0:T(8,128)(2,1)}, u32[]{:S(2)}, u32[]{:S(2)}) collective-permute-start(bf16[4,1024,512]{2,1,0:T(8,128)(2,1)} %constant_dynamic-slice_fusion), channel_id=1, source_target_pairs={{0,4},{4,0},{8,12},{12,8},{16,20},{20,16},{24,28},{28,24},{1,5},{5... | collective-permute-start | bytes 12582920 | tf_op jit(solution)/shard_map/ppermute | solution.py:19
  8.4 53.9 %collective-permute-start.9 = (bf16[4,1024,512]{2,1,0:T(8,128)(2,1)}, bf16[4,1024,512]{2,1,0:T(8,128)(2,1)}, u32[]{:S(2)}, u32[]{:S(2)}) collective-permute-start(bf16[4,1024,512]{2,1,0:T(8,128)(2,1)} %constant_dynamic-slice_fusion.1), channel_id=1, source_target_pairs={{0,4},{4,0},{8,12},{12,8},{16,20},{20,16},{24,28},{28,24},{1,5},{5... | collective-permute-start | bytes 12582920 | tf_op jit(solution)/shard_map/ppermute | solution.py:19
  8.8 4.6 %collective-permute-start = (bf16[128,1536]{1,0:T(8,128)(2,1)S(1)}, bf16[128,1536]{1,0:T(8,128)(2,1)S(1)}, u32[]{:S(2)}, u32[]{:S(2)}) collective-permute-start(bf16[128,1536]{1,0:T(8,128)(2,1)S(1)} %copy-done), channel_id=1, source_target_pairs={{0,4},{4,0},{8,12},{12,8},{16,20},{20,16},{24,28},{28,24},{1,5},{5... | collective-permute-start | bytes 1179656 | tf_op jit(solution)/shard_map/ppermute | solution.py:19
  9.0 4.4 %collective-permute-start.1 = (s32[128,4]{1,0:T(8,128)S(1)}, s32[128,4]{1,0:T(8,128)S(1)}, u32[]{:S(2)}, u32[]{:S(2)}) collective-permute-start(s32[128,4]{1,0:T(8,128)S(1)} %copy.21.code_ref), channel_id=1, source_target_pairs={{0,4},{4,0},{8,12},{12,8},{16,20},{20,16},{24,28},{28,24},{1,5},{5... | collective-permute-start | bytes 6152 | tf_op jit(solution)/shard_map/ppermute | solution.py:19
  17.2 6.1 %collective-permute-start.15 = (bf16[2,24,1024]{2,1,0:T(8,128)(2,1)S(1)}, bf16[2,24,1024]{2,1,0:T(8,128)(2,1)S(1)}, u32[]{:S(2)}, u32[]{:S(2)}) collective-permute-start(bf16[2,24,1024]{2,1,0:T(8,128)(2,1)S(1)} %get-tuple-element.39), channel_id=1, source_target_pairs={{0,1},{1,0},{2,3},{3,2},{4,5},{5,4},{6,7},{7,6},{8,9},{9,8},{10,11... | collective-permute-start | bytes 294920 | tf_op jit(solution)/shard_map/ppermute | solution.py:19
  20.2 10.7 %collective-permute-start.16 = (bf16[2,24,1024]{2,1,0:T(8,128)(2,1)S(1)}, bf16[2,24,1024]{2,1,0:T(8,128)(2,1)S(1)}, u32[]{:S(2)}, u32[]{:S(2)}) collective-permute-start(bf16[2,24,1024]{2,1,0:T(8,128)(2,1)S(1)} %get-tuple-element.40), channel_id=1, source_target_pairs={{0,2},{1,3},{2,0},{3,1},{4,6},{5,7},{6,4},{7,5},{8,10},{9,11},{10,... | collective-permute-start | bytes 294920 | tf_op jit(solution)/shard_map/ppermute | solution.py:19
  22.8 8.1 %collective-permute-start.17 = (bf16[2,24,1024]{2,1,0:T(8,128)(2,1)S(1)}, bf16[2,24,1024]{2,1,0:T(8,128)(2,1)S(1)}, u32[]{:S(2)}, u32[]{:S(2)}) collective-permute-start(bf16[2,24,1024]{2,1,0:T(8,128)(2,1)S(1)} %get-tuple-element.41), channel_id=1, source_target_pairs={{0,3},{1,2},{2,1},{3,0},{4,7},{5,6},{6,5},{7,4},{8,11},{9,10},{10,... | collective-permute-start | bytes 294920 | tf_op jit(solution)/shard_map/ppermute | solution.py:19
  23.3 12.4 %collective-permute-start.2 = (bf16[2,24,1024]{2,1,0:T(8,128)(2,1)S(1)}, bf16[2,24,1024]{2,1,0:T(8,128)(2,1)S(1)}, u32[]{:S(2)}, u32[]{:S(2)}) collective-permute-start(bf16[2,24,1024]{2,1,0:T(8,128)(2,1)S(1)} %get-tuple-element.30), channel_id=1, source_target_pairs={{0,1},{1,0},{2,3},{3,2},{4,5},{5,4},{6,7},{7,6},{8,9},{9,8},{10,11... | collective-permute-start | bytes 294920 | tf_op jit(solution)/shard_map/ppermute | solution.py:19
  30.8 8.5 %collective-permute-start.3 = (bf16[2,24,1024]{2,1,0:T(8,128)(2,1)S(1)}, bf16[2,24,1024]{2,1,0:T(8,128)(2,1)S(1)}, u32[]{:S(2)}, u32[]{:S(2)}) collective-permute-start(bf16[2,24,1024]{2,1,0:T(8,128)(2,1)S(1)} %get-tuple-element.31), channel_id=1, source_target_pairs={{0,2},{1,3},{2,0},{3,1},{4,6},{5,7},{6,4},{7,5},{8,10},{9,11},{10,... | collective-permute-start | bytes 294920 | tf_op jit(solution)/shard_map/ppermute | solution.py:19
  30.9 10.0 %collective-permute-start.4 = (bf16[2,24,1024]{2,1,0:T(8,128)(2,1)S(1)}, bf16[2,24,1024]{2,1,0:T(8,128)(2,1)S(1)}, u32[]{:S(2)}, u32[]{:S(2)}) collective-permute-start(bf16[2,24,1024]{2,1,0:T(8,128)(2,1)S(1)} %get-tuple-element.32), channel_id=1, source_target_pairs={{0,3},{1,2},{2,1},{3,0},{4,7},{5,6},{6,5},{7,4},{8,11},{9,10},{10,... | collective-permute-start | bytes 294920 | tf_op jit(solution)/shard_map/ppermute | solution.py:19
  35.6 11.7 %collective-permute-start.18 = (bf16[2,96,1024]{2,1,0:T(8,128)(2,1)S(1)}, bf16[2,96,1024]{2,1,0:T(8,128)(2,1)S(1)}, u32[]{:S(2)}, u32[]{:S(2)}) collective-permute-start(bf16[2,96,1024]{2,1,0:T(8,128)(2,1)S(1)} %constant_dynamic-update-slice_fusion.4.own_ref), channel_id=1, source_target_pairs={{0,8},{4,12},{8,0},{12,4},{16,24},{20,28},{24,16},{28,20},{1,9},{5... | collective-permute-start | bytes 1179656 | tf_op jit(solution)/shard_map/ppermute | solution.py:19
  39.4 12.1 %collective-permute-start.19 = (bf16[2,96,1024]{2,1,0:T(8,128)(2,1)S(1)}, bf16[2,96,1024]{2,1,0:T(8,128)(2,1)S(1)}, u32[]{:S(2)}, u32[]{:S(2)}) collective-permute-start(bf16[2,96,1024]{2,1,0:T(8,128)(2,1)S(1)} %constant_dynamic-update-slice_fusion.4.own_ref), channel_id=1, source_target_pairs={{0,16},{4,20},{8,24},{12,28},{16,0},{20,4},{24,8},{28,12},{1,17},{... | collective-permute-start | bytes 1179656 | tf_op jit(solution)/shard_map/ppermute | solution.py:19
  40.9 12.3 %collective-permute-start.5 = (bf16[2,96,1024]{2,1,0:T(8,128)(2,1)S(1)}, bf16[2,96,1024]{2,1,0:T(8,128)(2,1)S(1)}, u32[]{:S(2)}, u32[]{:S(2)}) collective-permute-start(bf16[2,96,1024]{2,1,0:T(8,128)(2,1)S(1)} %constant_dynamic-update-slice_fusion.own_ref), channel_id=1, source_target_pairs={{0,8},{4,12},{8,0},{12,4},{16,24},{20,28},{24,16},{28,20},{1,9},{5... | collective-permute-start | bytes 1179656 | tf_op jit(solution)/shard_map/ppermute | solution.py:19
  47.3 11.3 %collective-permute-start.6 = (bf16[2,96,1024]{2,1,0:T(8,128)(2,1)S(1)}, bf16[2,96,1024]{2,1,0:T(8,128)(2,1)S(1)}, u32[]{:S(2)}, u32[]{:S(2)}) collective-permute-start(bf16[2,96,1024]{2,1,0:T(8,128)(2,1)S(1)} %constant_dynamic-update-slice_fusion.own_ref), channel_id=1, source_target_pairs={{0,16},{4,20},{8,24},{12,28},{16,0},{20,4},{24,8},{28,12},{1,17},{... | collective-permute-start | bytes 1179656 | tf_op jit(solution)/shard_map/ppermute | solution.py:19
  51.4 9.3 %collective-permute-start.20 = (bf16[1,96,1024]{2,1,0:T(8,128)(2,1)S(1)}, bf16[1,96,1024]{2,1,0:T(8,128)(2,1)S(1)}, u32[]{:S(2)}, u32[]{:S(2)}) collective-permute-start(bf16[1,96,1024]{2,1,0:T(8,128)(2,1)S(1)} %slice.83), channel_id=1, source_target_pairs={{0,16},{4,20},{8,24},{12,28},{16,0},{20,4},{24,8},{28,12},{1,17},{... | collective-permute-start | bytes 589832 | tf_op jit(solution)/shard_map/ppermute | solution.py:19
  53.3 9.0 %collective-permute-start.21 = (bf16[1,96,1024]{2,1,0:T(8,128)(2,1)S(1)}, bf16[1,96,1024]{2,1,0:T(8,128)(2,1)S(1)}, u32[]{:S(2)}, u32[]{:S(2)}) collective-permute-start(bf16[1,96,1024]{2,1,0:T(8,128)(2,1)S(1)} %slice.84), channel_id=1, source_target_pairs={{0,8},{4,12},{8,0},{12,4},{16,24},{20,28},{24,16},{28,20},{1,9},{5... | collective-permute-start | bytes 589832 | tf_op jit(solution)/shard_map/ppermute | solution.py:19
  58.6 13.5 %collective-permute-start.7 = (bf16[1,96,1024]{2,1,0:T(8,128)(2,1)S(1)}, bf16[1,96,1024]{2,1,0:T(8,128)(2,1)S(1)}, u32[]{:S(2)}, u32[]{:S(2)}) collective-permute-start(bf16[1,96,1024]{2,1,0:T(8,128)(2,1)S(1)} %slice.80), channel_id=1, source_target_pairs={{0,16},{4,20},{8,24},{12,28},{16,0},{20,4},{24,8},{28,12},{1,17},{... | collective-permute-start | bytes 589832 | tf_op jit(solution)/shard_map/ppermute | solution.py:19
  60.7 11.4 %collective-permute-start.8 = (bf16[1,96,1024]{2,1,0:T(8,128)(2,1)S(1)}, bf16[1,96,1024]{2,1,0:T(8,128)(2,1)S(1)}, u32[]{:S(2)}, u32[]{:S(2)}) collective-permute-start(bf16[1,96,1024]{2,1,0:T(8,128)(2,1)S(1)} %slice.81), channel_id=1, source_target_pairs={{0,8},{4,12},{8,0},{12,4},{16,24},{20,28},{24,16},{28,20},{1,9},{5... | collective-permute-start | bytes 589832 | tf_op jit(solution)/shard_map/ppermute | solution.py:19
  70.0 11.9 %collective-permute-start.22 = (bf16[1,96,1024]{2,1,0:T(8,128)(2,1)S(1)}, bf16[1,96,1024]{2,1,0:T(8,128)(2,1)S(1)}, u32[]{:S(2)}, u32[]{:S(2)}) collective-permute-start(bf16[1,96,1024]{2,1,0:T(8,128)(2,1)S(1)} %get-tuple-element.44), channel_id=1, source_target_pairs={{0,16},{4,20},{8,24},{12,28},{16,0},{20,4},{24,8},{28,12},{1,17},{... | collective-permute-start | bytes 589832 | tf_op jit(solution)/shard_map/ppermute | solution.py:19
  71.6 11.0 %collective-permute-start.24 = (bf16[1,96,1024]{2,1,0:T(8,128)(2,1)S(1)}, bf16[1,96,1024]{2,1,0:T(8,128)(2,1)S(1)}, u32[]{:S(2)}, u32[]{:S(2)}) collective-permute-start(bf16[1,96,1024]{2,1,0:T(8,128)(2,1)S(1)} %get-tuple-element.46), channel_id=1, source_target_pairs={{0,8},{4,12},{8,0},{12,4},{16,24},{20,28},{24,16},{28,20},{1,9},{5... | collective-permute-start | bytes 589832 | tf_op jit(solution)/shard_map/ppermute | solution.py:19
  79.9 7.9 %collective-permute-start.11 = (bf16[1,96,1024]{2,1,0:T(8,128)(2,1)S(1)}, bf16[1,96,1024]{2,1,0:T(8,128)(2,1)S(1)}, u32[]{:S(2)}, u32[]{:S(2)}) collective-permute-start(bf16[1,96,1024]{2,1,0:T(8,128)(2,1)S(1)} %get-tuple-element.35), channel_id=1, source_target_pairs={{0,16},{4,20},{8,24},{12,28},{16,0},{20,4},{24,8},{28,12},{1,17},{... | collective-permute-start | bytes 589832 | tf_op jit(solution)/shard_map/ppermute | solution.py:19
  80.5 8.6 %collective-permute-start.13 = (bf16[1,96,1024]{2,1,0:T(8,128)(2,1)S(1)}, bf16[1,96,1024]{2,1,0:T(8,128)(2,1)S(1)}, u32[]{:S(2)}, u32[]{:S(2)}) collective-permute-start(bf16[1,96,1024]{2,1,0:T(8,128)(2,1)S(1)} %get-tuple-element.37), channel_id=1, source_target_pairs={{0,8},{4,12},{8,0},{12,4},{16,24},{20,28},{24,16},{28,20},{1,9},{5... | collective-permute-start | bytes 589832 | tf_op jit(solution)/shard_map/ppermute | solution.py:19
  82.1 11.4 %collective-permute-start.23 = (bf16[2,96,1024]{2,1,0:T(8,128)(2,1)S(1)}, bf16[2,96,1024]{2,1,0:T(8,128)(2,1)S(1)}, u32[]{:S(2)}, u32[]{:S(2)}) collective-permute-start(bf16[2,96,1024]{2,1,0:T(8,128)(2,1)S(1)} %pad_maximum_fusion.2), channel_id=1, source_target_pairs={{0,8},{4,12},{8,0},{12,4},{16,24},{20,28},{24,16},{28,20},{1,9},{5... | collective-permute-start | bytes 1179656 | tf_op jit(solution)/shard_map/ppermute | solution.py:19
  82.8 10.8 %collective-permute-start.25 = (bf16[2,96,1024]{2,1,0:T(8,128)(2,1)S(1)}, bf16[2,96,1024]{2,1,0:T(8,128)(2,1)S(1)}, u32[]{:S(2)}, u32[]{:S(2)}) collective-permute-start(bf16[2,96,1024]{2,1,0:T(8,128)(2,1)S(1)} %pad_maximum_fusion.3), channel_id=1, source_target_pairs={{0,16},{4,20},{8,24},{12,28},{16,0},{20,4},{24,8},{28,12},{1,17},{... | collective-permute-start | bytes 1179656 | tf_op jit(solution)/shard_map/ppermute | solution.py:19
  87.9 10.6 %collective-permute-start.12 = (bf16[2,96,1024]{2,1,0:T(8,128)(2,1)S(1)}, bf16[2,96,1024]{2,1,0:T(8,128)(2,1)S(1)}, u32[]{:S(2)}, u32[]{:S(2)}) collective-permute-start(bf16[2,96,1024]{2,1,0:T(8,128)(2,1)S(1)} %pad_maximum_fusion), channel_id=1, source_target_pairs={{0,8},{4,12},{8,0},{12,4},{16,24},{20,28},{24,16},{28,20},{1,9},{5... | collective-permute-start | bytes 1179656 | tf_op jit(solution)/shard_map/ppermute | solution.py:19
  89.2 9.3 %collective-permute-start.14 = (bf16[2,96,1024]{2,1,0:T(8,128)(2,1)S(1)}, bf16[2,96,1024]{2,1,0:T(8,128)(2,1)S(1)}, u32[]{:S(2)}, u32[]{:S(2)}) collective-permute-start(bf16[2,96,1024]{2,1,0:T(8,128)(2,1)S(1)} %pad_maximum_fusion.1), channel_id=1, source_target_pairs={{0,16},{4,20},{8,24},{12,28},{16,0},{20,4},{24,8},{28,12},{1,17},{... | collective-permute-start | bytes 1179656 | tf_op jit(solution)/shard_map/ppermute | solution.py:19
  93.7 9.5 %collective-permute-start.27 = (bf16[2,24,1024]{2,1,0:T(8,128)(2,1)S(1)}, bf16[2,24,1024]{2,1,0:T(8,128)(2,1)S(1)}, u32[]{:S(2)}, u32[]{:S(2)}) collective-permute-start(bf16[2,24,1024]{2,1,0:T(8,128)(2,1)S(1)} %get-tuple-element.51), channel_id=1, source_target_pairs={{0,1},{1,0},{2,3},{3,2},{4,5},{5,4},{6,7},{7,6},{8,9},{9,8},{10,11... | collective-permute-start | bytes 294920 | tf_op jit(solution)/shard_map/ppermute | solution.py:19
  95.4 8.9 %collective-permute-start.29 = (bf16[2,24,1024]{2,1,0:T(8,128)(2,1)S(1)}, bf16[2,24,1024]{2,1,0:T(8,128)(2,1)S(1)}, u32[]{:S(2)}, u32[]{:S(2)}) collective-permute-start(bf16[2,24,1024]{2,1,0:T(8,128)(2,1)S(1)} %get-tuple-element.50), channel_id=1, source_target_pairs={{0,2},{1,3},{2,0},{3,1},{4,6},{5,7},{6,4},{7,5},{8,10},{9,11},{10,... | collective-permute-start | bytes 294920 | tf_op jit(solution)/shard_map/ppermute | solution.py:19
  98.5 6.5 %collective-permute-start.31 = (bf16[2,24,1024]{2,1,0:T(8,128)(2,1)S(1)}, bf16[2,24,1024]{2,1,0:T(8,128)(2,1)S(1)}, u32[]{:S(2)}, u32[]{:S(2)}) collective-permute-start(bf16[2,24,1024]{2,1,0:T(8,128)(2,1)S(1)} %get-tuple-element.49), channel_id=1, source_target_pairs={{0,3},{1,2},{2,1},{3,0},{4,7},{5,6},{6,5},{7,4},{8,11},{9,10},{10,... | collective-permute-start | bytes 294920 | tf_op jit(solution)/shard_map/ppermute | solution.py:19
  98.7 6.3 %collective-permute-start.26 = (bf16[2,24,1024]{2,1,0:T(8,128)(2,1)S(1)}, bf16[2,24,1024]{2,1,0:T(8,128)(2,1)S(1)}, u32[]{:S(2)}, u32[]{:S(2)}) collective-permute-start(bf16[2,24,1024]{2,1,0:T(8,128)(2,1)S(1)} %get-tuple-element.55), channel_id=1, source_target_pairs={{0,1},{1,0},{2,3},{3,2},{4,5},{5,4},{6,7},{7,6},{8,9},{9,8},{10,11... | collective-permute-start | bytes 294920 | tf_op jit(solution)/shard_map/ppermute | solution.py:19
  99.6 7.7 %collective-permute-start.28 = (bf16[2,24,1024]{2,1,0:T(8,128)(2,1)S(1)}, bf16[2,24,1024]{2,1,0:T(8,128)(2,1)S(1)}, u32[]{:S(2)}, u32[]{:S(2)}) collective-permute-start(bf16[2,24,1024]{2,1,0:T(8,128)(2,1)S(1)} %get-tuple-element.54), channel_id=1, source_target_pairs={{0,2},{1,3},{2,0},{3,1},{4,6},{5,7},{6,4},{7,5},{8,10},{9,11},{10,... | collective-permute-start | bytes 294920 | tf_op jit(solution)/shard_map/ppermute | solution.py:19
  103.2 6.4 %collective-permute-start.30 = (bf16[2,24,1024]{2,1,0:T(8,128)(2,1)S(1)}, bf16[2,24,1024]{2,1,0:T(8,128)(2,1)S(1)}, u32[]{:S(2)}, u32[]{:S(2)}) collective-permute-start(bf16[2,24,1024]{2,1,0:T(8,128)(2,1)S(1)} %get-tuple-element.53), channel_id=1, source_target_pairs={{0,3},{1,2},{2,1},{3,0},{4,7},{5,6},{6,5},{7,4},{8,11},{9,10},{10,... | collective-permute-start | bytes 294920 | tf_op jit(solution)/shard_map/ppermute | solution.py:19
  (6 other events, 28.7 us)

commit v2 on v1

v2 whole, which is shorter than its diff:
```python
import functools

import jax
import jax.numpy as jnp
from jax import lax
from jax.experimental import pallas as pl
from jax.experimental.pallas import tpu as pltpu
from jax.sharding import PartitionSpec as P

F32 = jnp.float32
BF16 = jnp.bfloat16
CHUNKS = 2
CORE, NEAR_A, NEAR_B = 0, 1, 2
GROUP_BITS = 3
VMEM_LIMIT = 16 * 1024 * 1024


def swapped(array, axis, distance):
    return lax.ppermute(array, axis, [(i, i ^ distance) for i in range(lax.axis_size(axis))])


def after(value, *others):
    return lax.optimization_barrier((value, *others))[0]


def mm(a, b, dims=((1,), (0,))):
    return lax.dot_general(a, b, (dims, ((), ())), preferred_element_type=F32)


def vmem():
    return pl.BlockSpec(memory_space=pltpu.VMEM)


def smem():
    return pl.BlockSpec(memory_space=pltpu.SMEM)


def embed_kernel(tubelets_ref, weight_ref, gain_ref, emb_ref, normed_ref):
    embedded = mm(tubelets_ref[...], weight_ref[...]).astype(BF16)
    emb_ref[...] = embedded
    floats = embedded.astype(F32)
    centred = floats - jnp.mean(floats, axis=-1, keepdims=True)
    variance = jnp.mean(centred * centred, axis=-1, keepdims=True)
    normed_ref[...] = (centred * lax.rsqrt(variance + 1e-06) * gain_ref[...]).astype(BF16)


def embed(tubelets, weight, gain):
    tok, width = tubelets.shape[0], weight.shape[1]
    shape = jax.ShapeDtypeStruct((tok, width), BF16)
    return pl.pallas_call(
        embed_kernel,
        out_shape=[shape, shape],
        in_specs=[vmem()] * 3,
        out_specs=[vmem()] * 2,
        compiler_params=pltpu.CompilerParams(vmem_limit_bytes=VMEM_LIMIT),
        cost_estimate=pl.CostEstimate(flops=2 * tok * weight.size, bytes_accessed=weight.size * 2, transcendentals=0),
        name="embed",
    )(tubelets, weight, gain.reshape(1, width))


def route_kernel(n_exp, half, cap, place_ref, route_ref, sib_route_ref, code_ref, sib_code_ref, select_ref, gate_ref):
    tok = route_ref.shape[0]
    both = 2 * tok
    count = n_exp * half
    slots = 2 * cap
    rows = count * slots
    routes = jnp.concatenate([route_ref[...], sib_route_ref[...]], axis=0)
    codes = jnp.concatenate([code_ref[...], sib_code_ref[...]], axis=0)
    plane, core = place_ref[0], place_ref[1]

    column = lax.broadcasted_iota(jnp.int32, (both, count), 1)
    expert = (plane ^ (column // half)) * (2 * half) + core * half + column % half
    first = routes[:, 0:1] == expert
    second = routes[:, 1:2] == expert
    member = jnp.where(first | second, 1.0, 0.0)
    gates = 0.25 + 0.125 * codes.astype(F32)
    gated = jnp.where(first, gates[:, 0:1], 0.0) + jnp.where(second, gates[:, 1:2], 0.0)
    earlier_t = lax.broadcasted_iota(jnp.int32, (both, both), 0)
    later_t = lax.broadcasted_iota(jnp.int32, (both, both), 1)
    same = (earlier_t // tok) == (later_t // tok)
    before = jnp.where(same & (earlier_t < later_t), 1.0, 0.0).astype(BF16)
    after_t = jnp.where(same & (later_t < earlier_t), 1.0, 0.0).astype(BF16)
    equal = jnp.where(earlier_t == later_t, 1.0, 0.0).astype(BF16)
    member16 = member.astype(BF16)
    rank_t = mm(member16, before, ((0,), (0,)))
    member_t = mm(member16, equal, ((0,), (0,)))
    block_t = jnp.where(lax.broadcasted_iota(jnp.int32, (count, both), 1) >= tok, float(cap), 0.0)
    pos_t = jnp.where(member_t > 0.5, rank_t + block_t, -1.0).astype(BF16)
    spread = jnp.where(
        lax.broadcasted_iota(jnp.int32, (rows, count), 0) // slots
        == lax.broadcasted_iota(jnp.int32, (rows, count), 1), 1.0, 0.0).astype(BF16)
    slot_t = (lax.broadcasted_iota(jnp.int32, (rows, both), 0) % slots).astype(F32)
    select_ref[...] = jnp.where(mm(spread, pos_t) == slot_t, 1.0, 0.0).astype(BF16)

    rank = mm(after_t, member16)
    block = jnp.where(lax.broadcasted_iota(jnp.int32, (both, count), 0) >= tok, float(cap), 0.0)
    pos = jnp.where(member > 0.5, rank + block, -1.0).astype(BF16)
    slot = (lax.broadcasted_iota(jnp.int32, (both, rows), 1) % slots).astype(F32)
    spread_gate = mm(gated.astype(BF16), spread, ((1,), (1,)))
    gate_ref[...] = jnp.where(mm(pos, spread, ((1,), (1,))) == slot, spread_gate, 0.0).astype(BF16)


def route(place, routes, sib_routes, codes, sib_codes, n_exp, half, cap):
    both = 2 * routes.shape[0]
    rows = n_exp * half * 2 * cap
    return pl.pallas_call(
        functools.partial(route_kernel, n_exp, half, cap),
        out_shape=[jax.ShapeDtypeStruct((rows, both), BF16), jax.ShapeDtypeStruct((both, rows), BF16)],
        in_specs=[smem()] + [vmem()] * 4,
        out_specs=[vmem()] * 2,
        compiler_params=pltpu.CompilerParams(vmem_limit_bytes=VMEM_LIMIT),
        cost_estimate=pl.CostEstimate(flops=2 * rows * both * 64, bytes_accessed=rows * both * 4, transcendentals=0),
        name="route",
    )(place, routes, sib_routes, codes, sib_codes)


def pack_kernel(select_ref, normed_ref, sib_ref, *piece_refs):
    buffer = mm(select_ref[...], jnp.concatenate([normed_ref[...], sib_ref[...]], axis=0))
    per, slots, _ = piece_refs[0].shape
    for index, ref in enumerate(piece_refs):
        for e in range(per):
            start = (index * per + e) * slots
            ref[e] = buffer[start:start + slots].astype(BF16)


def pack(select, normed, sib_normed, n_exp, half, cap):
    width = normed.shape[1]
    rows = select.shape[0]
    shape = jax.ShapeDtypeStruct((half // CHUNKS, 2 * cap, width), BF16)
    pieces = pl.pallas_call(
        pack_kernel,
        out_shape=[shape] * (n_exp * CHUNKS),
        in_specs=[vmem()] * 3,
        out_specs=[vmem()] * (n_exp * CHUNKS),
        compiler_params=pltpu.CompilerParams(vmem_limit_bytes=VMEM_LIMIT),
        cost_estimate=pl.CostEstimate(
            flops=2 * select.size * width, bytes_accessed=rows * width * 4, transcendentals=0),
        name="pack",
    )(select, normed, sib_normed)
    return [[pieces[s * CHUNKS + c] for s in range(n_exp)] for c in range(CHUNKS)]


def experts_kernel(chunk, half, place_ref, own_ref, a_ref, b_ref, d1_ref, d2_ref,
                   in_own_ref, in_sib_ref, down_own_ref, down_sib_ref,
                   p_own_ref, p_a_ref, p_b_ref, p_d1_ref, p_d2_ref, h_ref):
    per, m, _ = own_ref.shape
    split = per // 2
    ff = in_own_ref.shape[2]
    for e in range(per):
        index = place_ref[1] * half + chunk * per + e
        diagonal, p_diagonal = (d1_ref, p_d1_ref) if e < split else (d2_ref, p_d2_ref)
        x = jnp.concatenate([own_ref[e], a_ref[e], b_ref[e], diagonal[e % split]], axis=0)
        h_ref[:, 0:ff] = jax.nn.gelu(mm(x, in_own_ref[index])).astype(BF16)
        h_ref[:, ff:] = jax.nn.gelu(mm(x, in_sib_ref[index])).astype(BF16)
        total = mm(h_ref[:, 0:ff], down_own_ref[index], ((1,), (1,))) + mm(
            h_ref[:, ff:], down_sib_ref[index], ((1,), (1,)))
        p_own_ref[e] = total[0:m].astype(BF16)
        p_a_ref[e] = total[m:2 * m].astype(BF16)
        p_b_ref[e] = total[2 * m:3 * m].astype(BF16)
        p_diagonal[e % split] = total[3 * m:4 * m].astype(BF16)


def experts(place, chunk, own, near_a, near_b, d1, d2, in_own, in_sib, down_own, down_sib):
    per, m, width = own.shape
    count, _, ff = in_own.shape
    shape = jax.ShapeDtypeStruct(own.shape, BF16)
    part = jax.ShapeDtypeStruct(d1.shape, BF16)
    return pl.pallas_call(
        functools.partial(experts_kernel, chunk, count // 2),
        out_shape=[shape, shape, shape, part, part],
        in_specs=[smem()] + [vmem()] * 9,
        out_specs=[vmem()] * 5,
        scratch_shapes=[pltpu.VMEM((4 * m, 2 * ff), BF16)],
        compiler_params=pltpu.CompilerParams(vmem_limit_bytes=VMEM_LIMIT),
        cost_estimate=pl.CostEstimate(
            flops=2 * per * 4 * m * width * 2 * ff * 2, bytes_accessed=per * m * width * 16,
            transcendentals=per * 4 * m * 2 * ff),
        name="experts",
    )(place, own, near_a, near_b, d1, d2, in_own, in_sib, down_own, down_sib)


def combine_kernel(tok, gate_ref, emb_ref, *refs):
    piece_refs, (mine_ref, send_ref, rows_ref) = refs[:-3], refs[-3:]
    per, slots, _ = piece_refs[0].shape
    for index, ref in enumerate(piece_refs):
        for e in range(per):
            start = (index * per + e) * slots
            rows_ref[start:start + slots] = ref[e].astype(F32)
    total = mm(gate_ref[...], rows_ref[...].astype(BF16))
    mine_ref[...] = total[0:tok] + emb_ref[...].astype(F32)
    send_ref[...] = total[tok:2 * tok].astype(BF16)


def combine(gate, embedded, pieces):
    tok, width = embedded.shape
    rows = gate.shape[1]
    return pl.pallas_call(
        functools.partial(combine_kernel, tok),
        out_shape=[jax.ShapeDtypeStruct((tok, width), F32), jax.ShapeDtypeStruct((tok, width), BF16)],
        in_specs=[vmem()] * (2 + len(pieces)),
        out_specs=[vmem()] * 2,
        scratch_shapes=[pltpu.VMEM((rows, width), F32)],
        compiler_params=pltpu.CompilerParams(vmem_limit_bytes=VMEM_LIMIT),
        cost_estimate=pl.CostEstimate(flops=4 * tok * rows * width, bytes_accessed=rows * width * 2, transcendentals=0),
        name="combine",
    )(gate, embedded, *pieces)


def on_device(tubelets, embed_weight, norm_gain, routes, gate_codes, w_in, w_down):
    tok = tubelets.shape[0]
    n_exp = lax.axis_size("exp")
    half = w_in.shape[0] // 2
    cap = 3 * tok // (w_in.shape[0] * n_exp)
    position = lax.axis_index("rep")
    core = position % 2
    place = jnp.stack([lax.axis_index("exp"), core]).astype(jnp.int32)

    core_bit = 1 << CORE
    sib_routes = swapped(routes, "rep", core_bit)
    sib_codes = swapped(gate_codes, "rep", core_bit)
    embedded, normed = embed(tubelets, embed_weight, norm_gain)
    sib_normed = swapped(normed, "rep", core_bit)
    select, gate = route(place, routes, sib_routes, gate_codes, sib_codes, n_exp, half, cap)

    for bit in range(GROUP_BITS, lax.axis_size("rep").bit_length() - 1):
        upper = position // (1 << bit) % 2 == 1

        def gathered(panel):
            partner = swapped(panel, "rep", 1 << bit)
            return jnp.where(upper, jnp.concatenate([partner, panel], axis=2), jnp.concatenate([panel, partner], axis=2))

        w_in, w_down = gathered(w_in), gathered(w_down)

    in_sib = swapped(after(w_in, sib_normed, select), "rep", core_bit)
    down_sib = swapped(after(w_down, sib_normed, select), "rep", core_bit)
    pieces = pack(select, normed, sib_normed, n_exp, half, cap)

    def from_planes(leaving):
        arrived = [leaving[0]] + [swapped(leaving[s], "exp", s) for s in range(1, n_exp)]
        return jnp.concatenate(arrived, axis=1)

    def to_planes(p_own, from_a, from_b):
        done = (p_own.astype(F32) + from_a.astype(F32) + from_b.astype(F32)).astype(BF16)
        done = done.reshape(done.shape[0], n_exp, 2 * cap, done.shape[2])
        return [done[:, 0]] + [swapped(done[:, s], "exp", s) for s in range(1, n_exp)]

    split = half // CHUNKS // 2
    a_bit, b_bit = 1 << NEAR_A, 1 << NEAR_B

    def reduced(parts, r):
        _, p_a, p_b, _, _ = parts
        to_b = jnp.concatenate([p_b[:split] + r[0], p_b[split:]], axis=0)
        to_a = jnp.concatenate([p_a[:split], p_a[split:] + r[1]], axis=0)
        return to_a, to_b

    early1 = swapped(pieces[1][1], "exp", 1)
    own0 = from_planes(pieces[0])
    late1 = lax.optimization_barrier((*pieces[1][2:], own0, in_sib))[:n_exp - 2]
    own1 = jnp.concatenate(
        [pieces[1][0], early1] + [swapped(piece, "exp", s + 2) for s, piece in enumerate(late1)], axis=1)
    a0, b0 = swapped(own0, "rep", a_bit), swapped(own0, "rep", b_bit)
    own1 = after(own1, a0, b0)
    d0 = swapped(a0[:split], "rep", b_bit), swapped(b0[split:], "rep", a_bit)
    a1, b1 = swapped(own1, "rep", a_bit), swapped(own1, "rep", b_bit)
    parts0 = experts(place, 0, own0, a0, b0, *d0, w_in, in_sib, w_down, down_sib)
    a1, b1, *parts0 = lax.optimization_barrier((a1, b1, *parts0))
    d1 = swapped(a1[:split], "rep", b_bit), swapped(b1[split:], "rep", a_bit)
    r0 = swapped(parts0[3], "rep", a_bit), swapped(parts0[4], "rep", b_bit)
    to_a0, to_b0 = reduced(parts0, r0)
    to_a0, to_b0, *d1 = lax.optimization_barrier((to_a0, to_b0, *d1))
    from_a0, from_b0 = swapped(to_a0, "rep", a_bit), swapped(to_b0, "rep", b_bit)
    parts1 = experts(place, 1, own1, a1, b1, *d1, w_in, in_sib, w_down, down_sib)
    *parts1, from_a0, from_b0 = lax.optimization_barrier((*parts1, from_a0, from_b0))
    r1 = swapped(parts1[3], "rep", a_bit), swapped(parts1[4], "rep", b_bit)
    returned0 = to_planes(parts0[0], from_a0, from_b0)
    to_a1, to_b1 = reduced(parts1, r1)
    from_a1, from_b1 = swapped(to_a1, "rep", a_bit), swapped(to_b1, "rep", b_bit)
    returned = [returned0, to_planes(parts1[0], from_a1, from_b1)]

    pieces_back = [returned[c][s] for s in range(n_exp) for c in range(CHUNKS)]
    mine, send = combine(gate, embedded, pieces_back)
    other = swapped(send, "rep", 1 << CORE)
    return (mine + other.astype(F32)).astype(BF16)


def solution(mesh):
    return jax.shard_map(
        on_device,
        mesh=mesh,
        in_specs=(
            P(("rep", "exp"), None),
            P(),
            P(),
            P(("rep", "exp"), None),
            P(("rep", "exp"), None),
            P("exp", None, "rep"),
            P("exp", None, "rep"),
        ),
        out_specs=P(("rep", "exp"), None),
        check_vma=False,
    )
```

time: 113 us -> 107 us (0.947)
  Pallas kernels: 19.7 us -> 11.4 us
  local copies, waits for them, and re-layouts: 8.14 us -> 12 us
  waiting for transfers between devices: 40.4 us -> 38.1 us
    unnamed x16 -> x15, local copies, waits for them, and re-layouts: 0.93 us -> 11.9 us
    pallas_call x3 -> x5, Pallas kernels: 19.3 us -> 11 us  [the longest x2 8.58 us: experts(): pl.pallas_call(functools.partial(experts_kernel, chunk, count // 2), out_...]
    dynamic_slice x2 -> x0, local copies, waits for them, and re-layouts: 6.96 us -> none  [the longest x1 4.76 us: on_device(): lax.dynamic_slice_in_dim(w_down, (1 - core) * half, half, 0)]
    ppermute x33 -> x34, waiting for transfers between devices: 40.4 us -> 38.1 us  [swapped(): lax.ppermute(array, axis, [(i, i ^ distance) for i in range(lax.axis_size...]
    ppermute x33 -> x34, starting transfers between devices: 42.5 us -> 43 us  [swapped(): lax.ppermute(array, axis, [(i, i ^ distance) for i in range(lax.axis_size...]
  transfers between devices with their start and end apart: 33 -> 34, of which waited for: 15 -> 17; matrix products, arithmetic and copies ran while one was open for 3% -> 2% of each run, Pallas kernels for 17% -> 10%
where the time goes in v2:
time: 107 us; the launch traced here: 106 us
  starting transfers between devices  43 us (40%)
  waiting for transfers between devices  38.1 us (36%)
  local copies, waits for them, and re-layouts  12 us (11%)
  Pallas kernels  11.4 us (11%)
  other arithmetic  1.55 us (1%)
    ppermute x34, starting transfers between devices, swapped(): lax.ppermute(array, axis, [(i, i ^ distance) for i in range(lax.axis_size...  43 us
    ppermute x34, waiting for transfers between devices, swapped(): lax.ppermute(array, axis, [(i, i ^ distance) for i in range(lax.axis_size...  38.1 us
    unnamed x15, local copies, waits for them, and re-layouts  11.9 us
    pallas_call x2, Pallas kernels, experts(): pl.pallas_call(functools.partial(experts_kernel, chunk, count // 2), out_...  8.58 us
  transfers between devices with their start and end apart: 34, of which 17 were waited for; matrix products, arithmetic and copies ran while one was open for 2% of the time, Pallas kernels for 10%

profile of v2, /device:TPU:0, one launch (start us, length us, event | category | flops | bytes accessed | tf_op | source)
XLA Modules:
  0.0 106.3 jit_solution(10205038863112633814)
XLA Ops:
  0.0 1.9 %copy-done.2 = bf16[1536,1024]{1,0:T(8,128)(2,1)S(1)} copy-done((bf16[1536,1024]{1,0:T(8,128)(2,1)S(1)}, bf16[1536,1024]{1,0:T(8,128)(2,1)}, u32[]{:S(2)}) %copy-start.2) | copy-done | bytes 3145752
  10.2 3.0 %collective-permute-start.4 = (bf16[2,24,1024]{2,1,0:T(8,128)(2,1)S(1)}, bf16[2,24,1024]{2,1,0:T(8,128)(2,1)S(1)}, u32[]{:S(2)}, u32[]{:S(2)}) collective-permute-start(bf16[2,24,1024]{2,1,0:T(8,128)(2,1)S(1)} %get-tuple-element.61), channel_id=1, source_target_pairs={{0,1},{1,0},{2,3},{3,2},{4,5},{5,4},{6,7},{7,6},{8,9},{9,8},{10,11... | collective-permute-start | bytes 294920 | tf_op jit(solution)/shard_map/ppermute | solution.py:19
  13.2 2.6 %collective-permute-start.5 = (bf16[2,24,1024]{2,1,0:T(8,128)(2,1)S(1)}, bf16[2,24,1024]{2,1,0:T(8,128)(2,1)S(1)}, u32[]{:S(2)}, u32[]{:S(2)}) collective-permute-start(bf16[2,24,1024]{2,1,0:T(8,128)(2,1)S(1)} %get-tuple-element.62), channel_id=1, source_target_pairs={{0,2},{1,3},{2,0},{3,1},{4,6},{5,7},{6,4},{7,5},{8,10},{9,11},{10,... | collective-permute-start | bytes 294920 | tf_op jit(solution)/shard_map/ppermute | solution.py:19
  16.3 7.5 %collective-permute-done.5 = bf16[2,24,1024]{2,1,0:T(8,128)(2,1)S(1)} collective-permute-done((bf16[2,24,1024]{2,1,0:T(8,128)(2,1)S(1)}, bf16[2,24,1024]{2,1,0:T(8,128)(2,1)S(1)}, u32[]{:S(2)}, u32[]{:S(2)}) %collective-permute-start.5) | collective-permute-done | bytes 98336 | tf_op jit(solution)/shard_map/ppermute | solution.py:19
  23.9 1.6 %collective-permute-start.11 = (bf16[2,96,1024]{2,1,0:T(8,128)(2,1)S(1)}, bf16[2,96,1024]{2,1,0:T(8,128)(2,1)S(1)}, u32[]{:S(2)}, u32[]{:S(2)}) collective-permute-start(bf16[2,96,1024]{2,1,0:T(8,128)(2,1)S(1)} %constant_dynamic-update-slice_fusion.own_ref), channel_id=1, source_target_pairs={{0,16},{4,20},{8,24},{12,28},{16,0},{20,4},{24,8},{28,12},{1,17},{... | collective-permute-start | bytes 1179656 | tf_op jit(solution)/shard_map/ppermute | solution.py:19
  25.5 1.5 %collective-permute-start.10 = (bf16[2,96,1024]{2,1,0:T(8,128)(2,1)S(1)}, bf16[2,96,1024]{2,1,0:T(8,128)(2,1)S(1)}, u32[]{:S(2)}, u32[]{:S(2)}) collective-permute-start(bf16[2,96,1024]{2,1,0:T(8,128)(2,1)S(1)} %constant_dynamic-update-slice_fusion.own_ref), channel_id=1, source_target_pairs={{0,8},{4,12},{8,0},{12,4},{16,24},{20,28},{24,16},{28,20},{1,9},{5... | collective-permute-start | bytes 1179656 | tf_op jit(solution)/shard_map/ppermute | solution.py:19
  27.0 1.7 %collective-permute-start.3 = (bf16[2,24,1024]{2,1,0:T(8,128)(2,1)S(1)}, bf16[2,24,1024]{2,1,0:T(8,128)(2,1)S(1)}, u32[]{:S(2)}, u32[]{:S(2)}) collective-permute-start(bf16[2,24,1024]{2,1,0:T(8,128)(2,1)S(1)} %get-tuple-element.57), channel_id=1, source_target_pairs={{0,1},{1,0},{2,3},{3,2},{4,5},{5,4},{6,7},{7,6},{8,9},{9,8},{10,11... | collective-permute-start | bytes 294920 | tf_op jit(solution)/shard_map/ppermute | solution.py:19
  28.7 1.5 %collective-permute-start.8 = (bf16[2,24,1024]{2,1,0:T(8,128)(2,1)S(1)}, bf16[2,24,1024]{2,1,0:T(8,128)(2,1)S(1)}, u32[]{:S(2)}, u32[]{:S(2)}) collective-permute-start(bf16[2,24,1024]{2,1,0:T(8,128)(2,1)S(1)} %get-tuple-element.65), channel_id=1, source_target_pairs={{0,2},{1,3},{2,0},{3,1},{4,6},{5,7},{6,4},{7,5},{8,10},{9,11},{10,... | collective-permute-start | bytes 294920 | tf_op jit(solution)/shard_map/ppermute | solution.py:19
  30.1 3.0 %collective-permute-done.11.b_ref = bf16[2,96,1024]{2,1,0:T(8,128)(2,1)S(1)} collective-permute-done((bf16[2,96,1024]{2,1,0:T(8,128)(2,1)S(1)}, bf16[2,96,1024]{2,1,0:T(8,128)(2,1)S(1)}, u32[]{:S(2)}, u32[]{:S(2)}) %collective-permute-start.11) | collective-permute-done | bytes 393248 | tf_op jit(solution)/shard_map/ppermute | solution.py:19
  34.7 1.5 %collective-permute-start.15 = (bf16[1,96,1024]{2,1,0:T(8,128)(2,1)S(1)}, bf16[1,96,1024]{2,1,0:T(8,128)(2,1)S(1)}, u32[]{:S(2)}, u32[]{:S(2)}) collective-permute-start(bf16[1,96,1024]{2,1,0:T(8,128)(2,1)S(1)} %slice.81), channel_id=1, source_target_pairs={{0,8},{4,12},{8,0},{12,4},{16,24},{20,28},{24,16},{28,20},{1,9},{5... | collective-permute-start | bytes 589832 | tf_op jit(solution)/shard_map/ppermute | solution.py:19
  37.5 2.1 %collective-permute-done.9 = bf16[2,24,1024]{2,1,0:T(8,128)(2,1)S(1)} collective-permute-done((bf16[2,24,1024]{2,1,0:T(8,128)(2,1)S(1)}, bf16[2,24,1024]{2,1,0:T(8,128)(2,1)S(1)}, u32[]{:S(2)}, u32[]{:S(2)}) %collective-permute-start.9) | collective-permute-done | bytes 98336 | tf_op jit(solution)/shard_map/ppermute | solution.py:19
  39.7 1.6 %collective-permute-start.13 = (bf16[2,96,1024]{2,1,0:T(8,128)(2,1)S(1)}, bf16[2,96,1024]{2,1,0:T(8,128)(2,1)S(1)}, u32[]{:S(2)}, u32[]{:S(2)}) collective-permute-start(bf16[2,96,1024]{2,1,0:T(8,128)(2,1)S(1)} %pad_maximum_fusion.own_ref), channel_id=1, source_target_pairs={{0,16},{4,20},{8,24},{12,28},{16,0},{20,4},{24,8},{28,12},{1,17},{... | collective-permute-start | bytes 1179656 | tf_op jit(solution)/shard_map/ppermute | solution.py:19
  41.3 1.5 %collective-permute-start.12 = (bf16[2,96,1024]{2,1,0:T(8,128)(2,1)S(1)}, bf16[2,96,1024]{2,1,0:T(8,128)(2,1)S(1)}, u32[]{:S(2)}, u32[]{:S(2)}) collective-permute-start(bf16[2,96,1024]{2,1,0:T(8,128)(2,1)S(1)} %pad_maximum_fusion.own_ref), channel_id=1, source_target_pairs={{0,8},{4,12},{8,0},{12,4},{16,24},{20,28},{24,16},{28,20},{1,9},{5... | collective-permute-start | bytes 1179656 | tf_op jit(solution)/shard_map/ppermute | solution.py:19
  44.2 3.4 %copy-done = bf16[8,1024,512]{2,1,0:T(8,128)(2,1)S(1)} copy-done((bf16[8,1024,512]{2,1,0:T(8,128)(2,1)S(1)}, bf16[8,1024,512]{2,1,0:T(8,128)(2,1)}, u32[]{:S(2)}) %copy-start) | copy-done | bytes 8388632
  47.5 3.4 %copy-done.1 = bf16[8,1024,512]{2,1,0:T(8,128)(2,1)S(1)} copy-done((bf16[8,1024,512]{2,1,0:T(8,128)(2,1)S(1)}, bf16[8,1024,512]{2,1,0:T(8,128)(2,1)}, u32[]{:S(2)}) %copy-start.1) | copy-done | bytes 8388632
  50.9 4.3 %experts.2 = (bf16[2,96,1024]{2,1,0:T(8,128)(2,1)S(1)}, bf16[2,96,1024]{2,1,0:T(8,128)(2,1)S(1)}, bf16[2,96,1024]{2,1,0:T(8,128)(2,1)S(1)}, bf16[1,96,1024]{2,1,0:T(8,128)(2,1)S(1)}, bf16[1,96,1024]{2,1,0:T(8,128)(2,1)S(1)}) custom-call(s32[2]{0:T(128)S(1)} %pad_add_fusion.place_ref, bf16[2,96,1024]{2,1,0:T(8,128)(2,1)S(1)} %constant_dynamic-update-slice_fusion.own_ref, ...), custom_call_target="tpu_custom_call" | custom-call | flops 3221225472 | bytes 3145728 | tf_op jit(solution)/shard_map/experts/pallas_call | solution.py:168
  57.8 1.6 %collective-permute-start.18 = (bf16[1,96,1024]{2,1,0:T(8,128)(2,1)S(1)}, bf16[1,96,1024]{2,1,0:T(8,128)(2,1)S(1)}, u32[]{:S(2)}, u32[]{:S(2)}) collective-permute-start(bf16[1,96,1024]{2,1,0:T(8,128)(2,1)S(1)} %get-tuple-element.80), channel_id=1, source_target_pairs={{0,8},{4,12},{8,0},{12,4},{16,24},{20,28},{24,16},{28,20},{1,9},{5... | collective-permute-start | bytes 589832 | tf_op jit(solution)/shard_map/ppermute | solution.py:19
  59.5 2.7 %collective-permute-done.17 = bf16[1,96,1024]{2,1,0:T(8,128)(2,1)S(1)} collective-permute-done((bf16[1,96,1024]{2,1,0:T(8,128)(2,1)S(1)}, bf16[1,96,1024]{2,1,0:T(8,128)(2,1)S(1)}, u32[]{:S(2)}, u32[]{:S(2)}) %collective-permute-start.17) | collective-permute-done | bytes 196640 | tf_op jit(solution)/shard_map/ppermute | solution.py:19
  62.2 5.4 %collective-permute-done.18 = bf16[1,96,1024]{2,1,0:T(8,128)(2,1)S(1)} collective-permute-done((bf16[1,96,1024]{2,1,0:T(8,128)(2,1)S(1)}, bf16[1,96,1024]{2,1,0:T(8,128)(2,1)S(1)}, u32[]{:S(2)}, u32[]{:S(2)}) %collective-permute-start.18) | collective-permute-done | bytes 196640 | tf_op jit(solution)/shard_map/ppermute | solution.py:19
  69.9 4.3 %experts.3 = (bf16[2,96,1024]{2,1,0:T(8,128)(2,1)S(1)}, bf16[2,96,1024]{2,1,0:T(8,128)(2,1)S(1)}, bf16[2,96,1024]{2,1,0:T(8,128)(2,1)S(1)}, bf16[1,96,1024]{2,1,0:T(8,128)(2,1)S(1)}, bf16[1,96,1024]{2,1,0:T(8,128)(2,1)S(1)}) custom-call(s32[2]{0:T(128)S(1)} %pad_add_fusion.place_ref, bf16[2,96,1024]{2,1,0:T(8,128)(2,1)S(1)} %pad_maximum_fusion.own_ref, ...), custom_call_target="tpu_custom_call" | custom-call | flops 3221225472 | bytes 3145728 | tf_op jit(solution)/shard_map/experts/pallas_call | solution.py:168
  74.2 2.1 %collective-permute-done.21 = bf16[2,96,1024]{2,1,0:T(8,128)(2,1)S(1)} collective-permute-done((bf16[2,96,1024]{2,1,0:T(8,128)(2,1)S(1)}, bf16[2,96,1024]{2,1,0:T(8,128)(2,1)S(1)}, u32[]{:S(2)}, u32[]{:S(2)}) %collective-permute-start.21) | collective-permute-done | bytes 393248 | tf_op jit(solution)/shard_map/ppermute | solution.py:19
  77.7 2.1 %collective-permute-start.25 = (bf16[1,96,1024]{2,1,0:T(8,128)(2,1)S(1)}, bf16[1,96,1024]{2,1,0:T(8,128)(2,1)S(1)}, u32[]{:S(2)}, u32[]{:S(2)}) collective-permute-start(bf16[1,96,1024]{2,1,0:T(8,128)(2,1)S(1)} %get-tuple-element.96), channel_id=1, source_target_pairs={{0,8},{4,12},{8,0},{12,4},{16,24},{20,28},{24,16},{28,20},{1,9},{5... | collective-permute-start | bytes 589832 | tf_op jit(solution)/shard_map/ppermute | solution.py:19
  81.1 2.3 %collective-permute-done.25 = bf16[1,96,1024]{2,1,0:T(8,128)(2,1)S(1)} collective-permute-done((bf16[1,96,1024]{2,1,0:T(8,128)(2,1)S(1)}, bf16[1,96,1024]{2,1,0:T(8,128)(2,1)S(1)}, u32[]{:S(2)}, u32[]{:S(2)}) %collective-permute-start.25) | collective-permute-done | bytes 196640 | tf_op jit(solution)/shard_map/ppermute | solution.py:19
  83.5 1.6 %collective-permute-start.26 = (bf16[2,96,1024]{2,1,0:T(8,128)(2,1)S(1)}, bf16[2,96,1024]{2,1,0:T(8,128)(2,1)S(1)}, u32[]{:S(2)}, u32[]{:S(2)}) collective-permute-start(bf16[2,96,1024]{2,1,0:T(8,128)(2,1)S(1)} %pad_maximum_fusion.4), channel_id=1, source_target_pairs={{0,16},{4,20},{8,24},{12,28},{16,0},{20,4},{24,8},{28,12},{1,17},{... | collective-permute-start | bytes 1179656 | tf_op jit(solution)/shard_map/ppermute | solution.py:19
  85.5 1.6 %collective-permute-start.24 = (bf16[2,96,1024]{2,1,0:T(8,128)(2,1)S(1)}, bf16[2,96,1024]{2,1,0:T(8,128)(2,1)S(1)}, u32[]{:S(2)}, u32[]{:S(2)}) collective-permute-start(bf16[2,96,1024]{2,1,0:T(8,128)(2,1)S(1)} %pad_maximum_fusion.3), channel_id=1, source_target_pairs={{0,8},{4,12},{8,0},{12,4},{16,24},{20,28},{24,16},{28,20},{1,9},{5... | collective-permute-start | bytes 1179656 | tf_op jit(solution)/shard_map/ppermute | solution.py:19
  87.3 3.2 %collective-permute-start.31 = (bf16[2,24,1024]{2,1,0:T(8,128)(2,1)S(1)}, bf16[2,24,1024]{2,1,0:T(8,128)(2,1)S(1)}, u32[]{:S(2)}, u32[]{:S(2)}) collective-permute-start(bf16[2,24,1024]{2,1,0:T(8,128)(2,1)S(1)} %get-tuple-element.103), channel_id=1, source_target_pairs={{0,3},{1,2},{2,1},{3,0},{4,7},{5,6},{6,5},{7,4},{8,11},{9,10},{10,... | collective-permute-start | bytes 294920 | tf_op jit(solution)/shard_map/ppermute | solution.py:19
  91.8 1.6 %collective-permute-done.24 = bf16[2,96,1024]{2,1,0:T(8,128)(2,1)S(1)} collective-permute-done((bf16[2,96,1024]{2,1,0:T(8,128)(2,1)S(1)}, bf16[2,96,1024]{2,1,0:T(8,128)(2,1)S(1)}, u32[]{:S(2)}, u32[]{:S(2)}) %collective-permute-start.24) | collective-permute-done | bytes 393248 | tf_op jit(solution)/shard_map/ppermute | solution.py:19
  93.6 2.8 %collective-permute-start.32 = (bf16[2,24,1024]{2,1,0:T(8,128)(2,1)S(1)}, bf16[2,24,1024]{2,1,0:T(8,128)(2,1)S(1)}, u32[]{:S(2)}, u32[]{:S(2)}) collective-permute-start(bf16[2,24,1024]{2,1,0:T(8,128)(2,1)S(1)} %get-tuple-element.99), channel_id=1, source_target_pairs={{0,3},{1,2},{2,1},{3,0},{4,7},{5,6},{6,5},{7,4},{8,11},{9,10},{10,... | collective-permute-start | bytes 294920 | tf_op jit(solution)/shard_map/ppermute | solution.py:19
  96.4 2.2 %collective-permute-start.30 = (bf16[2,24,1024]{2,1,0:T(8,128)(2,1)S(1)}, bf16[2,24,1024]{2,1,0:T(8,128)(2,1)S(1)}, u32[]{:S(2)}, u32[]{:S(2)}) collective-permute-start(bf16[2,24,1024]{2,1,0:T(8,128)(2,1)S(1)} %get-tuple-element.100), channel_id=1, source_target_pairs={{0,2},{1,3},{2,0},{3,1},{4,6},{5,7},{6,4},{7,5},{8,10},{9,11},{10,... | collective-permute-start | bytes 294920 | tf_op jit(solution)/shard_map/ppermute | solution.py:19
  98.7 1.4 %collective-permute-done.32.refs_7_ = bf16[2,24,1024]{2,1,0:T(8,128)(2,1)S(1)} collective-permute-done((bf16[2,24,1024]{2,1,0:T(8,128)(2,1)S(1)}, bf16[2,24,1024]{2,1,0:T(8,128)(2,1)S(1)}, u32[]{:S(2)}, u32[]{:S(2)}) %collective-permute-start.32) | collective-permute-done | bytes 98336 | tf_op jit(solution)/shard_map/ppermute | solution.py:19
  100.1 3.4 %collective-permute-done.30.refs_5_ = bf16[2,24,1024]{2,1,0:T(8,128)(2,1)S(1)} collective-permute-done((bf16[2,24,1024]{2,1,0:T(8,128)(2,1)S(1)}, bf16[2,24,1024]{2,1,0:T(8,128)(2,1)S(1)}, u32[]{:S(2)}, u32[]{:S(2)}) %collective-permute-start.30) | collective-permute-done | bytes 98336 | tf_op jit(solution)/shard_map/ppermute | solution.py:19
  104.0 1.5 %collective-permute-done.33 = bf16[128,1024]{1,0:T(8,128)(2,1)S(1)} collective-permute-done((bf16[128,1024]{1,0:T(8,128)(2,1)S(1)}, bf16[128,1024]{1,0:T(8,128)(2,1)S(1)}, u32[]{:S(2)}, u32[]{:S(2)}) %collective-permute-start.33) | collective-permute-done | bytes 262176 | tf_op jit(solution)/shard_map/ppermute | solution.py:19
  (76 shorter events, 24.2 us)
Async XLA Ops:
  4.4 4.9 %collective-permute-start.2 = (bf16[128,1024]{1,0:T(8,128)(2,1)S(1)}, bf16[128,1024]{1,0:T(8,128)(2,1)S(1)}, u32[]{:S(2)}, u32[]{:S(2)}) collective-permute-start(bf16[128,1024]{1,0:T(8,128)(2,1)S(1)} %get-tuple-element.55.normed_ref), channel_id=1, source_target_pairs={{0,4},{4,0},{8,12},{12,8},{16,20},{20,16},{24,28},{28,24},{1,5},{5... | collective-permute-start | bytes 786440 | tf_op jit(solution)/shard_map/ppermute | solution.py:19
  9.2 19.4 %collective-permute-start.7 = (bf16[8,1024,512]{2,1,0:T(8,128)(2,1)}, bf16[8,1024,512]{2,1,0:T(8,128)(2,1)S(1)}, u32[]{:S(2)}, u32[]{:S(2)}) collective-permute-start(bf16[8,1024,512]{2,1,0:T(8,128)(2,1)} %in_own_ref.3), channel_id=1, source_target_pairs={{0,4},{4,0},{8,12},{12,8},{16,20},{20,16},{24,28},{28,24},{1,5},{5... | collective-permute-start | bytes 25165832 | tf_op jit(solution)/shard_map/ppermute | solution.py:19
  9.7 34.5 %collective-permute-start.16 = (bf16[8,1024,512]{2,1,0:T(8,128)(2,1)}, bf16[8,1024,512]{2,1,0:T(8,128)(2,1)S(1)}, u32[]{:S(2)}, u32[]{:S(2)}) collective-permute-start(bf16[8,1024,512]{2,1,0:T(8,128)(2,1)} %down_own_ref.3), channel_id=1, source_target_pairs={{0,4},{4,0},{8,12},{12,8},{16,20},{20,16},{24,28},{28,24},{1,5},{5... | collective-permute-start | bytes 25165832 | tf_op jit(solution)/shard_map/ppermute | solution.py:19
  10.2 6.1 %collective-permute-start.4 = (bf16[2,24,1024]{2,1,0:T(8,128)(2,1)S(1)}, bf16[2,24,1024]{2,1,0:T(8,128)(2,1)S(1)}, u32[]{:S(2)}, u32[]{:S(2)}) collective-permute-start(bf16[2,24,1024]{2,1,0:T(8,128)(2,1)S(1)} %get-tuple-element.61), channel_id=1, source_target_pairs={{0,1},{1,0},{2,3},{3,2},{4,5},{5,4},{6,7},{7,6},{8,9},{9,8},{10,11... | collective-permute-start | bytes 294920 | tf_op jit(solution)/shard_map/ppermute | solution.py:19
  13.2 10.7 %collective-permute-start.5 = (bf16[2,24,1024]{2,1,0:T(8,128)(2,1)S(1)}, bf16[2,24,1024]{2,1,0:T(8,128)(2,1)S(1)}, u32[]{:S(2)}, u32[]{:S(2)}) collective-permute-start(bf16[2,24,1024]{2,1,0:T(8,128)(2,1)S(1)} %get-tuple-element.62), channel_id=1, source_target_pairs={{0,2},{1,3},{2,0},{3,1},{4,6},{5,7},{6,4},{7,5},{8,10},{9,11},{10,... | collective-permute-start | bytes 294920 | tf_op jit(solution)/shard_map/ppermute | solution.py:19
  15.8 8.1 %collective-permute-start.6 = (bf16[2,24,1024]{2,1,0:T(8,128)(2,1)S(1)}, bf16[2,24,1024]{2,1,0:T(8,128)(2,1)S(1)}, u32[]{:S(2)}, u32[]{:S(2)}) collective-permute-start(bf16[2,24,1024]{2,1,0:T(8,128)(2,1)S(1)} %get-tuple-element.63), channel_id=1, source_target_pairs={{0,3},{1,2},{2,1},{3,0},{4,7},{5,6},{6,5},{7,4},{8,11},{9,10},{10,... | collective-permute-start | bytes 294920 | tf_op jit(solution)/shard_map/ppermute | solution.py:19
  23.9 9.3 %collective-permute-start.11 = (bf16[2,96,1024]{2,1,0:T(8,128)(2,1)S(1)}, bf16[2,96,1024]{2,1,0:T(8,128)(2,1)S(1)}, u32[]{:S(2)}, u32[]{:S(2)}) collective-permute-start(bf16[2,96,1024]{2,1,0:T(8,128)(2,1)S(1)} %constant_dynamic-update-slice_fusion.own_ref), channel_id=1, source_target_pairs={{0,16},{4,20},{8,24},{12,28},{16,0},{20,4},{24,8},{28,12},{1,17},{... | collective-permute-start | bytes 1179656 | tf_op jit(solution)/shard_map/ppermute | solution.py:19
  25.5 9.3 %collective-permute-start.10 = (bf16[2,96,1024]{2,1,0:T(8,128)(2,1)S(1)}, bf16[2,96,1024]{2,1,0:T(8,128)(2,1)S(1)}, u32[]{:S(2)}, u32[]{:S(2)}) collective-permute-start(bf16[2,96,1024]{2,1,0:T(8,128)(2,1)S(1)} %constant_dynamic-update-slice_fusion.own_ref), channel_id=1, source_target_pairs={{0,8},{4,12},{8,0},{12,4},{16,24},{20,28},{24,16},{28,20},{1,9},{5... | collective-permute-start | bytes 1179656 | tf_op jit(solution)/shard_map/ppermute | solution.py:19
  27.0 9.3 %collective-permute-start.3 = (bf16[2,24,1024]{2,1,0:T(8,128)(2,1)S(1)}, bf16[2,24,1024]{2,1,0:T(8,128)(2,1)S(1)}, u32[]{:S(2)}, u32[]{:S(2)}) collective-permute-start(bf16[2,24,1024]{2,1,0:T(8,128)(2,1)S(1)} %get-tuple-element.57), channel_id=1, source_target_pairs={{0,1},{1,0},{2,3},{3,2},{4,5},{5,4},{6,7},{7,6},{8,9},{9,8},{10,11... | collective-permute-start | bytes 294920 | tf_op jit(solution)/shard_map/ppermute | solution.py:19
  28.7 8.8 %collective-permute-start.8 = (bf16[2,24,1024]{2,1,0:T(8,128)(2,1)S(1)}, bf16[2,24,1024]{2,1,0:T(8,128)(2,1)S(1)}, u32[]{:S(2)}, u32[]{:S(2)}) collective-permute-start(bf16[2,24,1024]{2,1,0:T(8,128)(2,1)S(1)} %get-tuple-element.65), channel_id=1, source_target_pairs={{0,2},{1,3},{2,0},{3,1},{4,6},{5,7},{6,4},{7,5},{8,10},{9,11},{10,... | collective-permute-start | bytes 294920 | tf_op jit(solution)/shard_map/ppermute | solution.py:19
  33.2 6.5 %collective-permute-start.9 = (bf16[2,24,1024]{2,1,0:T(8,128)(2,1)S(1)}, bf16[2,24,1024]{2,1,0:T(8,128)(2,1)S(1)}, u32[]{:S(2)}, u32[]{:S(2)}) collective-permute-start(bf16[2,24,1024]{2,1,0:T(8,128)(2,1)S(1)} %get-tuple-element.66), channel_id=1, source_target_pairs={{0,3},{1,2},{2,1},{3,0},{4,7},{5,6},{6,5},{7,4},{8,11},{9,10},{10,... | collective-permute-start | bytes 294920 | tf_op jit(solution)/shard_map/ppermute | solution.py:19
  34.7 8.0 %collective-permute-start.15 = (bf16[1,96,1024]{2,1,0:T(8,128)(2,1)S(1)}, bf16[1,96,1024]{2,1,0:T(8,128)(2,1)S(1)}, u32[]{:S(2)}, u32[]{:S(2)}) collective-permute-start(bf16[1,96,1024]{2,1,0:T(8,128)(2,1)S(1)} %slice.81), channel_id=1, source_target_pairs={{0,8},{4,12},{8,0},{12,4},{16,24},{20,28},{24,16},{28,20},{1,9},{5... | collective-permute-start | bytes 589832 | tf_op jit(solution)/shard_map/ppermute | solution.py:19
  36.3 7.9 %collective-permute-start.14 = (bf16[1,96,1024]{2,1,0:T(8,128)(2,1)S(1)}, bf16[1,96,1024]{2,1,0:T(8,128)(2,1)S(1)}, u32[]{:S(2)}, u32[]{:S(2)}) collective-permute-start(bf16[1,96,1024]{2,1,0:T(8,128)(2,1)S(1)} %slice.80), channel_id=1, source_target_pairs={{0,16},{4,20},{8,24},{12,28},{16,0},{20,4},{24,8},{28,12},{1,17},{... | collective-permute-start | bytes 589832 | tf_op jit(solution)/shard_map/ppermute | solution.py:19
  39.7 15.5 %collective-permute-start.13 = (bf16[2,96,1024]{2,1,0:T(8,128)(2,1)S(1)}, bf16[2,96,1024]{2,1,0:T(8,128)(2,1)S(1)}, u32[]{:S(2)}, u32[]{:S(2)}) collective-permute-start(bf16[2,96,1024]{2,1,0:T(8,128)(2,1)S(1)} %pad_maximum_fusion.own_ref), channel_id=1, source_target_pairs={{0,16},{4,20},{8,24},{12,28},{16,0},{20,4},{24,8},{28,12},{1,17},{... | collective-permute-start | bytes 1179656 | tf_op jit(solution)/shard_map/ppermute | solution.py:19
  41.3 13.9 %collective-permute-start.12 = (bf16[2,96,1024]{2,1,0:T(8,128)(2,1)S(1)}, bf16[2,96,1024]{2,1,0:T(8,128)(2,1)S(1)}, u32[]{:S(2)}, u32[]{:S(2)}) collective-permute-start(bf16[2,96,1024]{2,1,0:T(8,128)(2,1)S(1)} %pad_maximum_fusion.own_ref), channel_id=1, source_target_pairs={{0,8},{4,12},{8,0},{12,4},{16,24},{20,28},{24,16},{28,20},{1,9},{5... | collective-permute-start | bytes 1179656 | tf_op jit(solution)/shard_map/ppermute | solution.py:19
  55.2 6.9 %collective-permute-start.17 = (bf16[1,96,1024]{2,1,0:T(8,128)(2,1)S(1)}, bf16[1,96,1024]{2,1,0:T(8,128)(2,1)S(1)}, u32[]{:S(2)}, u32[]{:S(2)}) collective-permute-start(bf16[1,96,1024]{2,1,0:T(8,128)(2,1)S(1)} %get-tuple-element.78), channel_id=1, source_target_pairs={{0,16},{4,20},{8,24},{12,28},{16,0},{20,4},{24,8},{28,12},{1,17},{... | collective-permute-start | bytes 589832 | tf_op jit(solution)/shard_map/ppermute | solution.py:19
  56.5 11.2 %collective-permute-start.20 = (bf16[1,96,1024]{2,1,0:T(8,128)(2,1)S(1)}, bf16[1,96,1024]{2,1,0:T(8,128)(2,1)S(1)}, u32[]{:S(2)}, u32[]{:S(2)}) collective-permute-start(bf16[1,96,1024]{2,1,0:T(8,128)(2,1)S(1)} %slice.67), channel_id=1, source_target_pairs={{0,8},{4,12},{8,0},{12,4},{16,24},{20,28},{24,16},{28,20},{1,9},{5... | collective-permute-start | bytes 589832 | tf_op jit(solution)/shard_map/ppermute | solution.py:19
  57.1 10.6 %collective-permute-start.19 = (bf16[1,96,1024]{2,1,0:T(8,128)(2,1)S(1)}, bf16[1,96,1024]{2,1,0:T(8,128)(2,1)S(1)}, u32[]{:S(2)}, u32[]{:S(2)}) collective-permute-start(bf16[1,96,1024]{2,1,0:T(8,128)(2,1)S(1)} %slice.66), channel_id=1, source_target_pairs={{0,16},{4,20},{8,24},{12,28},{16,0},{20,4},{24,8},{28,12},{1,17},{... | collective-permute-start | bytes 589832 | tf_op jit(solution)/shard_map/ppermute | solution.py:19
  57.8 9.8 %collective-permute-start.18 = (bf16[1,96,1024]{2,1,0:T(8,128)(2,1)S(1)}, bf16[1,96,1024]{2,1,0:T(8,128)(2,1)S(1)}, u32[]{:S(2)}, u32[]{:S(2)}) collective-permute-start(bf16[1,96,1024]{2,1,0:T(8,128)(2,1)S(1)} %get-tuple-element.80), channel_id=1, source_target_pairs={{0,8},{4,12},{8,0},{12,4},{16,24},{20,28},{24,16},{28,20},{1,9},{5... | collective-permute-start | bytes 589832 | tf_op jit(solution)/shard_map/ppermute | solution.py:19
  67.8 8.6 %collective-permute-start.21 = (bf16[2,96,1024]{2,1,0:T(8,128)(2,1)S(1)}, bf16[2,96,1024]{2,1,0:T(8,128)(2,1)S(1)}, u32[]{:S(2)}, u32[]{:S(2)}) collective-permute-start(bf16[2,96,1024]{2,1,0:T(8,128)(2,1)S(1)} %get-tuple-element.88), channel_id=1, source_target_pairs={{0,8},{4,12},{8,0},{12,4},{16,24},{20,28},{24,16},{28,20},{1,9},{5... | collective-permute-start | bytes 1179656 | tf_op jit(solution)/shard_map/ppermute | solution.py:19
  68.7 9.0 %collective-permute-start.22 = (bf16[2,96,1024]{2,1,0:T(8,128)(2,1)S(1)}, bf16[2,96,1024]{2,1,0:T(8,128)(2,1)S(1)}, u32[]{:S(2)}, u32[]{:S(2)}) collective-permute-start(bf16[2,96,1024]{2,1,0:T(8,128)(2,1)S(1)} %get-tuple-element.89), channel_id=1, source_target_pairs={{0,16},{4,20},{8,24},{12,28},{16,0},{20,4},{24,8},{28,12},{1,17},{... | collective-permute-start | bytes 1179656 | tf_op jit(solution)/shard_map/ppermute | solution.py:19
  77.7 5.7 %collective-permute-start.25 = (bf16[1,96,1024]{2,1,0:T(8,128)(2,1)S(1)}, bf16[1,96,1024]{2,1,0:T(8,128)(2,1)S(1)}, u32[]{:S(2)}, u32[]{:S(2)}) collective-permute-start(bf16[1,96,1024]{2,1,0:T(8,128)(2,1)S(1)} %get-tuple-element.96), channel_id=1, source_target_pairs={{0,8},{4,12},{8,0},{12,4},{16,24},{20,28},{24,16},{28,20},{1,9},{5... | collective-permute-start | bytes 589832 | tf_op jit(solution)/shard_map/ppermute | solution.py:19
  79.8 5.7 %collective-permute-start.23 = (bf16[1,96,1024]{2,1,0:T(8,128)(2,1)S(1)}, bf16[1,96,1024]{2,1,0:T(8,128)(2,1)S(1)}, u32[]{:S(2)}, u32[]{:S(2)}) collective-permute-start(bf16[1,96,1024]{2,1,0:T(8,128)(2,1)S(1)} %get-tuple-element.94), channel_id=1, source_target_pairs={{0,16},{4,20},{8,24},{12,28},{16,0},{20,4},{24,8},{28,12},{1,17},{... | collective-permute-start | bytes 589832 | tf_op jit(solution)/shard_map/ppermute | solution.py:19
  83.5 8.3 %collective-permute-start.26 = (bf16[2,96,1024]{2,1,0:T(8,128)(2,1)S(1)}, bf16[2,96,1024]{2,1,0:T(8,128)(2,1)S(1)}, u32[]{:S(2)}, u32[]{:S(2)}) collective-permute-start(bf16[2,96,1024]{2,1,0:T(8,128)(2,1)S(1)} %pad_maximum_fusion.4), channel_id=1, source_target_pairs={{0,16},{4,20},{8,24},{12,28},{16,0},{20,4},{24,8},{28,12},{1,17},{... | collective-permute-start | bytes 1179656 | tf_op jit(solution)/shard_map/ppermute | solution.py:19
  85.5 7.8 %collective-permute-start.24 = (bf16[2,96,1024]{2,1,0:T(8,128)(2,1)S(1)}, bf16[2,96,1024]{2,1,0:T(8,128)(2,1)S(1)}, u32[]{:S(2)}, u32[]{:S(2)}) collective-permute-start(bf16[2,96,1024]{2,1,0:T(8,128)(2,1)S(1)} %pad_maximum_fusion.3), channel_id=1, source_target_pairs={{0,8},{4,12},{8,0},{12,4},{16,24},{20,28},{24,16},{28,20},{1,9},{5... | collective-permute-start | bytes 1179656 | tf_op jit(solution)/shard_map/ppermute | solution.py:19
  87.3 11.3 %collective-permute-start.31 = (bf16[2,24,1024]{2,1,0:T(8,128)(2,1)S(1)}, bf16[2,24,1024]{2,1,0:T(8,128)(2,1)S(1)}, u32[]{:S(2)}, u32[]{:S(2)}) collective-permute-start(bf16[2,24,1024]{2,1,0:T(8,128)(2,1)S(1)} %get-tuple-element.103), channel_id=1, source_target_pairs={{0,3},{1,2},{2,1},{3,0},{4,7},{5,6},{6,5},{7,4},{8,11},{9,10},{10,... | collective-permute-start | bytes 294920 | tf_op jit(solution)/shard_map/ppermute | solution.py:19
  90.5 8.2 %collective-permute-start.29 = (bf16[2,24,1024]{2,1,0:T(8,128)(2,1)S(1)}, bf16[2,24,1024]{2,1,0:T(8,128)(2,1)S(1)}, u32[]{:S(2)}, u32[]{:S(2)}) collective-permute-start(bf16[2,24,1024]{2,1,0:T(8,128)(2,1)S(1)} %get-tuple-element.104), channel_id=1, source_target_pairs={{0,2},{1,3},{2,0},{3,1},{4,6},{5,7},{6,4},{7,5},{8,10},{9,11},{10,... | collective-permute-start | bytes 294920 | tf_op jit(solution)/shard_map/ppermute | solution.py:19
  91.1 7.5 %collective-permute-start.27 = (bf16[2,24,1024]{2,1,0:T(8,128)(2,1)S(1)}, bf16[2,24,1024]{2,1,0:T(8,128)(2,1)S(1)}, u32[]{:S(2)}, u32[]{:S(2)}) collective-permute-start(bf16[2,24,1024]{2,1,0:T(8,128)(2,1)S(1)} %get-tuple-element.105), channel_id=1, source_target_pairs={{0,1},{1,0},{2,3},{3,2},{4,5},{5,4},{6,7},{7,6},{8,9},{9,8},{10,11... | collective-permute-start | bytes 294920 | tf_op jit(solution)/shard_map/ppermute | solution.py:19
  93.6 6.5 %collective-permute-start.32 = (bf16[2,24,1024]{2,1,0:T(8,128)(2,1)S(1)}, bf16[2,24,1024]{2,1,0:T(8,128)(2,1)S(1)}, u32[]{:S(2)}, u32[]{:S(2)}) collective-permute-start(bf16[2,24,1024]{2,1,0:T(8,128)(2,1)S(1)} %get-tuple-element.99), channel_id=1, source_target_pairs={{0,3},{1,2},{2,1},{3,0},{4,7},{5,6},{6,5},{7,4},{8,11},{9,10},{10,... | collective-permute-start | bytes 294920 | tf_op jit(solution)/shard_map/ppermute | solution.py:19
  96.4 7.0 %collective-permute-start.30 = (bf16[2,24,1024]{2,1,0:T(8,128)(2,1)S(1)}, bf16[2,24,1024]{2,1,0:T(8,128)(2,1)S(1)}, u32[]{:S(2)}, u32[]{:S(2)}) collective-permute-start(bf16[2,24,1024]{2,1,0:T(8,128)(2,1)S(1)} %get-tuple-element.100), channel_id=1, source_target_pairs={{0,2},{1,3},{2,0},{3,1},{4,6},{5,7},{6,4},{7,5},{8,10},{9,11},{10,... | collective-permute-start | bytes 294920 | tf_op jit(solution)/shard_map/ppermute | solution.py:19
  98.7 4.8 %collective-permute-start.28 = (bf16[2,24,1024]{2,1,0:T(8,128)(2,1)S(1)}, bf16[2,24,1024]{2,1,0:T(8,128)(2,1)S(1)}, u32[]{:S(2)}, u32[]{:S(2)}) collective-permute-start(bf16[2,24,1024]{2,1,0:T(8,128)(2,1)S(1)} %get-tuple-element.101), channel_id=1, source_target_pairs={{0,1},{1,0},{2,3},{3,2},{4,5},{5,4},{6,7},{7,6},{8,9},{9,8},{10,11... | collective-permute-start | bytes 294920 | tf_op jit(solution)/shard_map/ppermute | solution.py:19
  103.9 1.6 %collective-permute-start.33 = (bf16[128,1024]{1,0:T(8,128)(2,1)S(1)}, bf16[128,1024]{1,0:T(8,128)(2,1)S(1)}, u32[]{:S(2)}, u32[]{:S(2)}) collective-permute-start(bf16[128,1024]{1,0:T(8,128)(2,1)S(1)} %get-tuple-element.98), channel_id=1, source_target_pairs={{0,4},{4,0},{8,12},{12,8},{16,20},{20,16},{24,28},{28,24},{1,5},{5... | collective-permute-start | bytes 786440 | tf_op jit(solution)/shard_map/ppermute | solution.py:19
  (7 other events, 13.2 us)

commit v3 on v2

v3 whole, which is shorter than its diff:
```python
import functools

import jax
import jax.numpy as jnp
from jax import lax
from jax.experimental import pallas as pl
from jax.experimental.pallas import tpu as pltpu
from jax.sharding import PartitionSpec as P

F32 = jnp.float32
BF16 = jnp.bfloat16
CHUNKS = 2
CORE, NEAR_A, NEAR_B = 0, 1, 2
GROUP_BITS = 3
MIB = 1024 * 1024
VMEM_LIMIT = 20 * MIB


def swapped(array, axis, distance):
    return lax.ppermute(array, axis, [(i, i ^ distance) for i in range(lax.axis_size(axis))])


def after(value, *others):
    return lax.optimization_barrier((value, *others))[0]


def mm(a, b, dims=((1,), (0,))):
    return lax.dot_general(a, b, (dims, ((), ())), preferred_element_type=F32)


def vmem():
    return pl.BlockSpec(memory_space=pltpu.VMEM)


def hbm():
    return pl.BlockSpec(memory_space=pltpu.HBM)


def in_hbm(array):
    return pltpu.with_memory_space_constraint(array, pltpu.HBM)


def in_vmem(array):
    return pltpu.with_memory_space_constraint(array, pltpu.VMEM)


def smem():
    return pl.BlockSpec(memory_space=pltpu.SMEM)


def embed_kernel(tubelets_ref, weight_ref, gain_ref, emb_ref, normed_ref):
    embedded = mm(tubelets_ref[...], weight_ref[...]).astype(BF16)
    emb_ref[...] = embedded
    floats = embedded.astype(F32)
    centred = floats - jnp.mean(floats, axis=-1, keepdims=True)
    variance = jnp.mean(centred * centred, axis=-1, keepdims=True)
    normed_ref[...] = (centred * lax.rsqrt(variance + 1e-06) * gain_ref[...]).astype(BF16)


def embed(tubelets, weight, gain):
    tok, width = tubelets.shape[0], weight.shape[1]
    shape = jax.ShapeDtypeStruct((tok, width), BF16)
    return pl.pallas_call(
        embed_kernel,
        out_shape=[shape, shape],
        in_specs=[vmem()] * 3,
        out_specs=[vmem()] * 2,
        compiler_params=pltpu.CompilerParams(vmem_limit_bytes=VMEM_LIMIT),
        cost_estimate=pl.CostEstimate(flops=2 * tok * weight.size, bytes_accessed=weight.size * 2, transcendentals=0),
        name="embed",
    )(tubelets, weight, gain.reshape(1, width))


def route_kernel(n_exp, half, cap, place_ref, code_ref, sib_code_ref, select_ref, gate_ref):
    tok = code_ref.shape[1]
    both = 2 * tok
    count = n_exp * half
    slots = 2 * cap
    rows = count * slots
    codes = jnp.concatenate([code_ref[...], sib_code_ref[...]], axis=1)
    gates = 0.25 + 0.125 * codes[2:4].astype(F32)
    plane, core = place_ref[0], place_ref[1]

    row = lax.broadcasted_iota(jnp.int32, (count, both), 0)
    expert = (plane ^ (row // half)) * (2 * half) + core * half + row % half
    first = codes[0:1] == expert
    second = codes[1:2] == expert
    member = first | second
    gated = jnp.where(first, gates[0:1, :], 0.0) + jnp.where(second, gates[1:2, :], 0.0)
    earlier = lax.broadcasted_iota(jnp.int32, (both, both), 0)
    later = lax.broadcasted_iota(jnp.int32, (both, both), 1)
    before = jnp.where(((earlier // tok) == (later // tok)) & (earlier < later), 1.0, 0.0).astype(BF16)
    rank = mm(jnp.where(member, 1.0, 0.0).astype(BF16), before)
    block = jnp.where(lax.broadcasted_iota(jnp.int32, (count, both), 1) >= tok, float(cap), 0.0)
    pos = jnp.where(member, rank + block, -1.0).astype(BF16)
    spread = jnp.where(
        lax.broadcasted_iota(jnp.int32, (rows, count), 0) // slots
        == lax.broadcasted_iota(jnp.int32, (rows, count), 1), 1.0, 0.0).astype(BF16)
    slot = (lax.broadcasted_iota(jnp.int32, (rows, both), 0) % slots).astype(F32)
    chosen = mm(spread, pos) == slot
    select_ref[...] = jnp.where(chosen, 1.0, 0.0).astype(BF16)
    gate_ref[...] = jnp.where(chosen, mm(spread, gated.astype(BF16)), 0.0).astype(BF16)


def route(place, codes, sib_codes, n_exp, half, cap):
    both = 2 * codes.shape[1]
    rows = n_exp * half * 2 * cap
    shape = jax.ShapeDtypeStruct((rows, both), BF16)
    return pl.pallas_call(
        functools.partial(route_kernel, n_exp, half, cap),
        out_shape=[shape, shape],
        in_specs=[smem()] + [vmem()] * 2,
        out_specs=[vmem()] * 2,
        compiler_params=pltpu.CompilerParams(vmem_limit_bytes=VMEM_LIMIT),
        cost_estimate=pl.CostEstimate(flops=2 * rows * both * 64, bytes_accessed=rows * both * 4, transcendentals=0),
        name="route",
    )(place, codes, sib_codes)


def pack_kernel(spans, select_ref, normed_ref, sib_ref, *piece_refs):
    buffer = mm(select_ref[...], jnp.concatenate([normed_ref[...], sib_ref[...]], axis=0))
    slots = piece_refs[0].shape[1]
    for (start, count), ref in zip(spans, piece_refs):
        for e in range(count):
            ref[e] = buffer[(start + e) * slots:(start + e + 1) * slots].astype(BF16)


def pack(select, normed, sib_normed, n_exp, half, cap):
    width = normed.shape[1]
    rows = select.shape[0]
    per = half // CHUNKS
    spans = []
    for s in range(n_exp):
        spans += [(s * half, half)] if s == 1 else [(s * half + c * per, per) for c in range(CHUNKS)]
    pieces = list(pl.pallas_call(
        functools.partial(pack_kernel, spans),
        out_shape=[pltpu.VMEM((count, 2 * cap, width), BF16) for _, count in spans],
        in_specs=[vmem()] * 3,
        out_specs=[vmem()] * len(spans),
        compiler_params=pltpu.CompilerParams(vmem_limit_bytes=VMEM_LIMIT),
        cost_estimate=pl.CostEstimate(
            flops=2 * select.size * width, bytes_accessed=rows * width * 4, transcendentals=0),
        name="pack",
    )(select, normed, sib_normed))
    return [[pieces.pop(0)] if s == 1 else [pieces.pop(0) for _ in range(CHUNKS)] for s in range(n_exp)]


def experts_kernel(chunk, half, place_ref, own_ref, a_ref, b_ref, d1_ref, d2_ref,
                   in_sib_ref, down_sib_ref, in_ref, down_ref,
                   p_own_ref, p_a_ref, p_b_ref, p_d1_ref, p_d2_ref, x_ref, h_ref, acc_ref, bufs, sems):
    per, m, _ = own_ref.shape
    split = per // 2
    base = place_ref[1] * half + chunk * per
    width = in_ref.shape[1]
    parts = sems.shape[2]
    depth = width // parts
    copies = {}
    for e in range(per):
        for which, ref in enumerate((in_ref, down_ref)):
            for part in range(parts):
                rows = pl.ds(part * depth, depth)
                copy = pltpu.make_async_copy(ref.at[base + e, rows], bufs.at[which, e, rows], sems.at[which, e, part])
                copy.start()
                copies[which, e, part] = copy

    def ready(which, e):
        for part in range(parts):
            copies[which, e, part].wait()

    for e in range(per):
        diagonal = d1_ref if e < split else d2_ref
        x_ref[e] = jnp.concatenate([own_ref[e], a_ref[e], b_ref[e], diagonal[e % split]], axis=0)
        h_ref[...] = jax.nn.gelu(mm(x_ref[e], in_sib_ref[base + e])).astype(BF16)
        acc_ref[e] = mm(h_ref[...], down_sib_ref[base + e], ((1,), (1,)))
    for e in range(per):
        p_diagonal = p_d1_ref if e < split else p_d2_ref
        ready(0, e)
        h_ref[...] = jax.nn.gelu(mm(x_ref[e], bufs[0, e])).astype(BF16)
        ready(1, e)
        total = acc_ref[e] + mm(h_ref[...], bufs[1, e], ((1,), (1,)))
        p_own_ref[e] = total[0:m].astype(BF16)
        p_a_ref[e] = total[m:2 * m].astype(BF16)
        p_b_ref[e] = total[2 * m:3 * m].astype(BF16)
        p_diagonal[e % split] = total[3 * m:4 * m].astype(BF16)


def experts(place, chunk, own, near_a, near_b, d1, d2, in_sib, down_sib, w_in, w_down):
    per, m, width = own.shape
    half, ff = in_sib.shape[0] // 2, in_sib.shape[2]
    shape = pltpu.VMEM(own.shape, BF16)
    part = pltpu.VMEM(d1.shape, BF16)
    return pl.pallas_call(
        functools.partial(experts_kernel, chunk, half),
        out_shape=[shape, shape, shape, part, part],
        in_specs=[smem()] + [vmem()] * 7 + [hbm()] * 2,
        out_specs=[vmem()] * 5,
        scratch_shapes=[
            pltpu.VMEM((per, 4 * m, width), BF16), pltpu.VMEM((4 * m, ff), BF16), pltpu.VMEM((per, 4 * m, width), F32),
            pltpu.VMEM((2, per, width, ff), BF16), pltpu.SemaphoreType.DMA((2, per, 4))],
        compiler_params=pltpu.CompilerParams(vmem_limit_bytes=VMEM_LIMIT),
        cost_estimate=pl.CostEstimate(
            flops=2 * per * 4 * m * width * 2 * ff * 2, bytes_accessed=per * m * width * 16,
            transcendentals=per * 4 * m * 2 * ff),
        name="experts",
    )(place, own, near_a, near_b, d1, d2, in_vmem(in_sib), in_vmem(down_sib), in_hbm(w_in), in_hbm(w_down))


def combine_kernel(tok, gate_ref, emb_ref, *refs):
    piece_refs, (mine_ref, send_ref, rows_ref) = refs[:-3], refs[-3:]
    per, slots, _ = piece_refs[0].shape
    for index, ref in enumerate(piece_refs):
        for e in range(per):
            start = (index * per + e) * slots
            rows_ref[start:start + slots] = ref[e].astype(F32)
    total = mm(gate_ref[...], rows_ref[...].astype(BF16), ((0,), (0,)))
    mine_ref[...] = total[0:tok] + emb_ref[...].astype(F32)
    send_ref[...] = total[tok:2 * tok].astype(BF16)


def combine(gate, embedded, pieces):
    tok, width = embedded.shape
    rows = gate.shape[0]
    return pl.pallas_call(
        functools.partial(combine_kernel, tok),
        out_shape=[jax.ShapeDtypeStruct((tok, width), F32), jax.ShapeDtypeStruct((tok, width), BF16)],
        in_specs=[vmem()] * (2 + len(pieces)),
        out_specs=[vmem()] * 2,
        scratch_shapes=[pltpu.VMEM((rows, width), F32)],
        compiler_params=pltpu.CompilerParams(vmem_limit_bytes=VMEM_LIMIT),
        cost_estimate=pl.CostEstimate(flops=4 * tok * rows * width, bytes_accessed=rows * width * 2, transcendentals=0),
        name="combine",
    )(gate, embedded, *pieces)


def on_device(tubelets, embed_weight, norm_gain, routes, gate_codes, w_in, w_down):
    tok = tubelets.shape[0]
    n_exp = lax.axis_size("exp")
    half = w_in.shape[0] // 2
    cap = 3 * tok // (w_in.shape[0] * n_exp)
    position = lax.axis_index("rep")
    core = position % 2
    place = jnp.stack([lax.axis_index("exp"), core]).astype(jnp.int32)

    core_bit = 1 << CORE
    codes = jnp.concatenate([routes.T, gate_codes.T], axis=0)
    sib_codes = swapped(codes, "rep", core_bit)
    embedded, normed = embed(tubelets, embed_weight, norm_gain)
    sib_normed = swapped(normed, "rep", core_bit)
    select, gate = route(place, codes, sib_codes, n_exp, half, cap)

    for bit in range(GROUP_BITS, lax.axis_size("rep").bit_length() - 1):
        upper = position // (1 << bit) % 2 == 1

        def gathered(panel):
            partner = swapped(panel, "rep", 1 << bit)
            return jnp.where(upper, jnp.concatenate([partner, panel], axis=2), jnp.concatenate([panel, partner], axis=2))

        w_in, w_down = gathered(w_in), gathered(w_down)

    in_sib = swapped(after(w_in, sib_normed, select), "rep", core_bit)
    down_sib = swapped(after(w_down, sib_normed, select), "rep", core_bit)
    pieces = pack(select, normed, sib_normed, n_exp, half, cap)

    def to_planes(p_own, from_a, from_b):
        done = (p_own.astype(F32) + from_a.astype(F32) + from_b.astype(F32)).astype(BF16)
        done = done.reshape(done.shape[0], n_exp, 2 * cap, done.shape[2])
        return [done[:, 0]] + [swapped(done[:, s], "exp", s) for s in range(1, n_exp)]

    split = half // CHUNKS // 2
    a_bit, b_bit = 1 << NEAR_A, 1 << NEAR_B

    def reduced(parts, r):
        _, p_a, p_b, _, _ = parts
        to_b = jnp.concatenate([p_b[:split] + r[0], p_b[split:]], axis=0)
        to_a = jnp.concatenate([p_a[:split], p_a[split:] + r[1]], axis=0)
        return to_a, to_b

    per = half // CHUNKS
    first = swapped(pieces[1][0], "exp", 1)
    own0 = jnp.concatenate(
        [pieces[0][0], first[:per]] + [swapped(pieces[s][0], "exp", s) for s in range(2, n_exp)], axis=1)
    late = lax.optimization_barrier((own0, in_sib, *(pieces[s][1] for s in range(2, n_exp))))[2:]
    own1 = jnp.concatenate(
        [pieces[0][1], first[per:]] + [swapped(piece, "exp", s + 2) for s, piece in enumerate(late)], axis=1)
    a0, b0 = swapped(own0, "rep", a_bit), swapped(own0, "rep", b_bit)
    own1 = after(own1, a0, b0)
    d0 = swapped(a0[:split], "rep", b_bit), swapped(b0[split:], "rep", a_bit)
    a1, b1 = swapped(own1, "rep", a_bit), swapped(own1, "rep", b_bit)
    parts0 = experts(place, 0, own0, a0, b0, *d0, in_sib, down_sib, w_in, w_down)
    a1, b1, *parts0 = lax.optimization_barrier((a1, b1, *parts0))
    d1 = swapped(a1[:split], "rep", b_bit), swapped(b1[split:], "rep", a_bit)
    r0 = swapped(parts0[3], "rep", a_bit), swapped(parts0[4], "rep", b_bit)
    to_a0, to_b0 = reduced(parts0, r0)
    to_a0, to_b0, *d1 = lax.optimization_barrier((to_a0, to_b0, *d1))
    from_a0, from_b0 = swapped(to_a0, "rep", a_bit), swapped(to_b0, "rep", b_bit)
    parts1 = experts(place, 1, own1, a1, b1, *d1, in_sib, down_sib, w_in, w_down)
    *parts1, from_a0, from_b0 = lax.optimization_barrier((*parts1, from_a0, from_b0))
    r1 = swapped(parts1[3], "rep", a_bit), swapped(parts1[4], "rep", b_bit)
    returned0 = to_planes(parts0[0], from_a0, from_b0)
    to_a1, to_b1 = reduced(parts1, r1)
    from_a1, from_b1 = swapped(to_a1, "rep", a_bit), swapped(to_b1, "rep", b_bit)
    returned = [returned0, to_planes(parts1[0], from_a1, from_b1)]

    pieces_back = [returned[c][s] for s in range(n_exp) for c in range(CHUNKS)]
    mine, send = combine(gate, embedded, pieces_back)
    other = swapped(send, "rep", 1 << CORE)
    return (mine + other.astype(F32)).astype(BF16)


def solution(mesh):
    return jax.shard_map(
        on_device,
        mesh=mesh,
        in_specs=(
            P(("rep", "exp"), None),
            P(),
            P(),
            P(("rep", "exp"), None),
            P(("rep", "exp"), None),
            P("exp", None, "rep"),
            P("exp", None, "rep"),
        ),
        out_specs=P(("rep", "exp"), None),
        check_vma=False,
    )
```

time: 107 us -> 100 us (0.935)
  local copies, waits for them, and re-layouts: 12 us -> 3.7 us
  starting transfers between devices: 43 us -> 37.2 us
  waiting for transfers between devices: 38.1 us -> 42.2 us
  Pallas kernels: 11.4 us -> 14.4 us
    unnamed x15 -> x6, local copies, waits for them, and re-layouts: 11.9 us -> 3.57 us
    ppermute x34 -> x32, starting transfers between devices: 43 us -> 37.2 us  [swapped(): lax.ppermute(array, axis, [(i, i ^ distance) for i in range(lax.axis_size...]
    ppermute x34 -> x32, waiting for transfers between devices: 38.1 us -> 42.2 us  [swapped(): lax.ppermute(array, axis, [(i, i ^ distance) for i in range(lax.axis_size...]
    pallas_call x3, Pallas kernels: 8.94 us -> 12.2 us  [the longest x2 11.8 us: experts(): pl.pallas_call(functools.partial(experts_kernel, chunk, half), out_shape=...]
  transfers between devices with their start and end apart: 34 -> 32, of which waited for: 17 -> 16; matrix products, arithmetic and copies ran while one was open for 2% -> 2% of each run, Pallas kernels for 10% -> 13%
where the time goes in v3:
time: 100 us; the launch traced here: 99.9 us
  waiting for transfers between devices  42.2 us (42%)
  starting transfers between devices  37.2 us (37%)
  Pallas kernels  14.4 us (14%)
  local copies, waits for them, and re-layouts  3.7 us (4%)
  other arithmetic  2.27 us (2%)
    ppermute x32, waiting for transfers between devices, swapped(): lax.ppermute(array, axis, [(i, i ^ distance) for i in range(lax.axis_size...  42.2 us
    ppermute x32, starting transfers between devices, swapped(): lax.ppermute(array, axis, [(i, i ^ distance) for i in range(lax.axis_size...  37.2 us
    pallas_call x2, Pallas kernels, experts(): pl.pallas_call(functools.partial(experts_kernel, chunk, half), out_shape=...  11.8 us
    unnamed x6, local copies, waits for them, and re-layouts  3.57 us
  transfers between devices with their start and end apart: 32, of which 16 were waited for; matrix products, arithmetic and copies ran while one was open for 2% of the time, Pallas kernels for 13%

profile of v3, /device:TPU:0, one launch (start us, length us, event | category | flops | bytes accessed | tf_op | source)
XLA Modules:
  0.0 99.9 jit_solution(15057434466007992880)
XLA Ops:
  0.0 1.9 %copy-done = bf16[1536,1024]{1,0:T(8,128)(2,1)S(1)} copy-done((bf16[1536,1024]{1,0:T(8,128)(2,1)S(1)}, bf16[1536,1024]{1,0:T(8,128)(2,1)}, u32[]{:S(2)}) %copy-start) | copy-done | bytes 3145752
  8.7 2.8 %collective-permute-start.2 = (bf16[4,24,1024]{2,1,0:T(8,128)(2,1)S(1)}, bf16[4,24,1024]{2,1,0:T(8,128)(2,1)S(1)}, u32[]{:S(2)}, u32[]{:S(2)}) collective-permute-start(bf16[4,24,1024]{2,1,0:T(8,128)(2,1)S(1)} %get-tuple-element.56), channel_id=1, source_target_pairs={{0,1},{1,0},{2,3},{3,2},{4,5},{5,4},{6,7},{7,6},{8,9},{9,8},{10,11... | collective-permute-start | bytes 589832 | tf_op jit(solution)/shard_map/ppermute | solution.py:20
  11.5 2.6 %collective-permute-start.3 = (bf16[2,24,1024]{2,1,0:T(8,128)(2,1)S(1)}, bf16[2,24,1024]{2,1,0:T(8,128)(2,1)S(1)}, u32[]{:S(2)}, u32[]{:S(2)}) collective-permute-start(bf16[2,24,1024]{2,1,0:T(8,128)(2,1)S(1)} %get-tuple-element.58), channel_id=1, source_target_pairs={{0,2},{1,3},{2,0},{3,1},{4,6},{5,7},{6,4},{7,5},{8,10},{9,11},{10,... | collective-permute-start | bytes 294920 | tf_op jit(solution)/shard_map/ppermute | solution.py:20
  14.1 4.9 %collective-permute-done.2 = bf16[4,24,1024]{2,1,0:T(8,128)(2,1)S(1)} collective-permute-done((bf16[4,24,1024]{2,1,0:T(8,128)(2,1)S(1)}, bf16[4,24,1024]{2,1,0:T(8,128)(2,1)S(1)}, u32[]{:S(2)}, u32[]{:S(2)}) %collective-permute-start.2) | collective-permute-done | bytes 196640 | tf_op jit(solution)/shard_map/ppermute | solution.py:20
  19.0 4.4 %collective-permute-done.4 = bf16[2,24,1024]{2,1,0:T(8,128)(2,1)S(1)} collective-permute-done((bf16[2,24,1024]{2,1,0:T(8,128)(2,1)S(1)}, bf16[2,24,1024]{2,1,0:T(8,128)(2,1)S(1)}, u32[]{:S(2)}, u32[]{:S(2)}) %collective-permute-start.4) | collective-permute-done | bytes 98336 | tf_op jit(solution)/shard_map/ppermute | solution.py:20
  23.4 1.6 %collective-permute-start.9 = (bf16[2,96,1024]{2,1,0:T(8,128)(2,1)S(1)}, bf16[2,96,1024]{2,1,0:T(8,128)(2,1)S(1)}, u32[]{:S(2)}, u32[]{:S(2)}) collective-permute-start(bf16[2,96,1024]{2,1,0:T(8,128)(2,1)S(1)} %pad_maximum_fusion.own_ref), channel_id=1, source_target_pairs={{0,16},{4,20},{8,24},{12,28},{16,0},{20,4},{24,8},{28,12},{1,17},{... | collective-permute-start | bytes 1179656 | tf_op jit(solution)/shard_map/ppermute | solution.py:20
  25.0 1.5 %collective-permute-start.8 = (bf16[2,96,1024]{2,1,0:T(8,128)(2,1)S(1)}, bf16[2,96,1024]{2,1,0:T(8,128)(2,1)S(1)}, u32[]{:S(2)}, u32[]{:S(2)}) collective-permute-start(bf16[2,96,1024]{2,1,0:T(8,128)(2,1)S(1)} %pad_maximum_fusion.own_ref), channel_id=1, source_target_pairs={{0,8},{4,12},{8,0},{12,4},{16,24},{20,28},{24,16},{28,20},{1,9},{5... | collective-permute-start | bytes 1179656 | tf_op jit(solution)/shard_map/ppermute | solution.py:20
  26.5 1.7 %collective-permute-start.6 = (bf16[2,24,1024]{2,1,0:T(8,128)(2,1)S(1)}, bf16[2,24,1024]{2,1,0:T(8,128)(2,1)S(1)}, u32[]{:S(2)}, u32[]{:S(2)}) collective-permute-start(bf16[2,24,1024]{2,1,0:T(8,128)(2,1)S(1)} %get-tuple-element.63), channel_id=1, source_target_pairs={{0,2},{1,3},{2,0},{3,1},{4,6},{5,7},{6,4},{7,5},{8,10},{9,11},{10,... | collective-permute-start | bytes 294920 | tf_op jit(solution)/shard_map/ppermute | solution.py:20
  28.2 1.3 %collective-permute-start.7 = (bf16[2,24,1024]{2,1,0:T(8,128)(2,1)S(1)}, bf16[2,24,1024]{2,1,0:T(8,128)(2,1)S(1)}, u32[]{:S(2)}, u32[]{:S(2)}) collective-permute-start(bf16[2,24,1024]{2,1,0:T(8,128)(2,1)S(1)} %get-tuple-element.64), channel_id=1, source_target_pairs={{0,3},{1,2},{2,1},{3,0},{4,7},{5,6},{6,5},{7,4},{8,11},{9,10},{10,... | collective-permute-start | bytes 294920 | tf_op jit(solution)/shard_map/ppermute | solution.py:20
  29.5 4.4 %collective-permute-done.9.b_ref = bf16[2,96,1024]{2,1,0:T(8,128)(2,1)S(1)} collective-permute-done((bf16[2,96,1024]{2,1,0:T(8,128)(2,1)S(1)}, bf16[2,96,1024]{2,1,0:T(8,128)(2,1)S(1)}, u32[]{:S(2)}, u32[]{:S(2)}) %collective-permute-start.9) | collective-permute-done | bytes 393248 | tf_op jit(solution)/shard_map/ppermute | solution.py:20
  34.0 1.6 %collective-permute-start.13 = (bf16[1,96,1024]{2,1,0:T(8,128)(2,1)S(1)}, bf16[1,96,1024]{2,1,0:T(8,128)(2,1)S(1)}, u32[]{:S(2)}, u32[]{:S(2)}) collective-permute-start(bf16[1,96,1024]{2,1,0:T(8,128)(2,1)S(1)} %slice.91), channel_id=1, source_target_pairs={{0,8},{4,12},{8,0},{12,4},{16,24},{20,28},{24,16},{28,20},{1,9},{5... | collective-permute-start | bytes 589832 | tf_op jit(solution)/shard_map/ppermute | solution.py:20
  35.6 1.6 %collective-permute-start.12 = (bf16[1,96,1024]{2,1,0:T(8,128)(2,1)S(1)}, bf16[1,96,1024]{2,1,0:T(8,128)(2,1)S(1)}, u32[]{:S(2)}, u32[]{:S(2)}) collective-permute-start(bf16[1,96,1024]{2,1,0:T(8,128)(2,1)S(1)} %slice.90), channel_id=1, source_target_pairs={{0,16},{4,20},{8,24},{12,28},{16,0},{20,4},{24,8},{28,12},{1,17},{... | collective-permute-start | bytes 589832 | tf_op jit(solution)/shard_map/ppermute | solution.py:20
  37.8 1.2 %collective-permute-start.10 = (bf16[2,96,1024]{2,1,0:T(8,128)(2,1)S(1)}, bf16[2,96,1024]{2,1,0:T(8,128)(2,1)S(1)}, u32[]{:S(2)}, u32[]{:S(2)}) collective-permute-start(bf16[2,96,1024]{2,1,0:T(8,128)(2,1)S(1)} %pad_maximum_fusion.1.own_ref), channel_id=1, source_target_pairs={{0,8},{4,12},{8,0},{12,4},{16,24},{20,28},{24,16},{28,20},{1,9},{5... | collective-permute-start | bytes 1179656 | tf_op jit(solution)/shard_map/ppermute | solution.py:20
  38.9 2.5 %collective-permute-done.13.d2_ref = bf16[1,96,1024]{2,1,0:T(8,128)(2,1)S(1)} collective-permute-done((bf16[1,96,1024]{2,1,0:T(8,128)(2,1)S(1)}, bf16[1,96,1024]{2,1,0:T(8,128)(2,1)S(1)}, u32[]{:S(2)}, u32[]{:S(2)}) %collective-permute-start.13) | collective-permute-done | bytes 196640 | tf_op jit(solution)/shard_map/ppermute | solution.py:20
  41.4 2.1 %collective-permute-done.12.d1_ref = bf16[1,96,1024]{2,1,0:T(8,128)(2,1)S(1)} collective-permute-done((bf16[1,96,1024]{2,1,0:T(8,128)(2,1)S(1)}, bf16[1,96,1024]{2,1,0:T(8,128)(2,1)S(1)}, u32[]{:S(2)}, u32[]{:S(2)}) %collective-permute-start.12) | collective-permute-done | bytes 196640 | tf_op jit(solution)/shard_map/ppermute | solution.py:20
  43.5 5.9 %experts.2 = (bf16[2,96,1024]{2,1,0:T(8,128)(2,1)S(1)}, bf16[2,96,1024]{2,1,0:T(8,128)(2,1)S(1)}, bf16[2,96,1024]{2,1,0:T(8,128)(2,1)S(1)}, bf16[1,96,1024]{2,1,0:T(8,128)(2,1)S(1)}, bf16[1,96,1024]{2,1,0:T(8,128)(2,1)S(1)}) custom-call(s32[2]{0:T(128)S(1)} %pad_add_fusion.1.place_ref, bf16[2,96,1024]{2,1,0:T(8,128)(2,1)S(1)} %pad_maximum_fusion.own_ref, ...), custom_call_target="tpu_custom_call" | custom-call | flops 3221225472 | bytes 3145728 | tf_op jit(solution)/shard_map/experts/pallas_call | solution.py:192
  49.4 1.6 %collective-permute-start.15 = (bf16[1,96,1024]{2,1,0:T(8,128)(2,1)S(1)}, bf16[1,96,1024]{2,1,0:T(8,128)(2,1)S(1)}, u32[]{:S(2)}, u32[]{:S(2)}) collective-permute-start(bf16[1,96,1024]{2,1,0:T(8,128)(2,1)S(1)} %get-tuple-element.76), channel_id=1, source_target_pairs={{0,16},{4,20},{8,24},{12,28},{16,0},{20,4},{24,8},{28,12},{1,17},{... | collective-permute-start | bytes 589832 | tf_op jit(solution)/shard_map/ppermute | solution.py:20
  51.6 1.1 %collective-permute-start.17 = (bf16[1,96,1024]{2,1,0:T(8,128)(2,1)S(1)}, bf16[1,96,1024]{2,1,0:T(8,128)(2,1)S(1)}, u32[]{:S(2)}, u32[]{:S(2)}) collective-permute-start(bf16[1,96,1024]{2,1,0:T(8,128)(2,1)S(1)} %slice.74), channel_id=1, source_target_pairs={{0,16},{4,20},{8,24},{12,28},{16,0},{20,4},{24,8},{28,12},{1,17},{... | collective-permute-start | bytes 589832 | tf_op jit(solution)/shard_map/ppermute | solution.py:20
  53.7 1.8 %collective-permute-done.15 = bf16[1,96,1024]{2,1,0:T(8,128)(2,1)S(1)} collective-permute-done((bf16[1,96,1024]{2,1,0:T(8,128)(2,1)S(1)}, bf16[1,96,1024]{2,1,0:T(8,128)(2,1)S(1)}, u32[]{:S(2)}, u32[]{:S(2)}) %collective-permute-start.15) | collective-permute-done | bytes 196640 | tf_op jit(solution)/shard_map/ppermute | solution.py:20
  55.5 4.6 %collective-permute-done.16 = bf16[1,96,1024]{2,1,0:T(8,128)(2,1)S(1)} collective-permute-done((bf16[1,96,1024]{2,1,0:T(8,128)(2,1)S(1)}, bf16[1,96,1024]{2,1,0:T(8,128)(2,1)S(1)}, u32[]{:S(2)}, u32[]{:S(2)}) %collective-permute-start.16) | collective-permute-done | bytes 196640 | tf_op jit(solution)/shard_map/ppermute | solution.py:20
  60.9 1.7 %collective-permute-start.20 = (bf16[2,96,1024]{2,1,0:T(8,128)(2,1)S(1)}, bf16[2,96,1024]{2,1,0:T(8,128)(2,1)S(1)}, u32[]{:S(2)}, u32[]{:S(2)}) collective-permute-start(bf16[2,96,1024]{2,1,0:T(8,128)(2,1)S(1)} %get-tuple-element.87), channel_id=1, source_target_pairs={{0,16},{4,20},{8,24},{12,28},{16,0},{20,4},{24,8},{28,12},{1,17},{... | collective-permute-start | bytes 1179656 | tf_op jit(solution)/shard_map/ppermute | solution.py:20
  62.6 5.9 %experts.3 = (bf16[2,96,1024]{2,1,0:T(8,128)(2,1)S(1)}, bf16[2,96,1024]{2,1,0:T(8,128)(2,1)S(1)}, bf16[2,96,1024]{2,1,0:T(8,128)(2,1)S(1)}, bf16[1,96,1024]{2,1,0:T(8,128)(2,1)S(1)}, bf16[1,96,1024]{2,1,0:T(8,128)(2,1)S(1)}) custom-call(s32[2]{0:T(128)S(1)} %pad_add_fusion.1.place_ref, bf16[2,96,1024]{2,1,0:T(8,128)(2,1)S(1)} %pad_maximum_fusion.1.own_ref, ...), custom_call_target="tpu_custom_call" | custom-call | flops 3221225472 | bytes 3145728 | tf_op jit(solution)/shard_map/experts/pallas_call | solution.py:192
  68.5 1.8 %collective-permute-done.19 = bf16[2,96,1024]{2,1,0:T(8,128)(2,1)S(1)} collective-permute-done((bf16[2,96,1024]{2,1,0:T(8,128)(2,1)S(1)}, bf16[2,96,1024]{2,1,0:T(8,128)(2,1)S(1)}, u32[]{:S(2)}, u32[]{:S(2)}) %collective-permute-start.19) | collective-permute-done | bytes 393248 | tf_op jit(solution)/shard_map/ppermute | solution.py:20
  70.7 1.5 %collective-permute-start.23 = (bf16[1,96,1024]{2,1,0:T(8,128)(2,1)S(1)}, bf16[1,96,1024]{2,1,0:T(8,128)(2,1)S(1)}, u32[]{:S(2)}, u32[]{:S(2)}) collective-permute-start(bf16[1,96,1024]{2,1,0:T(8,128)(2,1)S(1)} %get-tuple-element.94), channel_id=1, source_target_pairs={{0,8},{4,12},{8,0},{12,4},{16,24},{20,28},{24,16},{28,20},{1,9},{5... | collective-permute-start | bytes 589832 | tf_op jit(solution)/shard_map/ppermute | solution.py:20
  72.8 5.8 %collective-permute-done.23 = bf16[1,96,1024]{2,1,0:T(8,128)(2,1)S(1)} collective-permute-done((bf16[1,96,1024]{2,1,0:T(8,128)(2,1)S(1)}, bf16[1,96,1024]{2,1,0:T(8,128)(2,1)S(1)}, u32[]{:S(2)}, u32[]{:S(2)}) %collective-permute-start.23) | collective-permute-done | bytes 196640 | tf_op jit(solution)/shard_map/ppermute | solution.py:20
  78.6 1.8 %collective-permute-start.24 = (bf16[2,96,1024]{2,1,0:T(8,128)(2,1)S(1)}, bf16[2,96,1024]{2,1,0:T(8,128)(2,1)S(1)}, u32[]{:S(2)}, u32[]{:S(2)}) collective-permute-start(bf16[2,96,1024]{2,1,0:T(8,128)(2,1)S(1)} %pad_maximum_fusion.5), channel_id=1, source_target_pairs={{0,16},{4,20},{8,24},{12,28},{16,0},{20,4},{24,8},{28,12},{1,17},{... | collective-permute-start | bytes 1179656 | tf_op jit(solution)/shard_map/ppermute | solution.py:20
  82.0 3.5 %collective-permute-start.25 = (bf16[2,24,1024]{2,1,0:T(8,128)(2,1)S(1)}, bf16[2,24,1024]{2,1,0:T(8,128)(2,1)S(1)}, u32[]{:S(2)}, u32[]{:S(2)}) collective-permute-start(bf16[2,24,1024]{2,1,0:T(8,128)(2,1)S(1)} %get-tuple-element.103), channel_id=1, source_target_pairs={{0,1},{1,0},{2,3},{3,2},{4,5},{5,4},{6,7},{7,6},{8,9},{9,8},{10,11... | collective-permute-start | bytes 294920 | tf_op jit(solution)/shard_map/ppermute | solution.py:20
  86.5 1.9 %collective-permute-done.22 = bf16[2,96,1024]{2,1,0:T(8,128)(2,1)S(1)} collective-permute-done((bf16[2,96,1024]{2,1,0:T(8,128)(2,1)S(1)}, bf16[2,96,1024]{2,1,0:T(8,128)(2,1)S(1)}, u32[]{:S(2)}, u32[]{:S(2)}) %collective-permute-start.22) | collective-permute-done | bytes 393248 | tf_op jit(solution)/shard_map/ppermute | solution.py:20
  89.5 3.6 %collective-permute-start.26 = (bf16[2,24,1024]{2,1,0:T(8,128)(2,1)S(1)}, bf16[2,24,1024]{2,1,0:T(8,128)(2,1)S(1)}, u32[]{:S(2)}, u32[]{:S(2)}) collective-permute-start(bf16[2,24,1024]{2,1,0:T(8,128)(2,1)S(1)} %get-tuple-element.99), channel_id=1, source_target_pairs={{0,1},{1,0},{2,3},{3,2},{4,5},{5,4},{6,7},{7,6},{8,9},{9,8},{10,11... | collective-permute-start | bytes 294920 | tf_op jit(solution)/shard_map/ppermute | solution.py:20
  93.1 2.2 %collective-permute-done.30.refs_7_ = bf16[2,24,1024]{2,1,0:T(8,128)(2,1)S(1)} collective-permute-done((bf16[2,24,1024]{2,1,0:T(8,128)(2,1)S(1)}, bf16[2,24,1024]{2,1,0:T(8,128)(2,1)S(1)}, u32[]{:S(2)}, u32[]{:S(2)}) %collective-permute-start.30) | collective-permute-done | bytes 98336 | tf_op jit(solution)/shard_map/ppermute | solution.py:20
  95.2 1.9 %collective-permute-done.28.refs_5_ = bf16[2,24,1024]{2,1,0:T(8,128)(2,1)S(1)} collective-permute-done((bf16[2,24,1024]{2,1,0:T(8,128)(2,1)S(1)}, bf16[2,24,1024]{2,1,0:T(8,128)(2,1)S(1)}, u32[]{:S(2)}, u32[]{:S(2)}) %collective-permute-start.28) | collective-permute-done | bytes 98336 | tf_op jit(solution)/shard_map/ppermute | solution.py:20
  97.6 1.5 %collective-permute-done.31 = bf16[128,1024]{1,0:T(8,128)(2,1)S(1)} collective-permute-done((bf16[128,1024]{1,0:T(8,128)(2,1)S(1)}, bf16[128,1024]{1,0:T(8,128)(2,1)S(1)}, u32[]{:S(2)}, u32[]{:S(2)}) %collective-permute-start.31) | collective-permute-done | bytes 262176 | tf_op jit(solution)/shard_map/ppermute | solution.py:20
  (65 shorter events, 15.6 us)
Async XLA Ops:
  4.4 3.3 %collective-permute-start.1 = (bf16[128,1024]{1,0:T(8,128)(2,1)S(1)}, bf16[128,1024]{1,0:T(8,128)(2,1)S(1)}, u32[]{:S(2)}, u32[]{:S(2)}) collective-permute-start(bf16[128,1024]{1,0:T(8,128)(2,1)S(1)} %get-tuple-element.54.normed_ref), channel_id=1, source_target_pairs={{0,4},{4,0},{8,12},{12,8},{16,20},{20,16},{24,28},{28,24},{1,5},{5... | collective-permute-start | bytes 786440 | tf_op jit(solution)/shard_map/ppermute | solution.py:20
  5.6 1.2 %collective-permute-start = (s32[4,128]{1,0:T(4,128)S(1)}, s32[4,128]{1,0:T(4,128)S(1)}, u32[]{:S(2)}, u32[]{:S(2)}) collective-permute-start(s32[4,128]{1,0:T(4,128)S(1)} %pad_add_fusion.code_ref), channel_id=1, source_target_pairs={{0,4},{4,0},{8,12},{12,8},{16,20},{20,16},{24,28},{28,24},{1,5},{5... | collective-permute-start | bytes 6152 | tf_op jit(solution)/shard_map/ppermute | solution.py:20
  7.7 18.8 %collective-permute-start.5 = (bf16[8,1024,512]{2,1,0:T(8,128)(2,1)}, bf16[8,1024,512]{2,1,0:T(8,128)(2,1)S(1)}, u32[]{:S(2)}, u32[]{:S(2)}) collective-permute-start(bf16[8,1024,512]{2,1,0:T(8,128)(2,1)} %in_ref.3), channel_id=1, source_target_pairs={{0,4},{4,0},{8,12},{12,8},{16,20},{20,16},{24,28},{28,24},{1,5},{5... | collective-permute-start | bytes 25165832 | tf_op jit(solution)/shard_map/ppermute | solution.py:20
  8.0 35.5 %collective-permute-start.14 = (bf16[8,1024,512]{2,1,0:T(8,128)(2,1)}, bf16[8,1024,512]{2,1,0:T(8,128)(2,1)S(1)}, u32[]{:S(2)}, u32[]{:S(2)}) collective-permute-start(bf16[8,1024,512]{2,1,0:T(8,128)(2,1)} %down_ref.3), channel_id=1, source_target_pairs={{0,4},{4,0},{8,12},{12,8},{16,20},{20,16},{24,28},{28,24},{1,5},{5... | collective-permute-start | bytes 25165832 | tf_op jit(solution)/shard_map/ppermute | solution.py:20
  8.7 10.3 %collective-permute-start.2 = (bf16[4,24,1024]{2,1,0:T(8,128)(2,1)S(1)}, bf16[4,24,1024]{2,1,0:T(8,128)(2,1)S(1)}, u32[]{:S(2)}, u32[]{:S(2)}) collective-permute-start(bf16[4,24,1024]{2,1,0:T(8,128)(2,1)S(1)} %get-tuple-element.56), channel_id=1, source_target_pairs={{0,1},{1,0},{2,3},{3,2},{4,5},{5,4},{6,7},{7,6},{8,9},{9,8},{10,11... | collective-permute-start | bytes 589832 | tf_op jit(solution)/shard_map/ppermute | solution.py:20
  11.5 7.5 %collective-permute-start.3 = (bf16[2,24,1024]{2,1,0:T(8,128)(2,1)S(1)}, bf16[2,24,1024]{2,1,0:T(8,128)(2,1)S(1)}, u32[]{:S(2)}, u32[]{:S(2)}) collective-permute-start(bf16[2,24,1024]{2,1,0:T(8,128)(2,1)S(1)} %get-tuple-element.58), channel_id=1, source_target_pairs={{0,2},{1,3},{2,0},{3,1},{4,6},{5,7},{6,4},{7,5},{8,10},{9,11},{10,... | collective-permute-start | bytes 294920 | tf_op jit(solution)/shard_map/ppermute | solution.py:20
  14.1 9.3 %collective-permute-start.4 = (bf16[2,24,1024]{2,1,0:T(8,128)(2,1)S(1)}, bf16[2,24,1024]{2,1,0:T(8,128)(2,1)S(1)}, u32[]{:S(2)}, u32[]{:S(2)}) collective-permute-start(bf16[2,24,1024]{2,1,0:T(8,128)(2,1)S(1)} %get-tuple-element.59), channel_id=1, source_target_pairs={{0,3},{1,2},{2,1},{3,0},{4,7},{5,6},{6,5},{7,4},{8,11},{9,10},{10,... | collective-permute-start | bytes 294920 | tf_op jit(solution)/shard_map/ppermute | solution.py:20
  23.4 10.6 %collective-permute-start.9 = (bf16[2,96,1024]{2,1,0:T(8,128)(2,1)S(1)}, bf16[2,96,1024]{2,1,0:T(8,128)(2,1)S(1)}, u32[]{:S(2)}, u32[]{:S(2)}) collective-permute-start(bf16[2,96,1024]{2,1,0:T(8,128)(2,1)S(1)} %pad_maximum_fusion.own_ref), channel_id=1, source_target_pairs={{0,16},{4,20},{8,24},{12,28},{16,0},{20,4},{24,8},{28,12},{1,17},{... | collective-permute-start | bytes 1179656 | tf_op jit(solution)/shard_map/ppermute | solution.py:20
  25.0 10.6 %collective-permute-start.8 = (bf16[2,96,1024]{2,1,0:T(8,128)(2,1)S(1)}, bf16[2,96,1024]{2,1,0:T(8,128)(2,1)S(1)}, u32[]{:S(2)}, u32[]{:S(2)}) collective-permute-start(bf16[2,96,1024]{2,1,0:T(8,128)(2,1)S(1)} %pad_maximum_fusion.own_ref), channel_id=1, source_target_pairs={{0,8},{4,12},{8,0},{12,4},{16,24},{20,28},{24,16},{28,20},{1,9},{5... | collective-permute-start | bytes 1179656 | tf_op jit(solution)/shard_map/ppermute | solution.py:20
  26.5 10.7 %collective-permute-start.6 = (bf16[2,24,1024]{2,1,0:T(8,128)(2,1)S(1)}, bf16[2,24,1024]{2,1,0:T(8,128)(2,1)S(1)}, u32[]{:S(2)}, u32[]{:S(2)}) collective-permute-start(bf16[2,24,1024]{2,1,0:T(8,128)(2,1)S(1)} %get-tuple-element.63), channel_id=1, source_target_pairs={{0,2},{1,3},{2,0},{3,1},{4,6},{5,7},{6,4},{7,5},{8,10},{9,11},{10,... | collective-permute-start | bytes 294920 | tf_op jit(solution)/shard_map/ppermute | solution.py:20
  28.2 8.9 %collective-permute-start.7 = (bf16[2,24,1024]{2,1,0:T(8,128)(2,1)S(1)}, bf16[2,24,1024]{2,1,0:T(8,128)(2,1)S(1)}, u32[]{:S(2)}, u32[]{:S(2)}) collective-permute-start(bf16[2,24,1024]{2,1,0:T(8,128)(2,1)S(1)} %get-tuple-element.64), channel_id=1, source_target_pairs={{0,3},{1,2},{2,1},{3,0},{4,7},{5,6},{6,5},{7,4},{8,11},{9,10},{10,... | collective-permute-start | bytes 294920 | tf_op jit(solution)/shard_map/ppermute | solution.py:20
  34.0 7.4 %collective-permute-start.13 = (bf16[1,96,1024]{2,1,0:T(8,128)(2,1)S(1)}, bf16[1,96,1024]{2,1,0:T(8,128)(2,1)S(1)}, u32[]{:S(2)}, u32[]{:S(2)}) collective-permute-start(bf16[1,96,1024]{2,1,0:T(8,128)(2,1)S(1)} %slice.91), channel_id=1, source_target_pairs={{0,8},{4,12},{8,0},{12,4},{16,24},{20,28},{24,16},{28,20},{1,9},{5... | collective-permute-start | bytes 589832 | tf_op jit(solution)/shard_map/ppermute | solution.py:20
  35.6 7.9 %collective-permute-start.12 = (bf16[1,96,1024]{2,1,0:T(8,128)(2,1)S(1)}, bf16[1,96,1024]{2,1,0:T(8,128)(2,1)S(1)}, u32[]{:S(2)}, u32[]{:S(2)}) collective-permute-start(bf16[1,96,1024]{2,1,0:T(8,128)(2,1)S(1)} %slice.90), channel_id=1, source_target_pairs={{0,16},{4,20},{8,24},{12,28},{16,0},{20,4},{24,8},{28,12},{1,17},{... | collective-permute-start | bytes 589832 | tf_op jit(solution)/shard_map/ppermute | solution.py:20
  37.2 12.2 %collective-permute-start.11 = (bf16[2,96,1024]{2,1,0:T(8,128)(2,1)S(1)}, bf16[2,96,1024]{2,1,0:T(8,128)(2,1)S(1)}, u32[]{:S(2)}, u32[]{:S(2)}) collective-permute-start(bf16[2,96,1024]{2,1,0:T(8,128)(2,1)S(1)} %pad_maximum_fusion.1.own_ref), channel_id=1, source_target_pairs={{0,16},{4,20},{8,24},{12,28},{16,0},{20,4},{24,8},{28,12},{1,17},{... | collective-permute-start | bytes 1179656 | tf_op jit(solution)/shard_map/ppermute | solution.py:20
  37.8 11.6 %collective-permute-start.10 = (bf16[2,96,1024]{2,1,0:T(8,128)(2,1)S(1)}, bf16[2,96,1024]{2,1,0:T(8,128)(2,1)S(1)}, u32[]{:S(2)}, u32[]{:S(2)}) collective-permute-start(bf16[2,96,1024]{2,1,0:T(8,128)(2,1)S(1)} %pad_maximum_fusion.1.own_ref), channel_id=1, source_target_pairs={{0,8},{4,12},{8,0},{12,4},{16,24},{20,28},{24,16},{28,20},{1,9},{5... | collective-permute-start | bytes 1179656 | tf_op jit(solution)/shard_map/ppermute | solution.py:20
  49.4 6.0 %collective-permute-start.15 = (bf16[1,96,1024]{2,1,0:T(8,128)(2,1)S(1)}, bf16[1,96,1024]{2,1,0:T(8,128)(2,1)S(1)}, u32[]{:S(2)}, u32[]{:S(2)}) collective-permute-start(bf16[1,96,1024]{2,1,0:T(8,128)(2,1)S(1)} %get-tuple-element.76), channel_id=1, source_target_pairs={{0,16},{4,20},{8,24},{12,28},{16,0},{20,4},{24,8},{28,12},{1,17},{... | collective-permute-start | bytes 589832 | tf_op jit(solution)/shard_map/ppermute | solution.py:20
  51.1 9.2 %collective-permute-start.18 = (bf16[1,96,1024]{2,1,0:T(8,128)(2,1)S(1)}, bf16[1,96,1024]{2,1,0:T(8,128)(2,1)S(1)}, u32[]{:S(2)}, u32[]{:S(2)}) collective-permute-start(bf16[1,96,1024]{2,1,0:T(8,128)(2,1)S(1)} %slice.75), channel_id=1, source_target_pairs={{0,8},{4,12},{8,0},{12,4},{16,24},{20,28},{24,16},{28,20},{1,9},{5... | collective-permute-start | bytes 589832 | tf_op jit(solution)/shard_map/ppermute | solution.py:20
  51.6 8.6 %collective-permute-start.17 = (bf16[1,96,1024]{2,1,0:T(8,128)(2,1)S(1)}, bf16[1,96,1024]{2,1,0:T(8,128)(2,1)S(1)}, u32[]{:S(2)}, u32[]{:S(2)}) collective-permute-start(bf16[1,96,1024]{2,1,0:T(8,128)(2,1)S(1)} %slice.74), channel_id=1, source_target_pairs={{0,16},{4,20},{8,24},{12,28},{16,0},{20,4},{24,8},{28,12},{1,17},{... | collective-permute-start | bytes 589832 | tf_op jit(solution)/shard_map/ppermute | solution.py:20
  52.8 7.4 %collective-permute-start.16 = (bf16[1,96,1024]{2,1,0:T(8,128)(2,1)S(1)}, bf16[1,96,1024]{2,1,0:T(8,128)(2,1)S(1)}, u32[]{:S(2)}, u32[]{:S(2)}) collective-permute-start(bf16[1,96,1024]{2,1,0:T(8,128)(2,1)S(1)} %get-tuple-element.78), channel_id=1, source_target_pairs={{0,8},{4,12},{8,0},{12,4},{16,24},{20,28},{24,16},{28,20},{1,9},{5... | collective-permute-start | bytes 589832 | tf_op jit(solution)/shard_map/ppermute | solution.py:20
  60.3 9.9 %collective-permute-start.19 = (bf16[2,96,1024]{2,1,0:T(8,128)(2,1)S(1)}, bf16[2,96,1024]{2,1,0:T(8,128)(2,1)S(1)}, u32[]{:S(2)}, u32[]{:S(2)}) collective-permute-start(bf16[2,96,1024]{2,1,0:T(8,128)(2,1)S(1)} %get-tuple-element.86), channel_id=1, source_target_pairs={{0,8},{4,12},{8,0},{12,4},{16,24},{20,28},{24,16},{28,20},{1,9},{5... | collective-permute-start | bytes 1179656 | tf_op jit(solution)/shard_map/ppermute | solution.py:20
  60.9 9.9 %collective-permute-start.20 = (bf16[2,96,1024]{2,1,0:T(8,128)(2,1)S(1)}, bf16[2,96,1024]{2,1,0:T(8,128)(2,1)S(1)}, u32[]{:S(2)}, u32[]{:S(2)}) collective-permute-start(bf16[2,96,1024]{2,1,0:T(8,128)(2,1)S(1)} %get-tuple-element.87), channel_id=1, source_target_pairs={{0,16},{4,20},{8,24},{12,28},{16,0},{20,4},{24,8},{28,12},{1,17},{... | collective-permute-start | bytes 1179656 | tf_op jit(solution)/shard_map/ppermute | solution.py:20
  70.7 7.8 %collective-permute-start.23 = (bf16[1,96,1024]{2,1,0:T(8,128)(2,1)S(1)}, bf16[1,96,1024]{2,1,0:T(8,128)(2,1)S(1)}, u32[]{:S(2)}, u32[]{:S(2)}) collective-permute-start(bf16[1,96,1024]{2,1,0:T(8,128)(2,1)S(1)} %get-tuple-element.94), channel_id=1, source_target_pairs={{0,8},{4,12},{8,0},{12,4},{16,24},{20,28},{24,16},{28,20},{1,9},{5... | collective-permute-start | bytes 589832 | tf_op jit(solution)/shard_map/ppermute | solution.py:20
  72.3 8.2 %collective-permute-start.21 = (bf16[1,96,1024]{2,1,0:T(8,128)(2,1)S(1)}, bf16[1,96,1024]{2,1,0:T(8,128)(2,1)S(1)}, u32[]{:S(2)}, u32[]{:S(2)}) collective-permute-start(bf16[1,96,1024]{2,1,0:T(8,128)(2,1)S(1)} %get-tuple-element.92), channel_id=1, source_target_pairs={{0,16},{4,20},{8,24},{12,28},{16,0},{20,4},{24,8},{28,12},{1,17},{... | collective-permute-start | bytes 589832 | tf_op jit(solution)/shard_map/ppermute | solution.py:20
  78.6 7.8 %collective-permute-start.24 = (bf16[2,96,1024]{2,1,0:T(8,128)(2,1)S(1)}, bf16[2,96,1024]{2,1,0:T(8,128)(2,1)S(1)}, u32[]{:S(2)}, u32[]{:S(2)}) collective-permute-start(bf16[2,96,1024]{2,1,0:T(8,128)(2,1)S(1)} %pad_maximum_fusion.5), channel_id=1, source_target_pairs={{0,16},{4,20},{8,24},{12,28},{16,0},{20,4},{24,8},{28,12},{1,17},{... | collective-permute-start | bytes 1179656 | tf_op jit(solution)/shard_map/ppermute | solution.py:20
  80.5 7.8 %collective-permute-start.22 = (bf16[2,96,1024]{2,1,0:T(8,128)(2,1)S(1)}, bf16[2,96,1024]{2,1,0:T(8,128)(2,1)S(1)}, u32[]{:S(2)}, u32[]{:S(2)}) collective-permute-start(bf16[2,96,1024]{2,1,0:T(8,128)(2,1)S(1)} %pad_maximum_fusion.4), channel_id=1, source_target_pairs={{0,8},{4,12},{8,0},{12,4},{16,24},{20,28},{24,16},{28,20},{1,9},{5... | collective-permute-start | bytes 1179656 | tf_op jit(solution)/shard_map/ppermute | solution.py:20
  81.1 8.4 %collective-permute-start.29 = (bf16[2,24,1024]{2,1,0:T(8,128)(2,1)S(1)}, bf16[2,24,1024]{2,1,0:T(8,128)(2,1)S(1)}, u32[]{:S(2)}, u32[]{:S(2)}) collective-permute-start(bf16[2,24,1024]{2,1,0:T(8,128)(2,1)S(1)} %get-tuple-element.101), channel_id=1, source_target_pairs={{0,3},{1,2},{2,1},{3,0},{4,7},{5,6},{6,5},{7,4},{8,11},{9,10},{10,... | collective-permute-start | bytes 294920 | tf_op jit(solution)/shard_map/ppermute | solution.py:20
  82.0 11.0 %collective-permute-start.27 = (bf16[2,24,1024]{2,1,0:T(8,128)(2,1)S(1)}, bf16[2,24,1024]{2,1,0:T(8,128)(2,1)S(1)}, u32[]{:S(2)}, u32[]{:S(2)}) collective-permute-start(bf16[2,24,1024]{2,1,0:T(8,128)(2,1)S(1)} %get-tuple-element.102), channel_id=1, source_target_pairs={{0,2},{1,3},{2,0},{3,1},{4,6},{5,7},{6,4},{7,5},{8,10},{9,11},{10,... | collective-permute-start | bytes 294920 | tf_op jit(solution)/shard_map/ppermute | solution.py:20
  82.0 11.0 %collective-permute-start.25 = (bf16[2,24,1024]{2,1,0:T(8,128)(2,1)S(1)}, bf16[2,24,1024]{2,1,0:T(8,128)(2,1)S(1)}, u32[]{:S(2)}, u32[]{:S(2)}) collective-permute-start(bf16[2,24,1024]{2,1,0:T(8,128)(2,1)S(1)} %get-tuple-element.103), channel_id=1, source_target_pairs={{0,1},{1,0},{2,3},{3,2},{4,5},{5,4},{6,7},{7,6},{8,9},{9,8},{10,11... | collective-permute-start | bytes 294920 | tf_op jit(solution)/shard_map/ppermute | solution.py:20
  88.6 6.6 %collective-permute-start.30 = (bf16[2,24,1024]{2,1,0:T(8,128)(2,1)S(1)}, bf16[2,24,1024]{2,1,0:T(8,128)(2,1)S(1)}, u32[]{:S(2)}, u32[]{:S(2)}) collective-permute-start(bf16[2,24,1024]{2,1,0:T(8,128)(2,1)S(1)} %get-tuple-element.97), channel_id=1, source_target_pairs={{0,3},{1,2},{2,1},{3,0},{4,7},{5,6},{6,5},{7,4},{8,11},{9,10},{10,... | collective-permute-start | bytes 294920 | tf_op jit(solution)/shard_map/ppermute | solution.py:20
  89.5 7.6 %collective-permute-start.28 = (bf16[2,24,1024]{2,1,0:T(8,128)(2,1)S(1)}, bf16[2,24,1024]{2,1,0:T(8,128)(2,1)S(1)}, u32[]{:S(2)}, u32[]{:S(2)}) collective-permute-start(bf16[2,24,1024]{2,1,0:T(8,128)(2,1)S(1)} %get-tuple-element.98), channel_id=1, source_target_pairs={{0,2},{1,3},{2,0},{3,1},{4,6},{5,7},{6,4},{7,5},{8,10},{9,11},{10,... | collective-permute-start | bytes 294920 | tf_op jit(solution)/shard_map/ppermute | solution.py:20
  89.5 7.6 %collective-permute-start.26 = (bf16[2,24,1024]{2,1,0:T(8,128)(2,1)S(1)}, bf16[2,24,1024]{2,1,0:T(8,128)(2,1)S(1)}, u32[]{:S(2)}, u32[]{:S(2)}) collective-permute-start(bf16[2,24,1024]{2,1,0:T(8,128)(2,1)S(1)} %get-tuple-element.99), channel_id=1, source_target_pairs={{0,1},{1,0},{2,3},{3,2},{4,5},{5,4},{6,7},{7,6},{8,9},{9,8},{10,11... | collective-permute-start | bytes 294920 | tf_op jit(solution)/shard_map/ppermute | solution.py:20
  97.6 1.6 %collective-permute-start.31 = (bf16[128,1024]{1,0:T(8,128)(2,1)S(1)}, bf16[128,1024]{1,0:T(8,128)(2,1)S(1)}, u32[]{:S(2)}, u32[]{:S(2)}) collective-permute-start(bf16[128,1024]{1,0:T(8,128)(2,1)S(1)} %get-tuple-element.96), channel_id=1, source_target_pairs={{0,4},{4,0},{8,12},{12,8},{16,20},{20,16},{24,28},{28,24},{1,5},{5... | collective-permute-start | bytes 786440 | tf_op jit(solution)/shard_map/ppermute | solution.py:20
  (3 other events, 3.6 us)

commit v4 on v3

--- a/solution.py
+++ b/solution.py
@@ -48,27 +48,48 @@
     return pl.BlockSpec(memory_space=pltpu.SMEM)
 
 
-def embed_kernel(tubelets_ref, weight_ref, gain_ref, emb_ref, normed_ref):
-    embedded = mm(tubelets_ref[...], weight_ref[...]).astype(BF16)
+def embed_kernel(tubelets_ref, weight_ref, gain_ref, emb_ref, normed_ref, tub, weight, gain, sems):
+    parts = sems.shape[0] - 2
+    depth = weight_ref.shape[0] // parts
+    copies = []
+    for k in range(parts):
+        rows = pl.ds(k * depth, depth)
+        copies.append(pltpu.make_async_copy(weight_ref.at[rows], weight.at[rows], sems.at[k]))
+    tub_copy = pltpu.make_async_copy(tubelets_ref, tub, sems.at[parts])
+    gain_copy = pltpu.make_async_copy(gain_ref, gain, sems.at[parts + 1])
+    for copy in (tub_copy, *copies, gain_copy):
+        copy.start()
+    tub_copy.wait()
+    total = None
+    for k in range(parts):
+        copies[k].wait()
+        rows = slice(k * depth, (k + 1) * depth)
+        term = mm(tub[:, rows], weight[rows, :])
+        total = term if total is None else total + term
+    embedded = total.astype(BF16)
     emb_ref[...] = embedded
     floats = embedded.astype(F32)
     centred = floats - jnp.mean(floats, axis=-1, keepdims=True)
     variance = jnp.mean(centred * centred, axis=-1, keepdims=True)
-    normed_ref[...] = (centred * lax.rsqrt(variance + 1e-06) * gain_ref[...]).astype(BF16)
+    gain_copy.wait()
+    normed_ref[...] = (centred * lax.rsqrt(variance + 1e-06) * gain[...]).astype(BF16)
 
 
 def embed(tubelets, weight, gain):
     tok, width = tubelets.shape[0], weight.shape[1]
-    shape = jax.ShapeDtypeStruct((tok, width), BF16)
+    parts = 6
+    shape = pltpu.VMEM((tok, width), BF16)
     return pl.pallas_call(
         embed_kernel,
         out_shape=[shape, shape],
-        in_specs=[vmem()] * 3,
+        in_specs=[hbm()] * 3,
         out_specs=[vmem()] * 2,
+        scratch_shapes=[pltpu.VMEM(tubelets.shape, BF16), pltpu.VMEM(weight.shape, BF16),
+                        pltpu.VMEM((1, width), F32), pltpu.SemaphoreType.DMA((parts + 2,))],
         compiler_params=pltpu.CompilerParams(vmem_limit_bytes=VMEM_LIMIT),
         cost_estimate=pl.CostEstimate(flops=2 * tok * weight.size, bytes_accessed=weight.size * 2, transcendentals=0),
         name="embed",
-    )(tubelets, weight, gain.reshape(1, width))
+    )(in_hbm(tubelets), in_hbm(weight), in_hbm(gain.reshape(1, width)))
 
 
 def route_kernel(n_exp, half, cap, place_ref, code_ref, sib_code_ref, select_ref, gate_ref):
@@ -244,7 +265,7 @@
     core_bit = 1 << CORE
     codes = jnp.concatenate([routes.T, gate_codes.T], axis=0)
     sib_codes = swapped(codes, "rep", core_bit)
-    embedded, normed = embed(tubelets, embed_weight, norm_gain)
+    embedded, normed = embed(after(tubelets, codes), embed_weight, norm_gain)
     sib_normed = swapped(normed, "rep", core_bit)
     select, gate = route(place, codes, sib_codes, n_exp, half, cap)
 
@@ -276,9 +297,9 @@
         return to_a, to_b
 
     per = half // CHUNKS
+    far0 = [swapped(pieces[s][0], "exp", s) for s in range(2, n_exp)]
     first = swapped(pieces[1][0], "exp", 1)
-    own0 = jnp.concatenate(
-        [pieces[0][0], first[:per]] + [swapped(pieces[s][0], "exp", s) for s in range(2, n_exp)], axis=1)
+    own0 = jnp.concatenate([pieces[0][0], first[:per]] + far0, axis=1)
     late = lax.optimization_barrier((own0, in_sib, *(pieces[s][1] for s in range(2, n_exp))))[2:]
     own1 = jnp.concatenate(
         [pieces[0][1], first[per:]] + [swapped(piece, "exp", s + 2) for s, piece in enumerate(late)], axis=1)

time: 100 us -> 97.9 us (0.979)
  local copies, waits for them, and re-layouts: 3.7 us -> 0.13 us
  Pallas kernels: 14.4 us -> 16.1 us
    unnamed x6 -> x0, local copies, waits for them, and re-layouts: 3.57 us -> none
    pallas_call x1, Pallas kernels: 0.8 us -> 2.51 us  [embed(): pl.pallas_call(embed_kernel, out_shape=[shape, shape], in_specs=[hbm()] *...]
  transfers between devices with their start and end apart: 32 -> 32, of which waited for: 16 -> 17; matrix products, arithmetic and copies ran while one was open for 2% -> 1% of each run, Pallas kernels for 13% -> 13%
where the time goes in v4:
time: 97.9 us; the launch traced here: 97.7 us
  waiting for transfers between devices  41.8 us (43%)
  starting transfers between devices  37.2 us (38%)
  Pallas kernels  16.1 us (16%)
  other arithmetic  2.27 us (2%)
    ppermute x32, waiting for transfers between devices, swapped(): lax.ppermute(array, axis, [(i, i ^ distance) for i in range(lax.axis_size...  41.8 us
    ppermute x32, starting transfers between devices, swapped(): lax.ppermute(array, axis, [(i, i ^ distance) for i in range(lax.axis_size...  37.2 us
    pallas_call x2, Pallas kernels, experts(): pl.pallas_call(functools.partial(experts_kernel, chunk, half), out_shape=...  11.8 us
    pallas_call x1, Pallas kernels, embed(): pl.pallas_call(embed_kernel, out_shape=[shape, shape], in_specs=[hbm()] *...  2.51 us
  transfers between devices with their start and end apart: 32, of which 17 were waited for; matrix products, arithmetic and copies ran while one was open for 1% of the time, Pallas kernels for 13%

profile of v4, /device:TPU:0, one launch (start us, length us, event | category | flops | bytes accessed | tf_op | source)
XLA Modules:
  0.0 97.7 jit_solution(9782060398078275430)
XLA Ops:
  0.7 2.5 %embed.1 = (bf16[128,1024]{1,0:T(8,128)(2,1)S(1)}, bf16[128,1024]{1,0:T(8,128)(2,1)S(1)}) custom-call(bf16[128,1536]{1,0:T(8,128)(2,1)} %tubelets_ref, bf16[1536,1024]{1,0:T(8,128)(2,1)} %weight_ref.1, f32[1,1024]{1,0:T(1,128)} %bitcast.41), custom_call_target="tpu_custom_call" | custom-call | flops 402653184 | bytes 3145728 | tf_op jit(solution)/shard_map/embed/pallas_call | solution.py:82
  6.8 3.0 %collective-permute-start.2 = (bf16[4,24,1024]{2,1,0:T(8,128)(2,1)S(1)}, bf16[4,24,1024]{2,1,0:T(8,128)(2,1)S(1)}, u32[]{:S(2)}, u32[]{:S(2)}) collective-permute-start(bf16[4,24,1024]{2,1,0:T(8,128)(2,1)S(1)} %get-tuple-element.58), channel_id=1, source_target_pairs={{0,1},{1,0},{2,3},{3,2},{4,5},{5,4},{6,7},{7,6},{8,9},{9,8},{10,11... | collective-permute-start | bytes 589832 | tf_op jit(solution)/shard_map/ppermute | solution.py:20
  9.8 2.6 %collective-permute-start.3 = (bf16[2,24,1024]{2,1,0:T(8,128)(2,1)S(1)}, bf16[2,24,1024]{2,1,0:T(8,128)(2,1)S(1)}, u32[]{:S(2)}, u32[]{:S(2)}) collective-permute-start(bf16[2,24,1024]{2,1,0:T(8,128)(2,1)S(1)} %get-tuple-element.60), channel_id=1, source_target_pairs={{0,2},{1,3},{2,0},{3,1},{4,6},{5,7},{6,4},{7,5},{8,10},{9,11},{10,... | collective-permute-start | bytes 294920 | tf_op jit(solution)/shard_map/ppermute | solution.py:20
  12.4 4.7 %collective-permute-done.2 = bf16[4,24,1024]{2,1,0:T(8,128)(2,1)S(1)} collective-permute-done((bf16[4,24,1024]{2,1,0:T(8,128)(2,1)S(1)}, bf16[4,24,1024]{2,1,0:T(8,128)(2,1)S(1)}, u32[]{:S(2)}, u32[]{:S(2)}) %collective-permute-start.2) | collective-permute-done | bytes 196640 | tf_op jit(solution)/shard_map/ppermute | solution.py:20
  17.2 4.3 %collective-permute-done.4 = bf16[2,24,1024]{2,1,0:T(8,128)(2,1)S(1)} collective-permute-done((bf16[2,24,1024]{2,1,0:T(8,128)(2,1)S(1)}, bf16[2,24,1024]{2,1,0:T(8,128)(2,1)S(1)}, u32[]{:S(2)}, u32[]{:S(2)}) %collective-permute-start.4) | collective-permute-done | bytes 98336 | tf_op jit(solution)/shard_map/ppermute | solution.py:20
  21.6 1.6 %collective-permute-start.9 = (bf16[2,96,1024]{2,1,0:T(8,128)(2,1)S(1)}, bf16[2,96,1024]{2,1,0:T(8,128)(2,1)S(1)}, u32[]{:S(2)}, u32[]{:S(2)}) collective-permute-start(bf16[2,96,1024]{2,1,0:T(8,128)(2,1)S(1)} %pad_maximum_fusion.own_ref), channel_id=1, source_target_pairs={{0,16},{4,20},{8,24},{12,28},{16,0},{20,4},{24,8},{28,12},{1,17},{... | collective-permute-start | bytes 1179656 | tf_op jit(solution)/shard_map/ppermute | solution.py:20
  23.1 1.5 %collective-permute-start.8 = (bf16[2,96,1024]{2,1,0:T(8,128)(2,1)S(1)}, bf16[2,96,1024]{2,1,0:T(8,128)(2,1)S(1)}, u32[]{:S(2)}, u32[]{:S(2)}) collective-permute-start(bf16[2,96,1024]{2,1,0:T(8,128)(2,1)S(1)} %pad_maximum_fusion.own_ref), channel_id=1, source_target_pairs={{0,8},{4,12},{8,0},{12,4},{16,24},{20,28},{24,16},{28,20},{1,9},{5... | collective-permute-start | bytes 1179656 | tf_op jit(solution)/shard_map/ppermute | solution.py:20
  24.6 1.7 %collective-permute-start.6 = (bf16[2,24,1024]{2,1,0:T(8,128)(2,1)S(1)}, bf16[2,24,1024]{2,1,0:T(8,128)(2,1)S(1)}, u32[]{:S(2)}, u32[]{:S(2)}) collective-permute-start(bf16[2,24,1024]{2,1,0:T(8,128)(2,1)S(1)} %get-tuple-element.65), channel_id=1, source_target_pairs={{0,2},{1,3},{2,0},{3,1},{4,6},{5,7},{6,4},{7,5},{8,10},{9,11},{10,... | collective-permute-start | bytes 294920 | tf_op jit(solution)/shard_map/ppermute | solution.py:20
  26.3 1.4 %collective-permute-start.7 = (bf16[2,24,1024]{2,1,0:T(8,128)(2,1)S(1)}, bf16[2,24,1024]{2,1,0:T(8,128)(2,1)S(1)}, u32[]{:S(2)}, u32[]{:S(2)}) collective-permute-start(bf16[2,24,1024]{2,1,0:T(8,128)(2,1)S(1)} %get-tuple-element.66), channel_id=1, source_target_pairs={{0,3},{1,2},{2,1},{3,0},{4,7},{5,6},{6,5},{7,4},{8,11},{9,10},{10,... | collective-permute-start | bytes 294920 | tf_op jit(solution)/shard_map/ppermute | solution.py:20
  27.7 4.2 %collective-permute-done.9.b_ref = bf16[2,96,1024]{2,1,0:T(8,128)(2,1)S(1)} collective-permute-done((bf16[2,96,1024]{2,1,0:T(8,128)(2,1)S(1)}, bf16[2,96,1024]{2,1,0:T(8,128)(2,1)S(1)}, u32[]{:S(2)}, u32[]{:S(2)}) %collective-permute-start.9) | collective-permute-done | bytes 393248 | tf_op jit(solution)/shard_map/ppermute | solution.py:20
  31.9 1.6 %collective-permute-start.13 = (bf16[1,96,1024]{2,1,0:T(8,128)(2,1)S(1)}, bf16[1,96,1024]{2,1,0:T(8,128)(2,1)S(1)}, u32[]{:S(2)}, u32[]{:S(2)}) collective-permute-start(bf16[1,96,1024]{2,1,0:T(8,128)(2,1)S(1)} %slice.91), channel_id=1, source_target_pairs={{0,8},{4,12},{8,0},{12,4},{16,24},{20,28},{24,16},{28,20},{1,9},{5... | collective-permute-start | bytes 589832 | tf_op jit(solution)/shard_map/ppermute | solution.py:20
  33.5 1.6 %collective-permute-start.12 = (bf16[1,96,1024]{2,1,0:T(8,128)(2,1)S(1)}, bf16[1,96,1024]{2,1,0:T(8,128)(2,1)S(1)}, u32[]{:S(2)}, u32[]{:S(2)}) collective-permute-start(bf16[1,96,1024]{2,1,0:T(8,128)(2,1)S(1)} %slice.90), channel_id=1, source_target_pairs={{0,16},{4,20},{8,24},{12,28},{16,0},{20,4},{24,8},{28,12},{1,17},{... | collective-permute-start | bytes 589832 | tf_op jit(solution)/shard_map/ppermute | solution.py:20
  35.7 1.3 %collective-permute-start.10 = (bf16[2,96,1024]{2,1,0:T(8,128)(2,1)S(1)}, bf16[2,96,1024]{2,1,0:T(8,128)(2,1)S(1)}, u32[]{:S(2)}, u32[]{:S(2)}) collective-permute-start(bf16[2,96,1024]{2,1,0:T(8,128)(2,1)S(1)} %pad_maximum_fusion.1.own_ref), channel_id=1, source_target_pairs={{0,8},{4,12},{8,0},{12,4},{16,24},{20,28},{24,16},{28,20},{1,9},{5... | collective-permute-start | bytes 1179656 | tf_op jit(solution)/shard_map/ppermute | solution.py:20
  37.0 2.5 %collective-permute-done.13.d2_ref = bf16[1,96,1024]{2,1,0:T(8,128)(2,1)S(1)} collective-permute-done((bf16[1,96,1024]{2,1,0:T(8,128)(2,1)S(1)}, bf16[1,96,1024]{2,1,0:T(8,128)(2,1)S(1)}, u32[]{:S(2)}, u32[]{:S(2)}) %collective-permute-start.13) | collective-permute-done | bytes 196640 | tf_op jit(solution)/shard_map/ppermute | solution.py:20
  39.5 1.9 %collective-permute-done.12.d1_ref = bf16[1,96,1024]{2,1,0:T(8,128)(2,1)S(1)} collective-permute-done((bf16[1,96,1024]{2,1,0:T(8,128)(2,1)S(1)}, bf16[1,96,1024]{2,1,0:T(8,128)(2,1)S(1)}, u32[]{:S(2)}, u32[]{:S(2)}) %collective-permute-start.12) | collective-permute-done | bytes 196640 | tf_op jit(solution)/shard_map/ppermute | solution.py:20
  41.4 5.9 %experts.2 = (bf16[2,96,1024]{2,1,0:T(8,128)(2,1)S(1)}, bf16[2,96,1024]{2,1,0:T(8,128)(2,1)S(1)}, bf16[2,96,1024]{2,1,0:T(8,128)(2,1)S(1)}, bf16[1,96,1024]{2,1,0:T(8,128)(2,1)S(1)}, bf16[1,96,1024]{2,1,0:T(8,128)(2,1)S(1)}) custom-call(s32[2]{0:T(128)S(1)} %pad_add_fusion.1.place_ref, bf16[2,96,1024]{2,1,0:T(8,128)(2,1)S(1)} %pad_maximum_fusion.own_ref, ...), custom_call_target="tpu_custom_call" | custom-call | flops 3221225472 | bytes 3145728 | tf_op jit(solution)/shard_map/experts/pallas_call | solution.py:213
  47.3 1.6 %collective-permute-start.15 = (bf16[1,96,1024]{2,1,0:T(8,128)(2,1)S(1)}, bf16[1,96,1024]{2,1,0:T(8,128)(2,1)S(1)}, u32[]{:S(2)}, u32[]{:S(2)}) collective-permute-start(bf16[1,96,1024]{2,1,0:T(8,128)(2,1)S(1)} %get-tuple-element.78), channel_id=1, source_target_pairs={{0,16},{4,20},{8,24},{12,28},{16,0},{20,4},{24,8},{28,12},{1,17},{... | collective-permute-start | bytes 589832 | tf_op jit(solution)/shard_map/ppermute | solution.py:20
  49.6 1.3 %collective-permute-start.17 = (bf16[1,96,1024]{2,1,0:T(8,128)(2,1)S(1)}, bf16[1,96,1024]{2,1,0:T(8,128)(2,1)S(1)}, u32[]{:S(2)}, u32[]{:S(2)}) collective-permute-start(bf16[1,96,1024]{2,1,0:T(8,128)(2,1)S(1)} %slice.74), channel_id=1, source_target_pairs={{0,16},{4,20},{8,24},{12,28},{16,0},{20,4},{24,8},{28,12},{1,17},{... | collective-permute-start | bytes 589832 | tf_op jit(solution)/shard_map/ppermute | solution.py:20
  51.6 1.7 %collective-permute-done.15 = bf16[1,96,1024]{2,1,0:T(8,128)(2,1)S(1)} collective-permute-done((bf16[1,96,1024]{2,1,0:T(8,128)(2,1)S(1)}, bf16[1,96,1024]{2,1,0:T(8,128)(2,1)S(1)}, u32[]{:S(2)}, u32[]{:S(2)}) %collective-permute-start.15) | collective-permute-done | bytes 196640 | tf_op jit(solution)/shard_map/ppermute | solution.py:20
  53.3 4.9 %collective-permute-done.16 = bf16[1,96,1024]{2,1,0:T(8,128)(2,1)S(1)} collective-permute-done((bf16[1,96,1024]{2,1,0:T(8,128)(2,1)S(1)}, bf16[1,96,1024]{2,1,0:T(8,128)(2,1)S(1)}, u32[]{:S(2)}, u32[]{:S(2)}) %collective-permute-start.16) | collective-permute-done | bytes 196640 | tf_op jit(solution)/shard_map/ppermute | solution.py:20
  59.1 1.6 %collective-permute-start.20 = (bf16[2,96,1024]{2,1,0:T(8,128)(2,1)S(1)}, bf16[2,96,1024]{2,1,0:T(8,128)(2,1)S(1)}, u32[]{:S(2)}, u32[]{:S(2)}) collective-permute-start(bf16[2,96,1024]{2,1,0:T(8,128)(2,1)S(1)} %get-tuple-element.89), channel_id=1, source_target_pairs={{0,16},{4,20},{8,24},{12,28},{16,0},{20,4},{24,8},{28,12},{1,17},{... | collective-permute-start | bytes 1179656 | tf_op jit(solution)/shard_map/ppermute | solution.py:20
  60.7 5.9 %experts.3 = (bf16[2,96,1024]{2,1,0:T(8,128)(2,1)S(1)}, bf16[2,96,1024]{2,1,0:T(8,128)(2,1)S(1)}, bf16[2,96,1024]{2,1,0:T(8,128)(2,1)S(1)}, bf16[1,96,1024]{2,1,0:T(8,128)(2,1)S(1)}, bf16[1,96,1024]{2,1,0:T(8,128)(2,1)S(1)}) custom-call(s32[2]{0:T(128)S(1)} %pad_add_fusion.1.place_ref, bf16[2,96,1024]{2,1,0:T(8,128)(2,1)S(1)} %pad_maximum_fusion.1.own_ref, ...), custom_call_target="tpu_custom_call" | custom-call | flops 3221225472 | bytes 3145728 | tf_op jit(solution)/shard_map/experts/pallas_call | solution.py:213
  66.7 1.6 %collective-permute-done.19 = bf16[2,96,1024]{2,1,0:T(8,128)(2,1)S(1)} collective-permute-done((bf16[2,96,1024]{2,1,0:T(8,128)(2,1)S(1)}, bf16[2,96,1024]{2,1,0:T(8,128)(2,1)S(1)}, u32[]{:S(2)}, u32[]{:S(2)}) %collective-permute-start.19) | collective-permute-done | bytes 393248 | tf_op jit(solution)/shard_map/ppermute | solution.py:20
  69.0 1.2 %collective-permute-start.23 = (bf16[1,96,1024]{2,1,0:T(8,128)(2,1)S(1)}, bf16[1,96,1024]{2,1,0:T(8,128)(2,1)S(1)}, u32[]{:S(2)}, u32[]{:S(2)}) collective-permute-start(bf16[1,96,1024]{2,1,0:T(8,128)(2,1)S(1)} %get-tuple-element.96), channel_id=1, source_target_pairs={{0,8},{4,12},{8,0},{12,4},{16,24},{20,28},{24,16},{28,20},{1,9},{5... | collective-permute-start | bytes 589832 | tf_op jit(solution)/shard_map/ppermute | solution.py:20
  70.8 6.1 %collective-permute-done.23 = bf16[1,96,1024]{2,1,0:T(8,128)(2,1)S(1)} collective-permute-done((bf16[1,96,1024]{2,1,0:T(8,128)(2,1)S(1)}, bf16[1,96,1024]{2,1,0:T(8,128)(2,1)S(1)}, u32[]{:S(2)}, u32[]{:S(2)}) %collective-permute-start.23) | collective-permute-done | bytes 196640 | tf_op jit(solution)/shard_map/ppermute | solution.py:20
  77.0 1.7 %collective-permute-start.24 = (bf16[2,96,1024]{2,1,0:T(8,128)(2,1)S(1)}, bf16[2,96,1024]{2,1,0:T(8,128)(2,1)S(1)}, u32[]{:S(2)}, u32[]{:S(2)}) collective-permute-start(bf16[2,96,1024]{2,1,0:T(8,128)(2,1)S(1)} %pad_maximum_fusion.5), channel_id=1, source_target_pairs={{0,16},{4,20},{8,24},{12,28},{16,0},{20,4},{24,8},{28,12},{1,17},{... | collective-permute-start | bytes 1179656 | tf_op jit(solution)/shard_map/ppermute | solution.py:20
  80.0 3.6 %collective-permute-start.25 = (bf16[2,24,1024]{2,1,0:T(8,128)(2,1)S(1)}, bf16[2,24,1024]{2,1,0:T(8,128)(2,1)S(1)}, u32[]{:S(2)}, u32[]{:S(2)}) collective-permute-start(bf16[2,24,1024]{2,1,0:T(8,128)(2,1)S(1)} %get-tuple-element.105), channel_id=1, source_target_pairs={{0,1},{1,0},{2,3},{3,2},{4,5},{5,4},{6,7},{7,6},{8,9},{9,8},{10,11... | collective-permute-start | bytes 294920 | tf_op jit(solution)/shard_map/ppermute | solution.py:20
  84.8 1.7 %collective-permute-done.22 = bf16[2,96,1024]{2,1,0:T(8,128)(2,1)S(1)} collective-permute-done((bf16[2,96,1024]{2,1,0:T(8,128)(2,1)S(1)}, bf16[2,96,1024]{2,1,0:T(8,128)(2,1)S(1)}, u32[]{:S(2)}, u32[]{:S(2)}) %collective-permute-start.22) | collective-permute-done | bytes 393248 | tf_op jit(solution)/shard_map/ppermute | solution.py:20
  87.3 4.0 %collective-permute-start.26 = (bf16[2,24,1024]{2,1,0:T(8,128)(2,1)S(1)}, bf16[2,24,1024]{2,1,0:T(8,128)(2,1)S(1)}, u32[]{:S(2)}, u32[]{:S(2)}) collective-permute-start(bf16[2,24,1024]{2,1,0:T(8,128)(2,1)S(1)} %get-tuple-element.101), channel_id=1, source_target_pairs={{0,1},{1,0},{2,3},{3,2},{4,5},{5,4},{6,7},{7,6},{8,9},{9,8},{10,11... | collective-permute-start | bytes 294920 | tf_op jit(solution)/shard_map/ppermute | solution.py:20
  91.2 2.2 %collective-permute-done.30.refs_7_ = bf16[2,24,1024]{2,1,0:T(8,128)(2,1)S(1)} collective-permute-done((bf16[2,24,1024]{2,1,0:T(8,128)(2,1)S(1)}, bf16[2,24,1024]{2,1,0:T(8,128)(2,1)S(1)}, u32[]{:S(2)}, u32[]{:S(2)}) %collective-permute-start.30) | collective-permute-done | bytes 98336 | tf_op jit(solution)/shard_map/ppermute | solution.py:20
  93.4 1.5 %collective-permute-done.28.refs_5_ = bf16[2,24,1024]{2,1,0:T(8,128)(2,1)S(1)} collective-permute-done((bf16[2,24,1024]{2,1,0:T(8,128)(2,1)S(1)}, bf16[2,24,1024]{2,1,0:T(8,128)(2,1)S(1)}, u32[]{:S(2)}, u32[]{:S(2)}) %collective-permute-start.28) | collective-permute-done | bytes 98336 | tf_op jit(solution)/shard_map/ppermute | solution.py:20
  95.4 1.5 %collective-permute-done.31 = bf16[128,1024]{1,0:T(8,128)(2,1)S(1)} collective-permute-done((bf16[128,1024]{1,0:T(8,128)(2,1)S(1)}, bf16[128,1024]{1,0:T(8,128)(2,1)S(1)}, u32[]{:S(2)}, u32[]{:S(2)}) %collective-permute-start.31) | collective-permute-done | bytes 262176 | tf_op jit(solution)/shard_map/ppermute | solution.py:20
  (59 shorter events, 13.5 us)
Async XLA Ops:
  3.2 2.6 %collective-permute-start.1 = (bf16[128,1024]{1,0:T(8,128)(2,1)S(1)}, bf16[128,1024]{1,0:T(8,128)(2,1)S(1)}, u32[]{:S(2)}, u32[]{:S(2)}) collective-permute-start(bf16[128,1024]{1,0:T(8,128)(2,1)S(1)} %get-tuple-element.56.normed_ref), channel_id=1, source_target_pairs={{0,4},{4,0},{8,12},{12,8},{16,20},{20,16},{24,28},{28,24},{1,5},{5... | collective-permute-start | bytes 786440 | tf_op jit(solution)/shard_map/ppermute | solution.py:20
  3.7 1.2 %collective-permute-start = (s32[4,128]{1,0:T(4,128)S(1)}, s32[4,128]{1,0:T(4,128)S(1)}, u32[]{:S(2)}, u32[]{:S(2)}) collective-permute-start(s32[4,128]{1,0:T(4,128)S(1)} %pad_add_fusion.code_ref), channel_id=1, source_target_pairs={{0,4},{4,0},{8,12},{12,8},{16,20},{20,16},{24,28},{28,24},{1,5},{5... | collective-permute-start | bytes 6152 | tf_op jit(solution)/shard_map/ppermute | solution.py:20
  5.9 18.8 %collective-permute-start.5 = (bf16[8,1024,512]{2,1,0:T(8,128)(2,1)}, bf16[8,1024,512]{2,1,0:T(8,128)(2,1)S(1)}, u32[]{:S(2)}, u32[]{:S(2)}) collective-permute-start(bf16[8,1024,512]{2,1,0:T(8,128)(2,1)} %in_ref.3), channel_id=1, source_target_pairs={{0,4},{4,0},{8,12},{12,8},{16,20},{20,16},{24,28},{28,24},{1,5},{5... | collective-permute-start | bytes 25165832 | tf_op jit(solution)/shard_map/ppermute | solution.py:20
  6.3 35.1 %collective-permute-start.14 = (bf16[8,1024,512]{2,1,0:T(8,128)(2,1)}, bf16[8,1024,512]{2,1,0:T(8,128)(2,1)S(1)}, u32[]{:S(2)}, u32[]{:S(2)}) collective-permute-start(bf16[8,1024,512]{2,1,0:T(8,128)(2,1)} %down_ref.3), channel_id=1, source_target_pairs={{0,4},{4,0},{8,12},{12,8},{16,20},{20,16},{24,28},{28,24},{1,5},{5... | collective-permute-start | bytes 25165832 | tf_op jit(solution)/shard_map/ppermute | solution.py:20
  6.8 10.3 %collective-permute-start.2 = (bf16[4,24,1024]{2,1,0:T(8,128)(2,1)S(1)}, bf16[4,24,1024]{2,1,0:T(8,128)(2,1)S(1)}, u32[]{:S(2)}, u32[]{:S(2)}) collective-permute-start(bf16[4,24,1024]{2,1,0:T(8,128)(2,1)S(1)} %get-tuple-element.58), channel_id=1, source_target_pairs={{0,1},{1,0},{2,3},{3,2},{4,5},{5,4},{6,7},{7,6},{8,9},{9,8},{10,11... | collective-permute-start | bytes 589832 | tf_op jit(solution)/shard_map/ppermute | solution.py:20
  9.8 7.4 %collective-permute-start.3 = (bf16[2,24,1024]{2,1,0:T(8,128)(2,1)S(1)}, bf16[2,24,1024]{2,1,0:T(8,128)(2,1)S(1)}, u32[]{:S(2)}, u32[]{:S(2)}) collective-permute-start(bf16[2,24,1024]{2,1,0:T(8,128)(2,1)S(1)} %get-tuple-element.60), channel_id=1, source_target_pairs={{0,2},{1,3},{2,0},{3,1},{4,6},{5,7},{6,4},{7,5},{8,10},{9,11},{10,... | collective-permute-start | bytes 294920 | tf_op jit(solution)/shard_map/ppermute | solution.py:20
  12.4 9.1 %collective-permute-start.4 = (bf16[2,24,1024]{2,1,0:T(8,128)(2,1)S(1)}, bf16[2,24,1024]{2,1,0:T(8,128)(2,1)S(1)}, u32[]{:S(2)}, u32[]{:S(2)}) collective-permute-start(bf16[2,24,1024]{2,1,0:T(8,128)(2,1)S(1)} %get-tuple-element.61), channel_id=1, source_target_pairs={{0,3},{1,2},{2,1},{3,0},{4,7},{5,6},{6,5},{7,4},{8,11},{9,10},{10,... | collective-permute-start | bytes 294920 | tf_op jit(solution)/shard_map/ppermute | solution.py:20
  21.6 10.3 %collective-permute-start.9 = (bf16[2,96,1024]{2,1,0:T(8,128)(2,1)S(1)}, bf16[2,96,1024]{2,1,0:T(8,128)(2,1)S(1)}, u32[]{:S(2)}, u32[]{:S(2)}) collective-permute-start(bf16[2,96,1024]{2,1,0:T(8,128)(2,1)S(1)} %pad_maximum_fusion.own_ref), channel_id=1, source_target_pairs={{0,16},{4,20},{8,24},{12,28},{16,0},{20,4},{24,8},{28,12},{1,17},{... | collective-permute-start | bytes 1179656 | tf_op jit(solution)/shard_map/ppermute | solution.py:20
  23.1 10.3 %collective-permute-start.8 = (bf16[2,96,1024]{2,1,0:T(8,128)(2,1)S(1)}, bf16[2,96,1024]{2,1,0:T(8,128)(2,1)S(1)}, u32[]{:S(2)}, u32[]{:S(2)}) collective-permute-start(bf16[2,96,1024]{2,1,0:T(8,128)(2,1)S(1)} %pad_maximum_fusion.own_ref), channel_id=1, source_target_pairs={{0,8},{4,12},{8,0},{12,4},{16,24},{20,28},{24,16},{28,20},{1,9},{5... | collective-permute-start | bytes 1179656 | tf_op jit(solution)/shard_map/ppermute | solution.py:20
  24.6 10.4 %collective-permute-start.6 = (bf16[2,24,1024]{2,1,0:T(8,128)(2,1)S(1)}, bf16[2,24,1024]{2,1,0:T(8,128)(2,1)S(1)}, u32[]{:S(2)}, u32[]{:S(2)}) collective-permute-start(bf16[2,24,1024]{2,1,0:T(8,128)(2,1)S(1)} %get-tuple-element.65), channel_id=1, source_target_pairs={{0,2},{1,3},{2,0},{3,1},{4,6},{5,7},{6,4},{7,5},{8,10},{9,11},{10,... | collective-permute-start | bytes 294920 | tf_op jit(solution)/shard_map/ppermute | solution.py:20
  26.3 8.8 %collective-permute-start.7 = (bf16[2,24,1024]{2,1,0:T(8,128)(2,1)S(1)}, bf16[2,24,1024]{2,1,0:T(8,128)(2,1)S(1)}, u32[]{:S(2)}, u32[]{:S(2)}) collective-permute-start(bf16[2,24,1024]{2,1,0:T(8,128)(2,1)S(1)} %get-tuple-element.66), channel_id=1, source_target_pairs={{0,3},{1,2},{2,1},{3,0},{4,7},{5,6},{6,5},{7,4},{8,11},{9,10},{10,... | collective-permute-start | bytes 294920 | tf_op jit(solution)/shard_map/ppermute | solution.py:20
  31.9 7.6 %collective-permute-start.13 = (bf16[1,96,1024]{2,1,0:T(8,128)(2,1)S(1)}, bf16[1,96,1024]{2,1,0:T(8,128)(2,1)S(1)}, u32[]{:S(2)}, u32[]{:S(2)}) collective-permute-start(bf16[1,96,1024]{2,1,0:T(8,128)(2,1)S(1)} %slice.91), channel_id=1, source_target_pairs={{0,8},{4,12},{8,0},{12,4},{16,24},{20,28},{24,16},{28,20},{1,9},{5... | collective-permute-start | bytes 589832 | tf_op jit(solution)/shard_map/ppermute | solution.py:20
  33.5 7.9 %collective-permute-start.12 = (bf16[1,96,1024]{2,1,0:T(8,128)(2,1)S(1)}, bf16[1,96,1024]{2,1,0:T(8,128)(2,1)S(1)}, u32[]{:S(2)}, u32[]{:S(2)}) collective-permute-start(bf16[1,96,1024]{2,1,0:T(8,128)(2,1)S(1)} %slice.90), channel_id=1, source_target_pairs={{0,16},{4,20},{8,24},{12,28},{16,0},{20,4},{24,8},{28,12},{1,17},{... | collective-permute-start | bytes 589832 | tf_op jit(solution)/shard_map/ppermute | solution.py:20
  35.1 12.2 %collective-permute-start.11 = (bf16[2,96,1024]{2,1,0:T(8,128)(2,1)S(1)}, bf16[2,96,1024]{2,1,0:T(8,128)(2,1)S(1)}, u32[]{:S(2)}, u32[]{:S(2)}) collective-permute-start(bf16[2,96,1024]{2,1,0:T(8,128)(2,1)S(1)} %pad_maximum_fusion.1.own_ref), channel_id=1, source_target_pairs={{0,16},{4,20},{8,24},{12,28},{16,0},{20,4},{24,8},{28,12},{1,17},{... | collective-permute-start | bytes 1179656 | tf_op jit(solution)/shard_map/ppermute | solution.py:20
  35.7 11.6 %collective-permute-start.10 = (bf16[2,96,1024]{2,1,0:T(8,128)(2,1)S(1)}, bf16[2,96,1024]{2,1,0:T(8,128)(2,1)S(1)}, u32[]{:S(2)}, u32[]{:S(2)}) collective-permute-start(bf16[2,96,1024]{2,1,0:T(8,128)(2,1)S(1)} %pad_maximum_fusion.1.own_ref), channel_id=1, source_target_pairs={{0,8},{4,12},{8,0},{12,4},{16,24},{20,28},{24,16},{28,20},{1,9},{5... | collective-permute-start | bytes 1179656 | tf_op jit(solution)/shard_map/ppermute | solution.py:20
  47.3 5.9 %collective-permute-start.15 = (bf16[1,96,1024]{2,1,0:T(8,128)(2,1)S(1)}, bf16[1,96,1024]{2,1,0:T(8,128)(2,1)S(1)}, u32[]{:S(2)}, u32[]{:S(2)}) collective-permute-start(bf16[1,96,1024]{2,1,0:T(8,128)(2,1)S(1)} %get-tuple-element.78), channel_id=1, source_target_pairs={{0,16},{4,20},{8,24},{12,28},{16,0},{20,4},{24,8},{28,12},{1,17},{... | collective-permute-start | bytes 589832 | tf_op jit(solution)/shard_map/ppermute | solution.py:20
  48.9 9.3 %collective-permute-start.18 = (bf16[1,96,1024]{2,1,0:T(8,128)(2,1)S(1)}, bf16[1,96,1024]{2,1,0:T(8,128)(2,1)S(1)}, u32[]{:S(2)}, u32[]{:S(2)}) collective-permute-start(bf16[1,96,1024]{2,1,0:T(8,128)(2,1)S(1)} %slice.75), channel_id=1, source_target_pairs={{0,8},{4,12},{8,0},{12,4},{16,24},{20,28},{24,16},{28,20},{1,9},{5... | collective-permute-start | bytes 589832 | tf_op jit(solution)/shard_map/ppermute | solution.py:20
  49.6 8.7 %collective-permute-start.17 = (bf16[1,96,1024]{2,1,0:T(8,128)(2,1)S(1)}, bf16[1,96,1024]{2,1,0:T(8,128)(2,1)S(1)}, u32[]{:S(2)}, u32[]{:S(2)}) collective-permute-start(bf16[1,96,1024]{2,1,0:T(8,128)(2,1)S(1)} %slice.74), channel_id=1, source_target_pairs={{0,16},{4,20},{8,24},{12,28},{16,0},{20,4},{24,8},{28,12},{1,17},{... | collective-permute-start | bytes 589832 | tf_op jit(solution)/shard_map/ppermute | solution.py:20
  50.8 7.3 %collective-permute-start.16 = (bf16[1,96,1024]{2,1,0:T(8,128)(2,1)S(1)}, bf16[1,96,1024]{2,1,0:T(8,128)(2,1)S(1)}, u32[]{:S(2)}, u32[]{:S(2)}) collective-permute-start(bf16[1,96,1024]{2,1,0:T(8,128)(2,1)S(1)} %get-tuple-element.80), channel_id=1, source_target_pairs={{0,8},{4,12},{8,0},{12,4},{16,24},{20,28},{24,16},{28,20},{1,9},{5... | collective-permute-start | bytes 589832 | tf_op jit(solution)/shard_map/ppermute | solution.py:20
  58.3 9.9 %collective-permute-start.19 = (bf16[2,96,1024]{2,1,0:T(8,128)(2,1)S(1)}, bf16[2,96,1024]{2,1,0:T(8,128)(2,1)S(1)}, u32[]{:S(2)}, u32[]{:S(2)}) collective-permute-start(bf16[2,96,1024]{2,1,0:T(8,128)(2,1)S(1)} %get-tuple-element.88), channel_id=1, source_target_pairs={{0,8},{4,12},{8,0},{12,4},{16,24},{20,28},{24,16},{28,20},{1,9},{5... | collective-permute-start | bytes 1179656 | tf_op jit(solution)/shard_map/ppermute | solution.py:20
  59.1 9.9 %collective-permute-start.20 = (bf16[2,96,1024]{2,1,0:T(8,128)(2,1)S(1)}, bf16[2,96,1024]{2,1,0:T(8,128)(2,1)S(1)}, u32[]{:S(2)}, u32[]{:S(2)}) collective-permute-start(bf16[2,96,1024]{2,1,0:T(8,128)(2,1)S(1)} %get-tuple-element.89), channel_id=1, source_target_pairs={{0,16},{4,20},{8,24},{12,28},{16,0},{20,4},{24,8},{28,12},{1,17},{... | collective-permute-start | bytes 1179656 | tf_op jit(solution)/shard_map/ppermute | solution.py:20
  69.0 7.8 %collective-permute-start.23 = (bf16[1,96,1024]{2,1,0:T(8,128)(2,1)S(1)}, bf16[1,96,1024]{2,1,0:T(8,128)(2,1)S(1)}, u32[]{:S(2)}, u32[]{:S(2)}) collective-permute-start(bf16[1,96,1024]{2,1,0:T(8,128)(2,1)S(1)} %get-tuple-element.96), channel_id=1, source_target_pairs={{0,8},{4,12},{8,0},{12,4},{16,24},{20,28},{24,16},{28,20},{1,9},{5... | collective-permute-start | bytes 589832 | tf_op jit(solution)/shard_map/ppermute | solution.py:20
  70.2 8.4 %collective-permute-start.21 = (bf16[1,96,1024]{2,1,0:T(8,128)(2,1)S(1)}, bf16[1,96,1024]{2,1,0:T(8,128)(2,1)S(1)}, u32[]{:S(2)}, u32[]{:S(2)}) collective-permute-start(bf16[1,96,1024]{2,1,0:T(8,128)(2,1)S(1)} %get-tuple-element.94), channel_id=1, source_target_pairs={{0,16},{4,20},{8,24},{12,28},{16,0},{20,4},{24,8},{28,12},{1,17},{... | collective-permute-start | bytes 589832 | tf_op jit(solution)/shard_map/ppermute | solution.py:20
  77.0 7.8 %collective-permute-start.24 = (bf16[2,96,1024]{2,1,0:T(8,128)(2,1)S(1)}, bf16[2,96,1024]{2,1,0:T(8,128)(2,1)S(1)}, u32[]{:S(2)}, u32[]{:S(2)}) collective-permute-start(bf16[2,96,1024]{2,1,0:T(8,128)(2,1)S(1)} %pad_maximum_fusion.5), channel_id=1, source_target_pairs={{0,16},{4,20},{8,24},{12,28},{16,0},{20,4},{24,8},{28,12},{1,17},{... | collective-permute-start | bytes 1179656 | tf_op jit(solution)/shard_map/ppermute | solution.py:20
  78.7 7.8 %collective-permute-start.22 = (bf16[2,96,1024]{2,1,0:T(8,128)(2,1)S(1)}, bf16[2,96,1024]{2,1,0:T(8,128)(2,1)S(1)}, u32[]{:S(2)}, u32[]{:S(2)}) collective-permute-start(bf16[2,96,1024]{2,1,0:T(8,128)(2,1)S(1)} %pad_maximum_fusion.4), channel_id=1, source_target_pairs={{0,8},{4,12},{8,0},{12,4},{16,24},{20,28},{24,16},{28,20},{1,9},{5... | collective-permute-start | bytes 1179656 | tf_op jit(solution)/shard_map/ppermute | solution.py:20
  79.2 8.1 %collective-permute-start.29 = (bf16[2,24,1024]{2,1,0:T(8,128)(2,1)S(1)}, bf16[2,24,1024]{2,1,0:T(8,128)(2,1)S(1)}, u32[]{:S(2)}, u32[]{:S(2)}) collective-permute-start(bf16[2,24,1024]{2,1,0:T(8,128)(2,1)S(1)} %get-tuple-element.103), channel_id=1, source_target_pairs={{0,3},{1,2},{2,1},{3,0},{4,7},{5,6},{6,5},{7,4},{8,11},{9,10},{10,... | collective-permute-start | bytes 294920 | tf_op jit(solution)/shard_map/ppermute | solution.py:20
  79.9 11.3 %collective-permute-start.27 = (bf16[2,24,1024]{2,1,0:T(8,128)(2,1)S(1)}, bf16[2,24,1024]{2,1,0:T(8,128)(2,1)S(1)}, u32[]{:S(2)}, u32[]{:S(2)}) collective-permute-start(bf16[2,24,1024]{2,1,0:T(8,128)(2,1)S(1)} %get-tuple-element.104), channel_id=1, source_target_pairs={{0,2},{1,3},{2,0},{3,1},{4,6},{5,7},{6,4},{7,5},{8,10},{9,11},{10,... | collective-permute-start | bytes 294920 | tf_op jit(solution)/shard_map/ppermute | solution.py:20
  80.0 11.2 %collective-permute-start.25 = (bf16[2,24,1024]{2,1,0:T(8,128)(2,1)S(1)}, bf16[2,24,1024]{2,1,0:T(8,128)(2,1)S(1)}, u32[]{:S(2)}, u32[]{:S(2)}) collective-permute-start(bf16[2,24,1024]{2,1,0:T(8,128)(2,1)S(1)} %get-tuple-element.105), channel_id=1, source_target_pairs={{0,1},{1,0},{2,3},{3,2},{4,5},{5,4},{6,7},{7,6},{8,9},{9,8},{10,11... | collective-permute-start | bytes 294920 | tf_op jit(solution)/shard_map/ppermute | solution.py:20
  86.8 6.6 %collective-permute-start.30 = (bf16[2,24,1024]{2,1,0:T(8,128)(2,1)S(1)}, bf16[2,24,1024]{2,1,0:T(8,128)(2,1)S(1)}, u32[]{:S(2)}, u32[]{:S(2)}) collective-permute-start(bf16[2,24,1024]{2,1,0:T(8,128)(2,1)S(1)} %get-tuple-element.99), channel_id=1, source_target_pairs={{0,3},{1,2},{2,1},{3,0},{4,7},{5,6},{6,5},{7,4},{8,11},{9,10},{10,... | collective-permute-start | bytes 294920 | tf_op jit(solution)/shard_map/ppermute | solution.py:20
  87.3 7.6 %collective-permute-start.28 = (bf16[2,24,1024]{2,1,0:T(8,128)(2,1)S(1)}, bf16[2,24,1024]{2,1,0:T(8,128)(2,1)S(1)}, u32[]{:S(2)}, u32[]{:S(2)}) collective-permute-start(bf16[2,24,1024]{2,1,0:T(8,128)(2,1)S(1)} %get-tuple-element.100), channel_id=1, source_target_pairs={{0,2},{1,3},{2,0},{3,1},{4,6},{5,7},{6,4},{7,5},{8,10},{9,11},{10,... | collective-permute-start | bytes 294920 | tf_op jit(solution)/shard_map/ppermute | solution.py:20
  87.3 7.6 %collective-permute-start.26 = (bf16[2,24,1024]{2,1,0:T(8,128)(2,1)S(1)}, bf16[2,24,1024]{2,1,0:T(8,128)(2,1)S(1)}, u32[]{:S(2)}, u32[]{:S(2)}) collective-permute-start(bf16[2,24,1024]{2,1,0:T(8,128)(2,1)S(1)} %get-tuple-element.101), channel_id=1, source_target_pairs={{0,1},{1,0},{2,3},{3,2},{4,5},{5,4},{6,7},{7,6},{8,9},{9,8},{10,11... | collective-permute-start | bytes 294920 | tf_op jit(solution)/shard_map/ppermute | solution.py:20
  95.3 1.6 %collective-permute-start.31 = (bf16[128,1024]{1,0:T(8,128)(2,1)S(1)}, bf16[128,1024]{1,0:T(8,128)(2,1)S(1)}, u32[]{:S(2)}, u32[]{:S(2)}) collective-permute-start(bf16[128,1024]{1,0:T(8,128)(2,1)S(1)} %get-tuple-element.98), channel_id=1, source_target_pairs={{0,4},{4,0},{8,12},{12,8},{16,20},{20,16},{24,28},{28,24},{1,5},{5... | collective-permute-start | bytes 786440 | tf_op jit(solution)/shard_map/ppermute | solution.py:20

commit v5 on v4

--- a/solution.py
+++ b/solution.py
@@ -166,64 +166,68 @@
     return [[pieces.pop(0)] if s == 1 else [pieces.pop(0) for _ in range(CHUNKS)] for s in range(n_exp)]
 
 
+def hold_kernel(place_ref, in_ref, down_ref, in_out, down_out, sems):
+    count = in_out.shape[0]
+    copies = []
+    for e in range(count):
+        index = place_ref[1] * count + e
+        for which, (source, target) in enumerate(((in_ref, in_out), (down_ref, down_out))):
+            copies.append(pltpu.make_async_copy(source.at[index], target.at[e], sems.at[which, e]))
+            copies[-1].start()
+    for copy in copies:
+        copy.wait()
+
+
+def hold(place, w_in, w_down):
+    shape = pltpu.VMEM((w_in.shape[0] // 2, *w_in.shape[1:]), BF16)
+    return pl.pallas_call(
+        hold_kernel,
+        out_shape=[shape, shape],
+        in_specs=[smem(), hbm(), hbm()],
+        out_specs=[vmem()] * 2,
+        scratch_shapes=[pltpu.SemaphoreType.DMA((2, w_in.shape[0] // 2))],
+        compiler_params=pltpu.CompilerParams(vmem_limit_bytes=VMEM_LIMIT),
+        cost_estimate=pl.CostEstimate(flops=0, bytes_accessed=w_in.size * 4, transcendentals=0),
+        name="hold",
+    )(place, in_hbm(w_in), in_hbm(w_down))
+
+
 def experts_kernel(chunk, half, place_ref, own_ref, a_ref, b_ref, d1_ref, d2_ref,
-                   in_sib_ref, down_sib_ref, in_ref, down_ref,
-                   p_own_ref, p_a_ref, p_b_ref, p_d1_ref, p_d2_ref, x_ref, h_ref, acc_ref, bufs, sems):
+                   in_own_ref, in_sib_ref, down_own_ref, down_sib_ref,
+                   p_own_ref, p_a_ref, p_b_ref, p_d1_ref, p_d2_ref, h_ref):
     per, m, _ = own_ref.shape
     split = per // 2
-    base = place_ref[1] * half + chunk * per
-    width = in_ref.shape[1]
-    parts = sems.shape[2]
-    depth = width // parts
-    copies = {}
     for e in range(per):
-        for which, ref in enumerate((in_ref, down_ref)):
-            for part in range(parts):
-                rows = pl.ds(part * depth, depth)
-                copy = pltpu.make_async_copy(ref.at[base + e, rows], bufs.at[which, e, rows], sems.at[which, e, part])
-                copy.start()
-                copies[which, e, part] = copy
-
-    def ready(which, e):
-        for part in range(parts):
-            copies[which, e, part].wait()
-
-    for e in range(per):
-        diagonal = d1_ref if e < split else d2_ref
-        x_ref[e] = jnp.concatenate([own_ref[e], a_ref[e], b_ref[e], diagonal[e % split]], axis=0)
-        h_ref[...] = jax.nn.gelu(mm(x_ref[e], in_sib_ref[base + e])).astype(BF16)
-        acc_ref[e] = mm(h_ref[...], down_sib_ref[base + e], ((1,), (1,)))
-    for e in range(per):
-        p_diagonal = p_d1_ref if e < split else p_d2_ref
-        ready(0, e)
-        h_ref[...] = jax.nn.gelu(mm(x_ref[e], bufs[0, e])).astype(BF16)
-        ready(1, e)
-        total = acc_ref[e] + mm(h_ref[...], bufs[1, e], ((1,), (1,)))
+        mine = chunk * per + e
+        index = place_ref[1] * half + mine
+        diagonal, p_diagonal = (d1_ref, p_d1_ref) if e < split else (d2_ref, p_d2_ref)
+        x = jnp.concatenate([own_ref[e], a_ref[e], b_ref[e], diagonal[e % split]], axis=0)
+        h_ref[0] = jax.nn.gelu(mm(x, in_own_ref[mine])).astype(BF16)
+        h_ref[1] = jax.nn.gelu(mm(x, in_sib_ref[index])).astype(BF16)
+        total = mm(h_ref[0], down_own_ref[mine], ((1,), (1,))) + mm(h_ref[1], down_sib_ref[index], ((1,), (1,)))
         p_own_ref[e] = total[0:m].astype(BF16)
         p_a_ref[e] = total[m:2 * m].astype(BF16)
         p_b_ref[e] = total[2 * m:3 * m].astype(BF16)
         p_diagonal[e % split] = total[3 * m:4 * m].astype(BF16)
 
 
-def experts(place, chunk, own, near_a, near_b, d1, d2, in_sib, down_sib, w_in, w_down):
+def experts(place, chunk, own, near_a, near_b, d1, d2, in_own, in_sib, down_own, down_sib):
     per, m, width = own.shape
-    half, ff = in_sib.shape[0] // 2, in_sib.shape[2]
+    half, _, ff = in_own.shape
     shape = pltpu.VMEM(own.shape, BF16)
     part = pltpu.VMEM(d1.shape, BF16)
     return pl.pallas_call(
         functools.partial(experts_kernel, chunk, half),
         out_shape=[shape, shape, shape, part, part],
-        in_specs=[smem()] + [vmem()] * 7 + [hbm()] * 2,
+        in_specs=[smem()] + [vmem()] * 9,
         out_specs=[vmem()] * 5,
-        scratch_shapes=[
-            pltpu.VMEM((per, 4 * m, width), BF16), pltpu.VMEM((4 * m, ff), BF16), pltpu.VMEM((per, 4 * m, width), F32),
-            pltpu.VMEM((2, per, width, ff), BF16), pltpu.SemaphoreType.DMA((2, per, 4))],
+        scratch_shapes=[pltpu.VMEM((2, 4 * m, ff), BF16)],
         compiler_params=pltpu.CompilerParams(vmem_limit_bytes=VMEM_LIMIT),
         cost_estimate=pl.CostEstimate(
             flops=2 * per * 4 * m * width * 2 * ff * 2, bytes_accessed=per * m * width * 16,
             transcendentals=per * 4 * m * 2 * ff),
         name="experts",
-    )(place, own, near_a, near_b, d1, d2, in_vmem(in_sib), in_vmem(down_sib), in_hbm(w_in), in_hbm(w_down))
+    )(place, own, near_a, near_b, d1, d2, *(in_vmem(panel) for panel in (in_own, in_sib, down_own, down_sib)))
 
 
 def combine_kernel(tok, gate_ref, emb_ref, *refs):
@@ -299,7 +303,8 @@
     per = half // CHUNKS
     far0 = [swapped(pieces[s][0], "exp", s) for s in range(2, n_exp)]
     first = swapped(pieces[1][0], "exp", 1)
-    own0 = jnp.concatenate([pieces[0][0], first[:per]] + far0, axis=1)
+    in_own, down_own = hold(after(place, first), w_in, w_down)
+    own0 = after(jnp.concatenate([pieces[0][0], first[:per]] + far0, axis=1), in_own)
     late = lax.optimization_barrier((own0, in_sib, *(pieces[s][1] for s in range(2, n_exp))))[2:]
     own1 = jnp.concatenate(
         [pieces[0][1], first[per:]] + [swapped(piece, "exp", s + 2) for s, piece in enumerate(late)], axis=1)
@@ -307,15 +312,15 @@
     own1 = after(own1, a0, b0)
     d0 = swapped(a0[:split], "rep", b_bit), swapped(b0[split:], "rep", a_bit)
     a1, b1 = swapped(own1, "rep", a_bit), swapped(own1, "rep", b_bit)
-    parts0 = experts(place, 0, own0, a0, b0, *d0, in_sib, down_sib, w_in, w_down)
+    parts0 = experts(place, 0, own0, a0, b0, *d0, in_own, in_sib, down_own, down_sib)
     a1, b1, *parts0 = lax.optimization_barrier((a1, b1, *parts0))
-    d1 = swapped(a1[:split], "rep", b_bit), swapped(b1[split:], "rep", a_bit)
     r0 = swapped(parts0[3], "rep", a_bit), swapped(parts0[4], "rep", b_bit)
+    d1 = swapped(after(a1[:split], r0[0]), "rep", b_bit), swapped(b1[split:], "rep", a_bit)
     to_a0, to_b0 = reduced(parts0, r0)
-    to_a0, to_b0, *d1 = lax.optimization_barrier((to_a0, to_b0, *d1))
+    d1 = lax.optimization_barrier((*d1, to_a0, to_b0))[:2]
     from_a0, from_b0 = swapped(to_a0, "rep", a_bit), swapped(to_b0, "rep", b_bit)
-    parts1 = experts(place, 1, own1, a1, b1, *d1, in_sib, down_sib, w_in, w_down)
-    *parts1, from_a0, from_b0 = lax.optimization_barrier((*parts1, from_a0, from_b0))
+    parts1 = list(experts(place, 1, own1, a1, b1, *d1, in_own, in_sib, down_own, down_sib))
+    parts1[4] = after(parts1[4], from_a0, from_b0)
     r1 = swapped(parts1[3], "rep", a_bit), swapped(parts1[4], "rep", b_bit)
     returned0 = to_planes(parts0[0], from_a0, from_b0)
     to_a1, to_b1 = reduced(parts1, r1)

time: 97.9 us -> 95.3 us (0.973)
  waiting for transfers between devices: 41.8 us -> 35.2 us
  starting transfers between devices: 37.2 us -> 40.4 us
    ppermute x32, waiting for transfers between devices: 41.8 us -> 35.2 us  [swapped(): lax.ppermute(array, axis, [(i, i ^ distance) for i in range(lax.axis_size...]
    pallas_call x0 -> x1, Pallas kernels: none -> 4.02 us  [hold(): pl.pallas_call(hold_kernel, out_shape=[shape, shape], in_specs=[smem(), h...]
    pallas_call x2, Pallas kernels: 11.8 us -> 8.6 us  [experts(): pl.pallas_call(functools.partial(experts_kernel, chunk, half), out_shape=...]
    ppermute x32, starting transfers between devices: 37.2 us -> 40.4 us  [swapped(): lax.ppermute(array, axis, [(i, i ^ distance) for i in range(lax.axis_size...]
  transfers between devices with their start and end apart: 32 -> 32, of which waited for: 17 -> 19; matrix products, arithmetic and copies ran while one was open for 1% -> 1% of each run, Pallas kernels for 13% -> 15%
where the time goes in v5:
time: 95.3 us; the launch traced here: 95.1 us
  starting transfers between devices  40.4 us (42%)
  waiting for transfers between devices  35.2 us (37%)
  Pallas kernels  16.9 us (18%)
  other arithmetic  2.27 us (2%)
    ppermute x32, starting transfers between devices, swapped(): lax.ppermute(array, axis, [(i, i ^ distance) for i in range(lax.axis_size...  40.4 us
    ppermute x32, waiting for transfers between devices, swapped(): lax.ppermute(array, axis, [(i, i ^ distance) for i in range(lax.axis_size...  35.2 us
    pallas_call x2, Pallas kernels, experts(): pl.pallas_call(functools.partial(experts_kernel, chunk, half), out_shape=...  8.6 us
    pallas_call x1, Pallas kernels, hold(): pl.pallas_call(hold_kernel, out_shape=[shape, shape], in_specs=[smem(), h...  4.02 us
    pallas_call x1, Pallas kernels, embed(): pl.pallas_call(embed_kernel, out_shape=[shape, shape], in_specs=[hbm()] *...  2.51 us
  transfers between devices with their start and end apart: 32, of which 19 were waited for; matrix products, arithmetic and copies ran while one was open for 1% of the time, Pallas kernels for 15%

profile of v5, /device:TPU:0, one launch (start us, length us, event | category | flops | bytes accessed | tf_op | source)
XLA Modules:
  0.0 95.1 jit_solution(1445970007831315586)
XLA Ops:
  0.7 2.5 %embed.1 = (bf16[128,1024]{1,0:T(8,128)(2,1)S(1)}, bf16[128,1024]{1,0:T(8,128)(2,1)S(1)}) custom-call(bf16[128,1536]{1,0:T(8,128)(2,1)} %tubelets_ref, bf16[1536,1024]{1,0:T(8,128)(2,1)} %weight_ref.1, f32[1,1024]{1,0:T(1,128)} %bitcast.41), custom_call_target="tpu_custom_call" | custom-call | flops 402653184 | bytes 3145728 | tf_op jit(solution)/shard_map/embed/pallas_call | solution.py:82
  6.8 3.0 %collective-permute-start.2 = (bf16[4,24,1024]{2,1,0:T(8,128)(2,1)S(1)}, bf16[4,24,1024]{2,1,0:T(8,128)(2,1)S(1)}, u32[]{:S(2)}, u32[]{:S(2)}) collective-permute-start(bf16[4,24,1024]{2,1,0:T(8,128)(2,1)S(1)} %get-tuple-element.55), channel_id=1, source_target_pairs={{0,1},{1,0},{2,3},{3,2},{4,5},{5,4},{6,7},{7,6},{8,9},{9,8},{10,11... | collective-permute-start | bytes 589832 | tf_op jit(solution)/shard_map/ppermute | solution.py:20
  9.8 2.6 %collective-permute-start.3 = (bf16[2,24,1024]{2,1,0:T(8,128)(2,1)S(1)}, bf16[2,24,1024]{2,1,0:T(8,128)(2,1)S(1)}, u32[]{:S(2)}, u32[]{:S(2)}) collective-permute-start(bf16[2,24,1024]{2,1,0:T(8,128)(2,1)S(1)} %get-tuple-element.57), channel_id=1, source_target_pairs={{0,2},{1,3},{2,0},{3,1},{4,6},{5,7},{6,4},{7,5},{8,10},{9,11},{10,... | collective-permute-start | bytes 294920 | tf_op jit(solution)/shard_map/ppermute | solution.py:20
  12.4 4.7 %collective-permute-done.2 = bf16[4,24,1024]{2,1,0:T(8,128)(2,1)S(1)} collective-permute-done((bf16[4,24,1024]{2,1,0:T(8,128)(2,1)S(1)}, bf16[4,24,1024]{2,1,0:T(8,128)(2,1)S(1)}, u32[]{:S(2)}, u32[]{:S(2)}) %collective-permute-start.2) | collective-permute-done | bytes 196640 | tf_op jit(solution)/shard_map/ppermute | solution.py:20
  17.1 4.0 %hold.1 = (bf16[4,1024,512]{2,1,0:T(8,128)(2,1)S(1)}, bf16[4,1024,512]{2,1,0:T(8,128)(2,1)S(1)}) custom-call(s32[2]{0:T(128)S(1)} %pad_add_fusion.1.place_ref, bf16[8,1024,512]{2,1,0:T(8,128)(2,1)} %in_ref.1, bf16[8,1024,512]{2,1,0:T(8,128)(2,1)} %down_ref.1), custom_call_target="tpu_custom_call" | custom-call | bytes 16777216 | tf_op jit(solution)/shard_map/hold/pallas_call | solution.py:183
  21.6 1.6 %collective-permute-start.9 = (bf16[2,96,1024]{2,1,0:T(8,128)(2,1)S(1)}, bf16[2,96,1024]{2,1,0:T(8,128)(2,1)S(1)}, u32[]{:S(2)}, u32[]{:S(2)}) collective-permute-start(bf16[2,96,1024]{2,1,0:T(8,128)(2,1)S(1)} %pad_maximum_fusion.own_ref), channel_id=1, source_target_pairs={{0,16},{4,20},{8,24},{12,28},{16,0},{20,4},{24,8},{28,12},{1,17},{... | collective-permute-start | bytes 1179656 | tf_op jit(solution)/shard_map/ppermute | solution.py:20
  23.1 1.5 %collective-permute-start.8 = (bf16[2,96,1024]{2,1,0:T(8,128)(2,1)S(1)}, bf16[2,96,1024]{2,1,0:T(8,128)(2,1)S(1)}, u32[]{:S(2)}, u32[]{:S(2)}) collective-permute-start(bf16[2,96,1024]{2,1,0:T(8,128)(2,1)S(1)} %pad_maximum_fusion.own_ref), channel_id=1, source_target_pairs={{0,8},{4,12},{8,0},{12,4},{16,24},{20,28},{24,16},{28,20},{1,9},{5... | collective-permute-start | bytes 1179656 | tf_op jit(solution)/shard_map/ppermute | solution.py:20
  24.6 2.1 %collective-permute-start.6 = (bf16[2,24,1024]{2,1,0:T(8,128)(2,1)S(1)}, bf16[2,24,1024]{2,1,0:T(8,128)(2,1)S(1)}, u32[]{:S(2)}, u32[]{:S(2)}) collective-permute-start(bf16[2,24,1024]{2,1,0:T(8,128)(2,1)S(1)} %get-tuple-element.65), channel_id=1, source_target_pairs={{0,2},{1,3},{2,0},{3,1},{4,6},{5,7},{6,4},{7,5},{8,10},{9,11},{10,... | collective-permute-start | bytes 294920 | tf_op jit(solution)/shard_map/ppermute | solution.py:20
  26.7 2.1 %collective-permute-start.7 = (bf16[2,24,1024]{2,1,0:T(8,128)(2,1)S(1)}, bf16[2,24,1024]{2,1,0:T(8,128)(2,1)S(1)}, u32[]{:S(2)}, u32[]{:S(2)}) collective-permute-start(bf16[2,24,1024]{2,1,0:T(8,128)(2,1)S(1)} %get-tuple-element.66), channel_id=1, source_target_pairs={{0,3},{1,2},{2,1},{3,0},{4,7},{5,6},{6,5},{7,4},{8,11},{9,10},{10,... | collective-permute-start | bytes 294920 | tf_op jit(solution)/shard_map/ppermute | solution.py:20
  28.8 3.2 %collective-permute-done.9.b_ref = bf16[2,96,1024]{2,1,0:T(8,128)(2,1)S(1)} collective-permute-done((bf16[2,96,1024]{2,1,0:T(8,128)(2,1)S(1)}, bf16[2,96,1024]{2,1,0:T(8,128)(2,1)S(1)}, u32[]{:S(2)}, u32[]{:S(2)}) %collective-permute-start.9) | collective-permute-done | bytes 393248 | tf_op jit(solution)/shard_map/ppermute | solution.py:20
  32.0 1.5 %collective-permute-start.13 = (bf16[1,96,1024]{2,1,0:T(8,128)(2,1)S(1)}, bf16[1,96,1024]{2,1,0:T(8,128)(2,1)S(1)}, u32[]{:S(2)}, u32[]{:S(2)}) collective-permute-start(bf16[1,96,1024]{2,1,0:T(8,128)(2,1)S(1)} %slice.91), channel_id=1, source_target_pairs={{0,8},{4,12},{8,0},{12,4},{16,24},{20,28},{24,16},{28,20},{1,9},{5... | collective-permute-start | bytes 589832 | tf_op jit(solution)/shard_map/ppermute | solution.py:20
  33.5 1.6 %collective-permute-start.12 = (bf16[1,96,1024]{2,1,0:T(8,128)(2,1)S(1)}, bf16[1,96,1024]{2,1,0:T(8,128)(2,1)S(1)}, u32[]{:S(2)}, u32[]{:S(2)}) collective-permute-start(bf16[1,96,1024]{2,1,0:T(8,128)(2,1)S(1)} %slice.90), channel_id=1, source_target_pairs={{0,16},{4,20},{8,24},{12,28},{16,0},{20,4},{24,8},{28,12},{1,17},{... | collective-permute-start | bytes 589832 | tf_op jit(solution)/shard_map/ppermute | solution.py:20
  35.7 1.3 %collective-permute-start.10 = (bf16[2,96,1024]{2,1,0:T(8,128)(2,1)S(1)}, bf16[2,96,1024]{2,1,0:T(8,128)(2,1)S(1)}, u32[]{:S(2)}, u32[]{:S(2)}) collective-permute-start(bf16[2,96,1024]{2,1,0:T(8,128)(2,1)S(1)} %pad_maximum_fusion.1.own_ref), channel_id=1, source_target_pairs={{0,8},{4,12},{8,0},{12,4},{16,24},{20,28},{24,16},{28,20},{1,9},{5... | collective-permute-start | bytes 1179656 | tf_op jit(solution)/shard_map/ppermute | solution.py:20
  37.0 2.6 %collective-permute-done.13.d2_ref = bf16[1,96,1024]{2,1,0:T(8,128)(2,1)S(1)} collective-permute-done((bf16[1,96,1024]{2,1,0:T(8,128)(2,1)S(1)}, bf16[1,96,1024]{2,1,0:T(8,128)(2,1)S(1)}, u32[]{:S(2)}, u32[]{:S(2)}) %collective-permute-start.13) | collective-permute-done | bytes 196640 | tf_op jit(solution)/shard_map/ppermute | solution.py:20
  39.6 1.8 %collective-permute-done.12.d1_ref = bf16[1,96,1024]{2,1,0:T(8,128)(2,1)S(1)} collective-permute-done((bf16[1,96,1024]{2,1,0:T(8,128)(2,1)S(1)}, bf16[1,96,1024]{2,1,0:T(8,128)(2,1)S(1)}, u32[]{:S(2)}, u32[]{:S(2)}) %collective-permute-start.12) | collective-permute-done | bytes 196640 | tf_op jit(solution)/shard_map/ppermute | solution.py:20
  41.4 4.3 %experts.2 = (bf16[2,96,1024]{2,1,0:T(8,128)(2,1)S(1)}, bf16[2,96,1024]{2,1,0:T(8,128)(2,1)S(1)}, bf16[2,96,1024]{2,1,0:T(8,128)(2,1)S(1)}, bf16[1,96,1024]{2,1,0:T(8,128)(2,1)S(1)}, bf16[1,96,1024]{2,1,0:T(8,128)(2,1)S(1)}) custom-call(s32[2]{0:T(128)S(1)} %pad_add_fusion.1.place_ref, bf16[2,96,1024]{2,1,0:T(8,128)(2,1)S(1)} %pad_maximum_fusion.own_ref, ...), custom_call_target="tpu_custom_call" | custom-call | flops 3221225472 | bytes 3145728 | tf_op jit(solution)/shard_map/experts/pallas_call | solution.py:219
  49.0 1.5 %collective-permute-start.15 = (bf16[1,96,1024]{2,1,0:T(8,128)(2,1)S(1)}, bf16[1,96,1024]{2,1,0:T(8,128)(2,1)S(1)}, u32[]{:S(2)}, u32[]{:S(2)}) collective-permute-start(bf16[1,96,1024]{2,1,0:T(8,128)(2,1)S(1)} %get-tuple-element.77), channel_id=1, source_target_pairs={{0,16},{4,20},{8,24},{12,28},{16,0},{20,4},{24,8},{28,12},{1,17},{... | collective-permute-start | bytes 589832 | tf_op jit(solution)/shard_map/ppermute | solution.py:20
  50.5 2.7 %collective-permute-done.17 = bf16[1,96,1024]{2,1,0:T(8,128)(2,1)S(1)} collective-permute-done((bf16[1,96,1024]{2,1,0:T(8,128)(2,1)S(1)}, bf16[1,96,1024]{2,1,0:T(8,128)(2,1)S(1)}, u32[]{:S(2)}, u32[]{:S(2)}) %collective-permute-start.17) | collective-permute-done | bytes 196640 | tf_op jit(solution)/shard_map/ppermute | solution.py:20
  53.2 1.5 %collective-permute-start.19 = (bf16[1,96,1024]{2,1,0:T(8,128)(2,1)S(1)}, bf16[1,96,1024]{2,1,0:T(8,128)(2,1)S(1)}, u32[]{:S(2)}, u32[]{:S(2)}) collective-permute-start(bf16[1,96,1024]{2,1,0:T(8,128)(2,1)S(1)} %slice.75), channel_id=1, source_target_pairs={{0,16},{4,20},{8,24},{12,28},{16,0},{20,4},{24,8},{28,12},{1,17},{... | collective-permute-start | bytes 589832 | tf_op jit(solution)/shard_map/ppermute | solution.py:20
  55.4 1.4 %collective-permute-done.15 = bf16[1,96,1024]{2,1,0:T(8,128)(2,1)S(1)} collective-permute-done((bf16[1,96,1024]{2,1,0:T(8,128)(2,1)S(1)}, bf16[1,96,1024]{2,1,0:T(8,128)(2,1)S(1)}, u32[]{:S(2)}, u32[]{:S(2)}) %collective-permute-start.15) | collective-permute-done | bytes 196640 | tf_op jit(solution)/shard_map/ppermute | solution.py:20
  58.1 3.0 %collective-permute-done.19.d1_ref = bf16[1,96,1024]{2,1,0:T(8,128)(2,1)S(1)} collective-permute-done((bf16[1,96,1024]{2,1,0:T(8,128)(2,1)S(1)}, bf16[1,96,1024]{2,1,0:T(8,128)(2,1)S(1)}, u32[]{:S(2)}, u32[]{:S(2)}) %collective-permute-start.19) | collective-permute-done | bytes 196640 | tf_op jit(solution)/shard_map/ppermute | solution.py:20
  61.1 4.3 %experts.3 = (bf16[2,96,1024]{2,1,0:T(8,128)(2,1)S(1)}, bf16[2,96,1024]{2,1,0:T(8,128)(2,1)S(1)}, bf16[2,96,1024]{2,1,0:T(8,128)(2,1)S(1)}, bf16[1,96,1024]{2,1,0:T(8,128)(2,1)S(1)}, bf16[1,96,1024]{2,1,0:T(8,128)(2,1)S(1)}) custom-call(s32[2]{0:T(128)S(1)} %pad_add_fusion.1.place_ref, bf16[2,96,1024]{2,1,0:T(8,128)(2,1)S(1)} %pad_maximum_fusion.1.own_ref, ...), custom_call_target="tpu_custom_call" | custom-call | flops 3221225472 | bytes 3145728 | tf_op jit(solution)/shard_map/experts/pallas_call | solution.py:219
  66.8 1.5 %collective-permute-start.21 = (bf16[1,96,1024]{2,1,0:T(8,128)(2,1)S(1)}, bf16[1,96,1024]{2,1,0:T(8,128)(2,1)S(1)}, u32[]{:S(2)}, u32[]{:S(2)}) collective-permute-start(bf16[1,96,1024]{2,1,0:T(8,128)(2,1)S(1)} %get-tuple-element.88), channel_id=1, source_target_pairs={{0,16},{4,20},{8,24},{12,28},{16,0},{20,4},{24,8},{28,12},{1,17},{... | collective-permute-start | bytes 589832 | tf_op jit(solution)/shard_map/ppermute | solution.py:20
  68.3 3.0 %collective-permute-done.23 = bf16[1,96,1024]{2,1,0:T(8,128)(2,1)S(1)} collective-permute-done((bf16[1,96,1024]{2,1,0:T(8,128)(2,1)S(1)}, bf16[1,96,1024]{2,1,0:T(8,128)(2,1)S(1)}, u32[]{:S(2)}, u32[]{:S(2)}) %collective-permute-start.23) | collective-permute-done | bytes 196640 | tf_op jit(solution)/shard_map/ppermute | solution.py:20
  71.4 1.6 %collective-permute-start.24 = (bf16[2,96,1024]{2,1,0:T(8,128)(2,1)S(1)}, bf16[2,96,1024]{2,1,0:T(8,128)(2,1)S(1)}, u32[]{:S(2)}, u32[]{:S(2)}) collective-permute-start(bf16[2,96,1024]{2,1,0:T(8,128)(2,1)S(1)} %pad_maximum_fusion.5), channel_id=1, source_target_pairs={{0,16},{4,20},{8,24},{12,28},{16,0},{20,4},{24,8},{28,12},{1,17},{... | collective-permute-start | bytes 1179656 | tf_op jit(solution)/shard_map/ppermute | solution.py:20
  73.0 1.7 %collective-permute-done.21 = bf16[1,96,1024]{2,1,0:T(8,128)(2,1)S(1)} collective-permute-done((bf16[1,96,1024]{2,1,0:T(8,128)(2,1)S(1)}, bf16[1,96,1024]{2,1,0:T(8,128)(2,1)S(1)}, u32[]{:S(2)}, u32[]{:S(2)}) %collective-permute-start.21) | collective-permute-done | bytes 196640 | tf_op jit(solution)/shard_map/ppermute | solution.py:20
  76.2 2.9 %collective-permute-start.29 = (bf16[2,24,1024]{2,1,0:T(8,128)(2,1)S(1)}, bf16[2,24,1024]{2,1,0:T(8,128)(2,1)S(1)}, u32[]{:S(2)}, u32[]{:S(2)}) collective-permute-start(bf16[2,24,1024]{2,1,0:T(8,128)(2,1)S(1)} %get-tuple-element.97), channel_id=1, source_target_pairs={{0,3},{1,2},{2,1},{3,0},{4,7},{5,6},{6,5},{7,4},{8,11},{9,10},{10,... | collective-permute-start | bytes 294920 | tf_op jit(solution)/shard_map/ppermute | solution.py:20
  79.1 1.6 %collective-permute-start.25 = (bf16[2,24,1024]{2,1,0:T(8,128)(2,1)S(1)}, bf16[2,24,1024]{2,1,0:T(8,128)(2,1)S(1)}, u32[]{:S(2)}, u32[]{:S(2)}) collective-permute-start(bf16[2,24,1024]{2,1,0:T(8,128)(2,1)S(1)} %get-tuple-element.99), channel_id=1, source_target_pairs={{0,1},{1,0},{2,3},{3,2},{4,5},{5,4},{6,7},{7,6},{8,9},{9,8},{10,11... | collective-permute-start | bytes 294920 | tf_op jit(solution)/shard_map/ppermute | solution.py:20
  80.7 1.9 %collective-permute-done.22 = bf16[2,96,1024]{2,1,0:T(8,128)(2,1)S(1)} collective-permute-done((bf16[2,96,1024]{2,1,0:T(8,128)(2,1)S(1)}, bf16[2,96,1024]{2,1,0:T(8,128)(2,1)S(1)}, u32[]{:S(2)}, u32[]{:S(2)}) %collective-permute-start.22) | collective-permute-done | bytes 393248 | tf_op jit(solution)/shard_map/ppermute | solution.py:20
  82.8 2.6 %collective-permute-start.30 = (bf16[2,24,1024]{2,1,0:T(8,128)(2,1)S(1)}, bf16[2,24,1024]{2,1,0:T(8,128)(2,1)S(1)}, u32[]{:S(2)}, u32[]{:S(2)}) collective-permute-start(bf16[2,24,1024]{2,1,0:T(8,128)(2,1)S(1)} %get-tuple-element.93), channel_id=1, source_target_pairs={{0,3},{1,2},{2,1},{3,0},{4,7},{5,6},{6,5},{7,4},{8,11},{9,10},{10,... | collective-permute-start | bytes 294920 | tf_op jit(solution)/shard_map/ppermute | solution.py:20
  89.4 2.9 %collective-permute-done.28.refs_5_ = bf16[2,24,1024]{2,1,0:T(8,128)(2,1)S(1)} collective-permute-done((bf16[2,24,1024]{2,1,0:T(8,128)(2,1)S(1)}, bf16[2,24,1024]{2,1,0:T(8,128)(2,1)S(1)}, u32[]{:S(2)}, u32[]{:S(2)}) %collective-permute-start.28) | collective-permute-done | bytes 98336 | tf_op jit(solution)/shard_map/ppermute | solution.py:20
  92.8 1.5 %collective-permute-done.31 = bf16[128,1024]{1,0:T(8,128)(2,1)S(1)} collective-permute-done((bf16[128,1024]{1,0:T(8,128)(2,1)S(1)}, bf16[128,1024]{1,0:T(8,128)(2,1)S(1)}, u32[]{:S(2)}, u32[]{:S(2)}) %collective-permute-start.31) | collective-permute-done | bytes 262176 | tf_op jit(solution)/shard_map/ppermute | solution.py:20
  (61 shorter events, 19.1 us)
Async XLA Ops:
  3.2 2.6 %collective-permute-start.1 = (bf16[128,1024]{1,0:T(8,128)(2,1)S(1)}, bf16[128,1024]{1,0:T(8,128)(2,1)S(1)}, u32[]{:S(2)}, u32[]{:S(2)}) collective-permute-start(bf16[128,1024]{1,0:T(8,128)(2,1)S(1)} %get-tuple-element.53.normed_ref), channel_id=1, source_target_pairs={{0,4},{4,0},{8,12},{12,8},{16,20},{20,16},{24,28},{28,24},{1,5},{5... | collective-permute-start | bytes 786440 | tf_op jit(solution)/shard_map/ppermute | solution.py:20
  3.7 1.2 %collective-permute-start = (s32[4,128]{1,0:T(4,128)S(1)}, s32[4,128]{1,0:T(4,128)S(1)}, u32[]{:S(2)}, u32[]{:S(2)}) collective-permute-start(s32[4,128]{1,0:T(4,128)S(1)} %pad_add_fusion.code_ref), channel_id=1, source_target_pairs={{0,4},{4,0},{8,12},{12,8},{16,20},{20,16},{24,28},{28,24},{1,5},{5... | collective-permute-start | bytes 6152 | tf_op jit(solution)/shard_map/ppermute | solution.py:20
  5.9 18.8 %collective-permute-start.5 = (bf16[8,1024,512]{2,1,0:T(8,128)(2,1)}, bf16[8,1024,512]{2,1,0:T(8,128)(2,1)S(1)}, u32[]{:S(2)}, u32[]{:S(2)}) collective-permute-start(bf16[8,1024,512]{2,1,0:T(8,128)(2,1)} %in_ref.1), channel_id=1, source_target_pairs={{0,4},{4,0},{8,12},{12,8},{16,20},{20,16},{24,28},{28,24},{1,5},{5... | collective-permute-start | bytes 25165832 | tf_op jit(solution)/shard_map/ppermute | solution.py:20
  6.3 35.1 %collective-permute-start.14 = (bf16[8,1024,512]{2,1,0:T(8,128)(2,1)}, bf16[8,1024,512]{2,1,0:T(8,128)(2,1)S(1)}, u32[]{:S(2)}, u32[]{:S(2)}) collective-permute-start(bf16[8,1024,512]{2,1,0:T(8,128)(2,1)} %down_ref.1), channel_id=1, source_target_pairs={{0,4},{4,0},{8,12},{12,8},{16,20},{20,16},{24,28},{28,24},{1,5},{5... | collective-permute-start | bytes 25165832 | tf_op jit(solution)/shard_map/ppermute | solution.py:20
  6.8 10.3 %collective-permute-start.2 = (bf16[4,24,1024]{2,1,0:T(8,128)(2,1)S(1)}, bf16[4,24,1024]{2,1,0:T(8,128)(2,1)S(1)}, u32[]{:S(2)}, u32[]{:S(2)}) collective-permute-start(bf16[4,24,1024]{2,1,0:T(8,128)(2,1)S(1)} %get-tuple-element.55), channel_id=1, source_target_pairs={{0,1},{1,0},{2,3},{3,2},{4,5},{5,4},{6,7},{7,6},{8,9},{9,8},{10,11... | collective-permute-start | bytes 589832 | tf_op jit(solution)/shard_map/ppermute | solution.py:20
  9.8 11.4 %collective-permute-start.3 = (bf16[2,24,1024]{2,1,0:T(8,128)(2,1)S(1)}, bf16[2,24,1024]{2,1,0:T(8,128)(2,1)S(1)}, u32[]{:S(2)}, u32[]{:S(2)}) collective-permute-start(bf16[2,24,1024]{2,1,0:T(8,128)(2,1)S(1)} %get-tuple-element.57), channel_id=1, source_target_pairs={{0,2},{1,3},{2,0},{3,1},{4,6},{5,7},{6,4},{7,5},{8,10},{9,11},{10,... | collective-permute-start | bytes 294920 | tf_op jit(solution)/shard_map/ppermute | solution.py:20
  12.4 9.1 %collective-permute-start.4 = (bf16[2,24,1024]{2,1,0:T(8,128)(2,1)S(1)}, bf16[2,24,1024]{2,1,0:T(8,128)(2,1)S(1)}, u32[]{:S(2)}, u32[]{:S(2)}) collective-permute-start(bf16[2,24,1024]{2,1,0:T(8,128)(2,1)S(1)} %get-tuple-element.58), channel_id=1, source_target_pairs={{0,3},{1,2},{2,1},{3,0},{4,7},{5,6},{6,5},{7,4},{8,11},{9,10},{10,... | collective-permute-start | bytes 294920 | tf_op jit(solution)/shard_map/ppermute | solution.py:20
  21.6 10.4 %collective-permute-start.9 = (bf16[2,96,1024]{2,1,0:T(8,128)(2,1)S(1)}, bf16[2,96,1024]{2,1,0:T(8,128)(2,1)S(1)}, u32[]{:S(2)}, u32[]{:S(2)}) collective-permute-start(bf16[2,96,1024]{2,1,0:T(8,128)(2,1)S(1)} %pad_maximum_fusion.own_ref), channel_id=1, source_target_pairs={{0,16},{4,20},{8,24},{12,28},{16,0},{20,4},{24,8},{28,12},{1,17},{... | collective-permute-start | bytes 1179656 | tf_op jit(solution)/shard_map/ppermute | solution.py:20
  23.1 10.3 %collective-permute-start.8 = (bf16[2,96,1024]{2,1,0:T(8,128)(2,1)S(1)}, bf16[2,96,1024]{2,1,0:T(8,128)(2,1)S(1)}, u32[]{:S(2)}, u32[]{:S(2)}) collective-permute-start(bf16[2,96,1024]{2,1,0:T(8,128)(2,1)S(1)} %pad_maximum_fusion.own_ref), channel_id=1, source_target_pairs={{0,8},{4,12},{8,0},{12,4},{16,24},{20,28},{24,16},{28,20},{1,9},{5... | collective-permute-start | bytes 1179656 | tf_op jit(solution)/shard_map/ppermute | solution.py:20
  24.6 10.4 %collective-permute-start.6 = (bf16[2,24,1024]{2,1,0:T(8,128)(2,1)S(1)}, bf16[2,24,1024]{2,1,0:T(8,128)(2,1)S(1)}, u32[]{:S(2)}, u32[]{:S(2)}) collective-permute-start(bf16[2,24,1024]{2,1,0:T(8,128)(2,1)S(1)} %get-tuple-element.65), channel_id=1, source_target_pairs={{0,2},{1,3},{2,0},{3,1},{4,6},{5,7},{6,4},{7,5},{8,10},{9,11},{10,... | collective-permute-start | bytes 294920 | tf_op jit(solution)/shard_map/ppermute | solution.py:20
  26.7 8.4 %collective-permute-start.7 = (bf16[2,24,1024]{2,1,0:T(8,128)(2,1)S(1)}, bf16[2,24,1024]{2,1,0:T(8,128)(2,1)S(1)}, u32[]{:S(2)}, u32[]{:S(2)}) collective-permute-start(bf16[2,24,1024]{2,1,0:T(8,128)(2,1)S(1)} %get-tuple-element.66), channel_id=1, source_target_pairs={{0,3},{1,2},{2,1},{3,0},{4,7},{5,6},{6,5},{7,4},{8,11},{9,10},{10,... | collective-permute-start | bytes 294920 | tf_op jit(solution)/shard_map/ppermute | solution.py:20
  32.0 7.7 %collective-permute-start.13 = (bf16[1,96,1024]{2,1,0:T(8,128)(2,1)S(1)}, bf16[1,96,1024]{2,1,0:T(8,128)(2,1)S(1)}, u32[]{:S(2)}, u32[]{:S(2)}) collective-permute-start(bf16[1,96,1024]{2,1,0:T(8,128)(2,1)S(1)} %slice.91), channel_id=1, source_target_pairs={{0,8},{4,12},{8,0},{12,4},{16,24},{20,28},{24,16},{28,20},{1,9},{5... | collective-permute-start | bytes 589832 | tf_op jit(solution)/shard_map/ppermute | solution.py:20
  33.5 7.9 %collective-permute-start.12 = (bf16[1,96,1024]{2,1,0:T(8,128)(2,1)S(1)}, bf16[1,96,1024]{2,1,0:T(8,128)(2,1)S(1)}, u32[]{:S(2)}, u32[]{:S(2)}) collective-permute-start(bf16[1,96,1024]{2,1,0:T(8,128)(2,1)S(1)} %slice.90), channel_id=1, source_target_pairs={{0,16},{4,20},{8,24},{12,28},{16,0},{20,4},{24,8},{28,12},{1,17},{... | collective-permute-start | bytes 589832 | tf_op jit(solution)/shard_map/ppermute | solution.py:20
  35.1 11.7 %collective-permute-start.11 = (bf16[2,96,1024]{2,1,0:T(8,128)(2,1)S(1)}, bf16[2,96,1024]{2,1,0:T(8,128)(2,1)S(1)}, u32[]{:S(2)}, u32[]{:S(2)}) collective-permute-start(bf16[2,96,1024]{2,1,0:T(8,128)(2,1)S(1)} %pad_maximum_fusion.1.own_ref), channel_id=1, source_target_pairs={{0,16},{4,20},{8,24},{12,28},{16,0},{20,4},{24,8},{28,12},{1,17},{... | collective-permute-start | bytes 1179656 | tf_op jit(solution)/shard_map/ppermute | solution.py:20
  35.7 11.2 %collective-permute-start.10 = (bf16[2,96,1024]{2,1,0:T(8,128)(2,1)S(1)}, bf16[2,96,1024]{2,1,0:T(8,128)(2,1)S(1)}, u32[]{:S(2)}, u32[]{:S(2)}) collective-permute-start(bf16[2,96,1024]{2,1,0:T(8,128)(2,1)S(1)} %pad_maximum_fusion.1.own_ref), channel_id=1, source_target_pairs={{0,8},{4,12},{8,0},{12,4},{16,24},{20,28},{24,16},{28,20},{1,9},{5... | collective-permute-start | bytes 1179656 | tf_op jit(solution)/shard_map/ppermute | solution.py:20
  46.8 6.4 %collective-permute-start.17 = (bf16[1,96,1024]{2,1,0:T(8,128)(2,1)S(1)}, bf16[1,96,1024]{2,1,0:T(8,128)(2,1)S(1)}, u32[]{:S(2)}, u32[]{:S(2)}) collective-permute-start(bf16[1,96,1024]{2,1,0:T(8,128)(2,1)S(1)} %get-tuple-element.79), channel_id=1, source_target_pairs={{0,8},{4,12},{8,0},{12,4},{16,24},{20,28},{24,16},{28,20},{1,9},{5... | collective-permute-start | bytes 589832 | tf_op jit(solution)/shard_map/ppermute | solution.py:20
  48.0 10.1 %collective-permute-start.20 = (bf16[1,96,1024]{2,1,0:T(8,128)(2,1)S(1)}, bf16[1,96,1024]{2,1,0:T(8,128)(2,1)S(1)}, u32[]{:S(2)}, u32[]{:S(2)}) collective-permute-start(bf16[1,96,1024]{2,1,0:T(8,128)(2,1)S(1)} %slice.76), channel_id=1, source_target_pairs={{0,8},{4,12},{8,0},{12,4},{16,24},{20,28},{24,16},{28,20},{1,9},{5... | collective-permute-start | bytes 589832 | tf_op jit(solution)/shard_map/ppermute | solution.py:20
  49.0 7.8 %collective-permute-start.15 = (bf16[1,96,1024]{2,1,0:T(8,128)(2,1)S(1)}, bf16[1,96,1024]{2,1,0:T(8,128)(2,1)S(1)}, u32[]{:S(2)}, u32[]{:S(2)}) collective-permute-start(bf16[1,96,1024]{2,1,0:T(8,128)(2,1)S(1)} %get-tuple-element.77), channel_id=1, source_target_pairs={{0,16},{4,20},{8,24},{12,28},{16,0},{20,4},{24,8},{28,12},{1,17},{... | collective-permute-start | bytes 589832 | tf_op jit(solution)/shard_map/ppermute | solution.py:20
  53.2 7.8 %collective-permute-start.19 = (bf16[1,96,1024]{2,1,0:T(8,128)(2,1)S(1)}, bf16[1,96,1024]{2,1,0:T(8,128)(2,1)S(1)}, u32[]{:S(2)}, u32[]{:S(2)}) collective-permute-start(bf16[1,96,1024]{2,1,0:T(8,128)(2,1)S(1)} %slice.75), channel_id=1, source_target_pairs={{0,16},{4,20},{8,24},{12,28},{16,0},{20,4},{24,8},{28,12},{1,17},{... | collective-permute-start | bytes 589832 | tf_op jit(solution)/shard_map/ppermute | solution.py:20
  54.8 11.9 %collective-permute-start.18 = (bf16[2,96,1024]{2,1,0:T(8,128)(2,1)S(1)}, bf16[2,96,1024]{2,1,0:T(8,128)(2,1)S(1)}, u32[]{:S(2)}, u32[]{:S(2)}) collective-permute-start(bf16[2,96,1024]{2,1,0:T(8,128)(2,1)S(1)} %pad_maximum_fusion.3), channel_id=1, source_target_pairs={{0,16},{4,20},{8,24},{12,28},{16,0},{20,4},{24,8},{28,12},{1,17},{... | collective-permute-start | bytes 1179656 | tf_op jit(solution)/shard_map/ppermute | solution.py:20
  56.9 9.9 %collective-permute-start.16 = (bf16[2,96,1024]{2,1,0:T(8,128)(2,1)S(1)}, bf16[2,96,1024]{2,1,0:T(8,128)(2,1)S(1)}, u32[]{:S(2)}, u32[]{:S(2)}) collective-permute-start(bf16[2,96,1024]{2,1,0:T(8,128)(2,1)S(1)} %pad_maximum_fusion.2), channel_id=1, source_target_pairs={{0,8},{4,12},{8,0},{12,4},{16,24},{20,28},{24,16},{28,20},{1,9},{5... | collective-permute-start | bytes 1179656 | tf_op jit(solution)/shard_map/ppermute | solution.py:20
  65.4 5.9 %collective-permute-start.23 = (bf16[1,96,1024]{2,1,0:T(8,128)(2,1)S(1)}, bf16[1,96,1024]{2,1,0:T(8,128)(2,1)S(1)}, u32[]{:S(2)}, u32[]{:S(2)}) collective-permute-start(bf16[1,96,1024]{2,1,0:T(8,128)(2,1)S(1)} %get-tuple-element.90), channel_id=1, source_target_pairs={{0,8},{4,12},{8,0},{12,4},{16,24},{20,28},{24,16},{28,20},{1,9},{5... | collective-permute-start | bytes 589832 | tf_op jit(solution)/shard_map/ppermute | solution.py:20
  66.8 7.8 %collective-permute-start.21 = (bf16[1,96,1024]{2,1,0:T(8,128)(2,1)S(1)}, bf16[1,96,1024]{2,1,0:T(8,128)(2,1)S(1)}, u32[]{:S(2)}, u32[]{:S(2)}) collective-permute-start(bf16[1,96,1024]{2,1,0:T(8,128)(2,1)S(1)} %get-tuple-element.88), channel_id=1, source_target_pairs={{0,16},{4,20},{8,24},{12,28},{16,0},{20,4},{24,8},{28,12},{1,17},{... | collective-permute-start | bytes 589832 | tf_op jit(solution)/shard_map/ppermute | solution.py:20
  71.4 9.3 %collective-permute-start.24 = (bf16[2,96,1024]{2,1,0:T(8,128)(2,1)S(1)}, bf16[2,96,1024]{2,1,0:T(8,128)(2,1)S(1)}, u32[]{:S(2)}, u32[]{:S(2)}) collective-permute-start(bf16[2,96,1024]{2,1,0:T(8,128)(2,1)S(1)} %pad_maximum_fusion.5), channel_id=1, source_target_pairs={{0,16},{4,20},{8,24},{12,28},{16,0},{20,4},{24,8},{28,12},{1,17},{... | collective-permute-start | bytes 1179656 | tf_op jit(solution)/shard_map/ppermute | solution.py:20
  74.7 7.8 %collective-permute-start.22 = (bf16[2,96,1024]{2,1,0:T(8,128)(2,1)S(1)}, bf16[2,96,1024]{2,1,0:T(8,128)(2,1)S(1)}, u32[]{:S(2)}, u32[]{:S(2)}) collective-permute-start(bf16[2,96,1024]{2,1,0:T(8,128)(2,1)S(1)} %pad_maximum_fusion.4), channel_id=1, source_target_pairs={{0,8},{4,12},{8,0},{12,4},{16,24},{20,28},{24,16},{28,20},{1,9},{5... | collective-permute-start | bytes 1179656 | tf_op jit(solution)/shard_map/ppermute | solution.py:20
  76.2 9.9 %collective-permute-start.29 = (bf16[2,24,1024]{2,1,0:T(8,128)(2,1)S(1)}, bf16[2,24,1024]{2,1,0:T(8,128)(2,1)S(1)}, u32[]{:S(2)}, u32[]{:S(2)}) collective-permute-start(bf16[2,24,1024]{2,1,0:T(8,128)(2,1)S(1)} %get-tuple-element.97), channel_id=1, source_target_pairs={{0,3},{1,2},{2,1},{3,0},{4,7},{5,6},{6,5},{7,4},{8,11},{9,10},{10,... | collective-permute-start | bytes 294920 | tf_op jit(solution)/shard_map/ppermute | solution.py:20
  79.1 9.0 %collective-permute-start.27 = (bf16[2,24,1024]{2,1,0:T(8,128)(2,1)S(1)}, bf16[2,24,1024]{2,1,0:T(8,128)(2,1)S(1)}, u32[]{:S(2)}, u32[]{:S(2)}) collective-permute-start(bf16[2,24,1024]{2,1,0:T(8,128)(2,1)S(1)} %get-tuple-element.98), channel_id=1, source_target_pairs={{0,2},{1,3},{2,0},{3,1},{4,6},{5,7},{6,4},{7,5},{8,10},{9,11},{10,... | collective-permute-start | bytes 294920 | tf_op jit(solution)/shard_map/ppermute | solution.py:20
  79.1 9.0 %collective-permute-start.25 = (bf16[2,24,1024]{2,1,0:T(8,128)(2,1)S(1)}, bf16[2,24,1024]{2,1,0:T(8,128)(2,1)S(1)}, u32[]{:S(2)}, u32[]{:S(2)}) collective-permute-start(bf16[2,24,1024]{2,1,0:T(8,128)(2,1)S(1)} %get-tuple-element.99), channel_id=1, source_target_pairs={{0,1},{1,0},{2,3},{3,2},{4,5},{5,4},{6,7},{7,6},{8,9},{9,8},{10,11... | collective-permute-start | bytes 294920 | tf_op jit(solution)/shard_map/ppermute | solution.py:20
  82.8 6.6 %collective-permute-start.30 = (bf16[2,24,1024]{2,1,0:T(8,128)(2,1)S(1)}, bf16[2,24,1024]{2,1,0:T(8,128)(2,1)S(1)}, u32[]{:S(2)}, u32[]{:S(2)}) collective-permute-start(bf16[2,24,1024]{2,1,0:T(8,128)(2,1)S(1)} %get-tuple-element.93), channel_id=1, source_target_pairs={{0,3},{1,2},{2,1},{3,0},{4,7},{5,6},{6,5},{7,4},{8,11},{9,10},{10,... | collective-permute-start | bytes 294920 | tf_op jit(solution)/shard_map/ppermute | solution.py:20
  85.4 6.9 %collective-permute-start.28 = (bf16[2,24,1024]{2,1,0:T(8,128)(2,1)S(1)}, bf16[2,24,1024]{2,1,0:T(8,128)(2,1)S(1)}, u32[]{:S(2)}, u32[]{:S(2)}) collective-permute-start(bf16[2,24,1024]{2,1,0:T(8,128)(2,1)S(1)} %get-tuple-element.94), channel_id=1, source_target_pairs={{0,2},{1,3},{2,0},{3,1},{4,6},{5,7},{6,4},{7,5},{8,10},{9,11},{10,... | collective-permute-start | bytes 294920 | tf_op jit(solution)/shard_map/ppermute | solution.py:20
  86.1 6.2 %collective-permute-start.26 = (bf16[2,24,1024]{2,1,0:T(8,128)(2,1)S(1)}, bf16[2,24,1024]{2,1,0:T(8,128)(2,1)S(1)}, u32[]{:S(2)}, u32[]{:S(2)}) collective-permute-start(bf16[2,24,1024]{2,1,0:T(8,128)(2,1)S(1)} %get-tuple-element.95), channel_id=1, source_target_pairs={{0,1},{1,0},{2,3},{3,2},{4,5},{5,4},{6,7},{7,6},{8,9},{9,8},{10,11... | collective-permute-start | bytes 294920 | tf_op jit(solution)/shard_map/ppermute | solution.py:20
  92.8 1.6 %collective-permute-start.31 = (bf16[128,1024]{1,0:T(8,128)(2,1)S(1)}, bf16[128,1024]{1,0:T(8,128)(2,1)S(1)}, u32[]{:S(2)}, u32[]{:S(2)}) collective-permute-start(bf16[128,1024]{1,0:T(8,128)(2,1)S(1)} %get-tuple-element.92), channel_id=1, source_target_pairs={{0,4},{4,0},{8,12},{12,8},{16,20},{20,16},{24,28},{28,24},{1,5},{5... | collective-permute-start | bytes 786440 | tf_op jit(solution)/shard_map/ppermute | solution.py:20

commit v6 on v5

--- a/solution.py
+++ b/solution.py
@@ -152,7 +152,7 @@
     per = half // CHUNKS
     spans = []
     for s in range(n_exp):
-        spans += [(s * half, half)] if s == 1 else [(s * half + c * per, per) for c in range(CHUNKS)]
+        spans += [(s * half, half)] if s < 2 else [(s * half + c * per, per) for c in range(CHUNKS)]
     pieces = list(pl.pallas_call(
         functools.partial(pack_kernel, spans),
         out_shape=[pltpu.VMEM((count, 2 * cap, width), BF16) for _, count in spans],
@@ -163,7 +163,33 @@
             flops=2 * select.size * width, bytes_accessed=rows * width * 4, transcendentals=0),
         name="pack",
     )(select, normed, sib_normed))
-    return [[pieces.pop(0)] if s == 1 else [pieces.pop(0) for _ in range(CHUNKS)] for s in range(n_exp)]
+    return [[pieces.pop(0)] if s < 2 else [pieces.pop(0) for _ in range(CHUNKS)] for s in range(n_exp)]
+
+
+def lend_kernel(place_ref, in_ref, down_ref, out_ref, sems):
+    count = out_ref.shape[1]
+    start = (1 - place_ref[1]) * count
+    copies = []
+    for e in range(count):
+        for which, source in enumerate((in_ref, down_ref)):
+            copies.append(pltpu.make_async_copy(source.at[start + e], out_ref.at[which, e], sems.at[which, e]))
+            copies[-1].start()
+    for copy in copies:
+        copy.wait()
+
+
+def lend(place, w_in, w_down):
+    shape = (2, w_in.shape[0] // 2, *w_in.shape[1:])
+    return pl.pallas_call(
+        lend_kernel,
+        out_shape=pltpu.VMEM(shape, BF16),
+        in_specs=[smem(), hbm(), hbm()],
+        out_specs=vmem(),
+        scratch_shapes=[pltpu.SemaphoreType.DMA(shape[:2])],
+        compiler_params=pltpu.CompilerParams(vmem_limit_bytes=VMEM_LIMIT),
+        cost_estimate=pl.CostEstimate(flops=0, bytes_accessed=w_in.size * 4, transcendentals=0),
+        name="lend",
+    )(place, in_hbm(w_in), in_hbm(w_down))
 
 
 def hold_kernel(place_ref, in_ref, down_ref, in_out, down_out, sems):
@@ -192,69 +218,81 @@
     )(place, in_hbm(w_in), in_hbm(w_down))
 
 
-def experts_kernel(chunk, half, place_ref, own_ref, a_ref, b_ref, d1_ref, d2_ref,
-                   in_own_ref, in_sib_ref, down_own_ref, down_sib_ref,
-                   p_own_ref, p_a_ref, p_b_ref, p_d1_ref, p_d2_ref, h_ref):
-    per, m, _ = own_ref.shape
+def experts_kernel(chunk, *refs):
+    rows_refs, (sib_ref, in_ref, down_ref), outs = refs[:9], refs[9:12], refs[12:21]
+    h_ref = refs[21]
+    per = rows_refs[0].shape[0]
     split = per // 2
+    first = chunk * per
+    def blocks(refs, e, whole):
+        far, far_a, far_b, d1, d2, own, own_a, own_b, own_d = refs
+        mine = first + e if whole else e
+        diagonal = (d1, e) if e < split else (d2, e - split)
+        return [(far, e), (far_a, e), (far_b, e), diagonal, (own, mine), (own_a, mine), (own_b, mine), (own_d, e)]
+
     for e in range(per):
-        mine = chunk * per + e
-        index = place_ref[1] * half + mine
-        diagonal, p_diagonal = (d1_ref, p_d1_ref) if e < split else (d2_ref, p_d2_ref)
-        x = jnp.concatenate([own_ref[e], a_ref[e], b_ref[e], diagonal[e % split]], axis=0)
-        h_ref[0] = jax.nn.gelu(mm(x, in_own_ref[mine])).astype(BF16)
-        h_ref[1] = jax.nn.gelu(mm(x, in_sib_ref[index])).astype(BF16)
-        total = mm(h_ref[0], down_own_ref[mine], ((1,), (1,))) + mm(h_ref[1], down_sib_ref[index], ((1,), (1,)))
-        p_own_ref[e] = total[0:m].astype(BF16)
-        p_a_ref[e] = total[m:2 * m].astype(BF16)
-        p_b_ref[e] = total[2 * m:3 * m].astype(BF16)
-        p_diagonal[e % split] = total[3 * m:4 * m].astype(BF16)
-
-
-def experts(place, chunk, own, near_a, near_b, d1, d2, in_own, in_sib, down_own, down_sib):
-    per, m, width = own.shape
-    half, _, ff = in_own.shape
-    shape = pltpu.VMEM(own.shape, BF16)
-    part = pltpu.VMEM(d1.shape, BF16)
-    return pl.pallas_call(
-        functools.partial(experts_kernel, chunk, half),
-        out_shape=[shape, shape, shape, part, part],
-        in_specs=[smem()] + [vmem()] * 9,
-        out_specs=[vmem()] * 5,
-        scratch_shapes=[pltpu.VMEM((2, 4 * m, ff), BF16)],
+        mine = first + e
+        x = jnp.concatenate([ref[i] for ref, i in blocks(rows_refs, e, True)], axis=0)
+        h_ref[0] = jax.nn.gelu(mm(x, in_ref[mine])).astype(BF16)
+        h_ref[1] = jax.nn.gelu(mm(x, sib_ref[0, mine])).astype(BF16)
+        total = mm(h_ref[0], down_ref[mine], ((1,), (1,))) + mm(h_ref[1], sib_ref[1, mine], ((1,), (1,)))
+        start = 0
+        for ref, i in blocks(outs, e, False):
+            ref[i] = total[start:start + ref.shape[1]].astype(BF16)
+            start += ref.shape[1]
+
+
+def experts(chunk, blocks, sib, in_own, down_own):
+    far, d1, own = blocks[0], blocks[3], blocks[5]
+    per, far_rows, width = far.shape
+    rows = 4 * (far_rows + own.shape[1])
+    ff = sib.shape[3]
+    own_shape = (per, *own.shape[1:])
+    shapes = [far.shape] * 3 + [d1.shape] * 2 + [own_shape] * 4
+    return list(pl.pallas_call(
+        functools.partial(experts_kernel, chunk),
+        out_shape=[pltpu.VMEM(shape, BF16) for shape in shapes],
+        in_specs=[vmem()] * 12,
+        out_specs=[vmem()] * 9,
+        scratch_shapes=[pltpu.VMEM((2, rows, ff), BF16)],
         compiler_params=pltpu.CompilerParams(vmem_limit_bytes=VMEM_LIMIT),
         cost_estimate=pl.CostEstimate(
-            flops=2 * per * 4 * m * width * 2 * ff * 2, bytes_accessed=per * m * width * 16,
-            transcendentals=per * 4 * m * 2 * ff),
+            flops=2 * per * rows * width * 2 * ff * 2, bytes_accessed=per * rows * width * 4,
+            transcendentals=per * rows * 2 * ff),
         name="experts",
-    )(place, own, near_a, near_b, d1, d2, *(in_vmem(panel) for panel in (in_own, in_sib, down_own, down_sib)))
-
-
-def combine_kernel(tok, gate_ref, emb_ref, *refs):
-    piece_refs, (mine_ref, send_ref, rows_ref) = refs[:-3], refs[-3:]
-    per, slots, _ = piece_refs[0].shape
-    for index, ref in enumerate(piece_refs):
+    )(*blocks, *(in_vmem(panel) for panel in (sib, in_own, down_own))))
+
+
+def combine_kernel(tok, spans, gate_ref, emb_ref, *refs):
+    own_refs, (from_a_ref, from_b_ref), piece_refs = refs[:CHUNKS], refs[CHUNKS:CHUNKS + 2], refs[CHUNKS + 2:-3]
+    mine_ref, send_ref, rows_ref = refs[-3:]
+    per, slots, _ = own_refs[0].shape
+    for c, ref in enumerate(own_refs):
         for e in range(per):
-            start = (index * per + e) * slots
-            rows_ref[start:start + slots] = ref[e].astype(F32)
+            i = c * per + e
+            done = ref[e].astype(F32) + from_a_ref[i].astype(F32) + from_b_ref[i].astype(F32)
+            rows_ref[i * slots:(i + 1) * slots] = done
+    for start, ref in zip(spans, piece_refs):
+        for e in range(ref.shape[0]):
+            rows_ref[(start + e) * slots:(start + e + 1) * slots] = ref[e].astype(F32)
     total = mm(gate_ref[...], rows_ref[...].astype(BF16), ((0,), (0,)))
     mine_ref[...] = total[0:tok] + emb_ref[...].astype(F32)
     send_ref[...] = total[tok:2 * tok].astype(BF16)
 
 
-def combine(gate, embedded, pieces):
+def combine(gate, embedded, own_parts, from_a, from_b, spans, pieces):
     tok, width = embedded.shape
     rows = gate.shape[0]
     return pl.pallas_call(
-        functools.partial(combine_kernel, tok),
-        out_shape=[jax.ShapeDtypeStruct((tok, width), F32), jax.ShapeDtypeStruct((tok, width), BF16)],
-        in_specs=[vmem()] * (2 + len(pieces)),
+        functools.partial(combine_kernel, tok, spans),
+        out_shape=[pltpu.VMEM((tok, width), F32), pltpu.VMEM((tok, width), BF16)],
+        in_specs=[vmem()] * (4 + len(own_parts) + len(pieces)),
         out_specs=[vmem()] * 2,
         scratch_shapes=[pltpu.VMEM((rows, width), F32)],
         compiler_params=pltpu.CompilerParams(vmem_limit_bytes=VMEM_LIMIT),
         cost_estimate=pl.CostEstimate(flops=4 * tok * rows * width, bytes_accessed=rows * width * 2, transcendentals=0),
         name="combine",
-    )(gate, embedded, *pieces)
+    )(gate, embedded, *own_parts, from_a, from_b, *pieces)
 
 
 def on_device(tubelets, embed_weight, norm_gain, routes, gate_codes, w_in, w_down):
@@ -282,53 +320,66 @@
 
         w_in, w_down = gathered(w_in), gathered(w_down)
 
-    in_sib = swapped(after(w_in, sib_normed, select), "rep", core_bit)
-    down_sib = swapped(after(w_down, sib_normed, select), "rep", core_bit)
     pieces = pack(select, normed, sib_normed, n_exp, half, cap)
-
-    def to_planes(p_own, from_a, from_b):
-        done = (p_own.astype(F32) + from_a.astype(F32) + from_b.astype(F32)).astype(BF16)
-        done = done.reshape(done.shape[0], n_exp, 2 * cap, done.shape[2])
-        return [done[:, 0]] + [swapped(done[:, s], "exp", s) for s in range(1, n_exp)]
-
-    split = half // CHUNKS // 2
+    per = half // CHUNKS
+    split = per // 2
     a_bit, b_bit = 1 << NEAR_A, 1 << NEAR_B
 
+    def to_a(rows):
+        return swapped(rows, "rep", a_bit)
+
+    def to_b(rows):
+        return swapped(rows, "rep", b_bit)
+
+    own = pieces[0][0]
+    first = swapped(pieces[1][0], "exp", 1)
+    far0 = jnp.concatenate([first[:per]] + [swapped(pieces[s][0], "exp", s) for s in range(2, n_exp)], axis=1)
+    own_a, own_b = to_a(own), to_b(own)
+    lent = lend(after(place, own_a, own_b), w_in, w_down)
+    own_d = to_b(own_a[:per]), to_a(own_b[per:])
+    far0, sib, *own_d = lax.optimization_barrier((far0, lent, *own_d))
+    sib = swapped(sib, "rep", core_bit)
+    late = lax.optimization_barrier((far0, *(pieces[s][1] for s in range(2, n_exp))))[1:]
+    far1 = jnp.concatenate([first[per:]] + [swapped(piece, "exp", s + 2) for s, piece in enumerate(late)], axis=1)
+    a0, b0 = to_a(far0), to_b(far0)
+    far1 = after(far1, a0, b0)
+    in_own, down_own = hold(after(place, far0), w_in, w_down)
+    a0, b0 = lax.optimization_barrier((a0, b0, in_own))[:2]
+    d0 = to_b(a0[:split]), to_a(b0[split:])
+    a1, b1 = to_a(far1), to_b(far1)
+    parts0 = experts(0, (far0, a0, b0, *d0, own, own_a, own_b, own_d[0]), sib, in_own, down_own)
+    a1, b1, *parts0 = lax.optimization_barrier((a1, b1, *parts0))
+    r0 = to_a(parts0[3]), to_b(parts0[4])
+    d1 = to_b(a1[:split]), to_a(b1[split:])
+
     def reduced(parts, r):
-        _, p_a, p_b, _, _ = parts
-        to_b = jnp.concatenate([p_b[:split] + r[0], p_b[split:]], axis=0)
-        to_a = jnp.concatenate([p_a[:split], p_a[split:] + r[1]], axis=0)
-        return to_a, to_b
-
-    per = half // CHUNKS
-    far0 = [swapped(pieces[s][0], "exp", s) for s in range(2, n_exp)]
-    first = swapped(pieces[1][0], "exp", 1)
-    in_own, down_own = hold(after(place, first), w_in, w_down)
-    own0 = after(jnp.concatenate([pieces[0][0], first[:per]] + far0, axis=1), in_own)
-    late = lax.optimization_barrier((own0, in_sib, *(pieces[s][1] for s in range(2, n_exp))))[2:]
-    own1 = jnp.concatenate(
-        [pieces[0][1], first[per:]] + [swapped(piece, "exp", s + 2) for s, piece in enumerate(late)], axis=1)
-    a0, b0 = swapped(own0, "rep", a_bit), swapped(own0, "rep", b_bit)
-    own1 = after(own1, a0, b0)
-    d0 = swapped(a0[:split], "rep", b_bit), swapped(b0[split:], "rep", a_bit)
-    a1, b1 = swapped(own1, "rep", a_bit), swapped(own1, "rep", b_bit)
-    parts0 = experts(place, 0, own0, a0, b0, *d0, in_own, in_sib, down_own, down_sib)
-    a1, b1, *parts0 = lax.optimization_barrier((a1, b1, *parts0))
-    r0 = swapped(parts0[3], "rep", a_bit), swapped(parts0[4], "rep", b_bit)
-    d1 = swapped(after(a1[:split], r0[0]), "rep", b_bit), swapped(b1[split:], "rep", a_bit)
-    to_a0, to_b0 = reduced(parts0, r0)
-    d1 = lax.optimization_barrier((*d1, to_a0, to_b0))[:2]
-    from_a0, from_b0 = swapped(to_a0, "rep", a_bit), swapped(to_b0, "rep", b_bit)
-    parts1 = list(experts(place, 1, own1, a1, b1, *d1, in_own, in_sib, down_own, down_sib))
-    parts1[4] = after(parts1[4], from_a0, from_b0)
-    r1 = swapped(parts1[3], "rep", a_bit), swapped(parts1[4], "rep", b_bit)
-    returned0 = to_planes(parts0[0], from_a0, from_b0)
-    to_a1, to_b1 = reduced(parts1, r1)
-    from_a1, from_b1 = swapped(to_a1, "rep", a_bit), swapped(to_b1, "rep", b_bit)
-    returned = [returned0, to_planes(parts1[0], from_a1, from_b1)]
-
-    pieces_back = [returned[c][s] for s in range(n_exp) for c in range(CHUNKS)]
-    mine, send = combine(gate, embedded, pieces_back)
+        return (jnp.concatenate([parts[1][:split], parts[1][split:] + r[1]], axis=0),
+                jnp.concatenate([parts[2][:split] + r[0], parts[2][split:]], axis=0))
+
+    def back(part, from_a, from_b):
+        done = (part.astype(F32) + from_a.astype(F32) + from_b.astype(F32)).astype(BF16)
+        shifts = jnp.split(done, n_exp - 1, axis=1)
+        return shifts[0], [swapped(rows, "exp", s + 2) for s, rows in enumerate(shifts[1:])]
+
+    sums0 = reduced(parts0, r0)
+    d1 = lax.optimization_barrier((*d1, *sums0))[:2]
+    from_a0, from_b0 = to_a(sums0[0]), to_b(sums0[1])
+    parts1 = experts(1, (far1, a1, b1, *d1, own, own_a, own_b, own_d[1]), sib, in_own, down_own)
+    parts1[3], parts1[4] = lax.optimization_barrier((parts1[3], parts1[4], from_a0, from_b0))[:2]
+    r1 = to_a(parts1[3]), to_b(parts1[4])
+    returned0 = back(parts0[0], from_a0, from_b0)
+    sums1 = reduced(parts1, r1)
+    from_a1, from_b1 = to_a(sums1[0]), to_b(sums1[1])
+    returned1 = back(parts1[0], from_a1, from_b1)
+    own_r = to_a(after(parts0[8], from_a0, from_b0)), to_b(after(parts1[8], from_a0, from_b0))
+    own_to_a = jnp.concatenate([parts0[6], parts1[6] + own_r[1]], axis=0)
+    own_to_b = jnp.concatenate([parts0[7] + own_r[0], parts1[7]], axis=0)
+    own_to_a, own_to_b = lax.optimization_barrier((own_to_a, own_to_b, *sums1))[:2]
+    spans = [half] + [s * half + c * per for s in range(2, n_exp) for c in range(CHUNKS)]
+    pieces_back = [swapped(jnp.concatenate([returned0[0], returned1[0]], axis=0), "exp", 1)]
+    pieces_back += [returned[s] for s in range(n_exp - 2) for returned in (returned0[1], returned1[1])]
+    mine, send = combine(
+        gate, embedded, (parts0[5], parts1[5]), to_a(own_to_a), to_b(own_to_b), spans, pieces_back)
     other = swapped(send, "rep", 1 << CORE)
     return (mine + other.astype(F32)).astype(BF16)
 

time: 95.3 us -> 92.1 us (0.966)
  waiting for transfers between devices: 35.2 us -> 19.3 us
  starting transfers between devices: 40.4 us -> 50.3 us
  Pallas kernels: 16.9 us -> 19.7 us
    ppermute x32 -> x38, waiting for transfers between devices: 35.2 us -> 19.3 us  [swapped(): lax.ppermute(array, axis, [(i, i ^ distance) for i in range(lax.axis_size...]
    ppermute x32 -> x38, starting transfers between devices: 40.4 us -> 50.3 us  [swapped(): lax.ppermute(array, axis, [(i, i ^ distance) for i in range(lax.axis_size...]
    pallas_call x3 -> x4, Pallas kernels: 9.05 us -> 11.9 us  [the longest x2 7.43 us: experts(): pl.pallas_call(functools.partial(experts_kernel, chunk), out_shape=[pltpu...]
  transfers between devices with their start and end apart: 32 -> 38, of which waited for: 19 -> 16; matrix products, arithmetic and copies ran while one was open for 1% -> 1% of each run, Pallas kernels for 15% -> 18%
where the time goes in v6:
time: 92.1 us; the launch traced here: 91.9 us
  starting transfers between devices  50.3 us (55%)
  Pallas kernels  19.7 us (21%)
  waiting for transfers between devices  19.3 us (21%)
  other arithmetic  2.19 us (2%)
    ppermute x38, starting transfers between devices, swapped(): lax.ppermute(array, axis, [(i, i ^ distance) for i in range(lax.axis_size...  50.3 us
    ppermute x38, waiting for transfers between devices, swapped(): lax.ppermute(array, axis, [(i, i ^ distance) for i in range(lax.axis_size...  19.3 us
    pallas_call x2, Pallas kernels, experts(): pl.pallas_call(functools.partial(experts_kernel, chunk), out_shape=[pltpu...  7.43 us
    pallas_call x1, Pallas kernels, lend(): pl.pallas_call(lend_kernel, out_shape=pltpu.VMEM(shape, BF16), in_specs=[...  4.02 us
    pallas_call x1, Pallas kernels, hold(): pl.pallas_call(hold_kernel, out_shape=[shape, shape], in_specs=[smem(), h...  4.02 us
    pallas_call x1, Pallas kernels, embed(): pl.pallas_call(embed_kernel, out_shape=[shape, shape], in_specs=[hbm()] *...  2.51 us
  transfers between devices with their start and end apart: 38, of which 16 were waited for; matrix products, arithmetic and copies ran while one was open for 1% of the time, Pallas kernels for 18%

profile of v6, /device:TPU:0, one launch (start us, length us, event | category | flops | bytes accessed | tf_op | source)
XLA Modules:
  0.0 91.9 jit_solution(1151907273671738840)
XLA Ops:
  0.7 2.5 %embed.1 = (bf16[128,1024]{1,0:T(8,128)(2,1)S(1)}, bf16[128,1024]{1,0:T(8,128)(2,1)S(1)}) custom-call(bf16[128,1536]{1,0:T(8,128)(2,1)} %tubelets_ref, bf16[1536,1024]{1,0:T(8,128)(2,1)} %weight_ref.1, f32[1,1024]{1,0:T(1,128)} %bitcast.5), custom_call_target="tpu_custom_call" | custom-call | flops 402653184 | bytes 3145728 | tf_op jit(solution)/shard_map/embed/pallas_call | solution.py:82
  6.2 2.9 %collective-permute-start.5 = (bf16[4,24,1024]{2,1,0:T(8,128)(2,1)S(1)}, bf16[4,24,1024]{2,1,0:T(8,128)(2,1)S(1)}, u32[]{:S(2)}, u32[]{:S(2)}) collective-permute-start(bf16[4,24,1024]{2,1,0:T(8,128)(2,1)S(1)} %get-tuple-element.76.refs_5_), channel_id=1, source_target_pairs={{0,8},{4,12},{8,0},{12,4},{16,24},{20,28},{24,16},{28,20},{1,9},{5... | collective-permute-start | bytes 589832 | tf_op jit(solution)/shard_map/ppermute | solution.py:20
  9.2 1.5 %collective-permute-start.6 = (bf16[4,24,1024]{2,1,0:T(8,128)(2,1)S(1)}, bf16[4,24,1024]{2,1,0:T(8,128)(2,1)S(1)}, u32[]{:S(2)}, u32[]{:S(2)}) collective-permute-start(bf16[4,24,1024]{2,1,0:T(8,128)(2,1)S(1)} %get-tuple-element.76.refs_5_), channel_id=1, source_target_pairs={{0,16},{4,20},{8,24},{12,28},{16,0},{20,4},{24,8},{28,12},{1,17},{... | collective-permute-start | bytes 589832 | tf_op jit(solution)/shard_map/ppermute | solution.py:20
  10.7 1.6 %collective-permute-start.2 = (bf16[4,24,1024]{2,1,0:T(8,128)(2,1)S(1)}, bf16[4,24,1024]{2,1,0:T(8,128)(2,1)S(1)}, u32[]{:S(2)}, u32[]{:S(2)}) collective-permute-start(bf16[4,24,1024]{2,1,0:T(8,128)(2,1)S(1)} %get-tuple-element.73), channel_id=1, source_target_pairs={{0,1},{1,0},{2,3},{3,2},{4,5},{5,4},{6,7},{7,6},{8,9},{9,8},{10,11... | collective-permute-start | bytes 589832 | tf_op jit(solution)/shard_map/ppermute | solution.py:20
  12.3 2.6 %collective-permute-start.3 = (bf16[2,24,1024]{2,1,0:T(8,128)(2,1)S(1)}, bf16[2,24,1024]{2,1,0:T(8,128)(2,1)S(1)}, u32[]{:S(2)}, u32[]{:S(2)}) collective-permute-start(bf16[2,24,1024]{2,1,0:T(8,128)(2,1)S(1)} %get-tuple-element.74), channel_id=1, source_target_pairs={{0,2},{1,3},{2,0},{3,1},{4,6},{5,7},{6,4},{7,5},{8,10},{9,11},{10,... | collective-permute-start | bytes 294920 | tf_op jit(solution)/shard_map/ppermute | solution.py:20
  16.2 1.6 %collective-permute-start.8 = (bf16[2,24,1024]{2,1,0:T(8,128)(2,1)S(1)}, bf16[2,24,1024]{2,1,0:T(8,128)(2,1)S(1)}, u32[]{:S(2)}, u32[]{:S(2)}) collective-permute-start(bf16[2,24,1024]{2,1,0:T(8,128)(2,1)S(1)} %slice.67), channel_id=1, source_target_pairs={{0,8},{4,12},{8,0},{12,4},{16,24},{20,28},{24,16},{28,20},{1,9},{5... | collective-permute-start | bytes 294920 | tf_op jit(solution)/shard_map/ppermute | solution.py:20
  17.8 1.3 %collective-permute-done.2 = bf16[4,24,1024]{2,1,0:T(8,128)(2,1)S(1)} collective-permute-done((bf16[4,24,1024]{2,1,0:T(8,128)(2,1)S(1)}, bf16[4,24,1024]{2,1,0:T(8,128)(2,1)S(1)}, u32[]{:S(2)}, u32[]{:S(2)}) %collective-permute-start.2) | collective-permute-done | bytes 196640 | tf_op jit(solution)/shard_map/ppermute | solution.py:20
  19.1 4.0 %lend.1 = bf16[2,4,1024,512]{3,2,1,0:T(8,128)(2,1)S(1)} custom-call(s32[2]{0:T(128)S(1)} %pad_add_fusion.1.place_ref, bf16[8,1024,512]{2,1,0:T(8,128)(2,1)} %in_ref.3, bf16[8,1024,512]{2,1,0:T(8,128)(2,1)} %down_ref.3), custom_call_target="tpu_custom_call" | custom-call | bytes 16777216 | tf_op jit(solution)/shard_map/lend/pallas_call | solution.py:183
  24.6 4.3 %collective-permute-start.10 = (bf16[2,24,1024]{2,1,0:T(8,128)(2,1)S(1)}, bf16[2,24,1024]{2,1,0:T(8,128)(2,1)S(1)}, u32[]{:S(2)}, u32[]{:S(2)}) collective-permute-start(bf16[2,24,1024]{2,1,0:T(8,128)(2,1)S(1)} %get-tuple-element.82), channel_id=1, source_target_pairs={{0,3},{1,2},{2,1},{3,0},{4,7},{5,6},{6,5},{7,4},{8,11},{9,10},{10,... | collective-permute-start | bytes 294920 | tf_op jit(solution)/shard_map/ppermute | solution.py:20
  28.9 4.0 %hold.1 = (bf16[4,1024,512]{2,1,0:T(8,128)(2,1)S(1)}, bf16[4,1024,512]{2,1,0:T(8,128)(2,1)S(1)}) custom-call(s32[2]{0:T(128)S(1)} %pad_add_fusion.1.place_ref, bf16[8,1024,512]{2,1,0:T(8,128)(2,1)} %in_ref.3, bf16[8,1024,512]{2,1,0:T(8,128)(2,1)} %down_ref.3), custom_call_target="tpu_custom_call" | custom-call | bytes 16777216 | tf_op jit(solution)/shard_map/hold/pallas_call | solution.py:209
  33.2 1.4 %collective-permute-start.15 = (bf16[1,72,1024]{2,1,0:T(8,128)(2,1)S(1)}, bf16[1,72,1024]{2,1,0:T(8,128)(2,1)S(1)}, u32[]{:S(2)}, u32[]{:S(2)}) collective-permute-start(bf16[1,72,1024]{2,1,0:T(8,128)(2,1)S(1)} %slice.52), channel_id=1, source_target_pairs={{0,16},{4,20},{8,24},{12,28},{16,0},{20,4},{24,8},{28,12},{1,17},{... | collective-permute-start | bytes 442376 | tf_op jit(solution)/shard_map/ppermute | solution.py:20
  34.6 1.6 %collective-permute-start.16 = (bf16[1,72,1024]{2,1,0:T(8,128)(2,1)S(1)}, bf16[1,72,1024]{2,1,0:T(8,128)(2,1)S(1)}, u32[]{:S(2)}, u32[]{:S(2)}) collective-permute-start(bf16[1,72,1024]{2,1,0:T(8,128)(2,1)S(1)} %slice.53), channel_id=1, source_target_pairs={{0,8},{4,12},{8,0},{12,4},{16,24},{20,28},{24,16},{28,20},{1,9},{5... | collective-permute-start | bytes 442376 | tf_op jit(solution)/shard_map/ppermute | solution.py:20
  36.2 1.6 %collective-permute-start.13 = (bf16[2,72,1024]{2,1,0:T(8,128)(2,1)S(1)}, bf16[2,72,1024]{2,1,0:T(8,128)(2,1)S(1)}, u32[]{:S(2)}, u32[]{:S(2)}) collective-permute-start(bf16[2,72,1024]{2,1,0:T(8,128)(2,1)S(1)} %pad_maximum_fusion.1.refs_0_), channel_id=1, source_target_pairs={{0,8},{4,12},{8,0},{12,4},{16,24},{20,28},{24,16},{28,20},{1,9},{5... | collective-permute-start | bytes 884744 | tf_op jit(solution)/shard_map/ppermute | solution.py:20
  37.8 1.5 %collective-permute-start.14 = (bf16[2,72,1024]{2,1,0:T(8,128)(2,1)S(1)}, bf16[2,72,1024]{2,1,0:T(8,128)(2,1)S(1)}, u32[]{:S(2)}, u32[]{:S(2)}) collective-permute-start(bf16[2,72,1024]{2,1,0:T(8,128)(2,1)S(1)} %pad_maximum_fusion.1.refs_0_), channel_id=1, source_target_pairs={{0,16},{4,20},{8,24},{12,28},{16,0},{20,4},{24,8},{28,12},{1,17},{... | collective-permute-start | bytes 884744 | tf_op jit(solution)/shard_map/ppermute | solution.py:20
  39.3 1.4 %collective-permute-done.16.refs_4_ = bf16[1,72,1024]{2,1,0:T(8,128)(2,1)S(1)} collective-permute-done((bf16[1,72,1024]{2,1,0:T(8,128)(2,1)S(1)}, bf16[1,72,1024]{2,1,0:T(8,128)(2,1)S(1)}, u32[]{:S(2)}, u32[]{:S(2)}) %collective-permute-start.16) | collective-permute-done | bytes 147488 | tf_op jit(solution)/shard_map/ppermute | solution.py:20
  40.7 3.7 %experts.2 = (bf16[2,72,1024]{2,1,0:T(8,128)(2,1)S(1)}, bf16[2,72,1024]{2,1,0:T(8,128)(2,1)S(1)}, bf16[2,72,1024]{2,1,0:T(8,128)(2,1)S(1)}, bf16[1,72,1024]{2,1,...) custom-call(bf16[2,72,1024]{2,1,0:T(8,128)(2,1)S(1)} %pad_maximum_fu, ...), custom_call_target="tpu_custom_call" | custom-call | flops 3221225472 | bytes 3145728 | tf_op jit(solution)/shard_map/experts/pallas_call | solution.py:252
  44.4 1.7 %collective-permute-done.13.refs_1_ = bf16[2,72,1024]{2,1,0:T(8,128)(2,1)S(1)} collective-permute-done((bf16[2,72,1024]{2,1,0:T(8,128)(2,1)S(1)}, bf16[2,72,1024]{2,1,0:T(8,128)(2,1)S(1)}, u32[]{:S(2)}, u32[]{:S(2)}) %collective-permute-start.13) | collective-permute-done | bytes 294944 | tf_op jit(solution)/shard_map/ppermute | solution.py:20
  50.7 1.8 %collective-permute-done.21 = bf16[1,72,1024]{2,1,0:T(8,128)(2,1)S(1)} collective-permute-done((bf16[1,72,1024]{2,1,0:T(8,128)(2,1)S(1)}, bf16[1,72,1024]{2,1,0:T(8,128)(2,1)S(1)}, u32[]{:S(2)}, u32[]{:S(2)}) %collective-permute-start.21) | collective-permute-done | bytes 147488 | tf_op jit(solution)/shard_map/ppermute | solution.py:20
  52.6 2.3 %collective-permute-start.23 = (bf16[2,72,1024]{2,1,0:T(8,128)(2,1)S(1)}, bf16[2,72,1024]{2,1,0:T(8,128)(2,1)S(1)}, u32[]{:S(2)}, u32[]{:S(2)}) collective-permute-start(bf16[2,72,1024]{2,1,0:T(8,128)(2,1)S(1)} %pad_maximum_fusion.3), channel_id=1, source_target_pairs={{0,16},{4,20},{8,24},{12,28},{16,0},{20,4},{24,8},{28,12},{1,17},{... | collective-permute-start | bytes 884744 | tf_op jit(solution)/shard_map/ppermute | solution.py:20
  55.4 2.1 %collective-permute-done.18.refs_3_ = bf16[1,72,1024]{2,1,0:T(8,128)(2,1)S(1)} collective-permute-done((bf16[1,72,1024]{2,1,0:T(8,128)(2,1)S(1)}, bf16[1,72,1024]{2,1,0:T(8,128)(2,1)S(1)}, u32[]{:S(2)}, u32[]{:S(2)}) %collective-permute-start.18) | collective-permute-done | bytes 147488 | tf_op jit(solution)/shard_map/ppermute | solution.py:20
  57.6 3.7 %experts.3 = (bf16[2,72,1024]{2,1,0:T(8,128)(2,1)S(1)}, bf16[2,72,1024]{2,1,0:T(8,128)(2,1)S(1)}, bf16[2,72,1024]{2,1,0:T(8,128)(2,1)S(1)}, bf16[1,72,1024]{2,1,...) custom-call(bf16[2,72,1024]{2,1,0:T(8,128)(2,1)S(1)} %pad_maximum_fu, ...), custom_call_target="tpu_custom_call" | custom-call | flops 3221225472 | bytes 3145728 | tf_op jit(solution)/shard_map/experts/pallas_call | solution.py:252
  62.7 1.2 %collective-permute-start.27 = (bf16[1,72,1024]{2,1,0:T(8,128)(2,1)S(1)}, bf16[1,72,1024]{2,1,0:T(8,128)(2,1)S(1)}, u32[]{:S(2)}, u32[]{:S(2)}) collective-permute-start(bf16[1,72,1024]{2,1,0:T(8,128)(2,1)S(1)} %get-tuple-element.124), channel_id=1, source_target_pairs={{0,8},{4,12},{8,0},{12,4},{16,24},{20,28},{24,16},{28,20},{1,9},{5... | collective-permute-start | bytes 442376 | tf_op jit(solution)/shard_map/ppermute | solution.py:20
  67.9 1.4 %collective-permute-start.31 = (bf16[2,72,1024]{2,1,0:T(8,128)(2,1)S(1)}, bf16[2,72,1024]{2,1,0:T(8,128)(2,1)S(1)}, u32[]{:S(2)}, u32[]{:S(2)}) collective-permute-start(bf16[2,72,1024]{2,1,0:T(8,128)(2,1)S(1)} %pad_maximum_fusion.5), channel_id=1, source_target_pairs={{0,16},{4,20},{8,24},{12,28},{16,0},{20,4},{24,8},{28,12},{1,17},{... | collective-permute-start | bytes 884744 | tf_op jit(solution)/shard_map/ppermute | solution.py:20
  70.0 2.8 %collective-permute-start.33 = (bf16[2,24,1024]{2,1,0:T(8,128)(2,1)S(1)}, bf16[2,24,1024]{2,1,0:T(8,128)(2,1)S(1)}, u32[]{:S(2)}, u32[]{:S(2)}) collective-permute-start(bf16[2,24,1024]{2,1,0:T(8,128)(2,1)S(1)} %get-tuple-element.135), channel_id=1, source_target_pairs={{0,2},{1,3},{2,0},{3,1},{4,6},{5,7},{6,4},{7,5},{8,10},{9,11},{10,... | collective-permute-start | bytes 294920 | tf_op jit(solution)/shard_map/ppermute | solution.py:20
  72.7 1.8 %collective-permute-start.35 = (bf16[2,24,1024]{2,1,0:T(8,128)(2,1)S(1)}, bf16[2,24,1024]{2,1,0:T(8,128)(2,1)S(1)}, u32[]{:S(2)}, u32[]{:S(2)}) collective-permute-start(bf16[2,24,1024]{2,1,0:T(8,128)(2,1)S(1)} %get-tuple-element.134), channel_id=1, source_target_pairs={{0,3},{1,2},{2,1},{3,0},{4,7},{5,6},{6,5},{7,4},{8,11},{9,10},{10,... | collective-permute-start | bytes 294920 | tf_op jit(solution)/shard_map/ppermute | solution.py:20
  75.8 1.4 %collective-permute-start.29 = (bf16[4,24,1024]{2,1,0:T(8,128)(2,1)S(1)}, bf16[4,24,1024]{2,1,0:T(8,128)(2,1)S(1)}, u32[]{:S(2)}, u32[]{:S(2)}) collective-permute-start(bf16[4,24,1024]{2,1,0:T(8,128)(2,1)S(1)} %pad_maximum_fusion.7), channel_id=1, source_target_pairs={{0,16},{4,20},{8,24},{12,28},{16,0},{20,4},{24,8},{28,12},{1,17},{... | collective-permute-start | bytes 589832 | tf_op jit(solution)/shard_map/ppermute | solution.py:20
  77.5 2.6 %collective-permute-start.32 = (bf16[4,24,1024]{2,1,0:T(8,128)(2,1)S(1)}, bf16[4,24,1024]{2,1,0:T(8,128)(2,1)S(1)}, u32[]{:S(2)}, u32[]{:S(2)}) collective-permute-start(bf16[4,24,1024]{2,1,0:T(8,128)(2,1)S(1)} %pad_maximum_fusion.8), channel_id=1, source_target_pairs={{0,1},{1,0},{2,3},{3,2},{4,5},{5,4},{6,7},{7,6},{8,9},{9,8},{10,11... | collective-permute-start | bytes 589832 | tf_op jit(solution)/shard_map/ppermute | solution.py:20
  80.1 2.5 %collective-permute-start.34 = (bf16[2,24,1024]{2,1,0:T(8,128)(2,1)S(1)}, bf16[2,24,1024]{2,1,0:T(8,128)(2,1)S(1)}, u32[]{:S(2)}, u32[]{:S(2)}) collective-permute-start(bf16[2,24,1024]{2,1,0:T(8,128)(2,1)S(1)} %get-tuple-element.132), channel_id=1, source_target_pairs={{0,2},{1,3},{2,0},{3,1},{4,6},{5,7},{6,4},{7,5},{8,10},{9,11},{10,... | collective-permute-start | bytes 294920 | tf_op jit(solution)/shard_map/ppermute | solution.py:20
  82.6 1.4 %collective-permute-start.36 = (bf16[2,24,1024]{2,1,0:T(8,128)(2,1)S(1)}, bf16[2,24,1024]{2,1,0:T(8,128)(2,1)S(1)}, u32[]{:S(2)}, u32[]{:S(2)}) collective-permute-start(bf16[2,24,1024]{2,1,0:T(8,128)(2,1)S(1)} %get-tuple-element.131), channel_id=1, source_target_pairs={{0,3},{1,2},{2,1},{3,0},{4,7},{5,6},{6,5},{7,4},{8,11},{9,10},{10,... | collective-permute-start | bytes 294920 | tf_op jit(solution)/shard_map/ppermute | solution.py:20
  84.0 1.6 %collective-permute-done.34.refs_6_ = bf16[2,24,1024]{2,1,0:T(8,128)(2,1)S(1)} collective-permute-done((bf16[2,24,1024]{2,1,0:T(8,128)(2,1)S(1)}, bf16[2,24,1024]{2,1,0:T(8,128)(2,1)S(1)}, u32[]{:S(2)}, u32[]{:S(2)}) %collective-permute-start.34) | collective-permute-done | bytes 98336 | tf_op jit(solution)/shard_map/ppermute | solution.py:20
  85.6 3.5 %collective-permute-done.36.refs_8_ = bf16[2,24,1024]{2,1,0:T(8,128)(2,1)S(1)} collective-permute-done((bf16[2,24,1024]{2,1,0:T(8,128)(2,1)S(1)}, bf16[2,24,1024]{2,1,0:T(8,128)(2,1)S(1)}, u32[]{:S(2)}, u32[]{:S(2)}) %collective-permute-start.36) | collective-permute-done | bytes 98336 | tf_op jit(solution)/shard_map/ppermute | solution.py:20
  89.7 1.5 %collective-permute-done.37 = bf16[128,1024]{1,0:T(8,128)(2,1)S(1)} collective-permute-done((bf16[128,1024]{1,0:T(8,128)(2,1)S(1)}, bf16[128,1024]{1,0:T(8,128)(2,1)S(1)}, u32[]{:S(2)}, u32[]{:S(2)}) %collective-permute-start.37) | collective-permute-done | bytes 262176 | tf_op jit(solution)/shard_map/ppermute | solution.py:20
  (80 shorter events, 20.8 us)
Async XLA Ops:
  6.2 8.8 %collective-permute-start.5 = (bf16[4,24,1024]{2,1,0:T(8,128)(2,1)S(1)}, bf16[4,24,1024]{2,1,0:T(8,128)(2,1)S(1)}, u32[]{:S(2)}, u32[]{:S(2)}) collective-permute-start(bf16[4,24,1024]{2,1,0:T(8,128)(2,1)S(1)} %get-tuple-element.76.refs_5_), channel_id=1, source_target_pairs={{0,8},{4,12},{8,0},{12,4},{16,24},{20,28},{24,16},{28,20},{1,9},{5... | collective-permute-start | bytes 589832 | tf_op jit(solution)/shard_map/ppermute | solution.py:20
  9.2 7.0 %collective-permute-start.6 = (bf16[4,24,1024]{2,1,0:T(8,128)(2,1)S(1)}, bf16[4,24,1024]{2,1,0:T(8,128)(2,1)S(1)}, u32[]{:S(2)}, u32[]{:S(2)}) collective-permute-start(bf16[4,24,1024]{2,1,0:T(8,128)(2,1)S(1)} %get-tuple-element.76.refs_5_), channel_id=1, source_target_pairs={{0,16},{4,20},{8,24},{12,28},{16,0},{20,4},{24,8},{28,12},{1,17},{... | collective-permute-start | bytes 589832 | tf_op jit(solution)/shard_map/ppermute | solution.py:20
  10.7 8.4 %collective-permute-start.2 = (bf16[4,24,1024]{2,1,0:T(8,128)(2,1)S(1)}, bf16[4,24,1024]{2,1,0:T(8,128)(2,1)S(1)}, u32[]{:S(2)}, u32[]{:S(2)}) collective-permute-start(bf16[4,24,1024]{2,1,0:T(8,128)(2,1)S(1)} %get-tuple-element.73), channel_id=1, source_target_pairs={{0,1},{1,0},{2,3},{3,2},{4,5},{5,4},{6,7},{7,6},{8,9},{9,8},{10,11... | collective-permute-start | bytes 589832 | tf_op jit(solution)/shard_map/ppermute | solution.py:20
  12.3 10.9 %collective-permute-start.3 = (bf16[2,24,1024]{2,1,0:T(8,128)(2,1)S(1)}, bf16[2,24,1024]{2,1,0:T(8,128)(2,1)S(1)}, u32[]{:S(2)}, u32[]{:S(2)}) collective-permute-start(bf16[2,24,1024]{2,1,0:T(8,128)(2,1)S(1)} %get-tuple-element.74), channel_id=1, source_target_pairs={{0,2},{1,3},{2,0},{3,1},{4,6},{5,7},{6,4},{7,5},{8,10},{9,11},{10,... | collective-permute-start | bytes 294920 | tf_op jit(solution)/shard_map/ppermute | solution.py:20
  14.8 8.6 %collective-permute-start.4 = (bf16[2,24,1024]{2,1,0:T(8,128)(2,1)S(1)}, bf16[2,24,1024]{2,1,0:T(8,128)(2,1)S(1)}, u32[]{:S(2)}, u32[]{:S(2)}) collective-permute-start(bf16[2,24,1024]{2,1,0:T(8,128)(2,1)S(1)} %get-tuple-element.75), channel_id=1, source_target_pairs={{0,3},{1,2},{2,1},{3,0},{4,7},{5,6},{6,5},{7,4},{8,11},{9,10},{10,... | collective-permute-start | bytes 294920 | tf_op jit(solution)/shard_map/ppermute | solution.py:20
  15.1 8.4 %collective-permute-start.7 = (bf16[2,24,1024]{2,1,0:T(8,128)(2,1)S(1)}, bf16[2,24,1024]{2,1,0:T(8,128)(2,1)S(1)}, u32[]{:S(2)}, u32[]{:S(2)}) collective-permute-start(bf16[2,24,1024]{2,1,0:T(8,128)(2,1)S(1)} %slice.66), channel_id=1, source_target_pairs={{0,16},{4,20},{8,24},{12,28},{16,0},{20,4},{24,8},{28,12},{1,17},{... | collective-permute-start | bytes 294920 | tf_op jit(solution)/shard_map/ppermute | solution.py:20
  16.2 7.2 %collective-permute-start.8 = (bf16[2,24,1024]{2,1,0:T(8,128)(2,1)S(1)}, bf16[2,24,1024]{2,1,0:T(8,128)(2,1)S(1)}, u32[]{:S(2)}, u32[]{:S(2)}) collective-permute-start(bf16[2,24,1024]{2,1,0:T(8,128)(2,1)S(1)} %slice.67), channel_id=1, source_target_pairs={{0,8},{4,12},{8,0},{12,4},{16,24},{20,28},{24,16},{28,20},{1,9},{5... | collective-permute-start | bytes 294920 | tf_op jit(solution)/shard_map/ppermute | solution.py:20
  23.5 17.3 %collective-permute-start.17 = (bf16[2,4,1024,512]{3,2,1,0:T(8,128)(2,1)S(1)}, bf16[2,4,1024,512]{3,2,1,0:T(8,128)(2,1)S(1)}, u32[]{:S(2)}, u32[]{:S(2)}) collective-permute-start(bf16[2,4,1024,512]{3,2,1,0:T(8,128)(2,1)S(1)} %lend.1), channel_id=1, source_target_pairs={{0,4},{4,0},{8,12},{12,8},{16,20},{20,16},{24,28},{28,24},{1,5},{5... | collective-permute-start | bytes 25165832 | tf_op jit(solution)/shard_map/ppermute | solution.py:20
  23.5 9.4 %collective-permute-start.11 = (bf16[2,72,1024]{2,1,0:T(8,128)(2,1)S(1)}, bf16[2,72,1024]{2,1,0:T(8,128)(2,1)S(1)}, u32[]{:S(2)}, u32[]{:S(2)}) collective-permute-start(bf16[2,72,1024]{2,1,0:T(8,128)(2,1)S(1)} %pad_maximum_fusion.refs_0_), channel_id=1, source_target_pairs={{0,8},{4,12},{8,0},{12,4},{16,24},{20,28},{24,16},{28,20},{1,9},{5... | collective-permute-start | bytes 884744 | tf_op jit(solution)/shard_map/ppermute | solution.py:20
  24.1 9.1 %collective-permute-start.12 = (bf16[2,72,1024]{2,1,0:T(8,128)(2,1)S(1)}, bf16[2,72,1024]{2,1,0:T(8,128)(2,1)S(1)}, u32[]{:S(2)}, u32[]{:S(2)}) collective-permute-start(bf16[2,72,1024]{2,1,0:T(8,128)(2,1)S(1)} %pad_maximum_fusion.refs_0_), channel_id=1, source_target_pairs={{0,16},{4,20},{8,24},{12,28},{16,0},{20,4},{24,8},{28,12},{1,17},{... | collective-permute-start | bytes 884744 | tf_op jit(solution)/shard_map/ppermute | solution.py:20
  24.6 11.5 %collective-permute-start.10 = (bf16[2,24,1024]{2,1,0:T(8,128)(2,1)S(1)}, bf16[2,24,1024]{2,1,0:T(8,128)(2,1)S(1)}, u32[]{:S(2)}, u32[]{:S(2)}) collective-permute-start(bf16[2,24,1024]{2,1,0:T(8,128)(2,1)S(1)} %get-tuple-element.82), channel_id=1, source_target_pairs={{0,3},{1,2},{2,1},{3,0},{4,7},{5,6},{6,5},{7,4},{8,11},{9,10},{10,... | collective-permute-start | bytes 294920 | tf_op jit(solution)/shard_map/ppermute | solution.py:20
  28.9 7.3 %collective-permute-start.9 = (bf16[2,24,1024]{2,1,0:T(8,128)(2,1)S(1)}, bf16[2,24,1024]{2,1,0:T(8,128)(2,1)S(1)}, u32[]{:S(2)}, u32[]{:S(2)}) collective-permute-start(bf16[2,24,1024]{2,1,0:T(8,128)(2,1)S(1)} %get-tuple-element.81), channel_id=1, source_target_pairs={{0,2},{1,3},{2,0},{3,1},{4,6},{5,7},{6,4},{7,5},{8,10},{9,11},{10,... | collective-permute-start | bytes 294920 | tf_op jit(solution)/shard_map/ppermute | solution.py:20
  33.2 6.1 %collective-permute-start.15 = (bf16[1,72,1024]{2,1,0:T(8,128)(2,1)S(1)}, bf16[1,72,1024]{2,1,0:T(8,128)(2,1)S(1)}, u32[]{:S(2)}, u32[]{:S(2)}) collective-permute-start(bf16[1,72,1024]{2,1,0:T(8,128)(2,1)S(1)} %slice.52), channel_id=1, source_target_pairs={{0,16},{4,20},{8,24},{12,28},{16,0},{20,4},{24,8},{28,12},{1,17},{... | collective-permute-start | bytes 442376 | tf_op jit(solution)/shard_map/ppermute | solution.py:20
  34.6 6.1 %collective-permute-start.16 = (bf16[1,72,1024]{2,1,0:T(8,128)(2,1)S(1)}, bf16[1,72,1024]{2,1,0:T(8,128)(2,1)S(1)}, u32[]{:S(2)}, u32[]{:S(2)}) collective-permute-start(bf16[1,72,1024]{2,1,0:T(8,128)(2,1)S(1)} %slice.53), channel_id=1, source_target_pairs={{0,8},{4,12},{8,0},{12,4},{16,24},{20,28},{24,16},{28,20},{1,9},{5... | collective-permute-start | bytes 442376 | tf_op jit(solution)/shard_map/ppermute | solution.py:20
  36.2 9.9 %collective-permute-start.13 = (bf16[2,72,1024]{2,1,0:T(8,128)(2,1)S(1)}, bf16[2,72,1024]{2,1,0:T(8,128)(2,1)S(1)}, u32[]{:S(2)}, u32[]{:S(2)}) collective-permute-start(bf16[2,72,1024]{2,1,0:T(8,128)(2,1)S(1)} %pad_maximum_fusion.1.refs_0_), channel_id=1, source_target_pairs={{0,8},{4,12},{8,0},{12,4},{16,24},{20,28},{24,16},{28,20},{1,9},{5... | collective-permute-start | bytes 884744 | tf_op jit(solution)/shard_map/ppermute | solution.py:20
  37.8 8.7 %collective-permute-start.14 = (bf16[2,72,1024]{2,1,0:T(8,128)(2,1)S(1)}, bf16[2,72,1024]{2,1,0:T(8,128)(2,1)S(1)}, u32[]{:S(2)}, u32[]{:S(2)}) collective-permute-start(bf16[2,72,1024]{2,1,0:T(8,128)(2,1)S(1)} %pad_maximum_fusion.1.refs_0_), channel_id=1, source_target_pairs={{0,16},{4,20},{8,24},{12,28},{16,0},{20,4},{24,8},{28,12},{1,17},{... | collective-permute-start | bytes 884744 | tf_op jit(solution)/shard_map/ppermute | solution.py:20
  46.5 6.0 %collective-permute-start.21 = (bf16[1,72,1024]{2,1,0:T(8,128)(2,1)S(1)}, bf16[1,72,1024]{2,1,0:T(8,128)(2,1)S(1)}, u32[]{:S(2)}, u32[]{:S(2)}) collective-permute-start(bf16[1,72,1024]{2,1,0:T(8,128)(2,1)S(1)} %get-tuple-element.106), channel_id=1, source_target_pairs={{0,8},{4,12},{8,0},{12,4},{16,24},{20,28},{24,16},{28,20},{1,9},{5... | collective-permute-start | bytes 442376 | tf_op jit(solution)/shard_map/ppermute | solution.py:20
  47.6 7.2 %collective-permute-start.20 = (bf16[1,72,1024]{2,1,0:T(8,128)(2,1)S(1)}, bf16[1,72,1024]{2,1,0:T(8,128)(2,1)S(1)}, u32[]{:S(2)}, u32[]{:S(2)}) collective-permute-start(bf16[1,72,1024]{2,1,0:T(8,128)(2,1)S(1)} %get-tuple-element.104), channel_id=1, source_target_pairs={{0,16},{4,20},{8,24},{12,28},{16,0},{20,4},{24,8},{28,12},{1,17},{... | collective-permute-start | bytes 442376 | tf_op jit(solution)/shard_map/ppermute | solution.py:20
  48.6 9.0 %collective-permute-start.18 = (bf16[1,72,1024]{2,1,0:T(8,128)(2,1)S(1)}, bf16[1,72,1024]{2,1,0:T(8,128)(2,1)S(1)}, u32[]{:S(2)}, u32[]{:S(2)}) collective-permute-start(bf16[1,72,1024]{2,1,0:T(8,128)(2,1)S(1)} %slice.54), channel_id=1, source_target_pairs={{0,16},{4,20},{8,24},{12,28},{16,0},{20,4},{24,8},{28,12},{1,17},{... | collective-permute-start | bytes 442376 | tf_op jit(solution)/shard_map/ppermute | solution.py:20
  49.8 7.8 %collective-permute-start.19 = (bf16[1,72,1024]{2,1,0:T(8,128)(2,1)S(1)}, bf16[1,72,1024]{2,1,0:T(8,128)(2,1)S(1)}, u32[]{:S(2)}, u32[]{:S(2)}) collective-permute-start(bf16[1,72,1024]{2,1,0:T(8,128)(2,1)S(1)} %slice.55), channel_id=1, source_target_pairs={{0,8},{4,12},{8,0},{12,4},{16,24},{20,28},{24,16},{28,20},{1,9},{5... | collective-permute-start | bytes 442376 | tf_op jit(solution)/shard_map/ppermute | solution.py:20
  52.6 9.2 %collective-permute-start.23 = (bf16[2,72,1024]{2,1,0:T(8,128)(2,1)S(1)}, bf16[2,72,1024]{2,1,0:T(8,128)(2,1)S(1)}, u32[]{:S(2)}, u32[]{:S(2)}) collective-permute-start(bf16[2,72,1024]{2,1,0:T(8,128)(2,1)S(1)} %pad_maximum_fusion.3), channel_id=1, source_target_pairs={{0,16},{4,20},{8,24},{12,28},{16,0},{20,4},{24,8},{28,12},{1,17},{... | collective-permute-start | bytes 884744 | tf_op jit(solution)/shard_map/ppermute | solution.py:20
  54.9 6.9 %collective-permute-start.22 = (bf16[2,72,1024]{2,1,0:T(8,128)(2,1)S(1)}, bf16[2,72,1024]{2,1,0:T(8,128)(2,1)S(1)}, u32[]{:S(2)}, u32[]{:S(2)}) collective-permute-start(bf16[2,72,1024]{2,1,0:T(8,128)(2,1)S(1)} %pad_maximum_fusion.2), channel_id=1, source_target_pairs={{0,8},{4,12},{8,0},{12,4},{16,24},{20,28},{24,16},{28,20},{1,9},{5... | collective-permute-start | bytes 884744 | tf_op jit(solution)/shard_map/ppermute | solution.py:20
  63.9 8.9 %collective-permute-start.25 = (bf16[2,24,1024]{2,1,0:T(8,128)(2,1)S(1)}, bf16[2,24,1024]{2,1,0:T(8,128)(2,1)S(1)}, u32[]{:S(2)}, u32[]{:S(2)}) collective-permute-start(bf16[2,24,1024]{2,1,0:T(8,128)(2,1)S(1)} %get-tuple-element.117), channel_id=1, source_target_pairs={{0,8},{4,12},{8,0},{12,4},{16,24},{20,28},{24,16},{28,20},{1,9},{5... | collective-permute-start | bytes 294920 | tf_op jit(solution)/shard_map/ppermute | solution.py:20
  64.7 9.9 %collective-permute-start.24 = (bf16[2,24,1024]{2,1,0:T(8,128)(2,1)S(1)}, bf16[2,24,1024]{2,1,0:T(8,128)(2,1)S(1)}, u32[]{:S(2)}, u32[]{:S(2)}) collective-permute-start(bf16[2,24,1024]{2,1,0:T(8,128)(2,1)S(1)} %get-tuple-element.114), channel_id=1, source_target_pairs={{0,16},{4,20},{8,24},{12,28},{16,0},{20,4},{24,8},{28,12},{1,17},{... | collective-permute-start | bytes 294920 | tf_op jit(solution)/shard_map/ppermute | solution.py:20
  67.9 7.9 %collective-permute-start.31 = (bf16[2,72,1024]{2,1,0:T(8,128)(2,1)S(1)}, bf16[2,72,1024]{2,1,0:T(8,128)(2,1)S(1)}, u32[]{:S(2)}, u32[]{:S(2)}) collective-permute-start(bf16[2,72,1024]{2,1,0:T(8,128)(2,1)S(1)} %pad_maximum_fusion.5), channel_id=1, source_target_pairs={{0,16},{4,20},{8,24},{12,28},{16,0},{20,4},{24,8},{28,12},{1,17},{... | collective-permute-start | bytes 884744 | tf_op jit(solution)/shard_map/ppermute | solution.py:20
  69.3 8.0 %collective-permute-start.30 = (bf16[2,72,1024]{2,1,0:T(8,128)(2,1)S(1)}, bf16[2,72,1024]{2,1,0:T(8,128)(2,1)S(1)}, u32[]{:S(2)}, u32[]{:S(2)}) collective-permute-start(bf16[2,72,1024]{2,1,0:T(8,128)(2,1)S(1)} %pad_maximum_fusion.4), channel_id=1, source_target_pairs={{0,8},{4,12},{8,0},{12,4},{16,24},{20,28},{24,16},{28,20},{1,9},{5... | collective-permute-start | bytes 884744 | tf_op jit(solution)/shard_map/ppermute | solution.py:20
  70.0 10.1 %collective-permute-start.33 = (bf16[2,24,1024]{2,1,0:T(8,128)(2,1)S(1)}, bf16[2,24,1024]{2,1,0:T(8,128)(2,1)S(1)}, u32[]{:S(2)}, u32[]{:S(2)}) collective-permute-start(bf16[2,24,1024]{2,1,0:T(8,128)(2,1)S(1)} %get-tuple-element.135), channel_id=1, source_target_pairs={{0,2},{1,3},{2,0},{3,1},{4,6},{5,7},{6,4},{7,5},{8,10},{9,11},{10,... | collective-permute-start | bytes 294920 | tf_op jit(solution)/shard_map/ppermute | solution.py:20
  72.7 9.9 %collective-permute-start.35 = (bf16[2,24,1024]{2,1,0:T(8,128)(2,1)S(1)}, bf16[2,24,1024]{2,1,0:T(8,128)(2,1)S(1)}, u32[]{:S(2)}, u32[]{:S(2)}) collective-permute-start(bf16[2,24,1024]{2,1,0:T(8,128)(2,1)S(1)} %get-tuple-element.134), channel_id=1, source_target_pairs={{0,3},{1,2},{2,1},{3,0},{4,7},{5,6},{6,5},{7,4},{8,11},{9,10},{10,... | collective-permute-start | bytes 294920 | tf_op jit(solution)/shard_map/ppermute | solution.py:20
  74.7 9.3 %collective-permute-start.28 = (bf16[4,24,1024]{2,1,0:T(8,128)(2,1)S(1)}, bf16[4,24,1024]{2,1,0:T(8,128)(2,1)S(1)}, u32[]{:S(2)}, u32[]{:S(2)}) collective-permute-start(bf16[4,24,1024]{2,1,0:T(8,128)(2,1)S(1)} %pad_maximum_fusion.6), channel_id=1, source_target_pairs={{0,8},{4,12},{8,0},{12,4},{16,24},{20,28},{24,16},{28,20},{1,9},{5... | collective-permute-start | bytes 589832 | tf_op jit(solution)/shard_map/ppermute | solution.py:20
  75.8 8.3 %collective-permute-start.29 = (bf16[4,24,1024]{2,1,0:T(8,128)(2,1)S(1)}, bf16[4,24,1024]{2,1,0:T(8,128)(2,1)S(1)}, u32[]{:S(2)}, u32[]{:S(2)}) collective-permute-start(bf16[4,24,1024]{2,1,0:T(8,128)(2,1)S(1)} %pad_maximum_fusion.7), channel_id=1, source_target_pairs={{0,16},{4,20},{8,24},{12,28},{16,0},{20,4},{24,8},{28,12},{1,17},{... | collective-permute-start | bytes 589832 | tf_op jit(solution)/shard_map/ppermute | solution.py:20
  77.5 11.6 %collective-permute-start.32 = (bf16[4,24,1024]{2,1,0:T(8,128)(2,1)S(1)}, bf16[4,24,1024]{2,1,0:T(8,128)(2,1)S(1)}, u32[]{:S(2)}, u32[]{:S(2)}) collective-permute-start(bf16[4,24,1024]{2,1,0:T(8,128)(2,1)S(1)} %pad_maximum_fusion.8), channel_id=1, source_target_pairs={{0,1},{1,0},{2,3},{3,2},{4,5},{5,4},{6,7},{7,6},{8,9},{9,8},{10,11... | collective-permute-start | bytes 589832 | tf_op jit(solution)/shard_map/ppermute | solution.py:20
  82.6 6.5 %collective-permute-start.36 = (bf16[2,24,1024]{2,1,0:T(8,128)(2,1)S(1)}, bf16[2,24,1024]{2,1,0:T(8,128)(2,1)S(1)}, u32[]{:S(2)}, u32[]{:S(2)}) collective-permute-start(bf16[2,24,1024]{2,1,0:T(8,128)(2,1)S(1)} %get-tuple-element.131), channel_id=1, source_target_pairs={{0,3},{1,2},{2,1},{3,0},{4,7},{5,6},{6,5},{7,4},{8,11},{9,10},{10,... | collective-permute-start | bytes 294920 | tf_op jit(solution)/shard_map/ppermute | solution.py:20
  (6 other events, 21.2 us)

commit v7 on v6

--- a/solution.py
+++ b/solution.py
@@ -22,6 +22,10 @@
 
 def after(value, *others):
     return lax.optimization_barrier((value, *others))[0]
+
+
+def early_experts(half):
+    return 2 * half // 4
 
 
 def mm(a, b, dims=((1,), (0,))):
@@ -149,10 +153,10 @@
 def pack(select, normed, sib_normed, n_exp, half, cap):
     width = normed.shape[1]
     rows = select.shape[0]
-    per = half // CHUNKS
+    cut = early_experts(half)
     spans = []
     for s in range(n_exp):
-        spans += [(s * half, half)] if s < 2 else [(s * half + c * per, per) for c in range(CHUNKS)]
+        spans += [(s * half, half)] if s < 2 else [(s * half, cut), (s * half + cut, half - cut)]
     pieces = list(pl.pallas_call(
         functools.partial(pack_kernel, spans),
         out_shape=[pltpu.VMEM((count, 2 * cap, width), BF16) for _, count in spans],
@@ -218,41 +222,34 @@
     )(place, in_hbm(w_in), in_hbm(w_down))
 
 
-def experts_kernel(chunk, *refs):
-    rows_refs, (sib_ref, in_ref, down_ref), outs = refs[:9], refs[9:12], refs[12:21]
-    h_ref = refs[21]
-    per = rows_refs[0].shape[0]
-    split = per // 2
-    first = chunk * per
-    def blocks(refs, e, whole):
-        far, far_a, far_b, d1, d2, own, own_a, own_b, own_d = refs
-        mine = first + e if whole else e
-        diagonal = (d1, e) if e < split else (d2, e - split)
-        return [(far, e), (far_a, e), (far_b, e), diagonal, (own, mine), (own_a, mine), (own_b, mine), (own_d, e)]
-
+def experts_kernel(first, *refs):
+    rows_refs, (sib_ref, in_ref, down_ref), outs, h_ref = refs[:10], refs[10:13], refs[13:22], refs[22]
+    far, far_a, far_b, d1, d2, own, own_a, own_b, own_d1, own_d2 = rows_refs
+    per, split = far.shape[0], own_d1.shape[0]
     for e in range(per):
         mine = first + e
-        x = jnp.concatenate([ref[i] for ref, i in blocks(rows_refs, e, True)], axis=0)
+        own_d = own_d1[mine] if mine < split else own_d2[mine - split]
+        x = jnp.concatenate(
+            [ref[e] for ref in (far, far_a, far_b, d1, d2)] + [ref[mine] for ref in (own, own_a, own_b)] + [own_d], axis=0)
         h_ref[0] = jax.nn.gelu(mm(x, in_ref[mine])).astype(BF16)
         h_ref[1] = jax.nn.gelu(mm(x, sib_ref[0, mine])).astype(BF16)
         total = mm(h_ref[0], down_ref[mine], ((1,), (1,))) + mm(h_ref[1], sib_ref[1, mine], ((1,), (1,)))
         start = 0
-        for ref, i in blocks(outs, e, False):
-            ref[i] = total[start:start + ref.shape[1]].astype(BF16)
+        for ref in outs:
+            ref[e] = total[start:start + ref.shape[1]].astype(BF16)
             start += ref.shape[1]
 
 
-def experts(chunk, blocks, sib, in_own, down_own):
-    far, d1, own = blocks[0], blocks[3], blocks[5]
+def experts(first, blocks, sib, in_own, down_own):
+    far, own = blocks[0], blocks[5]
     per, far_rows, width = far.shape
     rows = 4 * (far_rows + own.shape[1])
     ff = sib.shape[3]
-    own_shape = (per, *own.shape[1:])
-    shapes = [far.shape] * 3 + [d1.shape] * 2 + [own_shape] * 4
+    shapes = [block.shape for block in blocks[:5]] + [(per, *own.shape[1:])] * 4
     return list(pl.pallas_call(
-        functools.partial(experts_kernel, chunk),
+        functools.partial(experts_kernel, first),
         out_shape=[pltpu.VMEM(shape, BF16) for shape in shapes],
-        in_specs=[vmem()] * 12,
+        in_specs=[vmem()] * 13,
         out_specs=[vmem()] * 9,
         scratch_shapes=[pltpu.VMEM((2, rows, ff), BF16)],
         compiler_params=pltpu.CompilerParams(vmem_limit_bytes=VMEM_LIMIT),
@@ -266,10 +263,10 @@
 def combine_kernel(tok, spans, gate_ref, emb_ref, *refs):
     own_refs, (from_a_ref, from_b_ref), piece_refs = refs[:CHUNKS], refs[CHUNKS:CHUNKS + 2], refs[CHUNKS + 2:-3]
     mine_ref, send_ref, rows_ref = refs[-3:]
-    per, slots, _ = own_refs[0].shape
+    slots = own_refs[0].shape[1]
     for c, ref in enumerate(own_refs):
-        for e in range(per):
-            i = c * per + e
+        for e in range(ref.shape[0]):
+            i = c * own_refs[0].shape[0] + e
             done = ref[e].astype(F32) + from_a_ref[i].astype(F32) + from_b_ref[i].astype(F32)
             rows_ref[i * slots:(i + 1) * slots] = done
     for start, ref in zip(spans, piece_refs):
@@ -321,8 +318,7 @@
         w_in, w_down = gathered(w_in), gathered(w_down)
 
     pieces = pack(select, normed, sib_normed, n_exp, half, cap)
-    per = half // CHUNKS
-    split = per // 2
+    cut, split = early_experts(half), half // 2
     a_bit, b_bit = 1 << NEAR_A, 1 << NEAR_B
 
     def to_a(rows):
@@ -333,51 +329,57 @@
 
     own = pieces[0][0]
     first = swapped(pieces[1][0], "exp", 1)
-    far0 = jnp.concatenate([first[:per]] + [swapped(pieces[s][0], "exp", s) for s in range(2, n_exp)], axis=1)
+    far0 = jnp.concatenate([first[:cut]] + [swapped(pieces[s][0], "exp", s) for s in range(2, n_exp)], axis=1)
     own_a, own_b = to_a(own), to_b(own)
     lent = lend(after(place, own_a, own_b), w_in, w_down)
-    own_d = to_b(own_a[:per]), to_a(own_b[per:])
+    own_d = to_b(own_a[:split]), to_a(own_b[split:])
     far0, sib, *own_d = lax.optimization_barrier((far0, lent, *own_d))
     sib = swapped(sib, "rep", core_bit)
-    late = lax.optimization_barrier((far0, *(pieces[s][1] for s in range(2, n_exp))))[1:]
-    far1 = jnp.concatenate([first[per:]] + [swapped(piece, "exp", s + 2) for s, piece in enumerate(late)], axis=1)
+    shifts1 = list(range(n_exp - 1, 1, -1))
+    late = lax.optimization_barrier((far0, *(pieces[s][1] for s in shifts1)))[1:]
+    far1 = jnp.concatenate([first[cut:]] + [swapped(piece, "exp", s) for s, piece in zip(shifts1, late)], axis=1)
     a0, b0 = to_a(far0), to_b(far0)
     far1 = after(far1, a0, b0)
     in_own, down_own = hold(after(place, far0), w_in, w_down)
     a0, b0 = lax.optimization_barrier((a0, b0, in_own))[:2]
-    d0 = to_b(a0[:split]), to_a(b0[split:])
+    turn = far0.shape[1] // 16 * 8
+    d0 = to_b(a0[:, :turn]), to_a(b0[:, turn:])
     a1, b1 = to_a(far1), to_b(far1)
-    parts0 = experts(0, (far0, a0, b0, *d0, own, own_a, own_b, own_d[0]), sib, in_own, down_own)
+    parts0 = experts(0, (far0, a0, b0, *d0, own, own_a, own_b, *own_d), sib, in_own, down_own)
     a1, b1, *parts0 = lax.optimization_barrier((a1, b1, *parts0))
     r0 = to_a(parts0[3]), to_b(parts0[4])
-    d1 = to_b(a1[:split]), to_a(b1[split:])
+    d1 = to_b(a1[:, :turn]), to_a(b1[:, turn:])
 
     def reduced(parts, r):
-        return (jnp.concatenate([parts[1][:split], parts[1][split:] + r[1]], axis=0),
-                jnp.concatenate([parts[2][:split] + r[0], parts[2][split:]], axis=0))
-
-    def back(part, from_a, from_b):
+        return (jnp.concatenate([parts[1][:, :turn], parts[1][:, turn:] + r[1]], axis=1),
+                jnp.concatenate([parts[2][:, :turn] + r[0], parts[2][:, turn:]], axis=1))
+
+    def back(part, from_a, from_b, order):
         done = (part.astype(F32) + from_a.astype(F32) + from_b.astype(F32)).astype(BF16)
         shifts = jnp.split(done, n_exp - 1, axis=1)
-        return shifts[0], [swapped(rows, "exp", s + 2) for s, rows in enumerate(shifts[1:])]
+        return shifts[0], {s: swapped(rows, "exp", s) for s, rows in zip(order, shifts[1:])}
 
     sums0 = reduced(parts0, r0)
     d1 = lax.optimization_barrier((*d1, *sums0))[:2]
     from_a0, from_b0 = to_a(sums0[0]), to_b(sums0[1])
-    parts1 = experts(1, (far1, a1, b1, *d1, own, own_a, own_b, own_d[1]), sib, in_own, down_own)
+    parts1 = experts(cut, (far1, a1, b1, *d1, own, own_a, own_b, *own_d), sib, in_own, down_own)
     parts1[3], parts1[4] = lax.optimization_barrier((parts1[3], parts1[4], from_a0, from_b0))[:2]
     r1 = to_a(parts1[3]), to_b(parts1[4])
-    returned0 = back(parts0[0], from_a0, from_b0)
+    returned0 = back(parts0[0], from_a0, from_b0, range(2, n_exp))
     sums1 = reduced(parts1, r1)
     from_a1, from_b1 = to_a(sums1[0]), to_b(sums1[1])
-    returned1 = back(parts1[0], from_a1, from_b1)
-    own_r = to_a(after(parts0[8], from_a0, from_b0)), to_b(after(parts1[8], from_a0, from_b0))
-    own_to_a = jnp.concatenate([parts0[6], parts1[6] + own_r[1]], axis=0)
-    own_to_b = jnp.concatenate([parts0[7] + own_r[0], parts1[7]], axis=0)
+    returned1 = back(parts1[0], from_a1, from_b1, shifts1)
+    across = jnp.concatenate([parts0[8], parts1[8]], axis=0)
+    across = after(across, from_a0, from_b0)
+    own_r = to_a(across[:split]), to_b(across[split:])
+    own_to_a = jnp.concatenate([parts0[6], parts1[6]], axis=0)
+    own_to_b = jnp.concatenate([parts0[7], parts1[7]], axis=0)
+    own_to_a = jnp.concatenate([own_to_a[:split], own_to_a[split:] + own_r[1]], axis=0)
+    own_to_b = jnp.concatenate([own_to_b[:split] + own_r[0], own_to_b[split:]], axis=0)
     own_to_a, own_to_b = lax.optimization_barrier((own_to_a, own_to_b, *sums1))[:2]
-    spans = [half] + [s * half + c * per for s in range(2, n_exp) for c in range(CHUNKS)]
+    spans = [half] + [s * half + start for s in range(2, n_exp) for start in (0, cut)]
     pieces_back = [swapped(jnp.concatenate([returned0[0], returned1[0]], axis=0), "exp", 1)]
-    pieces_back += [returned[s] for s in range(n_exp - 2) for returned in (returned0[1], returned1[1])]
+    pieces_back += [returned[s] for s in range(2, n_exp) for returned in (returned0[1], returned1[1])]
     mine, send = combine(
         gate, embedded, (parts0[5], parts1[5]), to_a(own_to_a), to_b(own_to_b), spans, pieces_back)
     other = swapped(send, "rep", 1 << CORE)

time: 92.1 us -> 90.9 us (0.987)
  starting transfers between devices: 50.3 us -> 48.6 us
    ppermute x38, starting transfers between devices: 50.3 us -> 48.6 us  [swapped(): lax.ppermute(array, axis, [(i, i ^ distance) for i in range(lax.axis_size...]
  transfers between devices with their start and end apart: 38 -> 38, of which waited for: 16 -> 17; matrix products, arithmetic and copies ran while one was open for 1% -> 1% of each run, Pallas kernels for 18% -> 18%
where the time goes in v7:
time: 90.9 us; the launch traced here: 90.7 us
  starting transfers between devices  48.6 us (53%)
  Pallas kernels  19.8 us (22%)
  waiting for transfers between devices  19.7 us (22%)
  other arithmetic  2.15 us (2%)
    ppermute x38, starting transfers between devices, swapped(): lax.ppermute(array, axis, [(i, i ^ distance) for i in range(lax.axis_size...  48.6 us
    ppermute x38, waiting for transfers between devices, swapped(): lax.ppermute(array, axis, [(i, i ^ distance) for i in range(lax.axis_size...  19.7 us
    pallas_call x2, Pallas kernels, experts(): pl.pallas_call(functools.partial(experts_kernel, first), out_shape=[pltpu...  7.43 us
    pallas_call x1, Pallas kernels, lend(): pl.pallas_call(lend_kernel, out_shape=pltpu.VMEM(shape, BF16), in_specs=[...  4.02 us
    pallas_call x1, Pallas kernels, hold(): pl.pallas_call(hold_kernel, out_shape=[shape, shape], in_specs=[smem(), h...  4.02 us
    pallas_call x1, Pallas kernels, embed(): pl.pallas_call(embed_kernel, out_shape=[shape, shape], in_specs=[hbm()] *...  2.51 us
  transfers between devices with their start and end apart: 38, of which 17 were waited for; matrix products, arithmetic and copies ran while one was open for 1% of the time, Pallas kernels for 18%

profile of v7, /device:TPU:0, one launch (start us, length us, event | category | flops | bytes accessed | tf_op | source)
XLA Modules:
  0.0 90.7 jit_solution(14549802047898086280)
XLA Ops:
  0.7 2.5 %embed.1 = (bf16[128,1024]{1,0:T(8,128)(2,1)S(1)}, bf16[128,1024]{1,0:T(8,128)(2,1)S(1)}) custom-call(bf16[128,1536]{1,0:T(8,128)(2,1)} %tubelets_ref, bf16[1536,1024]{1,0:T(8,128)(2,1)} %weight_ref.1, f32[1,1024]{1,0:T(1,128)} %bitcast.5), custom_call_target="tpu_custom_call" | custom-call | flops 402653184 | bytes 3145728 | tf_op jit(solution)/shard_map/embed/pallas_call | solution.py:86
  6.2 2.9 %collective-permute-start.5 = (bf16[4,24,1024]{2,1,0:T(8,128)(2,1)S(1)}, bf16[4,24,1024]{2,1,0:T(8,128)(2,1)S(1)}, u32[]{:S(2)}, u32[]{:S(2)}) collective-permute-start(bf16[4,24,1024]{2,1,0:T(8,128)(2,1)S(1)} %get-tuple-element.75.refs_5_), channel_id=1, source_target_pairs={{0,8},{4,12},{8,0},{12,4},{16,24},{20,28},{24,16},{28,20},{1,9},{5... | collective-permute-start | bytes 589832 | tf_op jit(solution)/shard_map/ppermute | solution.py:20
  9.2 1.5 %collective-permute-start.6 = (bf16[4,24,1024]{2,1,0:T(8,128)(2,1)S(1)}, bf16[4,24,1024]{2,1,0:T(8,128)(2,1)S(1)}, u32[]{:S(2)}, u32[]{:S(2)}) collective-permute-start(bf16[4,24,1024]{2,1,0:T(8,128)(2,1)S(1)} %get-tuple-element.75.refs_5_), channel_id=1, source_target_pairs={{0,16},{4,20},{8,24},{12,28},{16,0},{20,4},{24,8},{28,12},{1,17},{... | collective-permute-start | bytes 589832 | tf_op jit(solution)/shard_map/ppermute | solution.py:20
  10.7 1.6 %collective-permute-start.2 = (bf16[4,24,1024]{2,1,0:T(8,128)(2,1)S(1)}, bf16[4,24,1024]{2,1,0:T(8,128)(2,1)S(1)}, u32[]{:S(2)}, u32[]{:S(2)}) collective-permute-start(bf16[4,24,1024]{2,1,0:T(8,128)(2,1)S(1)} %get-tuple-element.72), channel_id=1, source_target_pairs={{0,1},{1,0},{2,3},{3,2},{4,5},{5,4},{6,7},{7,6},{8,9},{9,8},{10,11... | collective-permute-start | bytes 589832 | tf_op jit(solution)/shard_map/ppermute | solution.py:20
  12.3 2.6 %collective-permute-start.3 = (bf16[2,24,1024]{2,1,0:T(8,128)(2,1)S(1)}, bf16[2,24,1024]{2,1,0:T(8,128)(2,1)S(1)}, u32[]{:S(2)}, u32[]{:S(2)}) collective-permute-start(bf16[2,24,1024]{2,1,0:T(8,128)(2,1)S(1)} %get-tuple-element.73), channel_id=1, source_target_pairs={{0,2},{1,3},{2,0},{3,1},{4,6},{5,7},{6,4},{7,5},{8,10},{9,11},{10,... | collective-permute-start | bytes 294920 | tf_op jit(solution)/shard_map/ppermute | solution.py:20
  16.2 1.6 %collective-permute-start.8 = (bf16[2,24,1024]{2,1,0:T(8,128)(2,1)S(1)}, bf16[2,24,1024]{2,1,0:T(8,128)(2,1)S(1)}, u32[]{:S(2)}, u32[]{:S(2)}) collective-permute-start(bf16[2,24,1024]{2,1,0:T(8,128)(2,1)S(1)} %slice.75), channel_id=1, source_target_pairs={{0,8},{4,12},{8,0},{12,4},{16,24},{20,28},{24,16},{28,20},{1,9},{5... | collective-permute-start | bytes 294920 | tf_op jit(solution)/shard_map/ppermute | solution.py:20
  17.8 1.3 %collective-permute-done.2 = bf16[4,24,1024]{2,1,0:T(8,128)(2,1)S(1)} collective-permute-done((bf16[4,24,1024]{2,1,0:T(8,128)(2,1)S(1)}, bf16[4,24,1024]{2,1,0:T(8,128)(2,1)S(1)}, u32[]{:S(2)}, u32[]{:S(2)}) %collective-permute-start.2) | collective-permute-done | bytes 196640 | tf_op jit(solution)/shard_map/ppermute | solution.py:20
  19.1 4.0 %lend.1 = bf16[2,4,1024,512]{3,2,1,0:T(8,128)(2,1)S(1)} custom-call(s32[2]{0:T(128)S(1)} %pad_add_fusion.1.place_ref, bf16[8,1024,512]{2,1,0:T(8,128)(2,1)} %in_ref.3, bf16[8,1024,512]{2,1,0:T(8,128)(2,1)} %down_ref.3), custom_call_target="tpu_custom_call" | custom-call | bytes 16777216 | tf_op jit(solution)/shard_map/lend/pallas_call | solution.py:187
  24.6 2.4 %collective-permute-start.10 = (bf16[2,24,1024]{2,1,0:T(8,128)(2,1)S(1)}, bf16[2,24,1024]{2,1,0:T(8,128)(2,1)S(1)}, u32[]{:S(2)}, u32[]{:S(2)}) collective-permute-start(bf16[2,24,1024]{2,1,0:T(8,128)(2,1)S(1)} %get-tuple-element.81), channel_id=1, source_target_pairs={{0,2},{1,3},{2,0},{3,1},{4,6},{5,7},{6,4},{7,5},{8,10},{9,11},{10,... | collective-permute-start | bytes 294920 | tf_op jit(solution)/shard_map/ppermute | solution.py:20
  27.1 1.9 %collective-permute-start.9 = (bf16[2,24,1024]{2,1,0:T(8,128)(2,1)S(1)}, bf16[2,24,1024]{2,1,0:T(8,128)(2,1)S(1)}, u32[]{:S(2)}, u32[]{:S(2)}) collective-permute-start(bf16[2,24,1024]{2,1,0:T(8,128)(2,1)S(1)} %get-tuple-element.80), channel_id=1, source_target_pairs={{0,3},{1,2},{2,1},{3,0},{4,7},{5,6},{6,5},{7,4},{8,11},{9,10},{10,... | collective-permute-start | bytes 294920 | tf_op jit(solution)/shard_map/ppermute | solution.py:20
  28.9 4.0 %hold.1 = (bf16[4,1024,512]{2,1,0:T(8,128)(2,1)S(1)}, bf16[4,1024,512]{2,1,0:T(8,128)(2,1)S(1)}) custom-call(s32[2]{0:T(128)S(1)} %pad_add_fusion.1.place_ref, bf16[8,1024,512]{2,1,0:T(8,128)(2,1)} %in_ref.3, bf16[8,1024,512]{2,1,0:T(8,128)(2,1)} %down_ref.3), custom_call_target="tpu_custom_call" | custom-call | bytes 16777216 | tf_op jit(solution)/shard_map/hold/pallas_call | solution.py:213
  33.2 1.6 %collective-permute-start.16 = (bf16[2,40,1024]{2,1,0:T(8,128)(2,1)S(1)}, bf16[2,40,1024]{2,1,0:T(8,128)(2,1)S(1)}, u32[]{:S(2)}, u32[]{:S(2)}) collective-permute-start(bf16[2,40,1024]{2,1,0:T(8,128)(2,1)S(1)} %slice.59), channel_id=1, source_target_pairs={{0,8},{4,12},{8,0},{12,4},{16,24},{20,28},{24,16},{28,20},{1,9},{5... | collective-permute-start | bytes 491528 | tf_op jit(solution)/shard_map/ppermute | solution.py:20
  34.8 1.4 %collective-permute-start.15 = (bf16[2,32,1024]{2,1,0:T(8,128)(2,1)S(1)}, bf16[2,32,1024]{2,1,0:T(8,128)(2,1)S(1)}, u32[]{:S(2)}, u32[]{:S(2)}) collective-permute-start(bf16[2,32,1024]{2,1,0:T(8,128)(2,1)S(1)} %slice.58), channel_id=1, source_target_pairs={{0,16},{4,20},{8,24},{12,28},{16,0},{20,4},{24,8},{28,12},{1,17},{... | collective-permute-start | bytes 393224 | tf_op jit(solution)/shard_map/ppermute | solution.py:20
  37.8 3.4 %collective-permute-done.15.refs_3_ = bf16[2,32,1024]{2,1,0:T(8,128)(2,1)S(1)} collective-permute-done((bf16[2,32,1024]{2,1,0:T(8,128)(2,1)S(1)}, bf16[2,32,1024]{2,1,0:T(8,128)(2,1)S(1)}, u32[]{:S(2)}, u32[]{:S(2)}) %collective-permute-start.15) | collective-permute-done | bytes 131104 | tf_op jit(solution)/shard_map/ppermute | solution.py:20
  41.2 3.7 %experts.2 = (bf16[2,72,1024]{2,1,0:T(8,128)(2,1)S(1)}, bf16[2,72,1024]{2,1,0:T(8,128)(2,1)S(1)}, bf16[2,72,1024]{2,1,0:T(8,128)(2,1)S(1)}, bf16[2,32,1024]{2,1,...) custom-call(bf16[2,72,1024]{2,1,0:T(8,128)(2,1)S(1)} %pad_maximum_fu, ...), custom_call_target="tpu_custom_call" | custom-call | flops 3221225472 | bytes 3145728 | tf_op jit(solution)/shard_map/experts/pallas_call | solution.py:249
  46.7 1.5 %collective-permute-start.20 = (bf16[2,40,1024]{2,1,0:T(8,128)(2,1)S(1)}, bf16[2,40,1024]{2,1,0:T(8,128)(2,1)S(1)}, u32[]{:S(2)}, u32[]{:S(2)}) collective-permute-start(bf16[2,40,1024]{2,1,0:T(8,128)(2,1)S(1)} %get-tuple-element.104), channel_id=1, source_target_pairs={{0,16},{4,20},{8,24},{12,28},{16,0},{20,4},{24,8},{28,12},{1,17},{... | collective-permute-start | bytes 491528 | tf_op jit(solution)/shard_map/ppermute | solution.py:20
  50.2 2.0 %collective-permute-done.21 = bf16[2,32,1024]{2,1,0:T(8,128)(2,1)S(1)} collective-permute-done((bf16[2,32,1024]{2,1,0:T(8,128)(2,1)S(1)}, bf16[2,32,1024]{2,1,0:T(8,128)(2,1)S(1)}, u32[]{:S(2)}, u32[]{:S(2)}) %collective-permute-start.21) | collective-permute-done | bytes 131104 | tf_op jit(solution)/shard_map/ppermute | solution.py:20
  53.8 1.3 %collective-permute-start.22 = (bf16[2,72,1024]{2,1,0:T(8,128)(2,1)S(1)}, bf16[2,72,1024]{2,1,0:T(8,128)(2,1)S(1)}, u32[]{:S(2)}, u32[]{:S(2)}) collective-permute-start(bf16[2,72,1024]{2,1,0:T(8,128)(2,1)S(1)} %pad_maximum_fusion.2), channel_id=1, source_target_pairs={{0,8},{4,12},{8,0},{12,4},{16,24},{20,28},{24,16},{28,20},{1,9},{5... | collective-permute-start | bytes 884744 | tf_op jit(solution)/shard_map/ppermute | solution.py:20
  55.1 1.5 %collective-permute-done.18.refs_3_ = bf16[2,32,1024]{2,1,0:T(8,128)(2,1)S(1)} collective-permute-done((bf16[2,32,1024]{2,1,0:T(8,128)(2,1)S(1)}, bf16[2,32,1024]{2,1,0:T(8,128)(2,1)S(1)}, u32[]{:S(2)}, u32[]{:S(2)}) %collective-permute-start.18) | collective-permute-done | bytes 131104 | tf_op jit(solution)/shard_map/ppermute | solution.py:20
  56.6 3.7 %experts.3 = (bf16[2,72,1024]{2,1,0:T(8,128)(2,1)S(1)}, bf16[2,72,1024]{2,1,0:T(8,128)(2,1)S(1)}, bf16[2,72,1024]{2,1,0:T(8,128)(2,1)S(1)}, bf16[2,32,1024]{2,1,...) custom-call(bf16[2,72,1024]{2,1,0:T(8,128)(2,1)S(1)} %pad_maximum_fu, ...), custom_call_target="tpu_custom_call" | custom-call | flops 3221225472 | bytes 3145728 | tf_op jit(solution)/shard_map/experts/pallas_call | solution.py:249
  60.6 1.2 %collective-permute-start.27 = (bf16[2,32,1024]{2,1,0:T(8,128)(2,1)S(1)}, bf16[2,32,1024]{2,1,0:T(8,128)(2,1)S(1)}, u32[]{:S(2)}, u32[]{:S(2)}) collective-permute-start(bf16[2,32,1024]{2,1,0:T(8,128)(2,1)S(1)} %get-tuple-element.122), channel_id=1, source_target_pairs={{0,8},{4,12},{8,0},{12,4},{16,24},{20,28},{24,16},{28,20},{1,9},{5... | collective-permute-start | bytes 393224 | tf_op jit(solution)/shard_map/ppermute | solution.py:20
  61.9 2.2 %collective-permute-start.26 = (bf16[2,40,1024]{2,1,0:T(8,128)(2,1)S(1)}, bf16[2,40,1024]{2,1,0:T(8,128)(2,1)S(1)}, u32[]{:S(2)}, u32[]{:S(2)}) collective-permute-start(bf16[2,40,1024]{2,1,0:T(8,128)(2,1)S(1)} %get-tuple-element.120), channel_id=1, source_target_pairs={{0,16},{4,20},{8,24},{12,28},{16,0},{20,4},{24,8},{28,12},{1,17},{... | collective-permute-start | bytes 491528 | tf_op jit(solution)/shard_map/ppermute | solution.py:20
  65.6 2.4 %collective-permute-start.31 = (bf16[2,72,1024]{2,1,0:T(8,128)(2,1)S(1)}, bf16[2,72,1024]{2,1,0:T(8,128)(2,1)S(1)}, u32[]{:S(2)}, u32[]{:S(2)}) collective-permute-start(bf16[2,72,1024]{2,1,0:T(8,128)(2,1)S(1)} %pad_maximum_fusion.5), channel_id=1, source_target_pairs={{0,16},{4,20},{8,24},{12,28},{16,0},{20,4},{24,8},{28,12},{1,17},{... | collective-permute-start | bytes 884744 | tf_op jit(solution)/shard_map/ppermute | solution.py:20
  69.1 1.2 %collective-permute-start.30 = (bf16[2,72,1024]{2,1,0:T(8,128)(2,1)S(1)}, bf16[2,72,1024]{2,1,0:T(8,128)(2,1)S(1)}, u32[]{:S(2)}, u32[]{:S(2)}) collective-permute-start(bf16[2,72,1024]{2,1,0:T(8,128)(2,1)S(1)} %pad_maximum_fusion.4), channel_id=1, source_target_pairs={{0,8},{4,12},{8,0},{12,4},{16,24},{20,28},{24,16},{28,20},{1,9},{5... | collective-permute-start | bytes 884744 | tf_op jit(solution)/shard_map/ppermute | solution.py:20
  70.4 3.1 %collective-permute-start.33 = (bf16[2,24,1024]{2,1,0:T(8,128)(2,1)S(1)}, bf16[2,24,1024]{2,1,0:T(8,128)(2,1)S(1)}, u32[]{:S(2)}, u32[]{:S(2)}) collective-permute-start(bf16[2,24,1024]{2,1,0:T(8,128)(2,1)S(1)} %get-tuple-element.133), channel_id=1, source_target_pairs={{0,2},{1,3},{2,0},{3,1},{4,6},{5,7},{6,4},{7,5},{8,10},{9,11},{10,... | collective-permute-start | bytes 294920 | tf_op jit(solution)/shard_map/ppermute | solution.py:20
  73.5 1.4 %collective-permute-start.35 = (bf16[2,24,1024]{2,1,0:T(8,128)(2,1)S(1)}, bf16[2,24,1024]{2,1,0:T(8,128)(2,1)S(1)}, u32[]{:S(2)}, u32[]{:S(2)}) collective-permute-start(bf16[2,24,1024]{2,1,0:T(8,128)(2,1)S(1)} %get-tuple-element.132), channel_id=1, source_target_pairs={{0,3},{1,2},{2,1},{3,0},{4,7},{5,6},{6,5},{7,4},{8,11},{9,10},{10,... | collective-permute-start | bytes 294920 | tf_op jit(solution)/shard_map/ppermute | solution.py:20
  75.0 1.2 %collective-permute-start.28 = (bf16[4,24,1024]{2,1,0:T(8,128)(2,1)S(1)}, bf16[4,24,1024]{2,1,0:T(8,128)(2,1)S(1)}, u32[]{:S(2)}, u32[]{:S(2)}) collective-permute-start(bf16[4,24,1024]{2,1,0:T(8,128)(2,1)S(1)} %pad_maximum_fusion.7), channel_id=1, source_target_pairs={{0,8},{4,12},{8,0},{12,4},{16,24},{20,28},{24,16},{28,20},{1,9},{5... | collective-permute-start | bytes 589832 | tf_op jit(solution)/shard_map/ppermute | solution.py:20
  77.6 3.8 %collective-permute-start.34 = (bf16[2,24,1024]{2,1,0:T(8,128)(2,1)S(1)}, bf16[2,24,1024]{2,1,0:T(8,128)(2,1)S(1)}, u32[]{:S(2)}, u32[]{:S(2)}) collective-permute-start(bf16[2,24,1024]{2,1,0:T(8,128)(2,1)S(1)} %get-tuple-element.130), channel_id=1, source_target_pairs={{0,2},{1,3},{2,0},{3,1},{4,6},{5,7},{6,4},{7,5},{8,10},{9,11},{10,... | collective-permute-start | bytes 294920 | tf_op jit(solution)/shard_map/ppermute | solution.py:20
  81.4 1.8 %collective-permute-start.36 = (bf16[2,24,1024]{2,1,0:T(8,128)(2,1)S(1)}, bf16[2,24,1024]{2,1,0:T(8,128)(2,1)S(1)}, u32[]{:S(2)}, u32[]{:S(2)}) collective-permute-start(bf16[2,24,1024]{2,1,0:T(8,128)(2,1)S(1)} %get-tuple-element.129), channel_id=1, source_target_pairs={{0,3},{1,2},{2,1},{3,0},{4,7},{5,6},{6,5},{7,4},{8,11},{9,10},{10,... | collective-permute-start | bytes 294920 | tf_op jit(solution)/shard_map/ppermute | solution.py:20
  83.2 1.7 %collective-permute-done.34.refs_6_ = bf16[2,24,1024]{2,1,0:T(8,128)(2,1)S(1)} collective-permute-done((bf16[2,24,1024]{2,1,0:T(8,128)(2,1)S(1)}, bf16[2,24,1024]{2,1,0:T(8,128)(2,1)S(1)}, u32[]{:S(2)}, u32[]{:S(2)}) %collective-permute-start.34) | collective-permute-done | bytes 98336 | tf_op jit(solution)/shard_map/ppermute | solution.py:20
  84.9 3.0 %collective-permute-done.36.refs_8_ = bf16[2,24,1024]{2,1,0:T(8,128)(2,1)S(1)} collective-permute-done((bf16[2,24,1024]{2,1,0:T(8,128)(2,1)S(1)}, bf16[2,24,1024]{2,1,0:T(8,128)(2,1)S(1)}, u32[]{:S(2)}, u32[]{:S(2)}) %collective-permute-start.36) | collective-permute-done | bytes 98336 | tf_op jit(solution)/shard_map/ppermute | solution.py:20
  88.4 1.5 %collective-permute-done.37 = bf16[128,1024]{1,0:T(8,128)(2,1)S(1)} collective-permute-done((bf16[128,1024]{1,0:T(8,128)(2,1)S(1)}, bf16[128,1024]{1,0:T(8,128)(2,1)S(1)}, u32[]{:S(2)}, u32[]{:S(2)}) %collective-permute-start.37) | collective-permute-done | bytes 262176 | tf_op jit(solution)/shard_map/ppermute | solution.py:20
  (87 shorter events, 19.4 us)
Async XLA Ops:
  6.2 8.8 %collective-permute-start.5 = (bf16[4,24,1024]{2,1,0:T(8,128)(2,1)S(1)}, bf16[4,24,1024]{2,1,0:T(8,128)(2,1)S(1)}, u32[]{:S(2)}, u32[]{:S(2)}) collective-permute-start(bf16[4,24,1024]{2,1,0:T(8,128)(2,1)S(1)} %get-tuple-element.75.refs_5_), channel_id=1, source_target_pairs={{0,8},{4,12},{8,0},{12,4},{16,24},{20,28},{24,16},{28,20},{1,9},{5... | collective-permute-start | bytes 589832 | tf_op jit(solution)/shard_map/ppermute | solution.py:20
  9.2 7.0 %collective-permute-start.6 = (bf16[4,24,1024]{2,1,0:T(8,128)(2,1)S(1)}, bf16[4,24,1024]{2,1,0:T(8,128)(2,1)S(1)}, u32[]{:S(2)}, u32[]{:S(2)}) collective-permute-start(bf16[4,24,1024]{2,1,0:T(8,128)(2,1)S(1)} %get-tuple-element.75.refs_5_), channel_id=1, source_target_pairs={{0,16},{4,20},{8,24},{12,28},{16,0},{20,4},{24,8},{28,12},{1,17},{... | collective-permute-start | bytes 589832 | tf_op jit(solution)/shard_map/ppermute | solution.py:20
  10.7 8.4 %collective-permute-start.2 = (bf16[4,24,1024]{2,1,0:T(8,128)(2,1)S(1)}, bf16[4,24,1024]{2,1,0:T(8,128)(2,1)S(1)}, u32[]{:S(2)}, u32[]{:S(2)}) collective-permute-start(bf16[4,24,1024]{2,1,0:T(8,128)(2,1)S(1)} %get-tuple-element.72), channel_id=1, source_target_pairs={{0,1},{1,0},{2,3},{3,2},{4,5},{5,4},{6,7},{7,6},{8,9},{9,8},{10,11... | collective-permute-start | bytes 589832 | tf_op jit(solution)/shard_map/ppermute | solution.py:20
  12.3 10.9 %collective-permute-start.3 = (bf16[2,24,1024]{2,1,0:T(8,128)(2,1)S(1)}, bf16[2,24,1024]{2,1,0:T(8,128)(2,1)S(1)}, u32[]{:S(2)}, u32[]{:S(2)}) collective-permute-start(bf16[2,24,1024]{2,1,0:T(8,128)(2,1)S(1)} %get-tuple-element.73), channel_id=1, source_target_pairs={{0,2},{1,3},{2,0},{3,1},{4,6},{5,7},{6,4},{7,5},{8,10},{9,11},{10,... | collective-permute-start | bytes 294920 | tf_op jit(solution)/shard_map/ppermute | solution.py:20
  14.8 8.6 %collective-permute-start.4 = (bf16[2,24,1024]{2,1,0:T(8,128)(2,1)S(1)}, bf16[2,24,1024]{2,1,0:T(8,128)(2,1)S(1)}, u32[]{:S(2)}, u32[]{:S(2)}) collective-permute-start(bf16[2,24,1024]{2,1,0:T(8,128)(2,1)S(1)} %get-tuple-element.74), channel_id=1, source_target_pairs={{0,3},{1,2},{2,1},{3,0},{4,7},{5,6},{6,5},{7,4},{8,11},{9,10},{10,... | collective-permute-start | bytes 294920 | tf_op jit(solution)/shard_map/ppermute | solution.py:20
  15.1 8.4 %collective-permute-start.7 = (bf16[2,24,1024]{2,1,0:T(8,128)(2,1)S(1)}, bf16[2,24,1024]{2,1,0:T(8,128)(2,1)S(1)}, u32[]{:S(2)}, u32[]{:S(2)}) collective-permute-start(bf16[2,24,1024]{2,1,0:T(8,128)(2,1)S(1)} %slice.74), channel_id=1, source_target_pairs={{0,16},{4,20},{8,24},{12,28},{16,0},{20,4},{24,8},{28,12},{1,17},{... | collective-permute-start | bytes 294920 | tf_op jit(solution)/shard_map/ppermute | solution.py:20
  16.2 7.2 %collective-permute-start.8 = (bf16[2,24,1024]{2,1,0:T(8,128)(2,1)S(1)}, bf16[2,24,1024]{2,1,0:T(8,128)(2,1)S(1)}, u32[]{:S(2)}, u32[]{:S(2)}) collective-permute-start(bf16[2,24,1024]{2,1,0:T(8,128)(2,1)S(1)} %slice.75), channel_id=1, source_target_pairs={{0,8},{4,12},{8,0},{12,4},{16,24},{20,28},{24,16},{28,20},{1,9},{5... | collective-permute-start | bytes 294920 | tf_op jit(solution)/shard_map/ppermute | solution.py:20
  23.5 17.8 %collective-permute-start.17 = (bf16[2,4,1024,512]{3,2,1,0:T(8,128)(2,1)S(1)}, bf16[2,4,1024,512]{3,2,1,0:T(8,128)(2,1)S(1)}, u32[]{:S(2)}, u32[]{:S(2)}) collective-permute-start(bf16[2,4,1024,512]{3,2,1,0:T(8,128)(2,1)S(1)} %lend.1), channel_id=1, source_target_pairs={{0,4},{4,0},{8,12},{12,8},{16,20},{20,16},{24,28},{28,24},{1,5},{5... | collective-permute-start | bytes 25165832 | tf_op jit(solution)/shard_map/ppermute | solution.py:20
  23.5 9.4 %collective-permute-start.11 = (bf16[2,72,1024]{2,1,0:T(8,128)(2,1)S(1)}, bf16[2,72,1024]{2,1,0:T(8,128)(2,1)S(1)}, u32[]{:S(2)}, u32[]{:S(2)}) collective-permute-start(bf16[2,72,1024]{2,1,0:T(8,128)(2,1)S(1)} %pad_maximum_fusion.refs_0_), channel_id=1, source_target_pairs={{0,8},{4,12},{8,0},{12,4},{16,24},{20,28},{24,16},{28,20},{1,9},{5... | collective-permute-start | bytes 884744 | tf_op jit(solution)/shard_map/ppermute | solution.py:20
  24.1 9.1 %collective-permute-start.12 = (bf16[2,72,1024]{2,1,0:T(8,128)(2,1)S(1)}, bf16[2,72,1024]{2,1,0:T(8,128)(2,1)S(1)}, u32[]{:S(2)}, u32[]{:S(2)}) collective-permute-start(bf16[2,72,1024]{2,1,0:T(8,128)(2,1)S(1)} %pad_maximum_fusion.refs_0_), channel_id=1, source_target_pairs={{0,16},{4,20},{8,24},{12,28},{16,0},{20,4},{24,8},{28,12},{1,17},{... | collective-permute-start | bytes 884744 | tf_op jit(solution)/shard_map/ppermute | solution.py:20
  24.6 11.5 %collective-permute-start.10 = (bf16[2,24,1024]{2,1,0:T(8,128)(2,1)S(1)}, bf16[2,24,1024]{2,1,0:T(8,128)(2,1)S(1)}, u32[]{:S(2)}, u32[]{:S(2)}) collective-permute-start(bf16[2,24,1024]{2,1,0:T(8,128)(2,1)S(1)} %get-tuple-element.81), channel_id=1, source_target_pairs={{0,2},{1,3},{2,0},{3,1},{4,6},{5,7},{6,4},{7,5},{8,10},{9,11},{10,... | collective-permute-start | bytes 294920 | tf_op jit(solution)/shard_map/ppermute | solution.py:20
  27.1 9.1 %collective-permute-start.9 = (bf16[2,24,1024]{2,1,0:T(8,128)(2,1)S(1)}, bf16[2,24,1024]{2,1,0:T(8,128)(2,1)S(1)}, u32[]{:S(2)}, u32[]{:S(2)}) collective-permute-start(bf16[2,24,1024]{2,1,0:T(8,128)(2,1)S(1)} %get-tuple-element.80), channel_id=1, source_target_pairs={{0,3},{1,2},{2,1},{3,0},{4,7},{5,6},{6,5},{7,4},{8,11},{9,10},{10,... | collective-permute-start | bytes 294920 | tf_op jit(solution)/shard_map/ppermute | solution.py:20
  33.2 8.0 %collective-permute-start.16 = (bf16[2,40,1024]{2,1,0:T(8,128)(2,1)S(1)}, bf16[2,40,1024]{2,1,0:T(8,128)(2,1)S(1)}, u32[]{:S(2)}, u32[]{:S(2)}) collective-permute-start(bf16[2,40,1024]{2,1,0:T(8,128)(2,1)S(1)} %slice.59), channel_id=1, source_target_pairs={{0,8},{4,12},{8,0},{12,4},{16,24},{20,28},{24,16},{28,20},{1,9},{5... | collective-permute-start | bytes 491528 | tf_op jit(solution)/shard_map/ppermute | solution.py:20
  36.2 8.9 %collective-permute-start.13 = (bf16[2,72,1024]{2,1,0:T(8,128)(2,1)S(1)}, bf16[2,72,1024]{2,1,0:T(8,128)(2,1)S(1)}, u32[]{:S(2)}, u32[]{:S(2)}) collective-permute-start(bf16[2,72,1024]{2,1,0:T(8,128)(2,1)S(1)} %pad_maximum_fusion.1.refs_0_), channel_id=1, source_target_pairs={{0,8},{4,12},{8,0},{12,4},{16,24},{20,28},{24,16},{28,20},{1,9},{5... | collective-permute-start | bytes 884744 | tf_op jit(solution)/shard_map/ppermute | solution.py:20
  36.8 9.1 %collective-permute-start.14 = (bf16[2,72,1024]{2,1,0:T(8,128)(2,1)S(1)}, bf16[2,72,1024]{2,1,0:T(8,128)(2,1)S(1)}, u32[]{:S(2)}, u32[]{:S(2)}) collective-permute-start(bf16[2,72,1024]{2,1,0:T(8,128)(2,1)S(1)} %pad_maximum_fusion.1.refs_0_), channel_id=1, source_target_pairs={{0,16},{4,20},{8,24},{12,28},{16,0},{20,4},{24,8},{28,12},{1,17},{... | collective-permute-start | bytes 884744 | tf_op jit(solution)/shard_map/ppermute | solution.py:20
  46.7 7.1 %collective-permute-start.20 = (bf16[2,40,1024]{2,1,0:T(8,128)(2,1)S(1)}, bf16[2,40,1024]{2,1,0:T(8,128)(2,1)S(1)}, u32[]{:S(2)}, u32[]{:S(2)}) collective-permute-start(bf16[2,40,1024]{2,1,0:T(8,128)(2,1)S(1)} %get-tuple-element.104), channel_id=1, source_target_pairs={{0,16},{4,20},{8,24},{12,28},{16,0},{20,4},{24,8},{28,12},{1,17},{... | collective-permute-start | bytes 491528 | tf_op jit(solution)/shard_map/ppermute | solution.py:20
  48.2 8.4 %collective-permute-start.19 = (bf16[2,40,1024]{2,1,0:T(8,128)(2,1)S(1)}, bf16[2,40,1024]{2,1,0:T(8,128)(2,1)S(1)}, u32[]{:S(2)}, u32[]{:S(2)}) collective-permute-start(bf16[2,40,1024]{2,1,0:T(8,128)(2,1)S(1)} %slice.61), channel_id=1, source_target_pairs={{0,8},{4,12},{8,0},{12,4},{16,24},{20,28},{24,16},{28,20},{1,9},{5... | collective-permute-start | bytes 491528 | tf_op jit(solution)/shard_map/ppermute | solution.py:20
  49.4 7.2 %collective-permute-start.18 = (bf16[2,32,1024]{2,1,0:T(8,128)(2,1)S(1)}, bf16[2,32,1024]{2,1,0:T(8,128)(2,1)S(1)}, u32[]{:S(2)}, u32[]{:S(2)}) collective-permute-start(bf16[2,32,1024]{2,1,0:T(8,128)(2,1)S(1)} %slice.60), channel_id=1, source_target_pairs={{0,16},{4,20},{8,24},{12,28},{16,0},{20,4},{24,8},{28,12},{1,17},{... | collective-permute-start | bytes 393224 | tf_op jit(solution)/shard_map/ppermute | solution.py:20
  52.2 8.3 %collective-permute-start.23 = (bf16[2,72,1024]{2,1,0:T(8,128)(2,1)S(1)}, bf16[2,72,1024]{2,1,0:T(8,128)(2,1)S(1)}, u32[]{:S(2)}, u32[]{:S(2)}) collective-permute-start(bf16[2,72,1024]{2,1,0:T(8,128)(2,1)S(1)} %pad_maximum_fusion.3), channel_id=1, source_target_pairs={{0,16},{4,20},{8,24},{12,28},{16,0},{20,4},{24,8},{28,12},{1,17},{... | collective-permute-start | bytes 884744 | tf_op jit(solution)/shard_map/ppermute | solution.py:20
  53.8 6.8 %collective-permute-start.22 = (bf16[2,72,1024]{2,1,0:T(8,128)(2,1)S(1)}, bf16[2,72,1024]{2,1,0:T(8,128)(2,1)S(1)}, u32[]{:S(2)}, u32[]{:S(2)}) collective-permute-start(bf16[2,72,1024]{2,1,0:T(8,128)(2,1)S(1)} %pad_maximum_fusion.2), channel_id=1, source_target_pairs={{0,8},{4,12},{8,0},{12,4},{16,24},{20,28},{24,16},{28,20},{1,9},{5... | collective-permute-start | bytes 884744 | tf_op jit(solution)/shard_map/ppermute | solution.py:20
  61.9 7.2 %collective-permute-start.26 = (bf16[2,40,1024]{2,1,0:T(8,128)(2,1)S(1)}, bf16[2,40,1024]{2,1,0:T(8,128)(2,1)S(1)}, u32[]{:S(2)}, u32[]{:S(2)}) collective-permute-start(bf16[2,40,1024]{2,1,0:T(8,128)(2,1)S(1)} %get-tuple-element.120), channel_id=1, source_target_pairs={{0,16},{4,20},{8,24},{12,28},{16,0},{20,4},{24,8},{28,12},{1,17},{... | collective-permute-start | bytes 491528 | tf_op jit(solution)/shard_map/ppermute | solution.py:20
  64.1 9.5 %collective-permute-start.25 = (bf16[2,24,1024]{2,1,0:T(8,128)(2,1)S(1)}, bf16[2,24,1024]{2,1,0:T(8,128)(2,1)S(1)}, u32[]{:S(2)}, u32[]{:S(2)}) collective-permute-start(bf16[2,24,1024]{2,1,0:T(8,128)(2,1)S(1)} %get-tuple-element.135), channel_id=1, source_target_pairs={{0,8},{4,12},{8,0},{12,4},{16,24},{20,28},{24,16},{28,20},{1,9},{5... | collective-permute-start | bytes 294920 | tf_op jit(solution)/shard_map/ppermute | solution.py:20
  64.5 10.5 %collective-permute-start.24 = (bf16[2,24,1024]{2,1,0:T(8,128)(2,1)S(1)}, bf16[2,24,1024]{2,1,0:T(8,128)(2,1)S(1)}, u32[]{:S(2)}, u32[]{:S(2)}) collective-permute-start(bf16[2,24,1024]{2,1,0:T(8,128)(2,1)S(1)} %get-tuple-element.136), channel_id=1, source_target_pairs={{0,16},{4,20},{8,24},{12,28},{16,0},{20,4},{24,8},{28,12},{1,17},{... | collective-permute-start | bytes 294920 | tf_op jit(solution)/shard_map/ppermute | solution.py:20
  65.6 10.6 %collective-permute-start.31 = (bf16[2,72,1024]{2,1,0:T(8,128)(2,1)S(1)}, bf16[2,72,1024]{2,1,0:T(8,128)(2,1)S(1)}, u32[]{:S(2)}, u32[]{:S(2)}) collective-permute-start(bf16[2,72,1024]{2,1,0:T(8,128)(2,1)S(1)} %pad_maximum_fusion.5), channel_id=1, source_target_pairs={{0,16},{4,20},{8,24},{12,28},{16,0},{20,4},{24,8},{28,12},{1,17},{... | collective-permute-start | bytes 884744 | tf_op jit(solution)/shard_map/ppermute | solution.py:20
  69.1 7.7 %collective-permute-start.30 = (bf16[2,72,1024]{2,1,0:T(8,128)(2,1)S(1)}, bf16[2,72,1024]{2,1,0:T(8,128)(2,1)S(1)}, u32[]{:S(2)}, u32[]{:S(2)}) collective-permute-start(bf16[2,72,1024]{2,1,0:T(8,128)(2,1)S(1)} %pad_maximum_fusion.4), channel_id=1, source_target_pairs={{0,8},{4,12},{8,0},{12,4},{16,24},{20,28},{24,16},{28,20},{1,9},{5... | collective-permute-start | bytes 884744 | tf_op jit(solution)/shard_map/ppermute | solution.py:20
  70.4 7.2 %collective-permute-start.33 = (bf16[2,24,1024]{2,1,0:T(8,128)(2,1)S(1)}, bf16[2,24,1024]{2,1,0:T(8,128)(2,1)S(1)}, u32[]{:S(2)}, u32[]{:S(2)}) collective-permute-start(bf16[2,24,1024]{2,1,0:T(8,128)(2,1)S(1)} %get-tuple-element.133), channel_id=1, source_target_pairs={{0,2},{1,3},{2,0},{3,1},{4,6},{5,7},{6,4},{7,5},{8,10},{9,11},{10,... | collective-permute-start | bytes 294920 | tf_op jit(solution)/shard_map/ppermute | solution.py:20
  73.5 7.9 %collective-permute-start.35 = (bf16[2,24,1024]{2,1,0:T(8,128)(2,1)S(1)}, bf16[2,24,1024]{2,1,0:T(8,128)(2,1)S(1)}, u32[]{:S(2)}, u32[]{:S(2)}) collective-permute-start(bf16[2,24,1024]{2,1,0:T(8,128)(2,1)S(1)} %get-tuple-element.132), channel_id=1, source_target_pairs={{0,3},{1,2},{2,1},{3,0},{4,7},{5,6},{6,5},{7,4},{8,11},{9,10},{10,... | collective-permute-start | bytes 294920 | tf_op jit(solution)/shard_map/ppermute | solution.py:20
  75.0 8.2 %collective-permute-start.28 = (bf16[4,24,1024]{2,1,0:T(8,128)(2,1)S(1)}, bf16[4,24,1024]{2,1,0:T(8,128)(2,1)S(1)}, u32[]{:S(2)}, u32[]{:S(2)}) collective-permute-start(bf16[4,24,1024]{2,1,0:T(8,128)(2,1)S(1)} %pad_maximum_fusion.7), channel_id=1, source_target_pairs={{0,8},{4,12},{8,0},{12,4},{16,24},{20,28},{24,16},{28,20},{1,9},{5... | collective-permute-start | bytes 589832 | tf_op jit(solution)/shard_map/ppermute | solution.py:20
  76.2 7.0 %collective-permute-start.29 = (bf16[4,24,1024]{2,1,0:T(8,128)(2,1)S(1)}, bf16[4,24,1024]{2,1,0:T(8,128)(2,1)S(1)}, u32[]{:S(2)}, u32[]{:S(2)}) collective-permute-start(bf16[4,24,1024]{2,1,0:T(8,128)(2,1)S(1)} %pad_maximum_fusion.8), channel_id=1, source_target_pairs={{0,16},{4,20},{8,24},{12,28},{16,0},{20,4},{24,8},{28,12},{1,17},{... | collective-permute-start | bytes 589832 | tf_op jit(solution)/shard_map/ppermute | solution.py:20
  77.1 10.8 %collective-permute-start.32 = (bf16[4,24,1024]{2,1,0:T(8,128)(2,1)S(1)}, bf16[4,24,1024]{2,1,0:T(8,128)(2,1)S(1)}, u32[]{:S(2)}, u32[]{:S(2)}) collective-permute-start(bf16[4,24,1024]{2,1,0:T(8,128)(2,1)S(1)} %pad_maximum_fusion.9), channel_id=1, source_target_pairs={{0,1},{1,0},{2,3},{3,2},{4,5},{5,4},{6,7},{7,6},{8,9},{9,8},{10,11... | collective-permute-start | bytes 589832 | tf_op jit(solution)/shard_map/ppermute | solution.py:20
  77.6 7.3 %collective-permute-start.34 = (bf16[2,24,1024]{2,1,0:T(8,128)(2,1)S(1)}, bf16[2,24,1024]{2,1,0:T(8,128)(2,1)S(1)}, u32[]{:S(2)}, u32[]{:S(2)}) collective-permute-start(bf16[2,24,1024]{2,1,0:T(8,128)(2,1)S(1)} %get-tuple-element.130), channel_id=1, source_target_pairs={{0,2},{1,3},{2,0},{3,1},{4,6},{5,7},{6,4},{7,5},{8,10},{9,11},{10,... | collective-permute-start | bytes 294920 | tf_op jit(solution)/shard_map/ppermute | solution.py:20
  81.4 6.5 %collective-permute-start.36 = (bf16[2,24,1024]{2,1,0:T(8,128)(2,1)S(1)}, bf16[2,24,1024]{2,1,0:T(8,128)(2,1)S(1)}, u32[]{:S(2)}, u32[]{:S(2)}) collective-permute-start(bf16[2,24,1024]{2,1,0:T(8,128)(2,1)S(1)} %get-tuple-element.129), channel_id=1, source_target_pairs={{0,3},{1,2},{2,1},{3,0},{4,7},{5,6},{6,5},{7,4},{8,11},{9,10},{10,... | collective-permute-start | bytes 294920 | tf_op jit(solution)/shard_map/ppermute | solution.py:20
  (6 other events, 23.1 us)

commit v8 on v7

--- a/solution.py
+++ b/solution.py
@@ -52,8 +52,9 @@
     return pl.BlockSpec(memory_space=pltpu.SMEM)
 
 
-def embed_kernel(tubelets_ref, weight_ref, gain_ref, emb_ref, normed_ref, tub, weight, gain, sems):
-    parts = sems.shape[0] - 2
+def embed_kernel(tubelets_ref, weight_ref, gain_ref, route_ref, code_ref,
+                 emb_ref, normed_ref, route_out, code_out, tub, weight, gain, sems):
+    parts = sems.shape[0] - 4
     depth = weight_ref.shape[0] // parts
     copies = []
     for k in range(parts):
@@ -61,7 +62,9 @@
         copies.append(pltpu.make_async_copy(weight_ref.at[rows], weight.at[rows], sems.at[k]))
     tub_copy = pltpu.make_async_copy(tubelets_ref, tub, sems.at[parts])
     gain_copy = pltpu.make_async_copy(gain_ref, gain, sems.at[parts + 1])
-    for copy in (tub_copy, *copies, gain_copy):
+    small = [gain_copy, pltpu.make_async_copy(route_ref, route_out, sems.at[parts + 2]),
+             pltpu.make_async_copy(code_ref, code_out, sems.at[parts + 3])]
+    for copy in (tub_copy, *copies, *small):
         copy.start()
     tub_copy.wait()
     total = None
@@ -75,41 +78,43 @@
     floats = embedded.astype(F32)
     centred = floats - jnp.mean(floats, axis=-1, keepdims=True)
     variance = jnp.mean(centred * centred, axis=-1, keepdims=True)
-    gain_copy.wait()
+    for copy in small:
+        copy.wait()
     normed_ref[...] = (centred * lax.rsqrt(variance + 1e-06) * gain[...]).astype(BF16)
 
 
-def embed(tubelets, weight, gain):
+def embed(tubelets, weight, gain, routes, codes):
     tok, width = tubelets.shape[0], weight.shape[1]
     parts = 6
     shape = pltpu.VMEM((tok, width), BF16)
     return pl.pallas_call(
         embed_kernel,
-        out_shape=[shape, shape],
-        in_specs=[hbm()] * 3,
-        out_specs=[vmem()] * 2,
+        out_shape=[shape, shape, pltpu.VMEM(routes.shape, routes.dtype), pltpu.VMEM(codes.shape, codes.dtype)],
+        in_specs=[hbm()] * 5,
+        out_specs=[vmem()] * 4,
         scratch_shapes=[pltpu.VMEM(tubelets.shape, BF16), pltpu.VMEM(weight.shape, BF16),
-                        pltpu.VMEM((1, width), F32), pltpu.SemaphoreType.DMA((parts + 2,))],
+                        pltpu.VMEM((1, width), F32), pltpu.SemaphoreType.DMA((parts + 4,))],
         compiler_params=pltpu.CompilerParams(vmem_limit_bytes=VMEM_LIMIT),
         cost_estimate=pl.CostEstimate(flops=2 * tok * weight.size, bytes_accessed=weight.size * 2, transcendentals=0),
         name="embed",
-    )(in_hbm(tubelets), in_hbm(weight), in_hbm(gain.reshape(1, width)))
-
-
-def route_kernel(n_exp, half, cap, place_ref, code_ref, sib_code_ref, select_ref, gate_ref):
+    )(in_hbm(tubelets), in_hbm(weight), in_hbm(gain.reshape(1, width)), in_hbm(routes), in_hbm(codes))
+
+
+def route_kernel(n_exp, half, cap, place_ref, route_ref, sib_route_ref, code_ref, sib_code_ref, select_ref, gate_ref):
     tok = code_ref.shape[1]
     both = 2 * tok
     count = n_exp * half
     slots = 2 * cap
     rows = count * slots
+    routes = jnp.concatenate([route_ref[...], sib_route_ref[...]], axis=1)
     codes = jnp.concatenate([code_ref[...], sib_code_ref[...]], axis=1)
-    gates = 0.25 + 0.125 * codes[2:4].astype(F32)
+    gates = 0.25 + 0.125 * codes.astype(F32)
     plane, core = place_ref[0], place_ref[1]
 
     row = lax.broadcasted_iota(jnp.int32, (count, both), 0)
     expert = (plane ^ (row // half)) * (2 * half) + core * half + row % half
-    first = codes[0:1] == expert
-    second = codes[1:2] == expert
+    first = routes[0:1] == expert
+    second = routes[1:2] == expert
     member = first | second
     gated = jnp.where(first, gates[0:1, :], 0.0) + jnp.where(second, gates[1:2, :], 0.0)
     earlier = lax.broadcasted_iota(jnp.int32, (both, both), 0)
@@ -127,19 +132,19 @@
     gate_ref[...] = jnp.where(chosen, mm(spread, gated.astype(BF16)), 0.0).astype(BF16)
 
 
-def route(place, codes, sib_codes, n_exp, half, cap):
+def route(place, routes, sib_routes, codes, sib_codes, n_exp, half, cap):
     both = 2 * codes.shape[1]
     rows = n_exp * half * 2 * cap
     shape = jax.ShapeDtypeStruct((rows, both), BF16)
     return pl.pallas_call(
         functools.partial(route_kernel, n_exp, half, cap),
         out_shape=[shape, shape],
-        in_specs=[smem()] + [vmem()] * 2,
+        in_specs=[smem()] + [vmem()] * 4,
         out_specs=[vmem()] * 2,
         compiler_params=pltpu.CompilerParams(vmem_limit_bytes=VMEM_LIMIT),
         cost_estimate=pl.CostEstimate(flops=2 * rows * both * 64, bytes_accessed=rows * both * 4, transcendentals=0),
         name="route",
-    )(place, codes, sib_codes)
+    )(place, routes, sib_routes, codes, sib_codes)
 
 
 def pack_kernel(spans, select_ref, normed_ref, sib_ref, *piece_refs):
@@ -302,11 +307,11 @@
     place = jnp.stack([lax.axis_index("exp"), core]).astype(jnp.int32)
 
     core_bit = 1 << CORE
-    codes = jnp.concatenate([routes.T, gate_codes.T], axis=0)
-    sib_codes = swapped(codes, "rep", core_bit)
-    embedded, normed = embed(after(tubelets, codes), embed_weight, norm_gain)
+    routes, codes = routes.T, gate_codes.T
+    sib_routes, sib_codes = swapped(routes, "rep", core_bit), swapped(codes, "rep", core_bit)
+    embedded, normed, routes, codes = embed(tubelets, embed_weight, norm_gain, routes, codes)
     sib_normed = swapped(normed, "rep", core_bit)
-    select, gate = route(place, codes, sib_codes, n_exp, half, cap)
+    select, gate = route(place, routes, sib_routes, codes, sib_codes, n_exp, half, cap)
 
     for bit in range(GROUP_BITS, lax.axis_size("rep").bit_length() - 1):
         upper = position // (1 << bit) % 2 == 1
@@ -363,7 +368,7 @@
     d1 = lax.optimization_barrier((*d1, *sums0))[:2]
     from_a0, from_b0 = to_a(sums0[0]), to_b(sums0[1])
     parts1 = experts(cut, (far1, a1, b1, *d1, own, own_a, own_b, *own_d), sib, in_own, down_own)
-    parts1[3], parts1[4] = lax.optimization_barrier((parts1[3], parts1[4], from_a0, from_b0))[:2]
+    parts1[3], parts1[4] = lax.optimization_barrier((parts1[3], parts1[4], from_b0))[:2]
     r1 = to_a(parts1[3]), to_b(parts1[4])
     returned0 = back(parts0[0], from_a0, from_b0, range(2, n_exp))
     sums1 = reduced(parts1, r1)

time: 90.9 us -> 89.7 us (0.987)
    ppermute x38 -> x39, waiting for transfers between devices: 19.7 us -> 19 us  [swapped(): lax.ppermute(array, axis, [(i, i ^ distance) for i in range(lax.axis_size...]
    ppermute x38 -> x39, starting transfers between devices: 48.6 us -> 48.8 us  [swapped(): lax.ppermute(array, axis, [(i, i ^ distance) for i in range(lax.axis_size...]
  transfers between devices with their start and end apart: 38 -> 39, of which waited for: 17 -> 18; matrix products, arithmetic and copies ran while one was open for 1% -> 1% of each run, Pallas kernels for 18% -> 18%
where the time goes in v8:
time: 89.7 us; the launch traced here: 89.6 us
  starting transfers between devices  48.8 us (54%)
  Pallas kernels  19.8 us (22%)
  waiting for transfers between devices  19 us (21%)
  other arithmetic  1.44 us (2%)
    ppermute x39, starting transfers between devices, swapped(): lax.ppermute(array, axis, [(i, i ^ distance) for i in range(lax.axis_size...  48.8 us
    ppermute x39, waiting for transfers between devices, swapped(): lax.ppermute(array, axis, [(i, i ^ distance) for i in range(lax.axis_size...  19 us
    pallas_call x2, Pallas kernels, experts(): pl.pallas_call(functools.partial(experts_kernel, first), out_shape=[pltpu...  7.42 us
    pallas_call x1, Pallas kernels, lend(): pl.pallas_call(lend_kernel, out_shape=pltpu.VMEM(shape, BF16), in_specs=[...  4.02 us
    pallas_call x1, Pallas kernels, hold(): pl.pallas_call(hold_kernel, out_shape=[shape, shape], in_specs=[smem(), h...  4.02 us
    pallas_call x1, Pallas kernels, embed(): pl.pallas_call(embed_kernel, out_shape=[shape, shape, pltpu.VMEM(routes.s...  2.53 us
  transfers between devices with their start and end apart: 39, of which 18 were waited for; matrix products, arithmetic and copies ran while one was open for 1% of the time, Pallas kernels for 18%

profile of v8, /device:TPU:0, one launch (start us, length us, event | category | flops | bytes accessed | tf_op | source)
XLA Modules:
  0.0 89.6 jit_solution(16722689296691016827)
XLA Ops:
  0.0 2.5 %embed.1 = (bf16[128,1024]{1,0:T(8,128)(2,1)S(1)}, bf16[128,1024]{1,0:T(8,128)(2,1)S(1)}, s32[2,128]{1,0:T(2,128)S(1)}, s32[2,128]{1,0:T(2,128)S(1)}) custom-call(bf16[128,1536]{1,0:T(8,128)(2,1)} %tubelets_ref.1, bf16[1536,1024]{1,0:T(8,128)(2,1)} %weight_ref.1, f32[1,1024]{1,0:T(1,128)} %bitcast.5, s32[2,128]{1,0:T(2,128)} %bitcast.6, s32[2,128]{1,0:T(2,128)} %bitcast.8), custom_call_target="tpu_custom_call" | custom-call | flops 402653184 | bytes 3145728 | tf_op jit(solution)/shard_map/embed/pallas_call | solution.py:90
  5.9 2.9 %collective-permute-start.6 = (bf16[4,24,1024]{2,1,0:T(8,128)(2,1)S(1)}, bf16[4,24,1024]{2,1,0:T(8,128)(2,1)S(1)}, u32[]{:S(2)}, u32[]{:S(2)}) collective-permute-start(bf16[4,24,1024]{2,1,0:T(8,128)(2,1)S(1)} %get-tuple-element.77.refs_5_), channel_id=1, source_target_pairs={{0,8},{4,12},{8,0},{12,4},{16,24},{20,28},{24,16},{28,20},{1,9},{5... | collective-permute-start | bytes 589832 | tf_op jit(solution)/shard_map/ppermute | solution.py:20
  8.8 1.5 %collective-permute-start.7 = (bf16[4,24,1024]{2,1,0:T(8,128)(2,1)S(1)}, bf16[4,24,1024]{2,1,0:T(8,128)(2,1)S(1)}, u32[]{:S(2)}, u32[]{:S(2)}) collective-permute-start(bf16[4,24,1024]{2,1,0:T(8,128)(2,1)S(1)} %get-tuple-element.77.refs_5_), channel_id=1, source_target_pairs={{0,16},{4,20},{8,24},{12,28},{16,0},{20,4},{24,8},{28,12},{1,17},{... | collective-permute-start | bytes 589832 | tf_op jit(solution)/shard_map/ppermute | solution.py:20
  10.3 1.6 %collective-permute-start.3 = (bf16[4,24,1024]{2,1,0:T(8,128)(2,1)S(1)}, bf16[4,24,1024]{2,1,0:T(8,128)(2,1)S(1)}, u32[]{:S(2)}, u32[]{:S(2)}) collective-permute-start(bf16[4,24,1024]{2,1,0:T(8,128)(2,1)S(1)} %get-tuple-element.74), channel_id=1, source_target_pairs={{0,1},{1,0},{2,3},{3,2},{4,5},{5,4},{6,7},{7,6},{8,9},{9,8},{10,11... | collective-permute-start | bytes 589832 | tf_op jit(solution)/shard_map/ppermute | solution.py:20
  11.9 2.6 %collective-permute-start.4 = (bf16[2,24,1024]{2,1,0:T(8,128)(2,1)S(1)}, bf16[2,24,1024]{2,1,0:T(8,128)(2,1)S(1)}, u32[]{:S(2)}, u32[]{:S(2)}) collective-permute-start(bf16[2,24,1024]{2,1,0:T(8,128)(2,1)S(1)} %get-tuple-element.75), channel_id=1, source_target_pairs={{0,2},{1,3},{2,0},{3,1},{4,6},{5,7},{6,4},{7,5},{8,10},{9,11},{10,... | collective-permute-start | bytes 294920 | tf_op jit(solution)/shard_map/ppermute | solution.py:20
  15.9 1.6 %collective-permute-start.9 = (bf16[2,24,1024]{2,1,0:T(8,128)(2,1)S(1)}, bf16[2,24,1024]{2,1,0:T(8,128)(2,1)S(1)}, u32[]{:S(2)}, u32[]{:S(2)}) collective-permute-start(bf16[2,24,1024]{2,1,0:T(8,128)(2,1)S(1)} %slice.75), channel_id=1, source_target_pairs={{0,8},{4,12},{8,0},{12,4},{16,24},{20,28},{24,16},{28,20},{1,9},{5... | collective-permute-start | bytes 294920 | tf_op jit(solution)/shard_map/ppermute | solution.py:20
  17.5 1.4 %collective-permute-done.3 = bf16[4,24,1024]{2,1,0:T(8,128)(2,1)S(1)} collective-permute-done((bf16[4,24,1024]{2,1,0:T(8,128)(2,1)S(1)}, bf16[4,24,1024]{2,1,0:T(8,128)(2,1)S(1)}, u32[]{:S(2)}, u32[]{:S(2)}) %collective-permute-start.3) | collective-permute-done | bytes 196640 | tf_op jit(solution)/shard_map/ppermute | solution.py:20
  18.9 4.0 %lend.1 = bf16[2,4,1024,512]{3,2,1,0:T(8,128)(2,1)S(1)} custom-call(s32[2]{0:T(128)S(1)} %pad_add_fusion.place_ref, bf16[8,1024,512]{2,1,0:T(8,128)(2,1)} %in_ref.3, bf16[8,1024,512]{2,1,0:T(8,128)(2,1)} %down_ref.3), custom_call_target="tpu_custom_call" | custom-call | bytes 16777216 | tf_op jit(solution)/shard_map/lend/pallas_call | solution.py:192
  24.3 4.3 %collective-permute-start.10 = (bf16[2,24,1024]{2,1,0:T(8,128)(2,1)S(1)}, bf16[2,24,1024]{2,1,0:T(8,128)(2,1)S(1)}, u32[]{:S(2)}, u32[]{:S(2)}) collective-permute-start(bf16[2,24,1024]{2,1,0:T(8,128)(2,1)S(1)} %get-tuple-element.82), channel_id=1, source_target_pairs={{0,3},{1,2},{2,1},{3,0},{4,7},{5,6},{6,5},{7,4},{8,11},{9,10},{10,... | collective-permute-start | bytes 294920 | tf_op jit(solution)/shard_map/ppermute | solution.py:20
  28.6 4.0 %hold.1 = (bf16[4,1024,512]{2,1,0:T(8,128)(2,1)S(1)}, bf16[4,1024,512]{2,1,0:T(8,128)(2,1)S(1)}) custom-call(s32[2]{0:T(128)S(1)} %pad_add_fusion.place_ref, bf16[8,1024,512]{2,1,0:T(8,128)(2,1)} %in_ref.3, bf16[8,1024,512]{2,1,0:T(8,128)(2,1)} %down_ref.3), custom_call_target="tpu_custom_call" | custom-call | bytes 16777216 | tf_op jit(solution)/shard_map/hold/pallas_call | solution.py:218
  32.9 1.6 %collective-permute-start.17 = (bf16[2,40,1024]{2,1,0:T(8,128)(2,1)S(1)}, bf16[2,40,1024]{2,1,0:T(8,128)(2,1)S(1)}, u32[]{:S(2)}, u32[]{:S(2)}) collective-permute-start(bf16[2,40,1024]{2,1,0:T(8,128)(2,1)S(1)} %slice.59), channel_id=1, source_target_pairs={{0,8},{4,12},{8,0},{12,4},{16,24},{20,28},{24,16},{28,20},{1,9},{5... | collective-permute-start | bytes 491528 | tf_op jit(solution)/shard_map/ppermute | solution.py:20
  34.5 1.4 %collective-permute-start.16 = (bf16[2,32,1024]{2,1,0:T(8,128)(2,1)S(1)}, bf16[2,32,1024]{2,1,0:T(8,128)(2,1)S(1)}, u32[]{:S(2)}, u32[]{:S(2)}) collective-permute-start(bf16[2,32,1024]{2,1,0:T(8,128)(2,1)S(1)} %slice.58), channel_id=1, source_target_pairs={{0,16},{4,20},{8,24},{12,28},{16,0},{20,4},{24,8},{28,12},{1,17},{... | collective-permute-start | bytes 393224 | tf_op jit(solution)/shard_map/ppermute | solution.py:20
  35.9 1.6 %collective-permute-start.14 = (bf16[2,72,1024]{2,1,0:T(8,128)(2,1)S(1)}, bf16[2,72,1024]{2,1,0:T(8,128)(2,1)S(1)}, u32[]{:S(2)}, u32[]{:S(2)}) collective-permute-start(bf16[2,72,1024]{2,1,0:T(8,128)(2,1)S(1)} %pad_maximum_fusion.1.refs_0_), channel_id=1, source_target_pairs={{0,8},{4,12},{8,0},{12,4},{16,24},{20,28},{24,16},{28,20},{1,9},{5... | collective-permute-start | bytes 884744 | tf_op jit(solution)/shard_map/ppermute | solution.py:20
  37.5 1.5 %collective-permute-start.15 = (bf16[2,72,1024]{2,1,0:T(8,128)(2,1)S(1)}, bf16[2,72,1024]{2,1,0:T(8,128)(2,1)S(1)}, u32[]{:S(2)}, u32[]{:S(2)}) collective-permute-start(bf16[2,72,1024]{2,1,0:T(8,128)(2,1)S(1)} %pad_maximum_fusion.1.refs_0_), channel_id=1, source_target_pairs={{0,16},{4,20},{8,24},{12,28},{16,0},{20,4},{24,8},{28,12},{1,17},{... | collective-permute-start | bytes 884744 | tf_op jit(solution)/shard_map/ppermute | solution.py:20
  39.5 3.7 %experts.2 = (bf16[2,72,1024]{2,1,0:T(8,128)(2,1)S(1)}, bf16[2,72,1024]{2,1,0:T(8,128)(2,1)S(1)}, bf16[2,72,1024]{2,1,0:T(8,128)(2,1)S(1)}, bf16[2,32,1024]{2,1,...) custom-call(bf16[2,72,1024]{2,1,0:T(8,128)(2,1)S(1)} %pad_maximum_fu, ...), custom_call_target="tpu_custom_call" | custom-call | flops 3221225472 | bytes 3145728 | tf_op jit(solution)/shard_map/experts/pallas_call | solution.py:254
  43.3 1.7 %collective-permute-done.14.refs_1_ = bf16[2,72,1024]{2,1,0:T(8,128)(2,1)S(1)} collective-permute-done((bf16[2,72,1024]{2,1,0:T(8,128)(2,1)S(1)}, bf16[2,72,1024]{2,1,0:T(8,128)(2,1)S(1)}, u32[]{:S(2)}, u32[]{:S(2)}) %collective-permute-start.14) | collective-permute-done | bytes 294944 | tf_op jit(solution)/shard_map/ppermute | solution.py:20
  46.7 1.6 %collective-permute-start.21 = (bf16[2,40,1024]{2,1,0:T(8,128)(2,1)S(1)}, bf16[2,40,1024]{2,1,0:T(8,128)(2,1)S(1)}, u32[]{:S(2)}, u32[]{:S(2)}) collective-permute-start(bf16[2,40,1024]{2,1,0:T(8,128)(2,1)S(1)} %get-tuple-element.106), channel_id=1, source_target_pairs={{0,16},{4,20},{8,24},{12,28},{16,0},{20,4},{24,8},{28,12},{1,17},{... | collective-permute-start | bytes 491528 | tf_op jit(solution)/shard_map/ppermute | solution.py:20
  48.4 1.6 %collective-permute-start.20 = (bf16[2,40,1024]{2,1,0:T(8,128)(2,1)S(1)}, bf16[2,40,1024]{2,1,0:T(8,128)(2,1)S(1)}, u32[]{:S(2)}, u32[]{:S(2)}) collective-permute-start(bf16[2,40,1024]{2,1,0:T(8,128)(2,1)S(1)} %slice.61), channel_id=1, source_target_pairs={{0,8},{4,12},{8,0},{12,4},{16,24},{20,28},{24,16},{28,20},{1,9},{5... | collective-permute-start | bytes 491528 | tf_op jit(solution)/shard_map/ppermute | solution.py:20
  50.5 2.1 %collective-permute-done.22 = bf16[2,32,1024]{2,1,0:T(8,128)(2,1)S(1)} collective-permute-done((bf16[2,32,1024]{2,1,0:T(8,128)(2,1)S(1)}, bf16[2,32,1024]{2,1,0:T(8,128)(2,1)S(1)}, u32[]{:S(2)}, u32[]{:S(2)}) %collective-permute-start.22) | collective-permute-done | bytes 131104 | tf_op jit(solution)/shard_map/ppermute | solution.py:20
  52.6 1.3 %collective-permute-start.24 = (bf16[2,72,1024]{2,1,0:T(8,128)(2,1)S(1)}, bf16[2,72,1024]{2,1,0:T(8,128)(2,1)S(1)}, u32[]{:S(2)}, u32[]{:S(2)}) collective-permute-start(bf16[2,72,1024]{2,1,0:T(8,128)(2,1)S(1)} %pad_maximum_fusion.3), channel_id=1, source_target_pairs={{0,16},{4,20},{8,24},{12,28},{16,0},{20,4},{24,8},{28,12},{1,17},{... | collective-permute-start | bytes 884744 | tf_op jit(solution)/shard_map/ppermute | solution.py:20
  53.9 1.6 %collective-permute-start.23 = (bf16[2,72,1024]{2,1,0:T(8,128)(2,1)S(1)}, bf16[2,72,1024]{2,1,0:T(8,128)(2,1)S(1)}, u32[]{:S(2)}, u32[]{:S(2)}) collective-permute-start(bf16[2,72,1024]{2,1,0:T(8,128)(2,1)S(1)} %pad_maximum_fusion.2), channel_id=1, source_target_pairs={{0,8},{4,12},{8,0},{12,4},{16,24},{20,28},{24,16},{28,20},{1,9},{5... | collective-permute-start | bytes 884744 | tf_op jit(solution)/shard_map/ppermute | solution.py:20
  56.4 3.7 %experts.3 = (bf16[2,72,1024]{2,1,0:T(8,128)(2,1)S(1)}, bf16[2,72,1024]{2,1,0:T(8,128)(2,1)S(1)}, bf16[2,72,1024]{2,1,0:T(8,128)(2,1)S(1)}, bf16[2,32,1024]{2,1,...) custom-call(bf16[2,72,1024]{2,1,0:T(8,128)(2,1)S(1)} %pad_maximum_fu, ...), custom_call_target="tpu_custom_call" | custom-call | flops 3221225472 | bytes 3145728 | tf_op jit(solution)/shard_map/experts/pallas_call | solution.py:254
  62.1 1.5 %collective-permute-start.27 = (bf16[2,40,1024]{2,1,0:T(8,128)(2,1)S(1)}, bf16[2,40,1024]{2,1,0:T(8,128)(2,1)S(1)}, u32[]{:S(2)}, u32[]{:S(2)}) collective-permute-start(bf16[2,40,1024]{2,1,0:T(8,128)(2,1)S(1)} %get-tuple-element.122), channel_id=1, source_target_pairs={{0,16},{4,20},{8,24},{12,28},{16,0},{20,4},{24,8},{28,12},{1,17},{... | collective-permute-start | bytes 491528 | tf_op jit(solution)/shard_map/ppermute | solution.py:20
  67.3 1.2 %collective-permute-done.27 = bf16[2,40,1024]{2,1,0:T(8,128)(2,1)S(1)} collective-permute-done((bf16[2,40,1024]{2,1,0:T(8,128)(2,1)S(1)}, bf16[2,40,1024]{2,1,0:T(8,128)(2,1)S(1)}, u32[]{:S(2)}, u32[]{:S(2)}) %collective-permute-start.27) | collective-permute-done | bytes 163872 | tf_op jit(solution)/shard_map/ppermute | solution.py:20
  68.6 1.9 %collective-permute-start.31 = (bf16[2,72,1024]{2,1,0:T(8,128)(2,1)S(1)}, bf16[2,72,1024]{2,1,0:T(8,128)(2,1)S(1)}, u32[]{:S(2)}, u32[]{:S(2)}) collective-permute-start(bf16[2,72,1024]{2,1,0:T(8,128)(2,1)S(1)} %pad_maximum_fusion.4), channel_id=1, source_target_pairs={{0,8},{4,12},{8,0},{12,4},{16,24},{20,28},{24,16},{28,20},{1,9},{5... | collective-permute-start | bytes 884744 | tf_op jit(solution)/shard_map/ppermute | solution.py:20
  70.5 1.7 %collective-permute-start.34 = (bf16[2,24,1024]{2,1,0:T(8,128)(2,1)S(1)}, bf16[2,24,1024]{2,1,0:T(8,128)(2,1)S(1)}, u32[]{:S(2)}, u32[]{:S(2)}) collective-permute-start(bf16[2,24,1024]{2,1,0:T(8,128)(2,1)S(1)} %get-tuple-element.135), channel_id=1, source_target_pairs={{0,2},{1,3},{2,0},{3,1},{4,6},{5,7},{6,4},{7,5},{8,10},{9,11},{10,... | collective-permute-start | bytes 294920 | tf_op jit(solution)/shard_map/ppermute | solution.py:20
  72.2 1.9 %collective-permute-start.36 = (bf16[2,24,1024]{2,1,0:T(8,128)(2,1)S(1)}, bf16[2,24,1024]{2,1,0:T(8,128)(2,1)S(1)}, u32[]{:S(2)}, u32[]{:S(2)}) collective-permute-start(bf16[2,24,1024]{2,1,0:T(8,128)(2,1)S(1)} %get-tuple-element.134), channel_id=1, source_target_pairs={{0,3},{1,2},{2,1},{3,0},{4,7},{5,6},{6,5},{7,4},{8,11},{9,10},{10,... | collective-permute-start | bytes 294920 | tf_op jit(solution)/shard_map/ppermute | solution.py:20
  75.1 1.3 %collective-permute-start.30 = (bf16[4,24,1024]{2,1,0:T(8,128)(2,1)S(1)}, bf16[4,24,1024]{2,1,0:T(8,128)(2,1)S(1)}, u32[]{:S(2)}, u32[]{:S(2)}) collective-permute-start(bf16[4,24,1024]{2,1,0:T(8,128)(2,1)S(1)} %pad_maximum_fusion.8), channel_id=1, source_target_pairs={{0,16},{4,20},{8,24},{12,28},{16,0},{20,4},{24,8},{28,12},{1,17},{... | collective-permute-start | bytes 589832 | tf_op jit(solution)/shard_map/ppermute | solution.py:20
  77.4 2.9 %collective-permute-start.35 = (bf16[2,24,1024]{2,1,0:T(8,128)(2,1)S(1)}, bf16[2,24,1024]{2,1,0:T(8,128)(2,1)S(1)}, u32[]{:S(2)}, u32[]{:S(2)}) collective-permute-start(bf16[2,24,1024]{2,1,0:T(8,128)(2,1)S(1)} %get-tuple-element.132), channel_id=1, source_target_pairs={{0,2},{1,3},{2,0},{3,1},{4,6},{5,7},{6,4},{7,5},{8,10},{9,11},{10,... | collective-permute-start | bytes 294920 | tf_op jit(solution)/shard_map/ppermute | solution.py:20
  80.3 1.5 %collective-permute-start.37 = (bf16[2,24,1024]{2,1,0:T(8,128)(2,1)S(1)}, bf16[2,24,1024]{2,1,0:T(8,128)(2,1)S(1)}, u32[]{:S(2)}, u32[]{:S(2)}) collective-permute-start(bf16[2,24,1024]{2,1,0:T(8,128)(2,1)S(1)} %get-tuple-element.131), channel_id=1, source_target_pairs={{0,3},{1,2},{2,1},{3,0},{4,7},{5,6},{6,5},{7,4},{8,11},{9,10},{10,... | collective-permute-start | bytes 294920 | tf_op jit(solution)/shard_map/ppermute | solution.py:20
  81.8 3.8 %collective-permute-done.35.refs_6_ = bf16[2,24,1024]{2,1,0:T(8,128)(2,1)S(1)} collective-permute-done((bf16[2,24,1024]{2,1,0:T(8,128)(2,1)S(1)}, bf16[2,24,1024]{2,1,0:T(8,128)(2,1)S(1)}, u32[]{:S(2)}, u32[]{:S(2)}) %collective-permute-start.35) | collective-permute-done | bytes 98336 | tf_op jit(solution)/shard_map/ppermute | solution.py:20
  87.3 1.5 %collective-permute-done.38 = bf16[128,1024]{1,0:T(8,128)(2,1)S(1)} collective-permute-done((bf16[128,1024]{1,0:T(8,128)(2,1)S(1)}, bf16[128,1024]{1,0:T(8,128)(2,1)S(1)}, u32[]{:S(2)}, u32[]{:S(2)}) %collective-permute-start.38) | collective-permute-done | bytes 262176 | tf_op jit(solution)/shard_map/ppermute | solution.py:20
  (88 shorter events, 20.4 us)
Async XLA Ops:
  5.9 8.8 %collective-permute-start.6 = (bf16[4,24,1024]{2,1,0:T(8,128)(2,1)S(1)}, bf16[4,24,1024]{2,1,0:T(8,128)(2,1)S(1)}, u32[]{:S(2)}, u32[]{:S(2)}) collective-permute-start(bf16[4,24,1024]{2,1,0:T(8,128)(2,1)S(1)} %get-tuple-element.77.refs_5_), channel_id=1, source_target_pairs={{0,8},{4,12},{8,0},{12,4},{16,24},{20,28},{24,16},{28,20},{1,9},{5... | collective-permute-start | bytes 589832 | tf_op jit(solution)/shard_map/ppermute | solution.py:20
  8.8 7.1 %collective-permute-start.7 = (bf16[4,24,1024]{2,1,0:T(8,128)(2,1)S(1)}, bf16[4,24,1024]{2,1,0:T(8,128)(2,1)S(1)}, u32[]{:S(2)}, u32[]{:S(2)}) collective-permute-start(bf16[4,24,1024]{2,1,0:T(8,128)(2,1)S(1)} %get-tuple-element.77.refs_5_), channel_id=1, source_target_pairs={{0,16},{4,20},{8,24},{12,28},{16,0},{20,4},{24,8},{28,12},{1,17},{... | collective-permute-start | bytes 589832 | tf_op jit(solution)/shard_map/ppermute | solution.py:20
  10.3 8.5 %collective-permute-start.3 = (bf16[4,24,1024]{2,1,0:T(8,128)(2,1)S(1)}, bf16[4,24,1024]{2,1,0:T(8,128)(2,1)S(1)}, u32[]{:S(2)}, u32[]{:S(2)}) collective-permute-start(bf16[4,24,1024]{2,1,0:T(8,128)(2,1)S(1)} %get-tuple-element.74), channel_id=1, source_target_pairs={{0,1},{1,0},{2,3},{3,2},{4,5},{5,4},{6,7},{7,6},{8,9},{9,8},{10,11... | collective-permute-start | bytes 589832 | tf_op jit(solution)/shard_map/ppermute | solution.py:20
  11.9 11.0 %collective-permute-start.4 = (bf16[2,24,1024]{2,1,0:T(8,128)(2,1)S(1)}, bf16[2,24,1024]{2,1,0:T(8,128)(2,1)S(1)}, u32[]{:S(2)}, u32[]{:S(2)}) collective-permute-start(bf16[2,24,1024]{2,1,0:T(8,128)(2,1)S(1)} %get-tuple-element.75), channel_id=1, source_target_pairs={{0,2},{1,3},{2,0},{3,1},{4,6},{5,7},{6,4},{7,5},{8,10},{9,11},{10,... | collective-permute-start | bytes 294920 | tf_op jit(solution)/shard_map/ppermute | solution.py:20
  14.5 8.6 %collective-permute-start.5 = (bf16[2,24,1024]{2,1,0:T(8,128)(2,1)S(1)}, bf16[2,24,1024]{2,1,0:T(8,128)(2,1)S(1)}, u32[]{:S(2)}, u32[]{:S(2)}) collective-permute-start(bf16[2,24,1024]{2,1,0:T(8,128)(2,1)S(1)} %get-tuple-element.76), channel_id=1, source_target_pairs={{0,3},{1,2},{2,1},{3,0},{4,7},{5,6},{6,5},{7,4},{8,11},{9,10},{10,... | collective-permute-start | bytes 294920 | tf_op jit(solution)/shard_map/ppermute | solution.py:20
  14.7 8.4 %collective-permute-start.8 = (bf16[2,24,1024]{2,1,0:T(8,128)(2,1)S(1)}, bf16[2,24,1024]{2,1,0:T(8,128)(2,1)S(1)}, u32[]{:S(2)}, u32[]{:S(2)}) collective-permute-start(bf16[2,24,1024]{2,1,0:T(8,128)(2,1)S(1)} %slice.74), channel_id=1, source_target_pairs={{0,16},{4,20},{8,24},{12,28},{16,0},{20,4},{24,8},{28,12},{1,17},{... | collective-permute-start | bytes 294920 | tf_op jit(solution)/shard_map/ppermute | solution.py:20
  15.9 7.2 %collective-permute-start.9 = (bf16[2,24,1024]{2,1,0:T(8,128)(2,1)S(1)}, bf16[2,24,1024]{2,1,0:T(8,128)(2,1)S(1)}, u32[]{:S(2)}, u32[]{:S(2)}) collective-permute-start(bf16[2,24,1024]{2,1,0:T(8,128)(2,1)S(1)} %slice.75), channel_id=1, source_target_pairs={{0,8},{4,12},{8,0},{12,4},{16,24},{20,28},{24,16},{28,20},{1,9},{5... | collective-permute-start | bytes 294920 | tf_op jit(solution)/shard_map/ppermute | solution.py:20
  23.2 16.4 %collective-permute-start.18 = (bf16[2,4,1024,512]{3,2,1,0:T(8,128)(2,1)S(1)}, bf16[2,4,1024,512]{3,2,1,0:T(8,128)(2,1)S(1)}, u32[]{:S(2)}, u32[]{:S(2)}) collective-permute-start(bf16[2,4,1024,512]{3,2,1,0:T(8,128)(2,1)S(1)} %lend.1), channel_id=1, source_target_pairs={{0,4},{4,0},{8,12},{12,8},{16,20},{20,16},{24,28},{28,24},{1,5},{5... | collective-permute-start | bytes 25165832 | tf_op jit(solution)/shard_map/ppermute | solution.py:20
  23.2 9.4 %collective-permute-start.12 = (bf16[2,72,1024]{2,1,0:T(8,128)(2,1)S(1)}, bf16[2,72,1024]{2,1,0:T(8,128)(2,1)S(1)}, u32[]{:S(2)}, u32[]{:S(2)}) collective-permute-start(bf16[2,72,1024]{2,1,0:T(8,128)(2,1)S(1)} %pad_maximum_fusion.refs_0_), channel_id=1, source_target_pairs={{0,8},{4,12},{8,0},{12,4},{16,24},{20,28},{24,16},{28,20},{1,9},{5... | collective-permute-start | bytes 884744 | tf_op jit(solution)/shard_map/ppermute | solution.py:20
  23.8 9.1 %collective-permute-start.13 = (bf16[2,72,1024]{2,1,0:T(8,128)(2,1)S(1)}, bf16[2,72,1024]{2,1,0:T(8,128)(2,1)S(1)}, u32[]{:S(2)}, u32[]{:S(2)}) collective-permute-start(bf16[2,72,1024]{2,1,0:T(8,128)(2,1)S(1)} %pad_maximum_fusion.refs_0_), channel_id=1, source_target_pairs={{0,16},{4,20},{8,24},{12,28},{16,0},{20,4},{24,8},{28,12},{1,17},{... | collective-permute-start | bytes 884744 | tf_op jit(solution)/shard_map/ppermute | solution.py:20
  24.3 11.5 %collective-permute-start.10 = (bf16[2,24,1024]{2,1,0:T(8,128)(2,1)S(1)}, bf16[2,24,1024]{2,1,0:T(8,128)(2,1)S(1)}, u32[]{:S(2)}, u32[]{:S(2)}) collective-permute-start(bf16[2,24,1024]{2,1,0:T(8,128)(2,1)S(1)} %get-tuple-element.82), channel_id=1, source_target_pairs={{0,3},{1,2},{2,1},{3,0},{4,7},{5,6},{6,5},{7,4},{8,11},{9,10},{10,... | collective-permute-start | bytes 294920 | tf_op jit(solution)/shard_map/ppermute | solution.py:20
  28.6 7.3 %collective-permute-start.11 = (bf16[2,24,1024]{2,1,0:T(8,128)(2,1)S(1)}, bf16[2,24,1024]{2,1,0:T(8,128)(2,1)S(1)}, u32[]{:S(2)}, u32[]{:S(2)}) collective-permute-start(bf16[2,24,1024]{2,1,0:T(8,128)(2,1)S(1)} %get-tuple-element.83), channel_id=1, source_target_pairs={{0,2},{1,3},{2,0},{3,1},{4,6},{5,7},{6,4},{7,5},{8,10},{9,11},{10,... | collective-permute-start | bytes 294920 | tf_op jit(solution)/shard_map/ppermute | solution.py:20
  32.9 6.6 %collective-permute-start.17 = (bf16[2,40,1024]{2,1,0:T(8,128)(2,1)S(1)}, bf16[2,40,1024]{2,1,0:T(8,128)(2,1)S(1)}, u32[]{:S(2)}, u32[]{:S(2)}) collective-permute-start(bf16[2,40,1024]{2,1,0:T(8,128)(2,1)S(1)} %slice.59), channel_id=1, source_target_pairs={{0,8},{4,12},{8,0},{12,4},{16,24},{20,28},{24,16},{28,20},{1,9},{5... | collective-permute-start | bytes 491528 | tf_op jit(solution)/shard_map/ppermute | solution.py:20
  35.9 9.0 %collective-permute-start.14 = (bf16[2,72,1024]{2,1,0:T(8,128)(2,1)S(1)}, bf16[2,72,1024]{2,1,0:T(8,128)(2,1)S(1)}, u32[]{:S(2)}, u32[]{:S(2)}) collective-permute-start(bf16[2,72,1024]{2,1,0:T(8,128)(2,1)S(1)} %pad_maximum_fusion.1.refs_0_), channel_id=1, source_target_pairs={{0,8},{4,12},{8,0},{12,4},{16,24},{20,28},{24,16},{28,20},{1,9},{5... | collective-permute-start | bytes 884744 | tf_op jit(solution)/shard_map/ppermute | solution.py:20
  37.5 8.7 %collective-permute-start.15 = (bf16[2,72,1024]{2,1,0:T(8,128)(2,1)S(1)}, bf16[2,72,1024]{2,1,0:T(8,128)(2,1)S(1)}, u32[]{:S(2)}, u32[]{:S(2)}) collective-permute-start(bf16[2,72,1024]{2,1,0:T(8,128)(2,1)S(1)} %pad_maximum_fusion.1.refs_0_), channel_id=1, source_target_pairs={{0,16},{4,20},{8,24},{12,28},{16,0},{20,4},{24,8},{28,12},{1,17},{... | collective-permute-start | bytes 884744 | tf_op jit(solution)/shard_map/ppermute | solution.py:20
  46.7 7.1 %collective-permute-start.21 = (bf16[2,40,1024]{2,1,0:T(8,128)(2,1)S(1)}, bf16[2,40,1024]{2,1,0:T(8,128)(2,1)S(1)}, u32[]{:S(2)}, u32[]{:S(2)}) collective-permute-start(bf16[2,40,1024]{2,1,0:T(8,128)(2,1)S(1)} %get-tuple-element.106), channel_id=1, source_target_pairs={{0,16},{4,20},{8,24},{12,28},{16,0},{20,4},{24,8},{28,12},{1,17},{... | collective-permute-start | bytes 491528 | tf_op jit(solution)/shard_map/ppermute | solution.py:20
  48.4 8.0 %collective-permute-start.20 = (bf16[2,40,1024]{2,1,0:T(8,128)(2,1)S(1)}, bf16[2,40,1024]{2,1,0:T(8,128)(2,1)S(1)}, u32[]{:S(2)}, u32[]{:S(2)}) collective-permute-start(bf16[2,40,1024]{2,1,0:T(8,128)(2,1)S(1)} %slice.61), channel_id=1, source_target_pairs={{0,8},{4,12},{8,0},{12,4},{16,24},{20,28},{24,16},{28,20},{1,9},{5... | collective-permute-start | bytes 491528 | tf_op jit(solution)/shard_map/ppermute | solution.py:20
  49.9 6.5 %collective-permute-start.19 = (bf16[2,32,1024]{2,1,0:T(8,128)(2,1)S(1)}, bf16[2,32,1024]{2,1,0:T(8,128)(2,1)S(1)}, u32[]{:S(2)}, u32[]{:S(2)}) collective-permute-start(bf16[2,32,1024]{2,1,0:T(8,128)(2,1)S(1)} %slice.60), channel_id=1, source_target_pairs={{0,16},{4,20},{8,24},{12,28},{16,0},{20,4},{24,8},{28,12},{1,17},{... | collective-permute-start | bytes 393224 | tf_op jit(solution)/shard_map/ppermute | solution.py:20
  52.6 8.6 %collective-permute-start.24 = (bf16[2,72,1024]{2,1,0:T(8,128)(2,1)S(1)}, bf16[2,72,1024]{2,1,0:T(8,128)(2,1)S(1)}, u32[]{:S(2)}, u32[]{:S(2)}) collective-permute-start(bf16[2,72,1024]{2,1,0:T(8,128)(2,1)S(1)} %pad_maximum_fusion.3), channel_id=1, source_target_pairs={{0,16},{4,20},{8,24},{12,28},{16,0},{20,4},{24,8},{28,12},{1,17},{... | collective-permute-start | bytes 884744 | tf_op jit(solution)/shard_map/ppermute | solution.py:20
  53.9 9.7 %collective-permute-start.23 = (bf16[2,72,1024]{2,1,0:T(8,128)(2,1)S(1)}, bf16[2,72,1024]{2,1,0:T(8,128)(2,1)S(1)}, u32[]{:S(2)}, u32[]{:S(2)}) collective-permute-start(bf16[2,72,1024]{2,1,0:T(8,128)(2,1)S(1)} %pad_maximum_fusion.2), channel_id=1, source_target_pairs={{0,8},{4,12},{8,0},{12,4},{16,24},{20,28},{24,16},{28,20},{1,9},{5... | collective-permute-start | bytes 884744 | tf_op jit(solution)/shard_map/ppermute | solution.py:20
  62.1 6.4 %collective-permute-start.27 = (bf16[2,40,1024]{2,1,0:T(8,128)(2,1)S(1)}, bf16[2,40,1024]{2,1,0:T(8,128)(2,1)S(1)}, u32[]{:S(2)}, u32[]{:S(2)}) collective-permute-start(bf16[2,40,1024]{2,1,0:T(8,128)(2,1)S(1)} %get-tuple-element.122), channel_id=1, source_target_pairs={{0,16},{4,20},{8,24},{12,28},{16,0},{20,4},{24,8},{28,12},{1,17},{... | collective-permute-start | bytes 491528 | tf_op jit(solution)/shard_map/ppermute | solution.py:20
  63.7 8.5 %collective-permute-start.26 = (bf16[2,24,1024]{2,1,0:T(8,128)(2,1)S(1)}, bf16[2,24,1024]{2,1,0:T(8,128)(2,1)S(1)}, u32[]{:S(2)}, u32[]{:S(2)}) collective-permute-start(bf16[2,24,1024]{2,1,0:T(8,128)(2,1)S(1)} %get-tuple-element.137), channel_id=1, source_target_pairs={{0,8},{4,12},{8,0},{12,4},{16,24},{20,28},{24,16},{28,20},{1,9},{5... | collective-permute-start | bytes 294920 | tf_op jit(solution)/shard_map/ppermute | solution.py:20
  64.4 9.8 %collective-permute-start.25 = (bf16[2,24,1024]{2,1,0:T(8,128)(2,1)S(1)}, bf16[2,24,1024]{2,1,0:T(8,128)(2,1)S(1)}, u32[]{:S(2)}, u32[]{:S(2)}) collective-permute-start(bf16[2,24,1024]{2,1,0:T(8,128)(2,1)S(1)} %get-tuple-element.138), channel_id=1, source_target_pairs={{0,16},{4,20},{8,24},{12,28},{16,0},{20,4},{24,8},{28,12},{1,17},{... | collective-permute-start | bytes 294920 | tf_op jit(solution)/shard_map/ppermute | solution.py:20
  66.4 8.7 %collective-permute-start.32 = (bf16[2,72,1024]{2,1,0:T(8,128)(2,1)S(1)}, bf16[2,72,1024]{2,1,0:T(8,128)(2,1)S(1)}, u32[]{:S(2)}, u32[]{:S(2)}) collective-permute-start(bf16[2,72,1024]{2,1,0:T(8,128)(2,1)S(1)} %pad_maximum_fusion.5), channel_id=1, source_target_pairs={{0,16},{4,20},{8,24},{12,28},{16,0},{20,4},{24,8},{28,12},{1,17},{... | collective-permute-start | bytes 884744 | tf_op jit(solution)/shard_map/ppermute | solution.py:20
  68.6 7.9 %collective-permute-start.31 = (bf16[2,72,1024]{2,1,0:T(8,128)(2,1)S(1)}, bf16[2,72,1024]{2,1,0:T(8,128)(2,1)S(1)}, u32[]{:S(2)}, u32[]{:S(2)}) collective-permute-start(bf16[2,72,1024]{2,1,0:T(8,128)(2,1)S(1)} %pad_maximum_fusion.4), channel_id=1, source_target_pairs={{0,8},{4,12},{8,0},{12,4},{16,24},{20,28},{24,16},{28,20},{1,9},{5... | collective-permute-start | bytes 884744 | tf_op jit(solution)/shard_map/ppermute | solution.py:20
  70.5 6.8 %collective-permute-start.34 = (bf16[2,24,1024]{2,1,0:T(8,128)(2,1)S(1)}, bf16[2,24,1024]{2,1,0:T(8,128)(2,1)S(1)}, u32[]{:S(2)}, u32[]{:S(2)}) collective-permute-start(bf16[2,24,1024]{2,1,0:T(8,128)(2,1)S(1)} %get-tuple-element.135), channel_id=1, source_target_pairs={{0,2},{1,3},{2,0},{3,1},{4,6},{5,7},{6,4},{7,5},{8,10},{9,11},{10,... | collective-permute-start | bytes 294920 | tf_op jit(solution)/shard_map/ppermute | solution.py:20
  72.2 8.1 %collective-permute-start.36 = (bf16[2,24,1024]{2,1,0:T(8,128)(2,1)S(1)}, bf16[2,24,1024]{2,1,0:T(8,128)(2,1)S(1)}, u32[]{:S(2)}, u32[]{:S(2)}) collective-permute-start(bf16[2,24,1024]{2,1,0:T(8,128)(2,1)S(1)} %get-tuple-element.134), channel_id=1, source_target_pairs={{0,3},{1,2},{2,1},{3,0},{4,7},{5,6},{6,5},{7,4},{8,11},{9,10},{10,... | collective-permute-start | bytes 294920 | tf_op jit(solution)/shard_map/ppermute | solution.py:20
  74.2 7.5 %collective-permute-start.29 = (bf16[4,24,1024]{2,1,0:T(8,128)(2,1)S(1)}, bf16[4,24,1024]{2,1,0:T(8,128)(2,1)S(1)}, u32[]{:S(2)}, u32[]{:S(2)}) collective-permute-start(bf16[4,24,1024]{2,1,0:T(8,128)(2,1)S(1)} %pad_maximum_fusion.7), channel_id=1, source_target_pairs={{0,8},{4,12},{8,0},{12,4},{16,24},{20,28},{24,16},{28,20},{1,9},{5... | collective-permute-start | bytes 589832 | tf_op jit(solution)/shard_map/ppermute | solution.py:20
  75.1 6.6 %collective-permute-start.30 = (bf16[4,24,1024]{2,1,0:T(8,128)(2,1)S(1)}, bf16[4,24,1024]{2,1,0:T(8,128)(2,1)S(1)}, u32[]{:S(2)}, u32[]{:S(2)}) collective-permute-start(bf16[4,24,1024]{2,1,0:T(8,128)(2,1)S(1)} %pad_maximum_fusion.8), channel_id=1, source_target_pairs={{0,16},{4,20},{8,24},{12,28},{16,0},{20,4},{24,8},{28,12},{1,17},{... | collective-permute-start | bytes 589832 | tf_op jit(solution)/shard_map/ppermute | solution.py:20
  76.7 10.0 %collective-permute-start.33 = (bf16[4,24,1024]{2,1,0:T(8,128)(2,1)S(1)}, bf16[4,24,1024]{2,1,0:T(8,128)(2,1)S(1)}, u32[]{:S(2)}, u32[]{:S(2)}) collective-permute-start(bf16[4,24,1024]{2,1,0:T(8,128)(2,1)S(1)} %pad_maximum_fusion.9), channel_id=1, source_target_pairs={{0,1},{1,0},{2,3},{3,2},{4,5},{5,4},{6,7},{7,6},{8,9},{9,8},{10,11... | collective-permute-start | bytes 589832 | tf_op jit(solution)/shard_map/ppermute | solution.py:20
  77.4 8.2 %collective-permute-start.35 = (bf16[2,24,1024]{2,1,0:T(8,128)(2,1)S(1)}, bf16[2,24,1024]{2,1,0:T(8,128)(2,1)S(1)}, u32[]{:S(2)}, u32[]{:S(2)}) collective-permute-start(bf16[2,24,1024]{2,1,0:T(8,128)(2,1)S(1)} %get-tuple-element.132), channel_id=1, source_target_pairs={{0,2},{1,3},{2,0},{3,1},{4,6},{5,7},{6,4},{7,5},{8,10},{9,11},{10,... | collective-permute-start | bytes 294920 | tf_op jit(solution)/shard_map/ppermute | solution.py:20
  80.3 6.4 %collective-permute-start.37 = (bf16[2,24,1024]{2,1,0:T(8,128)(2,1)S(1)}, bf16[2,24,1024]{2,1,0:T(8,128)(2,1)S(1)}, u32[]{:S(2)}, u32[]{:S(2)}) collective-permute-start(bf16[2,24,1024]{2,1,0:T(8,128)(2,1)S(1)} %get-tuple-element.131), channel_id=1, source_target_pairs={{0,3},{1,2},{2,1},{3,0},{4,7},{5,6},{6,5},{7,4},{8,11},{9,10},{10,... | collective-permute-start | bytes 294920 | tf_op jit(solution)/shard_map/ppermute | solution.py:20
  (7 other events, 23.9 us)

commit v9 on v8

--- a/solution.py
+++ b/solution.py
@@ -334,9 +334,9 @@
 
     own = pieces[0][0]
     first = swapped(pieces[1][0], "exp", 1)
-    far0 = jnp.concatenate([first[:cut]] + [swapped(pieces[s][0], "exp", s) for s in range(2, n_exp)], axis=1)
+    far0 = jnp.concatenate([swapped(pieces[s][0], "exp", s) for s in range(2, n_exp)] + [first[:cut]], axis=1)
     own_a, own_b = to_a(own), to_b(own)
-    lent = lend(after(place, own_a, own_b), w_in, w_down)
+    lent = lend(after(place, own_a), w_in, w_down)
     own_d = to_b(own_a[:split]), to_a(own_b[split:])
     far0, sib, *own_d = lax.optimization_barrier((far0, lent, *own_d))
     sib = swapped(sib, "rep", core_bit)
@@ -362,7 +362,8 @@
     def back(part, from_a, from_b, order):
         done = (part.astype(F32) + from_a.astype(F32) + from_b.astype(F32)).astype(BF16)
         shifts = jnp.split(done, n_exp - 1, axis=1)
-        return shifts[0], {s: swapped(rows, "exp", s) for s, rows in zip(order, shifts[1:])}
+        shifts = dict(zip(order, shifts))
+        return shifts[1], {s: swapped(shifts[s], "exp", s) for s in order if s > 1}
 
     sums0 = reduced(parts0, r0)
     d1 = lax.optimization_barrier((*d1, *sums0))[:2]
@@ -370,10 +371,10 @@
     parts1 = experts(cut, (far1, a1, b1, *d1, own, own_a, own_b, *own_d), sib, in_own, down_own)
     parts1[3], parts1[4] = lax.optimization_barrier((parts1[3], parts1[4], from_b0))[:2]
     r1 = to_a(parts1[3]), to_b(parts1[4])
-    returned0 = back(parts0[0], from_a0, from_b0, range(2, n_exp))
+    returned0 = back(parts0[0], from_a0, from_b0, (*range(2, n_exp), 1))
     sums1 = reduced(parts1, r1)
     from_a1, from_b1 = to_a(sums1[0]), to_b(sums1[1])
-    returned1 = back(parts1[0], from_a1, from_b1, shifts1)
+    returned1 = back(parts1[0], from_a1, from_b1, (1, *shifts1))
     across = jnp.concatenate([parts0[8], parts1[8]], axis=0)
     across = after(across, from_a0, from_b0)
     own_r = to_a(across[:split]), to_b(across[split:])

time: 89.7 us -> 89.7 us (level)
  no operation moved by 1% of the time
where the time goes in v9:
time: 89.7 us; the launch traced here: 89.6 us
  starting transfers between devices  48.8 us (54%)
  Pallas kernels  19.8 us (22%)
  waiting for transfers between devices  19 us (21%)
  other arithmetic  1.44 us (2%)
    ppermute x39, starting transfers between devices, swapped(): lax.ppermute(array, axis, [(i, i ^ distance) for i in range(lax.axis_size...  48.8 us
    ppermute x39, waiting for transfers between devices, swapped(): lax.ppermute(array, axis, [(i, i ^ distance) for i in range(lax.axis_size...  19 us
    pallas_call x2, Pallas kernels, experts(): pl.pallas_call(functools.partial(experts_kernel, first), out_shape=[pltpu...  7.42 us
    pallas_call x1, Pallas kernels, lend(): pl.pallas_call(lend_kernel, out_shape=pltpu.VMEM(shape, BF16), in_specs=[...  4.02 us
    pallas_call x1, Pallas kernels, hold(): pl.pallas_call(hold_kernel, out_shape=[shape, shape], in_specs=[smem(), h...  4.02 us
    pallas_call x1, Pallas kernels, embed(): pl.pallas_call(embed_kernel, out_shape=[shape, shape, pltpu.VMEM(routes.s...  2.53 us
  transfers between devices with their start and end apart: 39, of which 18 were waited for; matrix products, arithmetic and copies ran while one was open for 1% of the time, Pallas kernels for 18%

profile of v9, /device:TPU:0, one launch (start us, length us, event | category | flops | bytes accessed | tf_op | source)
XLA Modules:
  0.0 89.6 jit_solution(7691511297460258520)
XLA Ops:
  0.0 2.5 %embed.1 = (bf16[128,1024]{1,0:T(8,128)(2,1)S(1)}, bf16[128,1024]{1,0:T(8,128)(2,1)S(1)}, s32[2,128]{1,0:T(2,128)S(1)}, s32[2,128]{1,0:T(2,128)S(1)}) custom-call(bf16[128,1536]{1,0:T(8,128)(2,1)} %tubelets_ref.1, bf16[1536,1024]{1,0:T(8,128)(2,1)} %weight_ref.1, f32[1,1024]{1,0:T(1,128)} %bitcast.5, s32[2,128]{1,0:T(2,128)} %bitcast.6, s32[2,128]{1,0:T(2,128)} %bitcast.8), custom_call_target="tpu_custom_call" | custom-call | flops 402653184 | bytes 3145728 | tf_op jit(solution)/shard_map/embed/pallas_call | solution.py:90
  5.9 2.9 %collective-permute-start.6 = (bf16[4,24,1024]{2,1,0:T(8,128)(2,1)S(1)}, bf16[4,24,1024]{2,1,0:T(8,128)(2,1)S(1)}, u32[]{:S(2)}, u32[]{:S(2)}) collective-permute-start(bf16[4,24,1024]{2,1,0:T(8,128)(2,1)S(1)} %get-tuple-element.77.refs_5_), channel_id=1, source_target_pairs={{0,8},{4,12},{8,0},{12,4},{16,24},{20,28},{24,16},{28,20},{1,9},{5... | collective-permute-start | bytes 589832 | tf_op jit(solution)/shard_map/ppermute | solution.py:20
  8.8 1.5 %collective-permute-start.8 = (bf16[4,24,1024]{2,1,0:T(8,128)(2,1)S(1)}, bf16[4,24,1024]{2,1,0:T(8,128)(2,1)S(1)}, u32[]{:S(2)}, u32[]{:S(2)}) collective-permute-start(bf16[4,24,1024]{2,1,0:T(8,128)(2,1)S(1)} %get-tuple-element.77.refs_5_), channel_id=1, source_target_pairs={{0,16},{4,20},{8,24},{12,28},{16,0},{20,4},{24,8},{28,12},{1,17},{... | collective-permute-start | bytes 589832 | tf_op jit(solution)/shard_map/ppermute | solution.py:20
  10.3 1.6 %collective-permute-start.3 = (bf16[4,24,1024]{2,1,0:T(8,128)(2,1)S(1)}, bf16[4,24,1024]{2,1,0:T(8,128)(2,1)S(1)}, u32[]{:S(2)}, u32[]{:S(2)}) collective-permute-start(bf16[4,24,1024]{2,1,0:T(8,128)(2,1)S(1)} %get-tuple-element.74), channel_id=1, source_target_pairs={{0,1},{1,0},{2,3},{3,2},{4,5},{5,4},{6,7},{7,6},{8,9},{9,8},{10,11... | collective-permute-start | bytes 589832 | tf_op jit(solution)/shard_map/ppermute | solution.py:20
  11.9 2.6 %collective-permute-start.4 = (bf16[2,24,1024]{2,1,0:T(8,128)(2,1)S(1)}, bf16[2,24,1024]{2,1,0:T(8,128)(2,1)S(1)}, u32[]{:S(2)}, u32[]{:S(2)}) collective-permute-start(bf16[2,24,1024]{2,1,0:T(8,128)(2,1)S(1)} %get-tuple-element.75), channel_id=1, source_target_pairs={{0,2},{1,3},{2,0},{3,1},{4,6},{5,7},{6,4},{7,5},{8,10},{9,11},{10,... | collective-permute-start | bytes 294920 | tf_op jit(solution)/shard_map/ppermute | solution.py:20
  15.9 1.6 %collective-permute-start.9 = (bf16[2,24,1024]{2,1,0:T(8,128)(2,1)S(1)}, bf16[2,24,1024]{2,1,0:T(8,128)(2,1)S(1)}, u32[]{:S(2)}, u32[]{:S(2)}) collective-permute-start(bf16[2,24,1024]{2,1,0:T(8,128)(2,1)S(1)} %slice.75), channel_id=1, source_target_pairs={{0,8},{4,12},{8,0},{12,4},{16,24},{20,28},{24,16},{28,20},{1,9},{5... | collective-permute-start | bytes 294920 | tf_op jit(solution)/shard_map/ppermute | solution.py:20
  17.5 1.4 %collective-permute-done.3 = bf16[4,24,1024]{2,1,0:T(8,128)(2,1)S(1)} collective-permute-done((bf16[4,24,1024]{2,1,0:T(8,128)(2,1)S(1)}, bf16[4,24,1024]{2,1,0:T(8,128)(2,1)S(1)}, u32[]{:S(2)}, u32[]{:S(2)}) %collective-permute-start.3) | collective-permute-done | bytes 196640 | tf_op jit(solution)/shard_map/ppermute | solution.py:20
  18.9 4.0 %lend.1 = bf16[2,4,1024,512]{3,2,1,0:T(8,128)(2,1)S(1)} custom-call(s32[2]{0:T(128)S(1)} %pad_add_fusion.place_ref, bf16[8,1024,512]{2,1,0:T(8,128)(2,1)} %in_ref.3, bf16[8,1024,512]{2,1,0:T(8,128)(2,1)} %down_ref.3), custom_call_target="tpu_custom_call" | custom-call | bytes 16777216 | tf_op jit(solution)/shard_map/lend/pallas_call | solution.py:192
  24.3 4.3 %collective-permute-start.10 = (bf16[2,24,1024]{2,1,0:T(8,128)(2,1)S(1)}, bf16[2,24,1024]{2,1,0:T(8,128)(2,1)S(1)}, u32[]{:S(2)}, u32[]{:S(2)}) collective-permute-start(bf16[2,24,1024]{2,1,0:T(8,128)(2,1)S(1)} %get-tuple-element.82), channel_id=1, source_target_pairs={{0,3},{1,2},{2,1},{3,0},{4,7},{5,6},{6,5},{7,4},{8,11},{9,10},{10,... | collective-permute-start | bytes 294920 | tf_op jit(solution)/shard_map/ppermute | solution.py:20
  28.6 4.0 %hold.1 = (bf16[4,1024,512]{2,1,0:T(8,128)(2,1)S(1)}, bf16[4,1024,512]{2,1,0:T(8,128)(2,1)S(1)}) custom-call(s32[2]{0:T(128)S(1)} %pad_add_fusion.place_ref, bf16[8,1024,512]{2,1,0:T(8,128)(2,1)} %in_ref.3, bf16[8,1024,512]{2,1,0:T(8,128)(2,1)} %down_ref.3), custom_call_target="tpu_custom_call" | custom-call | bytes 16777216 | tf_op jit(solution)/shard_map/hold/pallas_call | solution.py:218
  32.9 1.6 %collective-permute-start.17 = (bf16[2,40,1024]{2,1,0:T(8,128)(2,1)S(1)}, bf16[2,40,1024]{2,1,0:T(8,128)(2,1)S(1)}, u32[]{:S(2)}, u32[]{:S(2)}) collective-permute-start(bf16[2,40,1024]{2,1,0:T(8,128)(2,1)S(1)} %slice.59), channel_id=1, source_target_pairs={{0,8},{4,12},{8,0},{12,4},{16,24},{20,28},{24,16},{28,20},{1,9},{5... | collective-permute-start | bytes 491528 | tf_op jit(solution)/shard_map/ppermute | solution.py:20
  34.5 1.4 %collective-permute-start.16 = (bf16[2,32,1024]{2,1,0:T(8,128)(2,1)S(1)}, bf16[2,32,1024]{2,1,0:T(8,128)(2,1)S(1)}, u32[]{:S(2)}, u32[]{:S(2)}) collective-permute-start(bf16[2,32,1024]{2,1,0:T(8,128)(2,1)S(1)} %slice.58), channel_id=1, source_target_pairs={{0,16},{4,20},{8,24},{12,28},{16,0},{20,4},{24,8},{28,12},{1,17},{... | collective-permute-start | bytes 393224 | tf_op jit(solution)/shard_map/ppermute | solution.py:20
  35.9 1.6 %collective-permute-start.14 = (bf16[2,72,1024]{2,1,0:T(8,128)(2,1)S(1)}, bf16[2,72,1024]{2,1,0:T(8,128)(2,1)S(1)}, u32[]{:S(2)}, u32[]{:S(2)}) collective-permute-start(bf16[2,72,1024]{2,1,0:T(8,128)(2,1)S(1)} %pad_maximum_fusion.1.refs_0_), channel_id=1, source_target_pairs={{0,8},{4,12},{8,0},{12,4},{16,24},{20,28},{24,16},{28,20},{1,9},{5... | collective-permute-start | bytes 884744 | tf_op jit(solution)/shard_map/ppermute | solution.py:20
  37.5 1.5 %collective-permute-start.15 = (bf16[2,72,1024]{2,1,0:T(8,128)(2,1)S(1)}, bf16[2,72,1024]{2,1,0:T(8,128)(2,1)S(1)}, u32[]{:S(2)}, u32[]{:S(2)}) collective-permute-start(bf16[2,72,1024]{2,1,0:T(8,128)(2,1)S(1)} %pad_maximum_fusion.1.refs_0_), channel_id=1, source_target_pairs={{0,16},{4,20},{8,24},{12,28},{16,0},{20,4},{24,8},{28,12},{1,17},{... | collective-permute-start | bytes 884744 | tf_op jit(solution)/shard_map/ppermute | solution.py:20
  39.5 3.7 %experts.2 = (bf16[2,72,1024]{2,1,0:T(8,128)(2,1)S(1)}, bf16[2,72,1024]{2,1,0:T(8,128)(2,1)S(1)}, bf16[2,72,1024]{2,1,0:T(8,128)(2,1)S(1)}, bf16[2,32,1024]{2,1,...) custom-call(bf16[2,72,1024]{2,1,0:T(8,128)(2,1)S(1)} %pad_maximum_fu, ...), custom_call_target="tpu_custom_call" | custom-call | flops 3221225472 | bytes 3145728 | tf_op jit(solution)/shard_map/experts/pallas_call | solution.py:254
  43.3 1.7 %collective-permute-done.14.refs_1_ = bf16[2,72,1024]{2,1,0:T(8,128)(2,1)S(1)} collective-permute-done((bf16[2,72,1024]{2,1,0:T(8,128)(2,1)S(1)}, bf16[2,72,1024]{2,1,0:T(8,128)(2,1)S(1)}, u32[]{:S(2)}, u32[]{:S(2)}) %collective-permute-start.14) | collective-permute-done | bytes 294944 | tf_op jit(solution)/shard_map/ppermute | solution.py:20
  46.7 1.6 %collective-permute-start.21 = (bf16[2,40,1024]{2,1,0:T(8,128)(2,1)S(1)}, bf16[2,40,1024]{2,1,0:T(8,128)(2,1)S(1)}, u32[]{:S(2)}, u32[]{:S(2)}) collective-permute-start(bf16[2,40,1024]{2,1,0:T(8,128)(2,1)S(1)} %get-tuple-element.106), channel_id=1, source_target_pairs={{0,16},{4,20},{8,24},{12,28},{16,0},{20,4},{24,8},{28,12},{1,17},{... | collective-permute-start | bytes 491528 | tf_op jit(solution)/shard_map/ppermute | solution.py:20
  48.4 1.6 %collective-permute-start.20 = (bf16[2,40,1024]{2,1,0:T(8,128)(2,1)S(1)}, bf16[2,40,1024]{2,1,0:T(8,128)(2,1)S(1)}, u32[]{:S(2)}, u32[]{:S(2)}) collective-permute-start(bf16[2,40,1024]{2,1,0:T(8,128)(2,1)S(1)} %slice.61), channel_id=1, source_target_pairs={{0,8},{4,12},{8,0},{12,4},{16,24},{20,28},{24,16},{28,20},{1,9},{5... | collective-permute-start | bytes 491528 | tf_op jit(solution)/shard_map/ppermute | solution.py:20
  50.5 2.1 %collective-permute-done.22 = bf16[2,32,1024]{2,1,0:T(8,128)(2,1)S(1)} collective-permute-done((bf16[2,32,1024]{2,1,0:T(8,128)(2,1)S(1)}, bf16[2,32,1024]{2,1,0:T(8,128)(2,1)S(1)}, u32[]{:S(2)}, u32[]{:S(2)}) %collective-permute-start.22) | collective-permute-done | bytes 131104 | tf_op jit(solution)/shard_map/ppermute | solution.py:20
  52.6 1.3 %collective-permute-start.24 = (bf16[2,72,1024]{2,1,0:T(8,128)(2,1)S(1)}, bf16[2,72,1024]{2,1,0:T(8,128)(2,1)S(1)}, u32[]{:S(2)}, u32[]{:S(2)}) collective-permute-start(bf16[2,72,1024]{2,1,0:T(8,128)(2,1)S(1)} %pad_maximum_fusion.3), channel_id=1, source_target_pairs={{0,16},{4,20},{8,24},{12,28},{16,0},{20,4},{24,8},{28,12},{1,17},{... | collective-permute-start | bytes 884744 | tf_op jit(solution)/shard_map/ppermute | solution.py:20
  53.9 1.6 %collective-permute-start.23 = (bf16[2,72,1024]{2,1,0:T(8,128)(2,1)S(1)}, bf16[2,72,1024]{2,1,0:T(8,128)(2,1)S(1)}, u32[]{:S(2)}, u32[]{:S(2)}) collective-permute-start(bf16[2,72,1024]{2,1,0:T(8,128)(2,1)S(1)} %pad_maximum_fusion.2), channel_id=1, source_target_pairs={{0,8},{4,12},{8,0},{12,4},{16,24},{20,28},{24,16},{28,20},{1,9},{5... | collective-permute-start | bytes 884744 | tf_op jit(solution)/shard_map/ppermute | solution.py:20
  56.4 3.7 %experts.3 = (bf16[2,72,1024]{2,1,0:T(8,128)(2,1)S(1)}, bf16[2,72,1024]{2,1,0:T(8,128)(2,1)S(1)}, bf16[2,72,1024]{2,1,0:T(8,128)(2,1)S(1)}, bf16[2,32,1024]{2,1,...) custom-call(bf16[2,72,1024]{2,1,0:T(8,128)(2,1)S(1)} %pad_maximum_fu, ...), custom_call_target="tpu_custom_call" | custom-call | flops 3221225472 | bytes 3145728 | tf_op jit(solution)/shard_map/experts/pallas_call | solution.py:254
  62.1 1.5 %collective-permute-start.27 = (bf16[2,40,1024]{2,1,0:T(8,128)(2,1)S(1)}, bf16[2,40,1024]{2,1,0:T(8,128)(2,1)S(1)}, u32[]{:S(2)}, u32[]{:S(2)}) collective-permute-start(bf16[2,40,1024]{2,1,0:T(8,128)(2,1)S(1)} %get-tuple-element.122), channel_id=1, source_target_pairs={{0,16},{4,20},{8,24},{12,28},{16,0},{20,4},{24,8},{28,12},{1,17},{... | collective-permute-start | bytes 491528 | tf_op jit(solution)/shard_map/ppermute | solution.py:20
  67.3 1.2 %collective-permute-done.27 = bf16[2,40,1024]{2,1,0:T(8,128)(2,1)S(1)} collective-permute-done((bf16[2,40,1024]{2,1,0:T(8,128)(2,1)S(1)}, bf16[2,40,1024]{2,1,0:T(8,128)(2,1)S(1)}, u32[]{:S(2)}, u32[]{:S(2)}) %collective-permute-start.27) | collective-permute-done | bytes 163872 | tf_op jit(solution)/shard_map/ppermute | solution.py:20
  68.6 1.9 %collective-permute-start.31 = (bf16[2,72,1024]{2,1,0:T(8,128)(2,1)S(1)}, bf16[2,72,1024]{2,1,0:T(8,128)(2,1)S(1)}, u32[]{:S(2)}, u32[]{:S(2)}) collective-permute-start(bf16[2,72,1024]{2,1,0:T(8,128)(2,1)S(1)} %pad_maximum_fusion.4), channel_id=1, source_target_pairs={{0,8},{4,12},{8,0},{12,4},{16,24},{20,28},{24,16},{28,20},{1,9},{5... | collective-permute-start | bytes 884744 | tf_op jit(solution)/shard_map/ppermute | solution.py:20
  70.5 1.7 %collective-permute-start.34 = (bf16[2,24,1024]{2,1,0:T(8,128)(2,1)S(1)}, bf16[2,24,1024]{2,1,0:T(8,128)(2,1)S(1)}, u32[]{:S(2)}, u32[]{:S(2)}) collective-permute-start(bf16[2,24,1024]{2,1,0:T(8,128)(2,1)S(1)} %get-tuple-element.135), channel_id=1, source_target_pairs={{0,2},{1,3},{2,0},{3,1},{4,6},{5,7},{6,4},{7,5},{8,10},{9,11},{10,... | collective-permute-start | bytes 294920 | tf_op jit(solution)/shard_map/ppermute | solution.py:20
  72.2 1.9 %collective-permute-start.36 = (bf16[2,24,1024]{2,1,0:T(8,128)(2,1)S(1)}, bf16[2,24,1024]{2,1,0:T(8,128)(2,1)S(1)}, u32[]{:S(2)}, u32[]{:S(2)}) collective-permute-start(bf16[2,24,1024]{2,1,0:T(8,128)(2,1)S(1)} %get-tuple-element.134), channel_id=1, source_target_pairs={{0,3},{1,2},{2,1},{3,0},{4,7},{5,6},{6,5},{7,4},{8,11},{9,10},{10,... | collective-permute-start | bytes 294920 | tf_op jit(solution)/shard_map/ppermute | solution.py:20
  75.1 1.3 %collective-permute-start.30 = (bf16[4,24,1024]{2,1,0:T(8,128)(2,1)S(1)}, bf16[4,24,1024]{2,1,0:T(8,128)(2,1)S(1)}, u32[]{:S(2)}, u32[]{:S(2)}) collective-permute-start(bf16[4,24,1024]{2,1,0:T(8,128)(2,1)S(1)} %pad_maximum_fusion.8), channel_id=1, source_target_pairs={{0,16},{4,20},{8,24},{12,28},{16,0},{20,4},{24,8},{28,12},{1,17},{... | collective-permute-start | bytes 589832 | tf_op jit(solution)/shard_map/ppermute | solution.py:20
  77.4 2.9 %collective-permute-start.35 = (bf16[2,24,1024]{2,1,0:T(8,128)(2,1)S(1)}, bf16[2,24,1024]{2,1,0:T(8,128)(2,1)S(1)}, u32[]{:S(2)}, u32[]{:S(2)}) collective-permute-start(bf16[2,24,1024]{2,1,0:T(8,128)(2,1)S(1)} %get-tuple-element.132), channel_id=1, source_target_pairs={{0,2},{1,3},{2,0},{3,1},{4,6},{5,7},{6,4},{7,5},{8,10},{9,11},{10,... | collective-permute-start | bytes 294920 | tf_op jit(solution)/shard_map/ppermute | solution.py:20
  80.3 1.5 %collective-permute-start.37 = (bf16[2,24,1024]{2,1,0:T(8,128)(2,1)S(1)}, bf16[2,24,1024]{2,1,0:T(8,128)(2,1)S(1)}, u32[]{:S(2)}, u32[]{:S(2)}) collective-permute-start(bf16[2,24,1024]{2,1,0:T(8,128)(2,1)S(1)} %get-tuple-element.131), channel_id=1, source_target_pairs={{0,3},{1,2},{2,1},{3,0},{4,7},{5,6},{6,5},{7,4},{8,11},{9,10},{10,... | collective-permute-start | bytes 294920 | tf_op jit(solution)/shard_map/ppermute | solution.py:20
  81.8 3.8 %collective-permute-done.35.refs_6_ = bf16[2,24,1024]{2,1,0:T(8,128)(2,1)S(1)} collective-permute-done((bf16[2,24,1024]{2,1,0:T(8,128)(2,1)S(1)}, bf16[2,24,1024]{2,1,0:T(8,128)(2,1)S(1)}, u32[]{:S(2)}, u32[]{:S(2)}) %collective-permute-start.35) | collective-permute-done | bytes 98336 | tf_op jit(solution)/shard_map/ppermute | solution.py:20
  87.3 1.5 %collective-permute-done.38 = bf16[128,1024]{1,0:T(8,128)(2,1)S(1)} collective-permute-done((bf16[128,1024]{1,0:T(8,128)(2,1)S(1)}, bf16[128,1024]{1,0:T(8,128)(2,1)S(1)}, u32[]{:S(2)}, u32[]{:S(2)}) %collective-permute-start.38) | collective-permute-done | bytes 262176 | tf_op jit(solution)/shard_map/ppermute | solution.py:20
  (88 shorter events, 20.4 us)
Async XLA Ops:
  5.9 8.8 %collective-permute-start.6 = (bf16[4,24,1024]{2,1,0:T(8,128)(2,1)S(1)}, bf16[4,24,1024]{2,1,0:T(8,128)(2,1)S(1)}, u32[]{:S(2)}, u32[]{:S(2)}) collective-permute-start(bf16[4,24,1024]{2,1,0:T(8,128)(2,1)S(1)} %get-tuple-element.77.refs_5_), channel_id=1, source_target_pairs={{0,8},{4,12},{8,0},{12,4},{16,24},{20,28},{24,16},{28,20},{1,9},{5... | collective-permute-start | bytes 589832 | tf_op jit(solution)/shard_map/ppermute | solution.py:20
  8.8 7.1 %collective-permute-start.8 = (bf16[4,24,1024]{2,1,0:T(8,128)(2,1)S(1)}, bf16[4,24,1024]{2,1,0:T(8,128)(2,1)S(1)}, u32[]{:S(2)}, u32[]{:S(2)}) collective-permute-start(bf16[4,24,1024]{2,1,0:T(8,128)(2,1)S(1)} %get-tuple-element.77.refs_5_), channel_id=1, source_target_pairs={{0,16},{4,20},{8,24},{12,28},{16,0},{20,4},{24,8},{28,12},{1,17},{... | collective-permute-start | bytes 589832 | tf_op jit(solution)/shard_map/ppermute | solution.py:20
  10.3 8.5 %collective-permute-start.3 = (bf16[4,24,1024]{2,1,0:T(8,128)(2,1)S(1)}, bf16[4,24,1024]{2,1,0:T(8,128)(2,1)S(1)}, u32[]{:S(2)}, u32[]{:S(2)}) collective-permute-start(bf16[4,24,1024]{2,1,0:T(8,128)(2,1)S(1)} %get-tuple-element.74), channel_id=1, source_target_pairs={{0,1},{1,0},{2,3},{3,2},{4,5},{5,4},{6,7},{7,6},{8,9},{9,8},{10,11... | collective-permute-start | bytes 589832 | tf_op jit(solution)/shard_map/ppermute | solution.py:20
  11.9 11.0 %collective-permute-start.4 = (bf16[2,24,1024]{2,1,0:T(8,128)(2,1)S(1)}, bf16[2,24,1024]{2,1,0:T(8,128)(2,1)S(1)}, u32[]{:S(2)}, u32[]{:S(2)}) collective-permute-start(bf16[2,24,1024]{2,1,0:T(8,128)(2,1)S(1)} %get-tuple-element.75), channel_id=1, source_target_pairs={{0,2},{1,3},{2,0},{3,1},{4,6},{5,7},{6,4},{7,5},{8,10},{9,11},{10,... | collective-permute-start | bytes 294920 | tf_op jit(solution)/shard_map/ppermute | solution.py:20
  14.5 8.6 %collective-permute-start.5 = (bf16[2,24,1024]{2,1,0:T(8,128)(2,1)S(1)}, bf16[2,24,1024]{2,1,0:T(8,128)(2,1)S(1)}, u32[]{:S(2)}, u32[]{:S(2)}) collective-permute-start(bf16[2,24,1024]{2,1,0:T(8,128)(2,1)S(1)} %get-tuple-element.76), channel_id=1, source_target_pairs={{0,3},{1,2},{2,1},{3,0},{4,7},{5,6},{6,5},{7,4},{8,11},{9,10},{10,... | collective-permute-start | bytes 294920 | tf_op jit(solution)/shard_map/ppermute | solution.py:20
  14.7 8.4 %collective-permute-start.7 = (bf16[2,24,1024]{2,1,0:T(8,128)(2,1)S(1)}, bf16[2,24,1024]{2,1,0:T(8,128)(2,1)S(1)}, u32[]{:S(2)}, u32[]{:S(2)}) collective-permute-start(bf16[2,24,1024]{2,1,0:T(8,128)(2,1)S(1)} %slice.74), channel_id=1, source_target_pairs={{0,16},{4,20},{8,24},{12,28},{16,0},{20,4},{24,8},{28,12},{1,17},{... | collective-permute-start | bytes 294920 | tf_op jit(solution)/shard_map/ppermute | solution.py:20
  15.9 7.2 %collective-permute-start.9 = (bf16[2,24,1024]{2,1,0:T(8,128)(2,1)S(1)}, bf16[2,24,1024]{2,1,0:T(8,128)(2,1)S(1)}, u32[]{:S(2)}, u32[]{:S(2)}) collective-permute-start(bf16[2,24,1024]{2,1,0:T(8,128)(2,1)S(1)} %slice.75), channel_id=1, source_target_pairs={{0,8},{4,12},{8,0},{12,4},{16,24},{20,28},{24,16},{28,20},{1,9},{5... | collective-permute-start | bytes 294920 | tf_op jit(solution)/shard_map/ppermute | solution.py:20
  23.2 16.4 %collective-permute-start.18 = (bf16[2,4,1024,512]{3,2,1,0:T(8,128)(2,1)S(1)}, bf16[2,4,1024,512]{3,2,1,0:T(8,128)(2,1)S(1)}, u32[]{:S(2)}, u32[]{:S(2)}) collective-permute-start(bf16[2,4,1024,512]{3,2,1,0:T(8,128)(2,1)S(1)} %lend.1), channel_id=1, source_target_pairs={{0,4},{4,0},{8,12},{12,8},{16,20},{20,16},{24,28},{28,24},{1,5},{5... | collective-permute-start | bytes 25165832 | tf_op jit(solution)/shard_map/ppermute | solution.py:20
  23.2 9.4 %collective-permute-start.12 = (bf16[2,72,1024]{2,1,0:T(8,128)(2,1)S(1)}, bf16[2,72,1024]{2,1,0:T(8,128)(2,1)S(1)}, u32[]{:S(2)}, u32[]{:S(2)}) collective-permute-start(bf16[2,72,1024]{2,1,0:T(8,128)(2,1)S(1)} %pad_maximum_fusion.refs_0_), channel_id=1, source_target_pairs={{0,8},{4,12},{8,0},{12,4},{16,24},{20,28},{24,16},{28,20},{1,9},{5... | collective-permute-start | bytes 884744 | tf_op jit(solution)/shard_map/ppermute | solution.py:20
  23.8 9.1 %collective-permute-start.13 = (bf16[2,72,1024]{2,1,0:T(8,128)(2,1)S(1)}, bf16[2,72,1024]{2,1,0:T(8,128)(2,1)S(1)}, u32[]{:S(2)}, u32[]{:S(2)}) collective-permute-start(bf16[2,72,1024]{2,1,0:T(8,128)(2,1)S(1)} %pad_maximum_fusion.refs_0_), channel_id=1, source_target_pairs={{0,16},{4,20},{8,24},{12,28},{16,0},{20,4},{24,8},{28,12},{1,17},{... | collective-permute-start | bytes 884744 | tf_op jit(solution)/shard_map/ppermute | solution.py:20
  24.3 11.5 %collective-permute-start.10 = (bf16[2,24,1024]{2,1,0:T(8,128)(2,1)S(1)}, bf16[2,24,1024]{2,1,0:T(8,128)(2,1)S(1)}, u32[]{:S(2)}, u32[]{:S(2)}) collective-permute-start(bf16[2,24,1024]{2,1,0:T(8,128)(2,1)S(1)} %get-tuple-element.82), channel_id=1, source_target_pairs={{0,3},{1,2},{2,1},{3,0},{4,7},{5,6},{6,5},{7,4},{8,11},{9,10},{10,... | collective-permute-start | bytes 294920 | tf_op jit(solution)/shard_map/ppermute | solution.py:20
  28.6 7.3 %collective-permute-start.11 = (bf16[2,24,1024]{2,1,0:T(8,128)(2,1)S(1)}, bf16[2,24,1024]{2,1,0:T(8,128)(2,1)S(1)}, u32[]{:S(2)}, u32[]{:S(2)}) collective-permute-start(bf16[2,24,1024]{2,1,0:T(8,128)(2,1)S(1)} %get-tuple-element.83), channel_id=1, source_target_pairs={{0,2},{1,3},{2,0},{3,1},{4,6},{5,7},{6,4},{7,5},{8,10},{9,11},{10,... | collective-permute-start | bytes 294920 | tf_op jit(solution)/shard_map/ppermute | solution.py:20
  32.9 6.6 %collective-permute-start.17 = (bf16[2,40,1024]{2,1,0:T(8,128)(2,1)S(1)}, bf16[2,40,1024]{2,1,0:T(8,128)(2,1)S(1)}, u32[]{:S(2)}, u32[]{:S(2)}) collective-permute-start(bf16[2,40,1024]{2,1,0:T(8,128)(2,1)S(1)} %slice.59), channel_id=1, source_target_pairs={{0,8},{4,12},{8,0},{12,4},{16,24},{20,28},{24,16},{28,20},{1,9},{5... | collective-permute-start | bytes 491528 | tf_op jit(solution)/shard_map/ppermute | solution.py:20
  35.9 9.0 %collective-permute-start.14 = (bf16[2,72,1024]{2,1,0:T(8,128)(2,1)S(1)}, bf16[2,72,1024]{2,1,0:T(8,128)(2,1)S(1)}, u32[]{:S(2)}, u32[]{:S(2)}) collective-permute-start(bf16[2,72,1024]{2,1,0:T(8,128)(2,1)S(1)} %pad_maximum_fusion.1.refs_0_), channel_id=1, source_target_pairs={{0,8},{4,12},{8,0},{12,4},{16,24},{20,28},{24,16},{28,20},{1,9},{5... | collective-permute-start | bytes 884744 | tf_op jit(solution)/shard_map/ppermute | solution.py:20
  37.5 8.7 %collective-permute-start.15 = (bf16[2,72,1024]{2,1,0:T(8,128)(2,1)S(1)}, bf16[2,72,1024]{2,1,0:T(8,128)(2,1)S(1)}, u32[]{:S(2)}, u32[]{:S(2)}) collective-permute-start(bf16[2,72,1024]{2,1,0:T(8,128)(2,1)S(1)} %pad_maximum_fusion.1.refs_0_), channel_id=1, source_target_pairs={{0,16},{4,20},{8,24},{12,28},{16,0},{20,4},{24,8},{28,12},{1,17},{... | collective-permute-start | bytes 884744 | tf_op jit(solution)/shard_map/ppermute | solution.py:20
  46.7 7.1 %collective-permute-start.21 = (bf16[2,40,1024]{2,1,0:T(8,128)(2,1)S(1)}, bf16[2,40,1024]{2,1,0:T(8,128)(2,1)S(1)}, u32[]{:S(2)}, u32[]{:S(2)}) collective-permute-start(bf16[2,40,1024]{2,1,0:T(8,128)(2,1)S(1)} %get-tuple-element.106), channel_id=1, source_target_pairs={{0,16},{4,20},{8,24},{12,28},{16,0},{20,4},{24,8},{28,12},{1,17},{... | collective-permute-start | bytes 491528 | tf_op jit(solution)/shard_map/ppermute | solution.py:20
  48.4 8.0 %collective-permute-start.20 = (bf16[2,40,1024]{2,1,0:T(8,128)(2,1)S(1)}, bf16[2,40,1024]{2,1,0:T(8,128)(2,1)S(1)}, u32[]{:S(2)}, u32[]{:S(2)}) collective-permute-start(bf16[2,40,1024]{2,1,0:T(8,128)(2,1)S(1)} %slice.61), channel_id=1, source_target_pairs={{0,8},{4,12},{8,0},{12,4},{16,24},{20,28},{24,16},{28,20},{1,9},{5... | collective-permute-start | bytes 491528 | tf_op jit(solution)/shard_map/ppermute | solution.py:20
  49.9 6.5 %collective-permute-start.19 = (bf16[2,32,1024]{2,1,0:T(8,128)(2,1)S(1)}, bf16[2,32,1024]{2,1,0:T(8,128)(2,1)S(1)}, u32[]{:S(2)}, u32[]{:S(2)}) collective-permute-start(bf16[2,32,1024]{2,1,0:T(8,128)(2,1)S(1)} %slice.60), channel_id=1, source_target_pairs={{0,16},{4,20},{8,24},{12,28},{16,0},{20,4},{24,8},{28,12},{1,17},{... | collective-permute-start | bytes 393224 | tf_op jit(solution)/shard_map/ppermute | solution.py:20
  52.6 8.6 %collective-permute-start.24 = (bf16[2,72,1024]{2,1,0:T(8,128)(2,1)S(1)}, bf16[2,72,1024]{2,1,0:T(8,128)(2,1)S(1)}, u32[]{:S(2)}, u32[]{:S(2)}) collective-permute-start(bf16[2,72,1024]{2,1,0:T(8,128)(2,1)S(1)} %pad_maximum_fusion.3), channel_id=1, source_target_pairs={{0,16},{4,20},{8,24},{12,28},{16,0},{20,4},{24,8},{28,12},{1,17},{... | collective-permute-start | bytes 884744 | tf_op jit(solution)/shard_map/ppermute | solution.py:20
  53.9 9.7 %collective-permute-start.23 = (bf16[2,72,1024]{2,1,0:T(8,128)(2,1)S(1)}, bf16[2,72,1024]{2,1,0:T(8,128)(2,1)S(1)}, u32[]{:S(2)}, u32[]{:S(2)}) collective-permute-start(bf16[2,72,1024]{2,1,0:T(8,128)(2,1)S(1)} %pad_maximum_fusion.2), channel_id=1, source_target_pairs={{0,8},{4,12},{8,0},{12,4},{16,24},{20,28},{24,16},{28,20},{1,9},{5... | collective-permute-start | bytes 884744 | tf_op jit(solution)/shard_map/ppermute | solution.py:20
  62.1 6.4 %collective-permute-start.27 = (bf16[2,40,1024]{2,1,0:T(8,128)(2,1)S(1)}, bf16[2,40,1024]{2,1,0:T(8,128)(2,1)S(1)}, u32[]{:S(2)}, u32[]{:S(2)}) collective-permute-start(bf16[2,40,1024]{2,1,0:T(8,128)(2,1)S(1)} %get-tuple-element.122), channel_id=1, source_target_pairs={{0,16},{4,20},{8,24},{12,28},{16,0},{20,4},{24,8},{28,12},{1,17},{... | collective-permute-start | bytes 491528 | tf_op jit(solution)/shard_map/ppermute | solution.py:20
  63.7 8.5 %collective-permute-start.26 = (bf16[2,24,1024]{2,1,0:T(8,128)(2,1)S(1)}, bf16[2,24,1024]{2,1,0:T(8,128)(2,1)S(1)}, u32[]{:S(2)}, u32[]{:S(2)}) collective-permute-start(bf16[2,24,1024]{2,1,0:T(8,128)(2,1)S(1)} %get-tuple-element.137), channel_id=1, source_target_pairs={{0,8},{4,12},{8,0},{12,4},{16,24},{20,28},{24,16},{28,20},{1,9},{5... | collective-permute-start | bytes 294920 | tf_op jit(solution)/shard_map/ppermute | solution.py:20
  64.4 9.8 %collective-permute-start.25 = (bf16[2,24,1024]{2,1,0:T(8,128)(2,1)S(1)}, bf16[2,24,1024]{2,1,0:T(8,128)(2,1)S(1)}, u32[]{:S(2)}, u32[]{:S(2)}) collective-permute-start(bf16[2,24,1024]{2,1,0:T(8,128)(2,1)S(1)} %get-tuple-element.138), channel_id=1, source_target_pairs={{0,16},{4,20},{8,24},{12,28},{16,0},{20,4},{24,8},{28,12},{1,17},{... | collective-permute-start | bytes 294920 | tf_op jit(solution)/shard_map/ppermute | solution.py:20
  66.4 8.7 %collective-permute-start.32 = (bf16[2,72,1024]{2,1,0:T(8,128)(2,1)S(1)}, bf16[2,72,1024]{2,1,0:T(8,128)(2,1)S(1)}, u32[]{:S(2)}, u32[]{:S(2)}) collective-permute-start(bf16[2,72,1024]{2,1,0:T(8,128)(2,1)S(1)} %pad_maximum_fusion.5), channel_id=1, source_target_pairs={{0,16},{4,20},{8,24},{12,28},{16,0},{20,4},{24,8},{28,12},{1,17},{... | collective-permute-start | bytes 884744 | tf_op jit(solution)/shard_map/ppermute | solution.py:20
  68.6 7.9 %collective-permute-start.31 = (bf16[2,72,1024]{2,1,0:T(8,128)(2,1)S(1)}, bf16[2,72,1024]{2,1,0:T(8,128)(2,1)S(1)}, u32[]{:S(2)}, u32[]{:S(2)}) collective-permute-start(bf16[2,72,1024]{2,1,0:T(8,128)(2,1)S(1)} %pad_maximum_fusion.4), channel_id=1, source_target_pairs={{0,8},{4,12},{8,0},{12,4},{16,24},{20,28},{24,16},{28,20},{1,9},{5... | collective-permute-start | bytes 884744 | tf_op jit(solution)/shard_map/ppermute | solution.py:20
  70.5 6.8 %collective-permute-start.34 = (bf16[2,24,1024]{2,1,0:T(8,128)(2,1)S(1)}, bf16[2,24,1024]{2,1,0:T(8,128)(2,1)S(1)}, u32[]{:S(2)}, u32[]{:S(2)}) collective-permute-start(bf16[2,24,1024]{2,1,0:T(8,128)(2,1)S(1)} %get-tuple-element.135), channel_id=1, source_target_pairs={{0,2},{1,3},{2,0},{3,1},{4,6},{5,7},{6,4},{7,5},{8,10},{9,11},{10,... | collective-permute-start | bytes 294920 | tf_op jit(solution)/shard_map/ppermute | solution.py:20
  72.2 8.1 %collective-permute-start.36 = (bf16[2,24,1024]{2,1,0:T(8,128)(2,1)S(1)}, bf16[2,24,1024]{2,1,0:T(8,128)(2,1)S(1)}, u32[]{:S(2)}, u32[]{:S(2)}) collective-permute-start(bf16[2,24,1024]{2,1,0:T(8,128)(2,1)S(1)} %get-tuple-element.134), channel_id=1, source_target_pairs={{0,3},{1,2},{2,1},{3,0},{4,7},{5,6},{6,5},{7,4},{8,11},{9,10},{10,... | collective-permute-start | bytes 294920 | tf_op jit(solution)/shard_map/ppermute | solution.py:20
  74.2 7.5 %collective-permute-start.29 = (bf16[4,24,1024]{2,1,0:T(8,128)(2,1)S(1)}, bf16[4,24,1024]{2,1,0:T(8,128)(2,1)S(1)}, u32[]{:S(2)}, u32[]{:S(2)}) collective-permute-start(bf16[4,24,1024]{2,1,0:T(8,128)(2,1)S(1)} %pad_maximum_fusion.7), channel_id=1, source_target_pairs={{0,8},{4,12},{8,0},{12,4},{16,24},{20,28},{24,16},{28,20},{1,9},{5... | collective-permute-start | bytes 589832 | tf_op jit(solution)/shard_map/ppermute | solution.py:20
  75.1 6.6 %collective-permute-start.30 = (bf16[4,24,1024]{2,1,0:T(8,128)(2,1)S(1)}, bf16[4,24,1024]{2,1,0:T(8,128)(2,1)S(1)}, u32[]{:S(2)}, u32[]{:S(2)}) collective-permute-start(bf16[4,24,1024]{2,1,0:T(8,128)(2,1)S(1)} %pad_maximum_fusion.8), channel_id=1, source_target_pairs={{0,16},{4,20},{8,24},{12,28},{16,0},{20,4},{24,8},{28,12},{1,17},{... | collective-permute-start | bytes 589832 | tf_op jit(solution)/shard_map/ppermute | solution.py:20
  76.7 10.0 %collective-permute-start.33 = (bf16[4,24,1024]{2,1,0:T(8,128)(2,1)S(1)}, bf16[4,24,1024]{2,1,0:T(8,128)(2,1)S(1)}, u32[]{:S(2)}, u32[]{:S(2)}) collective-permute-start(bf16[4,24,1024]{2,1,0:T(8,128)(2,1)S(1)} %pad_maximum_fusion.9), channel_id=1, source_target_pairs={{0,1},{1,0},{2,3},{3,2},{4,5},{5,4},{6,7},{7,6},{8,9},{9,8},{10,11... | collective-permute-start | bytes 589832 | tf_op jit(solution)/shard_map/ppermute | solution.py:20
  77.4 8.2 %collective-permute-start.35 = (bf16[2,24,1024]{2,1,0:T(8,128)(2,1)S(1)}, bf16[2,24,1024]{2,1,0:T(8,128)(2,1)S(1)}, u32[]{:S(2)}, u32[]{:S(2)}) collective-permute-start(bf16[2,24,1024]{2,1,0:T(8,128)(2,1)S(1)} %get-tuple-element.132), channel_id=1, source_target_pairs={{0,2},{1,3},{2,0},{3,1},{4,6},{5,7},{6,4},{7,5},{8,10},{9,11},{10,... | collective-permute-start | bytes 294920 | tf_op jit(solution)/shard_map/ppermute | solution.py:20
  80.3 6.4 %collective-permute-start.37 = (bf16[2,24,1024]{2,1,0:T(8,128)(2,1)S(1)}, bf16[2,24,1024]{2,1,0:T(8,128)(2,1)S(1)}, u32[]{:S(2)}, u32[]{:S(2)}) collective-permute-start(bf16[2,24,1024]{2,1,0:T(8,128)(2,1)S(1)} %get-tuple-element.131), channel_id=1, source_target_pairs={{0,3},{1,2},{2,1},{3,0},{4,7},{5,6},{6,5},{7,4},{8,11},{9,10},{10,... | collective-permute-start | bytes 294920 | tf_op jit(solution)/shard_map/ppermute | solution.py:20
  (7 other events, 23.9 us)
